TPU v7x, 32 devices: a whole 2x2x4 slice. The times are simulated.
32 devices in a mesh: groups: 2 (over x), blocks: 4 (over y, core), heads: 4 (over z).
Axes of the slice: x: 2, y: 2, z: 4, core: 2. Of those that a mesh axis runs over, the one named last changes fastest.
Arguments:
- queries: bfloat16 [4, 64, 6144], P(None, ('groups', 'blocks'), 'heads'), parts along dimension 1, may hold values from -200 to 200
- key_cache: bfloat16 [64, 128, 6144], P(('groups', 'blocks'), None, 'heads'), parts along dimension 0, may hold values from -6 to 6
- value_cache: bfloat16 [64, 128, 6144], P(('groups', 'blocks'), None, 'heads'), parts along dimension 0, may hold values from -6 to 6
- key_new: bfloat16 [4, 64, 6144], P(None, ('groups', 'blocks'), 'heads'), parts along dimension 1, may hold values from -6 to 6
- value_new: bfloat16 [4, 64, 6144], P(None, ('groups', 'blocks'), 'heads'), parts along dimension 1, may hold values from -6 to 6
- lengths: int32 [64], P(('groups', 'blocks')), parts along dimension 0, may hold values from 32 to 128, as said below
- out_proj: bfloat16 [6144, 6144], P('heads', 'blocks'), may hold values from -0.078125 to 0.078125
- residual: bfloat16 [4, 64, 6144], P(None, 'groups', 'blocks'), parts along dimension 1, may hold values from -12 to 12
- norm_gain: bfloat16 [6144], P('blocks'), may hold values from 0.099609375 to 1.8984375
- hot_up: bfloat16 [64, 6144, 128], P('heads', 'blocks'), may hold values from -0.078125 to 0.078125
- hot_down: bfloat16 [64, 128, 6144], P('heads', None, 'blocks'), may hold values from -0.0625 to 0.0625
- cold_up: bfloat16 [32, 6144, 128], P(('blocks', 'heads')), may hold values from -0.078125 to 0.078125
- cold_down: bfloat16 [32, 128, 6144], P(('blocks', 'heads')), may hold values from -0.25 to 0.25
- block_rows: int32 [8, 4, 2, 32], P('groups', 'heads'), parts along dimension 0, may hold values from 0 to 127, as said below
- block_counts: int32 [8, 4, 2], P('groups', 'heads'), parts along dimension 0, may hold values from 1 to 32, as said below
Outputs:
- attn_state: bfloat16 [4, 64, 6144], P(None, 'groups', 'blocks'), parts along dimension 1
- ffn_out: bfloat16 [4, 64, 6144], P(None, ('groups', 'heads'), 'blocks'), parts along dimension 1
There are 2 independent parts, one for each index of `groups`. A program takes and returns all parts, laid end to end along the dimension named above; an argument that names none is the same for every part. Nothing has to cross between parts.
Inputs may be any that keep to these rules, and one draw needn't show every extreme that they name: `block_rows`: entries beyond block_counts are 0; live entries of one list are distinct row-steps t * 32 + r. `block_counts`: some cold block has exactly 32 live entries. `lengths`: some row has all 128 slots live.
All inputs are finite; a program needn't handle non-finite values.
Results may differ from a plain program's by a relative error of at most 0.017.
Values may be sent and summed in bfloat16 or wider, within the bound.
No kernel may reach another device: no remote copies, remote signals or barrier semaphores. Data moves between devices by JAX's collectives and lax.ppermute only.
A program may use at most 128 MiB of HBM per device.

v0:
```python
import math

import jax
import jax.numpy as jnp
from jax import lax
from jax.sharding import PartitionSpec as P

HD = 128
D = 6144


def local(
    queries,
    key_cache,
    value_cache,
    key_new,
    value_new,
    lengths,
    out_proj,
    residual,
    norm_gain,
    hot_up,
    hot_down,
    cold_up,
    cold_down,
    block_rows,
    block_counts,
):
    steps, rows_here, width_here = queries.shape
    heads_here = width_here // HD
    context = key_cache.shape[1]
    query_heads = queries.reshape(steps, rows_here, heads_here, HD)
    cached_keys = key_cache.reshape(rows_here, context, heads_here, HD)
    cached_values = value_cache.reshape(rows_here, context, heads_here, HD)
    recent_keys = key_new.reshape(steps, rows_here, heads_here, HD)
    recent_values = value_new.reshape(steps, rows_here, heads_here, HD)
    factor = 1.0 / math.sqrt(HD)
    old_scores = (
        jnp.einsum("trhd,rphd->trhp", query_heads, cached_keys, preferred_element_type=jnp.float32)
        * factor
    )
    visible = jnp.arange(context)[None, :] < lengths[:, None]
    old_scores = jnp.where(visible[None, :, None, :], old_scores, -jnp.inf)
    new_scores = (
        jnp.einsum("trhd,srhd->trhs", query_heads, recent_keys, preferred_element_type=jnp.float32)
        * factor
    )
    causal = jnp.arange(steps)[None, :] <= jnp.arange(steps)[:, None]
    new_scores = jnp.where(causal[:, None, None, :], new_scores, -jnp.inf)
    highest = jnp.maximum(jnp.max(old_scores, axis=-1), jnp.max(new_scores, axis=-1))[..., None]
    old_weights = jnp.exp(old_scores - highest)
    new_weights = jnp.exp(new_scores - highest)
    denominator = jnp.sum(old_weights, axis=-1, keepdims=True) + jnp.sum(
        new_weights, axis=-1, keepdims=True
    )
    old_probs = (old_weights / denominator).astype(jnp.bfloat16)
    new_probs = (new_weights / denominator).astype(jnp.bfloat16)
    attended = jnp.einsum(
        "trhp,rphd->trhd", old_probs, cached_values, preferred_element_type=jnp.float32
    )
    attended = attended + jnp.einsum(
        "trhs,srhd->trhd", new_probs, recent_values, preferred_element_type=jnp.float32
    )
    attended = attended.reshape(steps, rows_here, width_here).astype(jnp.bfloat16)
    partial_out = jnp.einsum(
        "trk,kc->trc",
        lax.all_gather(attended, "blocks", axis=1, tiled=True),
        out_proj,
        preferred_element_type=jnp.float32,
    )
    summed = lax.psum(partial_out.astype(jnp.bfloat16), "heads").astype(jnp.float32)
    state = (residual.astype(jnp.float32) + summed).astype(jnp.bfloat16)
    state_wide = state.astype(jnp.float32)
    mean_row = lax.psum(jnp.sum(state_wide, axis=-1), "blocks") / D
    centred = state_wide - mean_row[..., None]
    variance = lax.psum(jnp.sum(centred * centred, axis=-1), "blocks") / D
    normed = (
        centred * lax.rsqrt(variance + 1e-05)[..., None] * norm_gain.astype(jnp.float32)
    ).astype(jnp.bfloat16)
    hot_inputs = jnp.einsum("trc,kch->trkh", normed, hot_up, preferred_element_type=jnp.float32)
    hot_total = lax.psum(hot_inputs.astype(jnp.bfloat16), "blocks").astype(jnp.float32)
    hot_hidden = jnp.maximum(hot_total, 0.0).astype(jnp.bfloat16)
    hot_sum = jnp.einsum("trkh,khc->trc", hot_hidden, hot_down, preferred_element_type=jnp.float32)
    all_rows = normed.shape[1]
    slice_width = normed.shape[2]
    flat_rows = normed.reshape(steps * all_rows, slice_width)
    slot_rows = block_rows[:, 0]
    slot_counts = block_counts[:, 0]
    outgoing = flat_rows[slot_rows]
    hidden = jnp.maximum(
        jnp.einsum(
            "ocnd,cdh->ocnh",
            lax.all_to_all(outgoing, "blocks", split_axis=0, concat_axis=3, tiled=True),
            cold_up,
            preferred_element_type=jnp.float32,
        ),
        0.0,
    ).astype(jnp.bfloat16)
    made = jnp.einsum(
        "ocnh,chd->ocnd", hidden, cold_down, preferred_element_type=jnp.float32
    ).astype(jnp.bfloat16)
    returned = lax.all_to_all(made, "blocks", split_axis=3, concat_axis=0, tiled=True)
    keep = jnp.arange(returned.shape[2])[None, None, :] < slot_counts[..., None]
    gained = jnp.where(keep[..., None], returned.astype(jnp.float32), 0.0)
    cold_sum = (
        jnp.zeros((steps * all_rows, slice_width), jnp.float32)
        .at[slot_rows.reshape(-1)]
        .add(gained.reshape(-1, slice_width))
    )
    total = cold_sum.reshape(steps, all_rows, slice_width) + hot_sum
    ffn_out = lax.psum_scatter(total.astype(jnp.bfloat16), "heads", scatter_dimension=1, tiled=True)
    return (state, ffn_out)


def solution(mesh):
    placed = (
        P(None, ("groups", "blocks"), "heads"),
        P(("groups", "blocks"), None, "heads"),
        P(("groups", "blocks"), None, "heads"),
        P(None, ("groups", "blocks"), "heads"),
        P(None, ("groups", "blocks"), "heads"),
        P(("groups", "blocks")),
        P("heads", "blocks"),
        P(None, "groups", "blocks"),
        P("blocks"),
        P("heads", "blocks", None),
        P("heads", None, "blocks"),
        P(("blocks", "heads"), None, None),
        P(("blocks", "heads"), None, None),
        P("groups", "heads", None, None),
        P("groups", "heads", None),
    )
    return jax.shard_map(
        local,
        mesh=mesh,
        in_specs=placed,
        out_specs=(P(None, "groups", "blocks"), P(None, ("groups", "heads"), "blocks")),
        check_vma=False,
    )
```

profile of v0, /device:TPU:0, one launch (start us, length us, event | category | flops | bytes accessed | tf_op | source)
XLA Modules:
  0.0 209.9 jit_solution(15196492291898842520)
XLA Ops:
  7.2 0.0 copy-start
  7.2 0.0 all-reduce.3.cloned.1.call-start
  7.2 0.0 copy-start.10
  7.2 4.8 %copy.66 = bf16[8,128,1536]{1,2,0:T(8,128)(2,1)} copy(bf16[8,128,1536]{2,1,0:T(8,128)(2,1)} %param.16) | data formatting | bytes 6291456 | tf_op args[1]
  12.0 0.0 copy-done.10
  12.1 0.1 iota_compare_fusion.1
  12.1 2.9 %fusion.52 = (f32[4,8,12]{0,2,1:T(8,128)S(1)}, f32[4,8,12,128]{3,0,2,1:T(4,128)S(1)}) fusion(bf16[8,128,12,128]{1,3,2,0:T(8,128)(2,1)} %bitcast.88, bf16[4,8,12,128]{3,1,2,0:T(8,128)(2,1)} %bitcast.96, pred[8,128]{1,0:T(8,128)(4,1)S(1)} %iota_compare_fusion.1), kind=kOutput, calls=%fused_computation.67 | convolution fusion | flops 12729984 | bytes 3443200 | tf_op jit(solution)/shard_map/trhd,rphd->trhp/dot_general | solution.py:39
  15.1 0.0 copy-done.7
  15.1 0.0 copy-done.8
  15.1 0.3 fusion.53
  15.4 0.0 copy-start.2
  15.4 0.3 fusion.38
  15.7 0.3 copy-done.2
  16.1 0.2 fusion.39
  16.2 4.6 %copy.71 = bf16[8,128,1536]{1,2,0:T(8,128)(2,1)} copy(bf16[8,128,1536]{2,1,0:T(8,128)(2,1)} %param.17) | data formatting | bytes 6291456 | tf_op args[2]
  20.9 3.7 %fusion.40 = f32[8,12,4,128]{3,2,1,0:T(4,128)S(1)} fusion(bf16[8,128,12,128]{1,3,2,0:T(8,128)(2,1)} %bitcast.87, f32[4,8,12,128]{3,0,2,1:T(4,128)S(1)} %get-tuple-element.5, f32[4,8,12]{0,2,1:T(8,128)S(1)} %add.62, f32[4,8,12]{0,2,1:T(8,128)S(1)} %max.22), kind=kOutput, calls=%fused_computation.46 | convolution fusion | flops 12730368 | bytes 3542016 | tf_op jit(solution)/shard_map/trhp,rphd->trhd/dot_general | solution.py:58
  24.6 0.0 copy-done.3
  24.6 0.3 fusion.27
  25.0 7.9 %all_gather.3 = bf16[4,32,1536]{2,1,0:T(8,128)(2,1)S(1)} all-gather(bf16[4,8,1536]{2,1,0:T(8,128)(2,1)S(1)} %bitcast.93), channel_id=1, replica_groups=mesh['groups'=2,'blocks'=4,'heads'=4] {'blocks'}, dimensions={1}, use_global_device_ids=true | all-gather | bytes 491520 | tf_op jit(solution)/shard_map/all_gather | solution.py:67
  32.9 3.9 %fusion.13 = bf16[4,32,1536]{2,1,0:T(8,128)(2,1)} fusion(bf16[4,32,1536]{2,1,0:T(8,128)(2,1)S(1)} %all_gather.3, bf16[1536,1536]{1,0:T(8,128)(2,1)} %param.21), kind=kOutput, calls=%fused_computation.12 | convolution fusion | flops 604176384 | bytes 5505024 | tf_op jit(solution)/shard_map/trk,kc->trc/dot_general | solution.py:65
  36.8 0.0 all-reduce.3.cloned.1.call-update
  36.8 0.0 copy-done.6
  36.9 0.1 reshape.163
  37.0 38.0 %all-reduce.3.cloned.1.call-done = bf16[4,32,1536]{2,1,0:T(8,128)(2,1)} async-done(((bf16[4,32,1536]{2,1,0:T(8,128)(2,1)}), bf16[4,32,1536]{2,1,0:T(8,128)(2,1)}) %all-reduce.3.cloned.1.call-update) | async-done | bytes 393232 | tf_op jit(solution)/shard_map/psum | solution.py:71
  75.0 1.3 convert_reduce_fusion
  76.3 6.2 %psum.29 = f32[4,32]{1,0:T(4,128)} all-reduce(f32[4,32]{1,0:T(4,128)S(1)} %get-tuple-element.2), channel_id=1, replica_groups=mesh['groups'=2,'blocks'=4,'heads'=4] {'blocks'}, use_global_device_ids=true, to_apply=%region_6.7 | all-reduce | flops 128 | bytes 1024 | tf_op jit(solution)/shard_map/psum | solution.py:74
  82.6 0.7 broadcast_multiply_fusion
  83.2 0.8 fusion.31
  84.1 7.3 %psum.30 = f32[4,32]{1,0:T(4,128)} all-reduce(f32[4,32]{1,0:T(4,128)} %fusion.31), channel_id=1, replica_groups=mesh['groups'=2,'blocks'=4,'heads'=4] {'blocks'}, use_global_device_ids=true, to_apply=%region_8.9 | all-reduce | flops 128 | bytes 1024 | tf_op jit(solution)/shard_map/psum | solution.py:76
  91.4 0.7 add_rsqrt_fusion
  92.1 1.3 fusion.33
  93.4 0.0 copy-start.5
  93.4 2.2 %gather_fusion = bf16[256,1536]{1,0:T(8,128)(2,1)} fusion(bf16[128,1536]{1,0:T(8,128)(2,1)S(1)} %bitcast.82, s32[1024]{0:T(1024)S(1)} %pad_clamp_fusion), kind=kCustom, calls=%fused_computation | custom fusion | bytes 1573888 | tf_op jit(solution)/shard_map/gather | solution.py:89
  95.6 4.2 %all-to-all-start = ((bf16[4,2,32,1536]{3,2,1,0:T(8,128)(2,1)}), bf16[4,2,32,1536]{3,2,1,0:T(8,128)(2,1)}, u32[]{:S(2)}, u32[]{:S(2)}) async-start(bf16[4,2,32,1536]{3,2,1,0:T(8,128)(2,1)} %bitcast.86), calls=%async_computation | async-start | bytes 1572864 | tf_op jit(solution)/shard_map/all_to_all | solution.py:93
  99.8 0.1 reshape_squeeze.3
  99.8 0.8 copy.76
  100.6 0.1 iota_compare_fusion
  100.7 0.1 lt.74
  100.8 10.7 %all-to-all-done = bf16[4,2,32,1536]{3,2,1,0:T(8,128)(2,1)} async-done(((bf16[4,2,32,1536]{3,2,1,0:T(8,128)(2,1)}), bf16[4,2,32,1536]{3,2,1,0:T(8,128)(2,1)}, u32[]{:S(2)}, u32[]{:S(2)}) %all-to-all-start) | async-done | bytes 786464 | tf_op jit(solution)/shard_map/all_to_all | solution.py:93
  111.5 2.6 %copy.77 = bf16[1,2,32,4,1536]{4,3,2,1,0:T(4,128)(2,1)} copy(bf16[1,2,32,4,1536]{4,2,1,3,0:T(8,128)(2,1)} %bitcast.16) | data formatting | bytes 1572864 | tf_op jit(solution)/shard_map/all_to_all | solution.py:93
  114.1 2.8 %reshape.157 = bf16[2,32,6144]{2,1,0:T(8,128)(2,1)} reshape(bf16[1,2,32,4,1536]{4,3,2,1,0:T(4,128)(2,1)} %copy.77) | data formatting | bytes 1572864 | tf_op jit(solution)/shard_map/reshape
  116.9 4.0 %fusion = bf16[1,2,32,6144]{3,2,1,0:T(8,128)(2,1)} fusion(bf16[2,128,6144]{2,1,0:T(8,128)(2,1)S(1)} %copy-done, bf16[2,32,6144]{2,1,0:T(8,128)(2,1)} %reshape.157, bf16[2,6144,128]{2,1,0:T(8,128)(2,1)} %param.26), kind=kOutput, calls=%fused_computation.3 | convolution fusion | flops 201736192 | bytes 7864320 | tf_op jit(solution)/shard_map/ocnh,chd->ocnd/dot_general | solution.py:99
  120.9 7.2 %copy.78 = bf16[1,2,32,6144]{2,1,0,3:T(2,128)(2,1)} copy(bf16[1,2,32,6144]{3,2,1,0:T(8,128)(2,1)} %fusion) | data formatting | bytes 1572864 | tf_op jit(solution)/shard_map/convert_element_type | solution.py:101
  128.2 5.4 %reshape.187 = bf16[4,2,49152]{2,1,0:T(2,128)(2,1)} reshape(bf16[6144,1,2,32]{3,2,1,0:T(2,128)(2,1)} %bitcast.83) | data formatting | bytes 1572864
  133.6 4.2 %all-to-all-start.1 = ((bf16[4,2,49152]{2,1,0:T(2,128)(2,1)}), bf16[4,2,49152]{2,1,0:T(2,128)(2,1)}, u32[]{:S(2)}, u32[]{:S(2)}) async-start(bf16[4,2,49152]{2,1,0:T(2,128)(2,1)} %reshape.187), calls=%async_computation.1 | async-start | bytes 1572864 | tf_op jit(solution)/shard_map/all_to_all | solution.py:102
  137.8 0.0 all-reduce.5.cloned.1.call-start
  137.9 4.6 %fusion.19 = bf16[4,32,16,128]{3,1,2,0:T(8,128)(2,1)} fusion(bf16[16,1536,128]{2,1,0:T(8,128)(2,1)} %param.24, bf16[4,32,1536]{2,1,0:T(8,128)(2,1)S(1)} %fusion.33), kind=kOutput, calls=%fused_computation.15 | convolution fusion | flops 805568512 | bytes 7208960 | tf_op jit(solution)/shard_map/trc,kch->trkh/dot_general | solution.py:80
  142.5 0.0 all-reduce.5.cloned.1.call-update
  142.5 0.2 reduce-scatter.4.cloned.1.call-start
  142.7 6.8 %all-to-all-done.1 = bf16[4,2,49152]{2,1,0:T(2,128)(2,1)} async-done(((bf16[4,2,49152]{2,1,0:T(2,128)(2,1)}), bf16[4,2,49152]{2,1,0:T(2,128)(2,1)}, u32[]{:S(2)}, u32[]{:S(2)}) %all-to-all-start.1) | async-done | bytes 786464 | tf_op jit(solution)/shard_map/all_to_all | solution.py:102
  149.5 4.5 %reshape.188 = bf16[6144,1,2,32]{3,2,1,0:T(2,128)(2,1)} reshape(bf16[4,2,49152]{2,1,0:T(2,128)(2,1)} %all-to-all-done.1) | data formatting | bytes 1572864
  154.0 7.2 %copy.79 = bf16[1,2,32,6144]{3,2,1,0:T(8,128)(2,1)} copy(bf16[1,2,32,6144]{2,1,0,3:T(2,128)(2,1)} %bitcast.84) | data formatting | bytes 1572864 | tf_op jit(solution)/shard_map/all_to_all | solution.py:102
  161.2 3.1 %reshape.160 = f32[1,2,32,4,1536]{4,3,2,1,0:T(4,128)} reshape(bf16[1,2,32,6144]{3,2,1,0:T(8,128)(2,1)} %copy.79) | data formatting | bytes 2359296 | tf_op jit(solution)/shard_map/convert_element_type | solution.py:104
  164.4 1.9 copy.80
  166.3 1.3 bitcast_select_fusion
  167.6 4.8 %scatter_custom_fusion = f32[128,1536]{1,0:T(8,128)} fusion(s32[256]{0:T(256)S(1)} %bitcast.95, f32[256,1536]{1,0:T(8,128)} %bitcast_select_fusion, f32[]{:T(128)} %constant.9.clone.1), kind=kCustom, calls=%fused_computation.38 | custom fusion | flops 393216 | bytes 786944 | tf_op jit(solution)/shard_map/scatter-add | solution.py:108
  172.4 3.4 %all-reduce.5.cloned.1.call-done = bf16[4,32,16,128]{3,1,2,0:T(8,128)(2,1)} async-done(((bf16[4,32,16,128]{3,1,2,0:T(8,128)(2,1)}), bf16[4,32,16,128]{3,1,2,0:T(8,128)(2,1)}) %all-reduce.5.cloned.1.call-update) | async-done | bytes 524304 | tf_op jit(solution)/shard_map/psum | solution.py:81
  175.8 4.1 %fusion.16 = bf16[4,32,1536]{2,1,0:T(8,128)(2,1)S(1)} fusion(f32[4,32,1536]{2,1,0:T(8,128)} %bitcast.89, bf16[16,128,1536]{2,1,0:T(8,128)(2,1)} %param.25, bf16[4,32,16,128]{3,1,2,0:T(8,128)(2,1)} %all-reduce.5.cloned.1.call-done), kind=kOutput, calls=%fused_computation.13 | convolution fusion | flops 806486016 | bytes 7995392 | tf_op jit(solution)/shard_map/trkh,khc->trc/dot_general | solution.py:83
  179.9 0.3 copy.86
  180.2 0.8 copy.88
  181.0 0.0 reduce-scatter.4.cloned.1.call-update
  181.1 20.7 %reduce-scatter.4.cloned.1.call-done = bf16[8,6144]{1,0:T(8,128)(2,1)} async-done(((bf16[32,6144]{1,0:T(8,128)(2,1)}), bf16[8,6144]{1,0:T(8,128)(2,1)}) %reduce-scatter.4.cloned.1.call-update) | async-done | bytes 98320
  201.8 0.9 reshape.184
  202.8 0.7 copy.87
  (20 shorter events, 0.1 us)
Async XLA Ops:
  7.2 109.7 %copy-start = (bf16[2,128,6144]{2,1,0:T(8,128)(2,1)S(1)}, bf16[2,128,6144]{2,1,0:T(8,128)(2,1)}, u32[]{:S(2)}) copy-start(bf16[2,128,6144]{2,1,0:T(8,128)(2,1)} %param.27) | copy-start | bytes 9437188
  7.2 67.8 %all-reduce.3.cloned.1.call-start = ((), (), s32[]{:S(2)}) async-start(), calls=%async_computation.3 | async-start | bytes 786432 | tf_op jit(solution)/shard_map/psum | solution.py:71
  7.2 4.8 %copy-start.10 = (s32[8]{0:T(128)S(1)}, s32[8]{0:T(128)}, u32[]{:S(2)}) copy-start(s32[8]{0:T(128)} %param.20) | copy-start | bytes 100
  12.1 3.0 %copy-start.7 = (bf16[4,8,1536]{2,1,0:T(8,128)(2,1)S(1)}, bf16[4,8,1536]{2,1,0:T(8,128)(2,1)}, u32[]{:S(2)}) copy-start(bf16[4,8,1536]{2,1,0:T(8,128)(2,1)} %param.15) | copy-start | bytes 294916
  12.1 3.0 %copy-start.8 = (bf16[4,8,1536]{2,1,0:T(8,128)(2,1)S(1)}, bf16[4,8,1536]{2,1,0:T(8,128)(2,1)}, u32[]{:S(2)}) copy-start(bf16[4,8,1536]{2,1,0:T(8,128)(2,1)} %param.18) | copy-start | bytes 294916
  15.4 0.7 copy-start.2
  20.9 3.7 %copy-start.3 = (f32[4,8,12,4]{0,3,2,1:T(4,128)S(1)}, f32[4,8,12,4]{0,3,2,1:T(4,128)}, u32[]{:S(2)}) copy-start(f32[4,8,12,4]{0,3,2,1:T(4,128)} %copy-done.2) | copy-start | bytes 18436
  20.9 3.7 %copy-start.9 = (bf16[4,8,1536]{2,1,0:T(8,128)(2,1)S(1)}, bf16[4,8,1536]{2,1,0:T(8,128)(2,1)}, u32[]{:S(2)}) copy-start(bf16[4,8,1536]{2,1,0:T(8,128)(2,1)} %param.19) | copy-start | bytes 294916
  32.9 3.9 %copy-start.6 = (bf16[1536]{0:T(1024)(128)(2,1)S(1)}, bf16[1536]{0:T(1024)(128)(2,1)}, u32[]{:S(2)}) copy-start(bf16[1536]{0:T(1024)(128)(2,1)} %param.23) | copy-start | bytes 9220
  32.9 4.0 %copy-start.4 = (s32[4,1,2,32]{3,2,1,0:T(2,128)S(1)}, s32[4,1,2,32]{3,2,1,0:T(2,128)}, u32[]{:S(2)}) copy-start(s32[4,1,2,32]{3,2,1,0:T(2,128)} %param.28) | copy-start | bytes 3076
  76.3 15.1 %copy-start.1 = (bf16[4,32,1536]{2,1,0:T(8,128)(2,1)}, bf16[4,32,1536]{2,1,0:T(8,128)(2,1)S(1)}, u32[]{:S(2)}) copy-start(bf16[4,32,1536]{2,1,0:T(8,128)(2,1)S(1)} %get-tuple-element.3) | copy-start | bytes 1179652
  93.4 6.4 %copy-start.5 = (s32[4,1,2,32]{3,2,1,0:T(2,128)S(1)}, s32[4,1,2,32]{3,2,1,0:T(2,128)}, u32[]{:S(2)}) copy-start(s32[4,1,2,32]{3,2,1,0:T(2,128)} %param.28) | copy-start | bytes 3076
  95.6 15.9 %all-to-all-start = ((bf16[4,2,32,1536]{3,2,1,0:T(8,128)(2,1)}), bf16[4,2,32,1536]{3,2,1,0:T(8,128)(2,1)}, u32[]{:S(2)}, u32[]{:S(2)}) async-start(bf16[4,2,32,1536]{3,2,1,0:T(8,128)(2,1)} %bitcast.86), calls=%async_computation | async-start | bytes 1572864 | tf_op jit(solution)/shard_map/all_to_all | solution.py:93
  133.6 15.9 %all-to-all-start.1 = ((bf16[4,2,49152]{2,1,0:T(2,128)(2,1)}), bf16[4,2,49152]{2,1,0:T(2,128)(2,1)}, u32[]{:S(2)}, u32[]{:S(2)}) async-start(bf16[4,2,49152]{2,1,0:T(2,128)(2,1)} %reshape.187), calls=%async_computation.1 | async-start | bytes 1572864 | tf_op jit(solution)/shard_map/all_to_all | solution.py:102
  137.8 38.0 %all-reduce.5.cloned.1.call-start = ((), (), s32[]{:S(2)}) async-start(), calls=%async_computation.4 | async-start | bytes 1048576 | tf_op jit(solution)/shard_map/psum | solution.py:81
  142.5 59.3 %reduce-scatter.4.cloned.1.call-start = ((), (), s32[]{:S(2)}) async-start(), calls=%async_computation.5 | async-start | bytes 491520
Sparse Core Ops, SparseCore 0:
  37.0 37.9 all-reduce.2
  142.6 33.1 all-reduce.4
  181.2 20.5 reduce-scatter.3
where the time goes:
time: 211 us; the launch traced here: 210 us
  waiting for transfers between devices  79.7 us (38%)
  local copies, waits for them, and re-layouts  50.6 us (24%)
  matrix products  23.9 us (11%)
  blocking collectives  21.5 us (10%)
  between operations  13.9 us (7%)
  other arithmetic  11.6 us (5%)
  starting transfers between devices  8.68 us (4%)
    psum x1, waiting for transfers between devices, local(): lax.psum(partial_out.astype(jnp.bfloat16), 'heads').astype(jnp.float32)  38 us
    unnamed x30, local copies, waits for them, and re-layouts  22.5 us
    unnamed x4, waiting for transfers between devices  20.8 us
    all_to_all x1, waiting for transfers between devices, local(): lax.all_to_all(outgoing, 'blocks', split_axis=0, concat_axis=3, tiled=True)  10.7 us
    all_gather x1, blocking collectives, local(): lax.all_gather(attended, 'blocks', axis=1, tiled=True)  7.94 us
    psum x1, blocking collectives, local(): variance = lax.psum(jnp.sum(centred * centred, axis=-1), 'blocks') / D  7.33 us
    convert_element_type x1, local copies, waits for them, and re-layouts, local(): made = jnp.einsum('ocnh,chd->ocnd', hidden, cold_down, preferred_element_...  7.24 us
    all_to_all x1, local copies, waits for them, and re-layouts, local(): lax.all_to_all(made, 'blocks', split_axis=3, concat_axis=0, tiled=True)  7.19 us
  transfers between devices with their start and end apart: 5, of which 5 were waited for; matrix products, arithmetic and copies ran while one was open for 14% of the time, Pallas kernels for 0%

commit v1 on v0

--- a/solution.py
+++ b/solution.py
@@ -1,8 +1,11 @@
+import functools
 import math
 
 import jax
 import jax.numpy as jnp
 from jax import lax
+from jax.experimental import pallas as pl
+from jax.experimental.pallas import tpu as pltpu
 from jax.sharding import PartitionSpec as P
 
 HD = 128
@@ -112,6 +115,384 @@
     return (state, ffn_out)
 
 
+def params(**more):
+    return pltpu.CompilerParams(vmem_limit_bytes=40 * 2**20, **more)
+
+
+def attention_kernel(lengths, q_ref, k_ref, v_ref, kn_ref, vn_ref, out_ref, *, here, steps, context):
+    rows = steps * here
+    wide = q_ref.shape[1]
+    parts = wide // HD
+    q = q_ref[...]
+    lane_head = lax.broadcasted_iota(jnp.int32, (rows, wide), 1) // HD
+    split = jnp.concatenate(
+        [jnp.where(lane_head == i, q, jnp.zeros_like(q)) for i in range(parts)], axis=0
+    )
+    nt = (((1,), (1,)), ((), ()))
+    scores = lax.dot_general(split, k_ref[...], nt, preferred_element_type=jnp.float32)
+    row = lax.broadcasted_iota(jnp.int32, (parts * rows, context), 0) % here
+    slot = lax.broadcasted_iota(jnp.int32, (parts * rows, context), 1)
+    limit = jnp.zeros_like(slot)
+    own = scores[:, :context]
+    for r in range(here):
+        limit = jnp.where(row == r, lengths[r], limit)
+        if r:
+            own = jnp.where(row == r, scores[:, r * context : (r + 1) * context], own)
+    factor = 1.0 / math.sqrt(HD)
+    own = jnp.where(slot < limit, own * factor, -jnp.inf)
+    fresh = lax.dot_general(split, kn_ref[...], nt, preferred_element_type=jnp.float32) * factor
+    at = lax.broadcasted_iota(jnp.int32, (parts * rows, rows), 0) % rows
+    to = lax.broadcasted_iota(jnp.int32, (parts * rows, rows), 1)
+    seen = (at % here == to % here) & (to // here <= at // here)
+    fresh = jnp.where(seen, fresh, -jnp.inf)
+    top = jnp.maximum(
+        jnp.max(own, axis=-1, keepdims=True), jnp.max(fresh, axis=-1, keepdims=True)
+    )
+    own = jnp.exp(own - top)
+    fresh = jnp.exp(fresh - top)
+    scale = 1.0 / (
+        jnp.sum(own, axis=-1, keepdims=True) + jnp.sum(fresh, axis=-1, keepdims=True)
+    )
+    own = own * scale
+    spread = jnp.concatenate(
+        [jnp.where(row == r, own, 0.0).astype(jnp.bfloat16) for r in range(here)], axis=1
+    )
+    got = jnp.dot(spread, v_ref[...], preferred_element_type=jnp.float32)
+    got = got + jnp.dot(
+        (fresh * scale).astype(jnp.bfloat16), vn_ref[...], preferred_element_type=jnp.float32
+    )
+    answer = got[:rows]
+    for i in range(1, parts):
+        answer = jnp.where(lane_head == i, got[i * rows : (i + 1) * rows], answer)
+    out_ref[...] = answer.astype(jnp.bfloat16)
+
+
+def attention(queries, key_cache, value_cache, key_new, value_new, lengths):
+    steps, here, width = queries.shape
+    context = key_cache.shape[1]
+    wide = 2 * HD
+    small = pl.BlockSpec((steps * here, wide), lambda i, *_: (0, i))
+    large = pl.BlockSpec((here * context, wide), lambda i, *_: (0, i))
+    flat = lambda a: a.reshape(-1, width)
+    return pl.pallas_call(
+        functools.partial(attention_kernel, here=here, steps=steps, context=context),
+        grid_spec=pltpu.PrefetchScalarGridSpec(
+            num_scalar_prefetch=1,
+            grid=(width // wide,),
+            in_specs=[small, large, large, small, small],
+            out_specs=small,
+        ),
+        out_shape=jax.ShapeDtypeStruct((steps * here, width), jnp.bfloat16),
+        compiler_params=params(),
+        name="attention",
+    )(lengths, flat(queries), flat(key_cache), flat(value_cache), flat(key_new), flat(value_new))
+
+
+def project_kernel(place, rows_ref, weight_ref, *outs):
+    chunk = outs[0].shape[0]
+    rows = jnp.concatenate(
+        [
+            rows_ref[pl.ds(pl.multiple_of((place[0] ^ m) * chunk, chunk), chunk), :]
+            for m in range(len(outs))
+        ],
+        axis=0,
+    )
+    made = jnp.dot(rows, weight_ref[...], preferred_element_type=jnp.float32)
+    for m, out in enumerate(outs):
+        out[...] = made[m * chunk : (m + 1) * chunk].astype(out.dtype)
+
+
+def project(place, rows, weight, parts):
+    total, depth = rows.shape
+    width = weight.shape[1]
+    chunk = total // parts
+    wide = width // 3
+    return pl.pallas_call(
+        project_kernel,
+        grid_spec=pltpu.PrefetchScalarGridSpec(
+            num_scalar_prefetch=1,
+            grid=(width // wide,),
+            in_specs=[
+                pl.BlockSpec((total, depth), lambda i, *_: (0, 0)),
+                pl.BlockSpec((depth, wide), lambda i, *_: (0, i)),
+            ],
+            out_specs=[pl.BlockSpec((chunk, wide), lambda i, *_: (0, i))] * parts,
+        ),
+        out_shape=[
+            jax.ShapeDtypeStruct((chunk, width), jnp.bfloat16 if m else jnp.float32)
+            for m in range(parts)
+        ],
+        compiler_params=params(),
+        name="project",
+    )(place, rows, weight)
+
+
+def join_kernel(residual, mine, *refs):
+    state_ref, mean_ref, spread_ref = refs[-3:]
+    total = residual[...].astype(jnp.float32) + mine[...]
+    for ref in refs[:-3]:
+        total = total + ref[...].astype(jnp.float32)
+    state = total.astype(jnp.bfloat16)
+    state_ref[...] = state
+    wide = state.astype(jnp.float32)
+    mean = jnp.mean(wide, axis=-1, keepdims=True)
+    off = wide - mean
+    mean_ref[...] = jnp.broadcast_to(mean, mean_ref.shape)
+    spread_ref[...] = jnp.broadcast_to(jnp.sum(off * off, axis=-1, keepdims=True), mean_ref.shape)
+
+
+def join(residual, mine, others):
+    chunk, width = mine.shape
+    stat = jax.ShapeDtypeStruct((chunk, HD), jnp.float32)
+    return pl.pallas_call(
+        join_kernel,
+        out_shape=[jax.ShapeDtypeStruct((chunk, width), jnp.bfloat16), stat, stat],
+        compiler_params=params(),
+        name="join",
+    )(residual, mine, *others)
+
+
+def up_kernel(place, *refs, parts, hot_steps):
+    states, stats = refs[:parts], refs[parts : 2 * parts]
+    gain_ref, hot_ref, near_ref, first_ref, second_ref, out_ref, normed = refs[2 * parts :]
+    step = pl.program_id(0)
+    y, g = place[1], place[2]
+
+    @pl.when(step == 0)
+    def _():
+        gain = gain_ref[...].astype(jnp.float32)
+        chunk = states[0].shape[0]
+        for m in range(parts):
+            mean = stats[m][0, :, :1]
+            variance = stats[m][1, :, :1] / D
+            off = states[m][...].astype(jnp.float32) - mean
+            normed[m * chunk : (m + 1) * chunk, :] = (
+                off * lax.rsqrt(variance + 1e-05) * gain
+            ).astype(jnp.bfloat16)
+
+    def put(first, second, column):
+        weight = jnp.concatenate([first, second], axis=1)
+        made = jnp.dot(normed[...], weight, preferred_element_type=jnp.float32)
+        at = pl.multiple_of(column * 2 * HD, 2 * HD)
+        out_ref[:, pl.ds(at, 2 * HD)] = made.astype(out_ref.dtype)
+
+    @pl.when(step < hot_steps)
+    def _():
+        put(hot_ref[0], hot_ref[1], step)
+
+    @pl.when(step == hot_steps)
+    def _():
+        put(near_ref[g], near_ref[1 - g], hot_steps + y)
+
+    @pl.when(step == hot_steps + 1)
+    def _():
+        put(first_ref[...], second_ref[...], hot_steps + 1 - y)
+
+
+def up(place, half, states, stats, gain, hot, near, first, second):
+    parts = len(states)
+    chunk, width = states[0].shape
+    hot_steps = hot.shape[0] // 4
+    whole = lambda a: pl.BlockSpec(a.shape, lambda i, *_: (0,) * a.ndim)
+    columns = (2 * hot_steps + 4) * HD
+    return pl.pallas_call(
+        functools.partial(up_kernel, parts=parts, hot_steps=hot_steps),
+        grid_spec=pltpu.PrefetchScalarGridSpec(
+            num_scalar_prefetch=1,
+            grid=(hot_steps + 2,),
+            in_specs=[whole(a) for a in states]
+            + [whole(a) for a in stats]
+            + [
+                whole(gain),
+                pl.BlockSpec(
+                    (2, width, HD),
+                    lambda i, place: (
+                        (place[3] ^ half) * hot_steps + jnp.minimum(i, hot_steps - 1),
+                        0,
+                        0,
+                    ),
+                ),
+                pl.BlockSpec((2, width, HD), lambda i, place: (0, place[4], 0)),
+                whole(first),
+                whole(second),
+            ],
+            out_specs=pl.BlockSpec((parts * chunk, columns), lambda i, *_: (0, 0)),
+            scratch_shapes=[pltpu.VMEM((parts * chunk, width), jnp.bfloat16)],
+        ),
+        out_shape=jax.ShapeDtypeStruct((parts * chunk, columns), jnp.bfloat16),
+        compiler_params=params(),
+        name="up_keep" if half == 0 else "up_send",
+    )(place, *states, *stats, gain, hot, near, first, second)
+
+
+def down_kernel(place, hidden_ref, hot_ref, near_ref, first_ref, second_ref, *refs):
+    y, g = place[1], place[2]
+    blocks, depth, wide = hot_ref.shape
+    made = jnp.dot(
+        hidden_ref[:, : blocks * depth],
+        hot_ref[...].reshape(blocks * depth, wide),
+        preferred_element_type=jnp.float32,
+    )
+
+    def add(made, first, second, pair):
+        at = pl.multiple_of(blocks * depth + pair * 2 * depth, 2 * depth)
+        return made + jnp.dot(
+            hidden_ref[:, pl.ds(at, 2 * depth)],
+            jnp.concatenate([first, second], axis=0),
+            preferred_element_type=jnp.float32,
+        )
+
+    made = add(made, near_ref[g], near_ref[1 - g], y)
+    made = add(made, first_ref[...], second_ref[...], 1 - y)
+    if len(refs) == 1:
+        refs[0][...] = made
+        return
+    made = made + refs[0][...]
+    outs = refs[1:]
+    chunk = outs[0].shape[0]
+    for m, out in enumerate(outs):
+        out[...] = made[m * chunk : (m + 1) * chunk].astype(out.dtype)
+
+
+def down(place, half, hidden, hot, near, first, second, before, parts):
+    rows = hidden.shape[0]
+    width = hot.shape[2]
+    wide = width // 3
+    per = width // wide
+    blocks = hot.shape[0] // 2
+    column = lambda i, *_: (0, i)
+    in_specs = [
+        pl.BlockSpec(hidden.shape, lambda i, *_: (0, 0)),
+        pl.BlockSpec((blocks, HD, wide), lambda i, place: (place[3] ^ half, 0, i)),
+        pl.BlockSpec((2, HD, wide), lambda i, place: (0, 0, place[4] * per + i)),
+        pl.BlockSpec((HD, wide), column),
+        pl.BlockSpec((HD, wide), column),
+    ]
+    operands = [hidden, hot, near, first, second]
+    if before is None:
+        out_specs = pl.BlockSpec((rows, wide), column)
+        out_shape = jax.ShapeDtypeStruct((rows, width), jnp.float32)
+    else:
+        in_specs.append(pl.BlockSpec((rows, wide), column))
+        operands.append(before)
+        out_specs = [pl.BlockSpec((rows // parts, wide), column)] * parts
+        out_shape = [
+            jax.ShapeDtypeStruct((rows // parts, width), jnp.bfloat16 if m else jnp.float32)
+            for m in range(parts)
+        ]
+    return pl.pallas_call(
+        down_kernel,
+        grid_spec=pltpu.PrefetchScalarGridSpec(
+            num_scalar_prefetch=1, grid=(per,), in_specs=in_specs, out_specs=out_specs
+        ),
+        out_shape=out_shape,
+        compiler_params=params(),
+        name="down_keep" if half == 0 else "down_got",
+    )(place, *operands)
+
+
+def swap(x, axis, m, size):
+    return lax.ppermute(x, axis, [(i, i ^ m) for i in range(size)])
+
+
+def local_fast(
+    queries,
+    key_cache,
+    value_cache,
+    key_new,
+    value_new,
+    lengths,
+    out_proj,
+    residual,
+    norm_gain,
+    hot_up,
+    hot_down,
+    cold_up,
+    cold_down,
+    block_rows,
+    block_counts,
+):
+    steps, here, _ = queries.shape
+    all_rows, width = residual.shape[1:]
+    n_heads = all_rows // here
+    g = lax.axis_index("groups")
+    b = lax.axis_index("blocks")
+    h = lax.axis_index("heads")
+    y, core = b // 2, b % 2
+    place = jnp.stack([h, y, g, core, b]).astype(jnp.int32)
+
+    near_up = swap(cold_up, "blocks", 1, 4)
+    near_down = swap(cold_down, "blocks", 1, 4)
+    far_up, far_down = {}, {}
+    for m in (2, 3):
+        piece = lax.dynamic_slice(cold_up, (g, (b ^ m) * width, 0), (1, width, HD))[0]
+        first = swap(piece, "blocks", m, 4)
+        far_up[m] = (first, swap(first, "groups", 1, 2))
+    for m in (2, 3):
+        piece = lax.dynamic_slice(cold_down, (g, 0, (b ^ m) * width), (1, HD, width))[0]
+        first = swap(piece, "blocks", m, 4)
+        far_down[m] = (first, swap(first, "groups", 1, 2))
+
+    attended = attention(queries, key_cache, value_cache, key_new, value_new, lengths)
+    gathered = lax.all_gather(attended, "blocks", axis=0, tiled=True)
+    pieces = project(place, gathered, out_proj, n_heads)
+    others = [swap(pieces[m], "heads", m, n_heads) for m in range(1, n_heads)]
+    mine = lax.dynamic_slice(residual, (0, h * here, 0), (steps, here, width))
+    state, mean, spread = join(mine.reshape(steps * here, width), pieces[0], others)
+    states = [state] + [swap(state, "heads", m, n_heads) for m in range(1, n_heads)]
+    stat = jnp.stack([mean, spread])
+    count = width
+    for m in (2, 1):
+        got = swap(stat, "blocks", m, 4)
+        gap = stat[0] - got[0]
+        stat = jnp.stack(
+            [(stat[0] + got[0]) * 0.5, stat[1] + got[1] + gap * gap * (count * 0.5)]
+        )
+        count = count * 2
+    stats = [stat] + [swap(stat, "heads", m, n_heads) for m in range(1, n_heads)]
+
+    index = jnp.arange(n_heads * steps * here)
+    chunk = (index // (steps * here)) ^ h
+    row = (index // here % steps) * all_rows + chunk * here + index % here
+    pair = jnp.arange(4)
+    owner = (pair // 2) * 2 + core
+    slot = (pair % 2) ^ g
+    lists = block_rows[:, 0][owner, slot]
+    counts = block_counts[:, 0][owner, slot]
+    live = jnp.arange(lists.shape[1])[None, :] < counts[:, None]
+    used = jnp.any((lists[None] == row[:, None, None]) & live[None], axis=-1)
+    hot_width = hot_up.shape[0] // 2 * HD
+    mask = jnp.concatenate(
+        [
+            jnp.ones((row.shape[0], hot_width), jnp.bfloat16),
+            jnp.repeat(used.astype(jnp.bfloat16), HD, axis=1),
+        ],
+        axis=1,
+    )
+
+    gain = norm_gain[None]
+    sent = up(place, 1, states, stats, gain, hot_up, near_up, *far_up[3])
+    got = swap(sent, "blocks", 1, 4)
+    kept = up(place, 0, states, stats, gain, hot_up, cold_up, *far_up[2])
+    summed = (kept.astype(jnp.float32) + got.astype(jnp.float32)).astype(jnp.bfloat16)
+    total = summed.astype(jnp.float32) + swap(summed, "blocks", 2, 4).astype(jnp.float32)
+    hidden = jnp.maximum(total, 0.0).astype(jnp.bfloat16) * mask
+    partner = swap(hidden, "blocks", 1, 4)
+    before = down(place, 0, hidden, hot_down, cold_down, *far_down[2], None, n_heads)
+    parts = down(place, 1, partner, hot_down, near_down, *far_down[3], before, n_heads)
+    out = parts[0]
+    for m in range(1, n_heads):
+        out = out + swap(parts[m], "heads", m, n_heads).astype(jnp.float32)
+    ffn_out = out.astype(jnp.bfloat16).reshape(steps, here, width)
+
+    stacked = jnp.stack(states).reshape(n_heads, steps, 1, here, width)
+    ordered = [
+        lax.dynamic_index_in_dim(stacked, c ^ h, axis=0, keepdims=False) for c in range(n_heads)
+    ]
+    attn_state = jnp.concatenate(ordered, axis=1).reshape(steps, all_rows, width)
+    return (attn_state, ffn_out)
+
+
 def solution(mesh):
     placed = (
         P(None, ("groups", "blocks"), "heads"),
@@ -130,8 +511,9 @@
         P("groups", "heads", None, None),
         P("groups", "heads", None),
     )
+    sizes = tuple(mesh.shape[a] for a in ("groups", "blocks", "heads"))
     return jax.shard_map(
-        local,
+        local_fast if sizes == (2, 4, 4) else local,
         mesh=mesh,
         in_specs=placed,
         out_specs=(P(None, "groups", "blocks"), P(None, ("groups", "heads"), "blocks")),

time: 211 us -> 149 us (0.71)
  waiting for transfers between devices: 79.7 us -> 50.5 us
  starting transfers between devices: 8.68 us -> 34.4 us
  local copies, waits for them, and re-layouts: 50.6 us -> 25.1 us
  matrix products: 23.9 us -> 0 us
  Pallas kernels: 0 us -> 23.2 us
  blocking collectives: 21.5 us -> 7.65 us
  between operations: 13.9 us -> 0.97 us
  other arithmetic: 11.6 us -> 6.14 us
    ppermute x0 -> x27, waiting for transfers between devices: none -> 50.5 us  [swap(): return lax.ppermute(x, axis, [(i, i ^ m) for i in range(size)])]
    psum x2 -> x0, waiting for transfers between devices: 41.4 us -> none  [the longest x1 38 us: local(): lax.psum(partial_out.astype(jnp.bfloat16), 'heads').astype(jnp.float32)]
    ppermute x0 -> x27, starting transfers between devices: none -> 34.4 us  [swap(): return lax.ppermute(x, axis, [(i, i ^ m) for i in range(size)])]
    dot_general x8 -> x0, matrix products: 23.9 us -> none  [the longest x1 4.58 us: local(): jnp.einsum('trc,kch->trkh', normed, hot_up, preferred_element_type=jnp.fl...]
    pallas_call x0 -> x7, Pallas kernels: none -> 23.2 us  [the longest x2 6.89 us: down(): pl.pallas_call(down_kernel, grid_spec=pltpu.PrefetchScalarGridSpec(num_sc...]
    unnamed x4 -> x0, waiting for transfers between devices: 20.8 us -> none
    all_to_all x2 -> x0, waiting for transfers between devices: 17.5 us -> none  [the longest x1 10.7 us: local(): lax.all_to_all(outgoing, 'blocks', split_axis=0, concat_axis=3, tiled=True)]
    psum x2 -> x0, blocking collectives: 13.6 us -> none  [the longest x1 7.33 us: local(): variance = lax.psum(jnp.sum(centred * centred, axis=-1), 'blocks') / D]
  transfers between devices with their start and end apart: 5 -> 27, of which waited for: 5 -> 15; matrix products, arithmetic and copies ran while one was open for 14% -> 8% of each run, Pallas kernels for 0% -> 13%
where the time goes in v1:
time: 149 us; the launch traced here: 148 us
  waiting for transfers between devices  50.5 us (34%)
  starting transfers between devices  34.4 us (23%)
  local copies, waits for them, and re-layouts  25.1 us (17%)
  Pallas kernels  23.2 us (16%)
  blocking collectives  7.65 us (5%)
  other arithmetic  6.14 us (4%)
    ppermute x27, waiting for transfers between devices, swap(): return lax.ppermute(x, axis, [(i, i ^ m) for i in range(size)])  50.5 us
    ppermute x27, starting transfers between devices, swap(): return lax.ppermute(x, axis, [(i, i ^ m) for i in range(size)])  34.4 us
    unnamed x47, local copies, waits for them, and re-layouts  18.7 us
    all_gather x1, blocking collectives, local_fast(): gathered = lax.all_gather(attended, 'blocks', axis=0, tiled=True)  7.65 us
    pallas_call x2, Pallas kernels, down(): pl.pallas_call(down_kernel, grid_spec=pltpu.PrefetchScalarGridSpec(num_sc...  6.89 us
    pallas_call x2, Pallas kernels, up(): pl.pallas_call(functools.partial(up_kernel, parts=parts, hot_steps=hot_st...  6.41 us
    pallas_call x1, Pallas kernels, attention(): pl.pallas_call(functools.partial(attention_kernel, here=here, steps=steps...  5.86 us
  transfers between devices with their start and end apart: 27, of which 15 were waited for; matrix products, arithmetic and copies ran while one was open for 8% of the time, Pallas kernels for 13%

profile of v1, /device:TPU:0, one launch (start us, length us, event | category | flops | bytes accessed | tf_op | source)
XLA Modules:
  0.0 147.9 jit_solution(5336695641112839898)
XLA Ops:
  1.2 1.9 %copy-done.7 = bf16[8,128,1536]{2,1,0:T(8,128)(2,1)S(1)} copy-done((bf16[8,128,1536]{2,1,0:T(8,128)(2,1)S(1)}, bf16[8,128,1536]{2,1,0:T(8,128)(2,1)}, u32[]{:S(2)}) %copy-start.7) | copy-done | bytes 3145752
  3.1 1.9 %copy-done.8 = bf16[8,128,1536]{2,1,0:T(8,128)(2,1)S(1)} copy-done((bf16[8,128,1536]{2,1,0:T(8,128)(2,1)S(1)}, bf16[8,128,1536]{2,1,0:T(8,128)(2,1)}, u32[]{:S(2)}) %copy-start.8) | copy-done | bytes 3145752
  5.0 0.9 copy-done.16
  5.9 0.9 copy-done.17
  6.8 0.9 copy-done.18
  7.7 0.7 copy-done.19
  8.4 5.9 %attention.1 = bf16[32,1536]{1,0:T(8,128)(2,1)S(1)} custom-call(s32[8]{0:T(128)S(1)} %copy-done.19, bf16[32,1536]{1,0:T(8,128)(2,1)S(1)} %bitcast.92, bf16[1024,1536]{1,0:T(8,128)(2,1)S(1)} %bitcast.85, bf16[1024,1536]{1,0:T(8,128)(2,1)S(1)} %bitcast.86, bf16[32,1536]{1,0:T(8,128)(2,1)S(1)} %bitcast.93, bf16[32,1536]{1,0:T(8,128)(2,1)S(1)} %bitcast.94), custom_call_target="tpu_custom_call" | custom-call | tf_op jit(solution)/shard_map/attention/pallas_call | solution.py:177
  14.2 7.7 %all_gather.3.rows_ref = bf16[128,1536]{1,0:T(8,128)(2,1)S(1)} all-gather(bf16[32,1536]{1,0:T(8,128)(2,1)S(1)} %attention.1), channel_id=1, replica_groups=mesh['groups'=2,'blocks'=4,'heads'=4] {'blocks'}, dimensions={0}, use_global_device_ids=true | all-gather | bytes 491520 | tf_op jit(solution)/shard_map/all_gather | solution.py:437
  21.9 2.9 %project.1 = (f32[32,1536]{1,0:T(8,128)S(1)}, bf16[32,1536]{1,0:T(8,128)(2,1)}, bf16[32,1536]{1,0:T(8,128)(2,1)}, bf16[32,1536]{1,0:T(8,128)(2,1)}) custom-call(s32[5]{0:T(128)S(1)} %stack.65.place, bf16[128,1536]{1,0:T(8,128)(2,1)S(1)} %all_gather.3.rows_ref, bf16[1536,1536]{1,0:T(8,128)(2,1)S(1)} %copy-done.6), custom_call_target="tpu_custom_call" | custom-call | tf_op jit(solution)/shard_map/project/pallas_call | solution.py:210
  24.8 0.7 copy-done.14
  25.4 1.8 %collective-permute-start = (bf16[32,1536]{1,0:T(8,128)(2,1)}, bf16[32,1536]{1,0:T(8,128)(2,1)}, u32[]{:S(2)}, u32[]{:S(2)}) collective-permute-start(bf16[32,1536]{1,0:T(8,128)(2,1)} %get-tuple-element.14), channel_id=1, source_target_pairs={{0,1},{1,0},{2,3},{3,2},{4,5},{5,4},{6,7},{7,6},{8,9},{9,8},{10,11... | collective-permute-start | bytes 294920 | tf_op jit(solution)/shard_map/ppermute | solution.py:395
  27.2 2.6 %collective-permute-start.1 = (bf16[32,1536]{1,0:T(8,128)(2,1)}, bf16[32,1536]{1,0:T(8,128)(2,1)}, u32[]{:S(2)}, u32[]{:S(2)}) collective-permute-start(bf16[32,1536]{1,0:T(8,128)(2,1)} %get-tuple-element.15), channel_id=1, source_target_pairs={{0,2},{1,3},{2,0},{3,1},{4,6},{5,7},{6,4},{7,5},{8,10},{9,11},{10,... | collective-permute-start | bytes 294920 | tf_op jit(solution)/shard_map/ppermute | solution.py:395
  29.8 0.6 dynamic-slice_bitcast_fusion.8.residual
  30.8 7.4 %collective-permute-done.1.refs_1_ = bf16[32,1536]{1,0:T(8,128)(2,1)} collective-permute-done((bf16[32,1536]{1,0:T(8,128)(2,1)}, bf16[32,1536]{1,0:T(8,128)(2,1)}, u32[]{:S(2)}, u32[]{:S(2)}) %collective-permute-start.1) | collective-permute-done | bytes 98336 | tf_op jit(solution)/shard_map/ppermute | solution.py:395
  38.2 0.9 copy-done.13
  39.1 0.9 copy-done.15
  40.0 1.2 join.1
  41.3 1.6 %collective-permute-start.6 = (f32[2,32,128]{2,1,0:T(8,128)S(1)}, f32[2,32,128]{2,1,0:T(8,128)S(1)}, u32[]{:S(2)}, u32[]{:S(2)}) collective-permute-start(f32[2,32,128]{2,1,0:T(8,128)S(1)} %pad_maximum_fusion.1), channel_id=1, source_target_pairs={{0,8},{4,12},{8,0},{12,4},{1,9},{5,13},{9,1},{13,5},{2,10},{6,14},... | collective-permute-start | bytes 98312 | tf_op jit(solution)/shard_map/ppermute | solution.py:395
  43.6 1.6 %collective-permute-done.6 = f32[2,32,128]{2,1,0:T(8,128)S(1)} collective-permute-done((f32[2,32,128]{2,1,0:T(8,128)S(1)}, f32[2,32,128]{2,1,0:T(8,128)S(1)}, u32[]{:S(2)}, u32[]{:S(2)}) %collective-permute-start.6) | collective-permute-done | bytes 32800 | tf_op jit(solution)/shard_map/ppermute | solution.py:395
  45.4 3.6 %collective-permute-done.7 = f32[2,32,128]{2,1,0:T(8,128)S(1)} collective-permute-done((f32[2,32,128]{2,1,0:T(8,128)S(1)}, f32[2,32,128]{2,1,0:T(8,128)S(1)}, u32[]{:S(2)}, u32[]{:S(2)}) %collective-permute-start.7) | collective-permute-done | bytes 32800 | tf_op jit(solution)/shard_map/ppermute | solution.py:395
  49.0 2.7 %collective-permute-start.10 = (f32[2,32,128]{2,1,0:T(8,128)S(1)}, f32[2,32,128]{2,1,0:T(8,128)S(1)}, u32[]{:S(2)}, u32[]{:S(2)}) collective-permute-start(f32[2,32,128]{2,1,0:T(8,128)S(1)} %pad_maximum_fusion.3.refs_4_), channel_id=1, source_target_pairs={{0,3},{1,2},{2,1},{3,0},{4,7},{5,6},{6,5},{7,4},{8,11},{9,10},{10,... | collective-permute-start | bytes 98312 | tf_op jit(solution)/shard_map/ppermute | solution.py:395
  51.7 1.5 %collective-permute-start.11 = (bf16[1536,128]{1,0:T(8,128)(2,1)S(1)}, bf16[1536,128]{1,0:T(8,128)(2,1)S(1)}, u32[]{:S(2)}, u32[]{:S(2)}) collective-permute-start(bf16[1536,128]{1,0:T(8,128)(2,1)S(1)} %get-tuple-element.26), channel_id=1, source_target_pairs={{0,8},{4,12},{8,0},{12,4},{1,9},{5,13},{9,1},{13,5},{2,10},{6,14},... | collective-permute-start | bytes 1179656 | tf_op jit(solution)/shard_map/ppermute | solution.py:395
  53.7 1.5 %collective-permute-start.15 = (bf16[1536,128]{1,0:T(8,128)(2,1)S(1)}, bf16[1536,128]{1,0:T(8,128)(2,1)S(1)}, u32[]{:S(2)}, u32[]{:S(2)}) collective-permute-start(bf16[1536,128]{1,0:T(8,128)(2,1)S(1)} %collective-permute-done.14.refs_11_), channel_id=1, source_target_pairs={{0,16},{16,0},{1,17},{17,1},{2,18},{18,2},{3,19},{19,3},{4,20},{20... | collective-permute-start | bytes 1179656 | tf_op jit(solution)/shard_map/ppermute | solution.py:395
  55.2 1.9 %collective-permute-start.8 = (f32[2,32,128]{2,1,0:T(8,128)S(1)}, f32[2,32,128]{2,1,0:T(8,128)S(1)}, u32[]{:S(2)}, u32[]{:S(2)}) collective-permute-start(f32[2,32,128]{2,1,0:T(8,128)S(1)} %pad_maximum_fusion.3.refs_4_), channel_id=1, source_target_pairs={{0,1},{1,0},{2,3},{3,2},{4,5},{5,4},{6,7},{7,6},{8,9},{9,8},{10,11... | collective-permute-start | bytes 98312 | tf_op jit(solution)/shard_map/ppermute | solution.py:395
  57.0 2.1 %collective-permute-done.8.refs_5_ = f32[2,32,128]{2,1,0:T(8,128)S(1)} collective-permute-done((f32[2,32,128]{2,1,0:T(8,128)S(1)}, f32[2,32,128]{2,1,0:T(8,128)S(1)}, u32[]{:S(2)}, u32[]{:S(2)}) %collective-permute-start.8) | collective-permute-done | bytes 32800 | tf_op jit(solution)/shard_map/ppermute | solution.py:395
  59.1 3.5 %collective-permute-start.9 = (f32[2,32,128]{2,1,0:T(8,128)S(1)}, f32[2,32,128]{2,1,0:T(8,128)S(1)}, u32[]{:S(2)}, u32[]{:S(2)}) collective-permute-start(f32[2,32,128]{2,1,0:T(8,128)S(1)} %pad_maximum_fusion.3.refs_4_), channel_id=1, source_target_pairs={{0,2},{1,3},{2,0},{3,1},{4,6},{5,7},{6,4},{7,5},{8,10},{9,11},{10,... | collective-permute-start | bytes 98312 | tf_op jit(solution)/shard_map/ppermute | solution.py:395
  62.6 2.0 %collective-permute-done.9.refs_6_ = f32[2,32,128]{2,1,0:T(8,128)S(1)} collective-permute-done((f32[2,32,128]{2,1,0:T(8,128)S(1)}, f32[2,32,128]{2,1,0:T(8,128)S(1)}, u32[]{:S(2)}, u32[]{:S(2)}) %collective-permute-start.9) | collective-permute-done | bytes 32800 | tf_op jit(solution)/shard_map/ppermute | solution.py:395
  64.6 1.2 collective-permute-start.3
  65.8 4.5 %collective-permute-done.3.refs_1_ = bf16[32,1536]{1,0:T(8,128)(2,1)S(1)} collective-permute-done((bf16[32,1536]{1,0:T(8,128)(2,1)S(1)}, bf16[32,1536]{1,0:T(8,128)(2,1)S(1)}, u32[]{:S(2)}, u32[]{:S(2)}) %collective-permute-start.3) | collective-permute-done | bytes 98336 | tf_op jit(solution)/shard_map/ppermute | solution.py:395
  70.3 2.1 %collective-permute-start.4 = (bf16[32,1536]{1,0:T(8,128)(2,1)S(1)}, bf16[32,1536]{1,0:T(8,128)(2,1)S(1)}, u32[]{:S(2)}, u32[]{:S(2)}) collective-permute-start(bf16[32,1536]{1,0:T(8,128)(2,1)S(1)} %get-tuple-element.17.refs_0_), channel_id=1, source_target_pairs={{0,2},{1,3},{2,0},{3,1},{4,6},{5,7},{6,4},{7,5},{8,10},{9,11},{10,... | collective-permute-start | bytes 294920 | tf_op jit(solution)/shard_map/ppermute | solution.py:395
  72.4 5.0 %collective-permute-done.4.refs_2_ = bf16[32,1536]{1,0:T(8,128)(2,1)S(1)} collective-permute-done((bf16[32,1536]{1,0:T(8,128)(2,1)S(1)}, bf16[32,1536]{1,0:T(8,128)(2,1)S(1)}, u32[]{:S(2)}, u32[]{:S(2)}) %collective-permute-start.4) | collective-permute-done | bytes 98336 | tf_op jit(solution)/shard_map/ppermute | solution.py:395
  77.4 2.5 %collective-permute-start.5 = (bf16[32,1536]{1,0:T(8,128)(2,1)S(1)}, bf16[32,1536]{1,0:T(8,128)(2,1)S(1)}, u32[]{:S(2)}, u32[]{:S(2)}) collective-permute-start(bf16[32,1536]{1,0:T(8,128)(2,1)S(1)} %get-tuple-element.17.refs_0_), channel_id=1, source_target_pairs={{0,3},{1,2},{2,1},{3,0},{4,7},{5,6},{6,5},{7,4},{8,11},{9,10},{10,... | collective-permute-start | bytes 294920 | tf_op jit(solution)/shard_map/ppermute | solution.py:395
  79.9 0.9 collective-permute-start.12
  80.8 3.0 %collective-permute-done.5.refs_3_ = bf16[32,1536]{1,0:T(8,128)(2,1)S(1)} collective-permute-done((bf16[32,1536]{1,0:T(8,128)(2,1)S(1)}, bf16[32,1536]{1,0:T(8,128)(2,1)S(1)}, u32[]{:S(2)}, u32[]{:S(2)}) %collective-permute-start.5) | collective-permute-done | bytes 98336 | tf_op jit(solution)/shard_map/ppermute | solution.py:395
  83.8 2.8 %copy-done.1 = bf16[16,1536,128]{2,1,0:T(8,128)(2,1)S(1)} copy-done((bf16[16,1536,128]{2,1,0:T(8,128)(2,1)S(1)}, bf16[16,1536,128]{2,1,0:T(8,128)(2,1)}, u32[]{:S(2)}) %copy-start.1) | copy-done | bytes 6291480
  86.6 3.8 %up_send.1 = bf16[128,1536]{1,0:T(8,128)(2,1)S(1)} custom-call(s32[5]{0:T(128)S(1)} %stack.65.place, bf16[32,1536]{1,0:T(8,128)(2,1)S(1)} %get-tuple-element.17.refs_0_, bf16[32,1536]{1,0:T(8,128)(2,1)S(1)} %collective-permute-done.3.refs_1_, bf16[32,1536]{1,0:T(8,128)(2,1)S(1)} %collective-permute-done.4.refs_2_, ...), custom_call_target="tpu_custom_call" | custom-call | tf_op jit(solution)/shard_map/up_send/pallas_call | solution.py:298
  90.5 2.1 %dynamic-slice_bitcast_fusion = (bf16[128,1536]{1,0:T(8,128)(2,1)}, bf16[128,1536]{1,0:T(8,128)(2,1)}) fusion(bf16[2,128,6144]{2,1,0:T(8,128)(2,1)} %near_ref.1, s32[]{:T(128)S(6)} %select_n.129, s32[]{:T(128)S(6)} %select_n.130, s32[]{:T(128)S(6)} %select_n.131), kind=kLoop, calls=%fused_computation.7 | loop fusion | bytes 1572876 | tf_op jit(solution)/shard_map/squeeze | solution.py:432
  92.6 1.0 collective-permute-start.22
  93.6 0.8 collective-permute-start.20
  94.5 2.6 %up_keep.1 = bf16[128,1536]{1,0:T(8,128)(2,1)S(1)} custom-call(s32[5]{0:T(128)S(1)} %stack.65.place, bf16[32,1536]{1,0:T(8,128)(2,1)S(1)} %get-tuple-element.17.refs_0_, bf16[32,1536]{1,0:T(8,128)(2,1)S(1)} %collective-permute-done.3.refs_1_, bf16[32,1536]{1,0:T(8,128)(2,1)S(1)} %collective-permute-done.4.refs_2_, ...), custom_call_target="tpu_custom_call" | custom-call | tf_op jit(solution)/shard_map/up_keep/pallas_call | solution.py:298
  97.2 0.8 add_convert_fusion
  98.0 1.0 collective-permute-start.17
  99.6 1.1 gather_fusion
  100.7 0.6 gather_fusion.1
  101.4 0.8 and_reduce_fusion
  102.2 0.7 copy.17
  103.0 1.0 broadcast_in_dim.5
  103.9 0.7 copy.20
  104.8 1.0 collective-permute-start.23
  105.8 6.6 %collective-permute-done.20.first_ref = bf16[128,1536]{1,0:T(8,128)(2,1)} collective-permute-done((bf16[128,1536]{1,0:T(8,128)(2,1)}, bf16[128,1536]{1,0:T(8,128)(2,1)}, u32[]{:S(2)}, u32[]{:S(2)}) %collective-permute-start.20) | collective-permute-done | bytes 393248 | tf_op jit(solution)/shard_map/ppermute | solution.py:395
  112.4 1.0 collective-permute-start.21
  113.5 7.8 %collective-permute-done.17 = bf16[128,1536]{1,0:T(8,128)(2,1)} collective-permute-done((bf16[128,1536]{1,0:T(8,128)(2,1)}, bf16[128,1536]{1,0:T(8,128)(2,1)}, u32[]{:S(2)}, u32[]{:S(2)}) %collective-permute-start.17) | collective-permute-done | bytes 393248 | tf_op jit(solution)/shard_map/ppermute | solution.py:395
  121.3 1.3 fusion.hidden_ref
  122.6 1.1 pad_maximum_fusion
  123.8 2.8 %copy-done.2 = bf16[16,128,1536]{2,1,0:T(8,128)(2,1)S(1)} copy-done((bf16[16,128,1536]{2,1,0:T(8,128)(2,1)S(1)}, bf16[16,128,1536]{2,1,0:T(8,128)(2,1)}, u32[]{:S(2)}) %copy-start.2) | copy-done | bytes 6291480
  126.6 3.4 %down_keep.1.refs_0_ = f32[128,1536]{1,0:T(8,128)S(1)} custom-call(s32[5]{0:T(128)S(1)} %stack.65.place, bf16[128,1536]{1,0:T(8,128)(2,1)S(1)} %fusion.hidden_ref, bf16[16,128,1536]{2,1,0:T(8,128)(2,1)S(1)} %copy-done.2, bf16[2,128,6144]{2,1,0:T(8,128)(2,1)S(1)} %copy-done.5, bf16[128,1536]{1,0:T(8,128)(2,1)} %collective-permute-done.22.first_ref, ...), custom_call_target="tpu_custom_call" | custom-call | tf_op jit(solution)/shard_map/down_keep/pallas_call | solution.py:383
  130.0 2.8 %copy-done.3 = bf16[16,128,1536]{2,1,0:T(8,128)(2,1)S(1)} copy-done((bf16[16,128,1536]{2,1,0:T(8,128)(2,1)S(1)}, bf16[16,128,1536]{2,1,0:T(8,128)(2,1)}, u32[]{:S(2)}) %copy-start.3) | copy-done | bytes 6291480
  132.8 3.5 %down_got.1 = (f32[32,1536]{1,0:T(8,128)S(1)}, bf16[32,1536]{1,0:T(8,128)(2,1)S(1)}, bf16[32,1536]{1,0:T(8,128)(2,1)S(1)}, bf16[32,1536]{1,0:T(8,128)(2,1)S(1)}) custom-call(s32[5]{0:T(128)S(1)} %stack.65.place, bf16[128,1536]{1,0:T(8,128)(2,1)S(1)} %collective-permute-done.18.hidden_ref, bf16[16,128,1536]{2,1,0:T(8,128)(2,1)S(1)} %copy-done.3, ...), custom_call_target="tpu_custom_call" | custom-call | tf_op jit(solution)/shard_map/down_got/pallas_call | solution.py:383
  136.4 3.0 %collective-permute-start.25 = (bf16[32,1536]{1,0:T(8,128)(2,1)S(1)}, bf16[32,1536]{1,0:T(8,128)(2,1)S(1)}, u32[]{:S(2)}, u32[]{:S(2)}) collective-permute-start(bf16[32,1536]{1,0:T(8,128)(2,1)S(1)} %get-tuple-element.22), channel_id=1, source_target_pairs={{0,2},{1,3},{2,0},{3,1},{4,6},{5,7},{6,4},{7,5},{8,10},{9,11},{10,... | collective-permute-start | bytes 294920 | tf_op jit(solution)/shard_map/ppermute | solution.py:395
  139.4 1.3 collective-permute-start.26
  140.7 0.8 maximum_bitcast_fusion
  141.5 1.8 %collective-permute-done.24 = bf16[32,1536]{1,0:T(8,128)(2,1)S(1)} collective-permute-done((bf16[32,1536]{1,0:T(8,128)(2,1)S(1)}, bf16[32,1536]{1,0:T(8,128)(2,1)S(1)}, u32[]{:S(2)}, u32[]{:S(2)}) %collective-permute-start.24) | collective-permute-done | bytes 98336 | tf_op jit(solution)/shard_map/ppermute | solution.py:395
  143.3 3.9 %collective-permute-done.25 = bf16[32,1536]{1,0:T(8,128)(2,1)S(1)} collective-permute-done((bf16[32,1536]{1,0:T(8,128)(2,1)S(1)}, bf16[32,1536]{1,0:T(8,128)(2,1)S(1)}, u32[]{:S(2)}, u32[]{:S(2)}) %collective-permute-start.25) | collective-permute-done | bytes 98336 | tf_op jit(solution)/shard_map/ppermute | solution.py:395
  147.2 0.7 fusion.1
  (70 shorter events, 3.6 us)
Async XLA Ops:
  0.6 29.2 %copy-start = (bf16[4,32,1536]{2,1,0:T(8,128)(2,1)S(1)}, bf16[4,32,1536]{2,1,0:T(8,128)(2,1)}, u32[]{:S(2)}) copy-start(bf16[4,32,1536]{2,1,0:T(8,128)(2,1)} %param.22) | copy-start | bytes 1179652
  0.6 83.2 %collective-permute-start.13 = (bf16[2,6144,128]{2,1,0:T(8,128)(2,1)}, bf16[2,6144,128]{2,1,0:T(8,128)(2,1)}, u32[]{:S(2)}, u32[]{:S(2)}) collective-permute-start(bf16[2,6144,128]{2,1,0:T(8,128)(2,1)} %refs_10_.1), channel_id=1, source_target_pairs={{0,4},{4,0},{8,12},{12,8},{1,5},{5,1},{9,13},{13,9},{2,6},{6,2},{1... | collective-permute-start | bytes 9437192 | tf_op jit(solution)/shard_map/ppermute | solution.py:395
  1.2 1.9 %copy-start.7 = (bf16[8,128,1536]{2,1,0:T(8,128)(2,1)S(1)}, bf16[8,128,1536]{2,1,0:T(8,128)(2,1)}, u32[]{:S(2)}) copy-start(bf16[8,128,1536]{2,1,0:T(8,128)(2,1)} %param.16) | copy-start | bytes 9437188
  3.1 1.9 %copy-start.8 = (bf16[8,128,1536]{2,1,0:T(8,128)(2,1)S(1)}, bf16[8,128,1536]{2,1,0:T(8,128)(2,1)}, u32[]{:S(2)}) copy-start(bf16[8,128,1536]{2,1,0:T(8,128)(2,1)} %param.17) | copy-start | bytes 9437188
  5.0 0.9 copy-start.16
  5.9 0.9 copy-start.17
  6.8 0.9 copy-start.18
  7.7 0.7 copy-start.19
  8.4 13.5 %copy-start.6 = (bf16[1536,1536]{1,0:T(8,128)(2,1)S(1)}, bf16[1536,1536]{1,0:T(8,128)(2,1)}, u32[]{:S(2)}) copy-start(bf16[1536,1536]{1,0:T(8,128)(2,1)} %weight_ref.1) | copy-start | bytes 14155780
  14.2 28.6 %copy-start.4 = (bf16[2,6144,128]{2,1,0:T(8,128)(2,1)S(1)}, bf16[2,6144,128]{2,1,0:T(8,128)(2,1)}, u32[]{:S(2)}) copy-start(bf16[2,6144,128]{2,1,0:T(8,128)(2,1)} %refs_10_.1) | copy-start | bytes 9437188
  21.9 58.0 %copy-start.22 = (bf16[1536]{0:T(1024)(128)(2,1)S(1)}, bf16[1536]{0:T(1024)(128)(2,1)}, u32[]{:S(2)}) copy-start(bf16[1536]{0:T(1024)(128)(2,1)} %param.23) | copy-start | bytes 9220
  24.8 0.7 copy-start.14
  25.4 5.4 %collective-permute-start = (bf16[32,1536]{1,0:T(8,128)(2,1)}, bf16[32,1536]{1,0:T(8,128)(2,1)}, u32[]{:S(2)}, u32[]{:S(2)}) collective-permute-start(bf16[32,1536]{1,0:T(8,128)(2,1)} %get-tuple-element.14), channel_id=1, source_target_pairs={{0,1},{1,0},{2,3},{3,2},{4,5},{5,4},{6,7},{7,6},{8,9},{9,8},{10,11... | collective-permute-start | bytes 294920 | tf_op jit(solution)/shard_map/ppermute | solution.py:395
  27.2 11.0 %collective-permute-start.1 = (bf16[32,1536]{1,0:T(8,128)(2,1)}, bf16[32,1536]{1,0:T(8,128)(2,1)}, u32[]{:S(2)}, u32[]{:S(2)}) collective-permute-start(bf16[32,1536]{1,0:T(8,128)(2,1)} %get-tuple-element.15), channel_id=1, source_target_pairs={{0,2},{1,3},{2,0},{3,1},{4,6},{5,7},{6,4},{7,5},{8,10},{9,11},{10,... | collective-permute-start | bytes 294920 | tf_op jit(solution)/shard_map/ppermute | solution.py:395
  29.8 8.4 %collective-permute-start.2 = (bf16[32,1536]{1,0:T(8,128)(2,1)}, bf16[32,1536]{1,0:T(8,128)(2,1)}, u32[]{:S(2)}, u32[]{:S(2)}) collective-permute-start(bf16[32,1536]{1,0:T(8,128)(2,1)} %get-tuple-element.16), channel_id=1, source_target_pairs={{0,3},{1,2},{2,1},{3,0},{4,7},{5,6},{6,5},{7,4},{8,11},{9,10},{10,... | collective-permute-start | bytes 294920 | tf_op jit(solution)/shard_map/ppermute | solution.py:395
  38.2 0.9 copy-start.13
  39.1 0.9 copy-start.15
  41.3 53.2 %copy-start.9 = (bf16[32,1536]{1,0:T(8,128)(2,1)}, bf16[32,1536]{1,0:T(8,128)(2,1)S(1)}, u32[]{:S(2)}) copy-start(bf16[32,1536]{1,0:T(8,128)(2,1)S(1)} %get-tuple-element.17.refs_0_) | copy-start | bytes 294916
  41.3 4.0 %collective-permute-start.6 = (f32[2,32,128]{2,1,0:T(8,128)S(1)}, f32[2,32,128]{2,1,0:T(8,128)S(1)}, u32[]{:S(2)}, u32[]{:S(2)}) collective-permute-start(f32[2,32,128]{2,1,0:T(8,128)S(1)} %pad_maximum_fusion.1), channel_id=1, source_target_pairs={{0,8},{4,12},{8,0},{12,4},{1,9},{5,13},{9,1},{13,5},{2,10},{6,14},... | collective-permute-start | bytes 98312 | tf_op jit(solution)/shard_map/ppermute | solution.py:395
  42.9 10.8 %collective-permute-start.14 = (bf16[1536,128]{1,0:T(8,128)(2,1)S(1)}, bf16[1536,128]{1,0:T(8,128)(2,1)S(1)}, u32[]{:S(2)}, u32[]{:S(2)}) collective-permute-start(bf16[1536,128]{1,0:T(8,128)(2,1)S(1)} %get-tuple-element.27), channel_id=1, source_target_pairs={{0,12},{4,8},{8,4},{12,0},{1,13},{5,9},{9,5},{13,1},{2,14},{6,10},... | collective-permute-start | bytes 1179656 | tf_op jit(solution)/shard_map/ppermute | solution.py:395
  43.0 87.0 %collective-permute-start.19 = (bf16[2,128,6144]{2,1,0:T(8,128)(2,1)}, bf16[2,128,6144]{2,1,0:T(8,128)(2,1)}, u32[]{:S(2)}, u32[]{:S(2)}) collective-permute-start(bf16[2,128,6144]{2,1,0:T(8,128)(2,1)} %near_ref.1), channel_id=1, source_target_pairs={{0,4},{4,0},{8,12},{12,8},{1,5},{5,1},{9,13},{13,9},{2,6},{6,2},{1... | collective-permute-start | bytes 9437192 | tf_op jit(solution)/shard_map/ppermute | solution.py:395
  45.3 3.7 %collective-permute-start.7 = (f32[2,32,128]{2,1,0:T(8,128)S(1)}, f32[2,32,128]{2,1,0:T(8,128)S(1)}, u32[]{:S(2)}, u32[]{:S(2)}) collective-permute-start(f32[2,32,128]{2,1,0:T(8,128)S(1)} %pad_maximum_fusion.2), channel_id=1, source_target_pairs={{0,4},{4,0},{8,12},{12,8},{1,5},{5,1},{9,13},{13,9},{2,6},{6,2},{1... | collective-permute-start | bytes 98312 | tf_op jit(solution)/shard_map/ppermute | solution.py:395
  49.0 6.2 %collective-permute-start.10 = (f32[2,32,128]{2,1,0:T(8,128)S(1)}, f32[2,32,128]{2,1,0:T(8,128)S(1)}, u32[]{:S(2)}, u32[]{:S(2)}) collective-permute-start(f32[2,32,128]{2,1,0:T(8,128)S(1)} %pad_maximum_fusion.3.refs_4_), channel_id=1, source_target_pairs={{0,3},{1,2},{2,1},{3,0},{4,7},{5,6},{6,5},{7,4},{8,11},{9,10},{10,... | collective-permute-start | bytes 98312 | tf_op jit(solution)/shard_map/ppermute | solution.py:395
  51.7 28.2 %collective-permute-start.11 = (bf16[1536,128]{1,0:T(8,128)(2,1)S(1)}, bf16[1536,128]{1,0:T(8,128)(2,1)S(1)}, u32[]{:S(2)}, u32[]{:S(2)}) collective-permute-start(bf16[1536,128]{1,0:T(8,128)(2,1)S(1)} %get-tuple-element.26), channel_id=1, source_target_pairs={{0,8},{4,12},{8,0},{12,4},{1,9},{5,13},{9,1},{13,5},{2,10},{6,14},... | collective-permute-start | bytes 1179656 | tf_op jit(solution)/shard_map/ppermute | solution.py:395
  53.7 30.1 %collective-permute-start.15 = (bf16[1536,128]{1,0:T(8,128)(2,1)S(1)}, bf16[1536,128]{1,0:T(8,128)(2,1)S(1)}, u32[]{:S(2)}, u32[]{:S(2)}) collective-permute-start(bf16[1536,128]{1,0:T(8,128)(2,1)S(1)} %collective-permute-done.14.refs_11_), channel_id=1, source_target_pairs={{0,16},{16,0},{1,17},{17,1},{2,18},{18,2},{3,19},{19,3},{4,20},{20... | collective-permute-start | bytes 1179656 | tf_op jit(solution)/shard_map/ppermute | solution.py:395
  55.2 3.9 %collective-permute-start.8 = (f32[2,32,128]{2,1,0:T(8,128)S(1)}, f32[2,32,128]{2,1,0:T(8,128)S(1)}, u32[]{:S(2)}, u32[]{:S(2)}) collective-permute-start(f32[2,32,128]{2,1,0:T(8,128)S(1)} %pad_maximum_fusion.3.refs_4_), channel_id=1, source_target_pairs={{0,1},{1,0},{2,3},{3,2},{4,5},{5,4},{6,7},{7,6},{8,9},{9,8},{10,11... | collective-permute-start | bytes 98312 | tf_op jit(solution)/shard_map/ppermute | solution.py:395
  59.1 5.5 %collective-permute-start.9 = (f32[2,32,128]{2,1,0:T(8,128)S(1)}, f32[2,32,128]{2,1,0:T(8,128)S(1)}, u32[]{:S(2)}, u32[]{:S(2)}) collective-permute-start(f32[2,32,128]{2,1,0:T(8,128)S(1)} %pad_maximum_fusion.3.refs_4_), channel_id=1, source_target_pairs={{0,2},{1,3},{2,0},{3,1},{4,6},{5,7},{6,4},{7,5},{8,10},{9,11},{10,... | collective-permute-start | bytes 98312 | tf_op jit(solution)/shard_map/ppermute | solution.py:395
  64.6 5.7 %collective-permute-start.3 = (bf16[32,1536]{1,0:T(8,128)(2,1)S(1)}, bf16[32,1536]{1,0:T(8,128)(2,1)S(1)}, u32[]{:S(2)}, u32[]{:S(2)}) collective-permute-start(bf16[32,1536]{1,0:T(8,128)(2,1)S(1)} %get-tuple-element.17.refs_0_), channel_id=1, source_target_pairs={{0,1},{1,0},{2,3},{3,2},{4,5},{5,4},{6,7},{7,6},{8,9},{9,8},{10,11... | collective-permute-start | bytes 294920 | tf_op jit(solution)/shard_map/ppermute | solution.py:395
  70.3 24.2 %copy-start.10 = (bf16[32,1536]{1,0:T(8,128)(2,1)}, bf16[32,1536]{1,0:T(8,128)(2,1)S(1)}, u32[]{:S(2)}) copy-start(bf16[32,1536]{1,0:T(8,128)(2,1)S(1)} %collective-permute-done.3.refs_1_) | copy-start | bytes 294916
  70.3 7.1 %collective-permute-start.4 = (bf16[32,1536]{1,0:T(8,128)(2,1)S(1)}, bf16[32,1536]{1,0:T(8,128)(2,1)S(1)}, u32[]{:S(2)}, u32[]{:S(2)}) collective-permute-start(bf16[32,1536]{1,0:T(8,128)(2,1)S(1)} %get-tuple-element.17.refs_0_), channel_id=1, source_target_pairs={{0,2},{1,3},{2,0},{3,1},{4,6},{5,7},{6,4},{7,5},{8,10},{9,11},{10,... | collective-permute-start | bytes 294920 | tf_op jit(solution)/shard_map/ppermute | solution.py:395
  77.4 17.1 %copy-start.11 = (bf16[32,1536]{1,0:T(8,128)(2,1)}, bf16[32,1536]{1,0:T(8,128)(2,1)S(1)}, u32[]{:S(2)}) copy-start(bf16[32,1536]{1,0:T(8,128)(2,1)S(1)} %collective-permute-done.4.refs_2_) | copy-start | bytes 294916
  77.4 6.4 %collective-permute-start.5 = (bf16[32,1536]{1,0:T(8,128)(2,1)S(1)}, bf16[32,1536]{1,0:T(8,128)(2,1)S(1)}, u32[]{:S(2)}, u32[]{:S(2)}) collective-permute-start(bf16[32,1536]{1,0:T(8,128)(2,1)S(1)} %get-tuple-element.17.refs_0_), channel_id=1, source_target_pairs={{0,3},{1,2},{2,1},{3,0},{4,7},{5,6},{6,5},{7,4},{8,11},{9,10},{10,... | collective-permute-start | bytes 294920 | tf_op jit(solution)/shard_map/ppermute | solution.py:395
  79.9 14.6 %collective-permute-start.12 = (bf16[1536,128]{1,0:T(8,128)(2,1)S(1)}, bf16[1536,128]{1,0:T(8,128)(2,1)S(1)}, u32[]{:S(2)}, u32[]{:S(2)}) collective-permute-start(bf16[1536,128]{1,0:T(8,128)(2,1)S(1)} %collective-permute-done.11.refs_11_), channel_id=1, source_target_pairs={{0,16},{16,0},{1,17},{17,1},{2,18},{18,2},{3,19},{19,3},{4,20},{20... | collective-permute-start | bytes 1179656 | tf_op jit(solution)/shard_map/ppermute | solution.py:395
  83.8 10.7 %copy-start.12 = (bf16[32,1536]{1,0:T(8,128)(2,1)}, bf16[32,1536]{1,0:T(8,128)(2,1)S(1)}, u32[]{:S(2)}) copy-start(bf16[32,1536]{1,0:T(8,128)(2,1)S(1)} %collective-permute-done.5.refs_3_) | copy-start | bytes 294916
  83.8 2.8 %copy-start.1 = (bf16[16,1536,128]{2,1,0:T(8,128)(2,1)S(1)}, bf16[16,1536,128]{2,1,0:T(8,128)(2,1)}, u32[]{:S(2)}) copy-start(bf16[16,1536,128]{2,1,0:T(8,128)(2,1)} %refs_9_.3) | copy-start | bytes 18874372
  90.4 6.8 %collective-permute-start.16 = (bf16[128,1536]{1,0:T(8,128)(2,1)S(1)}, bf16[128,1536]{1,0:T(8,128)(2,1)S(1)}, u32[]{:S(2)}, u32[]{:S(2)}) collective-permute-start(bf16[128,1536]{1,0:T(8,128)(2,1)S(1)} %up_send.1), channel_id=1, source_target_pairs={{0,4},{4,0},{8,12},{12,8},{1,5},{5,1},{9,13},{13,9},{2,6},{6,2},{1... | collective-permute-start | bytes 1179656 | tf_op jit(solution)/shard_map/ppermute | solution.py:395
  92.6 12.2 %collective-permute-start.22 = (bf16[128,1536]{1,0:T(8,128)(2,1)}, bf16[128,1536]{1,0:T(8,128)(2,1)}, u32[]{:S(2)}, u32[]{:S(2)}) collective-permute-start(bf16[128,1536]{1,0:T(8,128)(2,1)} %get-tuple-element.24), channel_id=1, source_target_pairs={{0,8},{4,12},{8,0},{12,4},{1,9},{5,13},{9,1},{13,5},{2,10},{6,14},... | collective-permute-start | bytes 1179656 | tf_op jit(solution)/shard_map/ppermute | solution.py:395
  93.6 18.8 %collective-permute-start.20 = (bf16[128,1536]{1,0:T(8,128)(2,1)}, bf16[128,1536]{1,0:T(8,128)(2,1)}, u32[]{:S(2)}, u32[]{:S(2)}) collective-permute-start(bf16[128,1536]{1,0:T(8,128)(2,1)} %get-tuple-element.25), channel_id=1, source_target_pairs={{0,12},{4,8},{8,4},{12,0},{1,13},{5,9},{9,5},{13,1},{2,14},{6,10},... | collective-permute-start | bytes 1179656 | tf_op jit(solution)/shard_map/ppermute | solution.py:395
  94.4 5.1 %copy-start.21 = (s32[4,1,2,32]{3,2,1,0:T(2,128)S(1)}, s32[4,1,2,32]{3,2,1,0:T(2,128)}, u32[]{:S(2)}) copy-start(s32[4,1,2,32]{3,2,1,0:T(2,128)} %param.28) | copy-start | bytes 3076
  94.5 6.3 %copy-start.20 = (s32[4,1,2]{0,2,1:T(2,128)S(1)}, s32[4,1,2]{0,2,1:T(2,128)}, u32[]{:S(2)}) copy-start(s32[4,1,2]{0,2,1:T(2,128)} %param.29) | copy-start | bytes 100
  97.2 26.6 %copy-start.5 = (bf16[2,128,6144]{2,1,0:T(8,128)(2,1)S(1)}, bf16[2,128,6144]{2,1,0:T(8,128)(2,1)}, u32[]{:S(2)}) copy-start(bf16[2,128,6144]{2,1,0:T(8,128)(2,1)} %near_ref.1) | copy-start | bytes 9437188
  98.0 23.2 %collective-permute-start.17 = (bf16[128,1536]{1,0:T(8,128)(2,1)}, bf16[128,1536]{1,0:T(8,128)(2,1)}, u32[]{:S(2)}, u32[]{:S(2)}) collective-permute-start(bf16[128,1536]{1,0:T(8,128)(2,1)} %add_convert_fusion), channel_id=1, source_target_pairs={{0,8},{4,12},{8,0},{12,4},{1,9},{5,13},{9,1},{13,5},{2,10},{6,14},... | collective-permute-start | bytes 1179656 | tf_op jit(solution)/shard_map/ppermute | solution.py:395
  104.8 18.9 %collective-permute-start.23 = (bf16[128,1536]{1,0:T(8,128)(2,1)}, bf16[128,1536]{1,0:T(8,128)(2,1)S(1)}, u32[]{:S(2)}, u32[]{:S(2)}) collective-permute-start(bf16[128,1536]{1,0:T(8,128)(2,1)} %collective-permute-done.22.first_ref), channel_id=1, source_target_pairs={{0,16},{16,0},{1,17},{17,1},{2,18},{18,2},{3,19},{19,3},{4,20},{20... | collective-permute-start | bytes 1179656 | tf_op jit(solution)/shard_map/ppermute | solution.py:395
  112.4 17.5 %collective-permute-start.21 = (bf16[128,1536]{1,0:T(8,128)(2,1)}, bf16[128,1536]{1,0:T(8,128)(2,1)S(1)}, u32[]{:S(2)}, u32[]{:S(2)}) collective-permute-start(bf16[128,1536]{1,0:T(8,128)(2,1)} %collective-permute-done.20.first_ref), channel_id=1, source_target_pairs={{0,16},{16,0},{1,17},{17,1},{2,18},{18,2},{3,19},{19,3},{4,20},{20... | collective-permute-start | bytes 1179656 | tf_op jit(solution)/shard_map/ppermute | solution.py:395
  122.5 7.4 %collective-permute-start.18 = (bf16[128,1536]{1,0:T(8,128)(2,1)S(1)}, bf16[128,1536]{1,0:T(8,128)(2,1)S(1)}, u32[]{:S(2)}, u32[]{:S(2)}) collective-permute-start(bf16[128,1536]{1,0:T(8,128)(2,1)S(1)} %fusion.hidden_ref), channel_id=1, source_target_pairs={{0,4},{4,0},{8,12},{12,8},{1,5},{5,1},{9,13},{13,9},{2,6},{6,2},{1... | collective-permute-start | bytes 1179656 | tf_op jit(solution)/shard_map/ppermute | solution.py:395
  123.8 2.8 %copy-start.2 = (bf16[16,128,1536]{2,1,0:T(8,128)(2,1)S(1)}, bf16[16,128,1536]{2,1,0:T(8,128)(2,1)}, u32[]{:S(2)}) copy-start(bf16[16,128,1536]{2,1,0:T(8,128)(2,1)} %hot_ref.3) | copy-start | bytes 18874372
  130.0 2.8 %copy-start.3 = (bf16[16,128,1536]{2,1,0:T(8,128)(2,1)S(1)}, bf16[16,128,1536]{2,1,0:T(8,128)(2,1)}, u32[]{:S(2)}) copy-start(bf16[16,128,1536]{2,1,0:T(8,128)(2,1)} %hot_ref.3) | copy-start | bytes 18874372
  136.3 7.1 %collective-permute-start.24 = (bf16[32,1536]{1,0:T(8,128)(2,1)S(1)}, bf16[32,1536]{1,0:T(8,128)(2,1)S(1)}, u32[]{:S(2)}, u32[]{:S(2)}) collective-permute-start(bf16[32,1536]{1,0:T(8,128)(2,1)S(1)} %get-tuple-element.21), channel_id=1, source_target_pairs={{0,1},{1,0},{2,3},{3,2},{4,5},{5,4},{6,7},{7,6},{8,9},{9,8},{10,11... | collective-permute-start | bytes 294920 | tf_op jit(solution)/shard_map/ppermute | solution.py:395
  136.4 10.9 %collective-permute-start.25 = (bf16[32,1536]{1,0:T(8,128)(2,1)S(1)}, bf16[32,1536]{1,0:T(8,128)(2,1)S(1)}, u32[]{:S(2)}, u32[]{:S(2)}) collective-permute-start(bf16[32,1536]{1,0:T(8,128)(2,1)S(1)} %get-tuple-element.22), channel_id=1, source_target_pairs={{0,2},{1,3},{2,0},{3,1},{4,6},{5,7},{6,4},{7,5},{8,10},{9,11},{10,... | collective-permute-start | bytes 294920 | tf_op jit(solution)/shard_map/ppermute | solution.py:395
  139.4 7.8 %collective-permute-start.26 = (bf16[32,1536]{1,0:T(8,128)(2,1)S(1)}, bf16[32,1536]{1,0:T(8,128)(2,1)S(1)}, u32[]{:S(2)}, u32[]{:S(2)}) collective-permute-start(bf16[32,1536]{1,0:T(8,128)(2,1)S(1)} %get-tuple-element.23), channel_id=1, source_target_pairs={{0,3},{1,2},{2,1},{3,0},{4,7},{5,6},{6,5},{7,4},{8,11},{9,10},{10,... | collective-permute-start | bytes 294920 | tf_op jit(solution)/shard_map/ppermute | solution.py:395

commit v2 on v0

--- a/solution.py
+++ b/solution.py
@@ -1,8 +1,11 @@
+import functools
 import math
 
 import jax
 import jax.numpy as jnp
 from jax import lax
+from jax.experimental import pallas as pl
+from jax.experimental.pallas import tpu as pltpu
 from jax.sharding import PartitionSpec as P
 
 HD = 128
@@ -112,6 +115,433 @@
     return (state, ffn_out)
 
 
+BIG = 60 * 2**20
+PAD = 16
+
+
+def params(limit=BIG):
+    return pltpu.CompilerParams(vmem_limit_bytes=limit)
+
+
+def attention_kernel(
+    lengths, q_ref, k_ref, v_ref, kn_ref, vn_ref, gain_ref, out_ref, *, here, steps, context
+):
+    rows = steps * here
+    wide = q_ref.shape[1]
+    parts = wide // HD
+    q = q_ref[...]
+    lane_head = lax.broadcasted_iota(jnp.int32, (rows, wide), 1) // HD
+    split = jnp.concatenate(
+        [jnp.where(lane_head == i, q, jnp.zeros_like(q)) for i in range(parts)], axis=0
+    )
+    nt = (((1,), (1,)), ((), ()))
+    scores = lax.dot_general(split, k_ref[...], nt, preferred_element_type=jnp.float32)
+    row = lax.broadcasted_iota(jnp.int32, (parts * rows, context), 0) % here
+    slot = lax.broadcasted_iota(jnp.int32, (parts * rows, context), 1)
+    limit = jnp.zeros_like(slot)
+    own = scores[:, :context]
+    for r in range(here):
+        limit = jnp.where(row == r, lengths[r], limit)
+        if r:
+            own = jnp.where(row == r, scores[:, r * context : (r + 1) * context], own)
+    factor = 1.0 / math.sqrt(HD)
+    own = jnp.where(slot < limit, own * factor, -jnp.inf)
+    fresh = lax.dot_general(split, kn_ref[...], nt, preferred_element_type=jnp.float32) * factor
+    at = lax.broadcasted_iota(jnp.int32, (parts * rows, rows), 0) % rows
+    to = lax.broadcasted_iota(jnp.int32, (parts * rows, rows), 1)
+    seen = (at % here == to % here) & (to // here <= at // here)
+    fresh = jnp.where(seen, fresh, -jnp.inf)
+    top = jnp.maximum(
+        jnp.max(own, axis=-1, keepdims=True), jnp.max(fresh, axis=-1, keepdims=True)
+    )
+    own = jnp.exp(own - top)
+    fresh = jnp.exp(fresh - top)
+    scale = 1.0 / (
+        jnp.sum(own, axis=-1, keepdims=True) + jnp.sum(fresh, axis=-1, keepdims=True)
+    )
+    own = own * scale
+    spread = jnp.concatenate(
+        [jnp.where(row == r, own, 0.0).astype(jnp.bfloat16) for r in range(here)], axis=1
+    )
+    got = jnp.dot(spread, v_ref[...], preferred_element_type=jnp.float32)
+    got = got + jnp.dot(
+        (fresh * scale).astype(jnp.bfloat16), vn_ref[...], preferred_element_type=jnp.float32
+    )
+    answer = got[:rows]
+    for i in range(1, parts):
+        answer = jnp.where(lane_head == i, got[i * rows : (i + 1) * rows], answer)
+    gain = jnp.broadcast_to(gain_ref[...].astype(jnp.float32), (PAD, wide))
+    out_ref[...] = jnp.concatenate([answer, gain], axis=0).astype(jnp.bfloat16)
+
+
+def attention(queries, key_cache, value_cache, key_new, value_new, gain, lengths):
+    steps, here, width = queries.shape
+    context = key_cache.shape[1]
+    wide = 2 * HD
+    rows = steps * here
+    column = lambda i, *_: (0, i)
+    small = pl.BlockSpec((rows, wide), column)
+    large = pl.BlockSpec((here * context, wide), column)
+    flat = lambda a: a.reshape(-1, width)
+    return pl.pallas_call(
+        functools.partial(attention_kernel, here=here, steps=steps, context=context),
+        grid_spec=pltpu.PrefetchScalarGridSpec(
+            num_scalar_prefetch=1,
+            grid=(width // wide,),
+            in_specs=[small, large, large, small, small, pl.BlockSpec((1, wide), column)],
+            out_specs=pl.BlockSpec((rows + PAD, wide), column),
+        ),
+        out_shape=jax.ShapeDtypeStruct((rows + PAD, width), jnp.bfloat16),
+        compiler_params=params(),
+        name="attention",
+    )(
+        lengths,
+        flat(queries),
+        flat(key_cache),
+        flat(value_cache),
+        flat(key_new),
+        flat(value_new),
+        gain,
+    )
+
+
+def project_kernel(place, rows_ref, weight_ref, *outs):
+    chunk = outs[0].shape[0]
+    rows = jnp.concatenate(
+        [rows_ref[place[0] ^ m, :chunk, :] for m in range(len(outs))], axis=0
+    )
+    made = jnp.dot(rows, weight_ref[...], preferred_element_type=jnp.float32)
+    for m, out in enumerate(outs):
+        out[...] = made[m * chunk : (m + 1) * chunk].astype(out.dtype)
+
+
+def project(place, gathered, weight):
+    parts, padded, depth = gathered.shape
+    width = weight.shape[1]
+    chunk = padded - PAD
+    wide = width // 3
+    return pl.pallas_call(
+        project_kernel,
+        grid_spec=pltpu.PrefetchScalarGridSpec(
+            num_scalar_prefetch=1,
+            grid=(width // wide,),
+            in_specs=[
+                pl.BlockSpec(gathered.shape, lambda i, *_: (0, 0, 0)),
+                pl.BlockSpec((depth, wide), lambda i, *_: (0, i)),
+            ],
+            out_specs=[pl.BlockSpec((chunk, wide), lambda i, *_: (0, i))] * parts,
+        ),
+        out_shape=[
+            jax.ShapeDtypeStruct((chunk, width), jnp.bfloat16 if m else jnp.float32)
+            for m in range(parts)
+        ],
+        compiler_params=params(),
+        name="project",
+    )(place, gathered, weight)
+
+
+def join_kernel(*refs):
+    total = refs[0][...].astype(jnp.float32)
+    for ref in refs[1:-1]:
+        total = total + ref[...].astype(jnp.float32)
+    refs[-1][...] = total.astype(refs[-1].dtype)
+
+
+def join(name, *terms):
+    return pl.pallas_call(
+        join_kernel,
+        out_shape=jax.ShapeDtypeStruct(terms[0].shape, jnp.bfloat16),
+        compiler_params=params(),
+        name=name,
+    )(*terms)
+
+
+def norm_kernel(place, gathered_ref, *refs, parts):
+    out_ref = refs[-1]
+    blocks = (len(refs) - 1) // parts
+    chunk, width = refs[0].shape
+    b = place[4]
+    for m in range(parts):
+        rows = [refs[k * parts + m][...].astype(jnp.float32) for k in range(blocks)]
+        mean = sum(jnp.sum(r, axis=-1, keepdims=True) for r in rows) / D
+        rows = [r - mean for r in rows]
+        variance = sum(jnp.sum(r * r, axis=-1, keepdims=True) for r in rows) / D
+        scale = lax.rsqrt(variance + 1e-05)
+        for k in range(blocks):
+            gain = gathered_ref[b ^ k, chunk : chunk + PAD, :].astype(jnp.float32)[:1]
+            out_ref[m * chunk : (m + 1) * chunk, k * width : (k + 1) * width] = (
+                rows[k] * scale * gain
+            ).astype(jnp.bfloat16)
+
+
+def norm(place, gathered, columns):
+    blocks, parts = len(columns), len(columns[0])
+    chunk, width = columns[0][0].shape
+    whole = lambda a: pl.BlockSpec(a.shape, lambda i, *_: (0,) * a.ndim)
+    flat = [a for column in columns for a in column]
+    return pl.pallas_call(
+        functools.partial(norm_kernel, parts=parts),
+        grid_spec=pltpu.PrefetchScalarGridSpec(
+            num_scalar_prefetch=1,
+            grid=(1,),
+            in_specs=[whole(gathered)] + [whole(a) for a in flat],
+            out_specs=pl.BlockSpec((parts * chunk, blocks * width), lambda i, *_: (0, 0)),
+        ),
+        out_shape=jax.ShapeDtypeStruct((parts * chunk, blocks * width), jnp.bfloat16),
+        compiler_params=params(),
+        name="norm",
+    )(place, gathered, *flat)
+
+
+def up_kernel(place, rows_ref, hot_ref, out_ref):
+    weight = jnp.concatenate([hot_ref[i] for i in range(hot_ref.shape[0])], axis=1)
+    out_ref[...] = jnp.dot(
+        rows_ref[...], weight, preferred_element_type=jnp.float32
+    ).astype(out_ref.dtype)
+
+
+def up(place, half, normed, hot):
+    width = hot.shape[1]
+    rows = normed.shape[0]
+    per = 2
+    steps = hot.shape[0] // (2 * per)
+    return pl.pallas_call(
+        up_kernel,
+        grid_spec=pltpu.PrefetchScalarGridSpec(
+            num_scalar_prefetch=1,
+            grid=(steps,),
+            in_specs=[
+                pl.BlockSpec((rows, width), lambda i, *_: (0, 0)),
+                pl.BlockSpec(
+                    (per, width, HD), lambda i, place: ((place[3] ^ half) * steps + i, 0, 0)
+                ),
+            ],
+            out_specs=pl.BlockSpec((rows, per * HD), lambda i, *_: (0, i)),
+        ),
+        out_shape=jax.ShapeDtypeStruct((rows, steps * per * HD), jnp.bfloat16),
+        compiler_params=params(),
+        name="up_keep" if half == 0 else "up_send",
+    )(place, normed, hot)
+
+
+def hidden_kernel(place, counts, rows_ref, lists_ref, up_ref, out_ref, sums, *, parts, steps):
+    step = pl.program_id(0)
+    total = rows_ref.shape[0]
+    chunk = total // parts
+    here = chunk // steps
+
+    @pl.when(step == 0)
+    def _():
+        sums[...] = jnp.zeros_like(sums)
+
+    weight = jnp.concatenate([up_ref[0], up_ref[1]], axis=1)
+    sums[...] += jnp.dot(rows_ref[...], weight, preferred_element_type=jnp.float32)
+
+    @pl.when(step == pl.num_programs(0) - 1)
+    def _():
+        slots = lists_ref.shape[3]
+        index = lax.broadcasted_iota(jnp.int32, (total, slots), 0)
+        slot = lax.broadcasted_iota(jnp.int32, (total, slots), 1)
+        owner = (index // chunk) ^ place[0]
+        row = (index // here % steps) * (parts * here) + owner * here + index % here
+        for c in range(2):
+            hit = (row == lists_ref[0, 0, c : c + 1, :]) & (slot < counts[2 * place[4] + c])
+            used = jnp.max(jnp.where(hit, 1.0, 0.0), axis=-1, keepdims=True)
+            made = jnp.maximum(sums[:, c * HD : (c + 1) * HD], 0.0) * used
+            out_ref[:, c * HD : (c + 1) * HD] = made.astype(out_ref.dtype)
+
+
+def cold_hidden(place, counts, normed, lists, cold_up, parts, steps):
+    rows = normed.shape[0]
+    blocks = lists.shape[0]
+    width = normed.shape[1] // blocks
+    return pl.pallas_call(
+        functools.partial(hidden_kernel, parts=parts, steps=steps),
+        grid_spec=pltpu.PrefetchScalarGridSpec(
+            num_scalar_prefetch=2,
+            grid=(blocks,),
+            in_specs=[
+                pl.BlockSpec((rows, width), lambda i, *_: (0, i)),
+                pl.BlockSpec((1,) + lists.shape[1:], lambda i, place, _: (place[4], 0, 0, 0)),
+                pl.BlockSpec((2, width, HD), lambda i, place, _: (0, place[4] ^ i, 0)),
+            ],
+            out_specs=pl.BlockSpec((rows, 2 * HD), lambda i, *_: (0, 0)),
+            scratch_shapes=[pltpu.VMEM((rows, 2 * HD), jnp.float32)],
+        ),
+        out_shape=jax.ShapeDtypeStruct((rows, 2 * HD), jnp.bfloat16),
+        compiler_params=params(),
+        name="cold_hidden",
+    )(place, counts, normed, lists, cold_up)
+
+
+def piece_kernel(place, hidden_ref, down_ref, out_ref):
+    depth, wide = down_ref.shape[1:]
+    out_ref[0] = jnp.dot(
+        hidden_ref[...],
+        down_ref[...].reshape(2 * depth, wide),
+        preferred_element_type=jnp.float32,
+    ).astype(out_ref.dtype)
+
+
+def cold_pieces(place, odd, hidden, cold_down, blocks):
+    rows = hidden.shape[0]
+    width = cold_down.shape[2] // blocks
+    return pl.pallas_call(
+        piece_kernel,
+        grid_spec=pltpu.PrefetchScalarGridSpec(
+            num_scalar_prefetch=1,
+            grid=(2,),
+            in_specs=[
+                pl.BlockSpec(hidden.shape, lambda i, *_: (0, 0)),
+                pl.BlockSpec((2, HD, width), lambda i, place: (0, 0, place[4] ^ (2 * i + odd))),
+            ],
+            out_specs=pl.BlockSpec((1, rows, width), lambda i, *_: (i, 0, 0)),
+        ),
+        out_shape=jax.ShapeDtypeStruct((2, rows, width), jnp.bfloat16),
+        compiler_params=params(),
+        name="cold_send" if odd else "cold_keep",
+    )(place, hidden, cold_down)
+
+
+def down_kernel(place, hidden_ref, hot_ref, *refs):
+    blocks, depth, wide = hot_ref.shape
+    made = jnp.dot(
+        hidden_ref[...],
+        hot_ref[...].reshape(blocks * depth, wide),
+        preferred_element_type=jnp.float32,
+    )
+    for ref in refs[:-1]:
+        made = made + (ref[0] if ref.ndim == 3 else ref[...]).astype(jnp.float32)
+    refs[-1][...] = made
+
+
+def down(place, half, hidden, hot, *before):
+    rows = hidden.shape[0]
+    width = hot.shape[2]
+    wide = width // 3
+    blocks = hot.shape[0] // 2
+    column = lambda i, *_: (0, i)
+    return pl.pallas_call(
+        down_kernel,
+        grid_spec=pltpu.PrefetchScalarGridSpec(
+            num_scalar_prefetch=1,
+            grid=(width // wide,),
+            in_specs=[
+                pl.BlockSpec(hidden.shape, lambda i, *_: (0, 0)),
+                pl.BlockSpec((blocks, HD, wide), lambda i, place: (place[3] ^ half, 0, i)),
+            ]
+            + [
+                pl.BlockSpec((1, rows, wide), lambda i, *_: (0, 0, i))
+                if a.ndim == 3
+                else pl.BlockSpec((rows, wide), column)
+                for a in before
+            ],
+            out_specs=pl.BlockSpec((rows, wide), column),
+        ),
+        out_shape=jax.ShapeDtypeStruct((rows, width), jnp.float32),
+        compiler_params=params(),
+        name="down_keep" if half == 0 else "down_got",
+    )(place, hidden, hot, *before)
+
+
+def chunks_kernel(base_ref, more_ref, *outs):
+    made = base_ref[...] + more_ref[...].astype(jnp.float32)
+    chunk = outs[0].shape[0]
+    for m, out in enumerate(outs):
+        out[...] = made[m * chunk : (m + 1) * chunk].astype(out.dtype)
+
+
+def into_chunks(base, more, parts):
+    rows, width = base.shape
+    return pl.pallas_call(
+        chunks_kernel,
+        out_shape=[
+            jax.ShapeDtypeStruct((rows // parts, width), jnp.bfloat16 if m else jnp.float32)
+            for m in range(parts)
+        ],
+        compiler_params=params(),
+        name="into_chunks",
+    )(base, more)
+
+
+def swap(x, axis, m, size=4):
+    return lax.ppermute(x, axis, [(i, i ^ m) for i in range(size)])
+
+
+def local_fast(
+    queries,
+    key_cache,
+    value_cache,
+    key_new,
+    value_new,
+    lengths,
+    out_proj,
+    residual,
+    norm_gain,
+    hot_up,
+    hot_down,
+    cold_up,
+    cold_down,
+    block_rows,
+    block_counts,
+):
+    steps, here, _ = queries.shape
+    all_rows, width = residual.shape[1:]
+    parts = all_rows // here
+    blocks = block_rows.shape[0]
+    others = range(1, parts)
+    b = lax.axis_index("blocks")
+    h = lax.axis_index("heads")
+    place = jnp.stack([h, b // 2, b, b % 2, b]).astype(jnp.int32)
+    counts = block_counts.reshape(-1)
+
+    gain = norm_gain[None]
+    attended = attention(queries, key_cache, value_cache, key_new, value_new, gain, lengths)
+    gathered = lax.all_gather(attended, "blocks", axis=0)
+    pieces = project(place, gathered, out_proj)
+    got = [swap(pieces[m], "heads", m) for m in others]
+    mine = lax.dynamic_slice(residual, (0, h * here, 0), (steps, here, width))
+    state = join("join", mine.reshape(steps * here, width), pieces[0], *got)
+    states = [state] + [swap(state, "heads", m) for m in others]
+    across = [swap(s, "blocks", 2) for s in states]
+    columns = [
+        states,
+        [swap(s, "blocks", 1) for s in states],
+        across,
+        [swap(s, "blocks", 1) for s in across],
+    ]
+    normed = norm(place, gathered, columns)
+
+    sent = swap(up(place, 1, normed, hot_up), "blocks", 1)
+    kept = up(place, 0, normed, hot_up)
+    summed = join("join_hot", kept, sent)
+    arrived = swap(summed, "blocks", 2)
+
+    cold = cold_hidden(place, counts, normed, block_rows, cold_up, parts, steps)
+    cold_got = swap(cold_pieces(place, 1, cold, cold_down, blocks), "blocks", 1)
+    cold_kept = cold_pieces(place, 0, cold, cold_down, blocks)
+    far = (cold_kept[1].astype(jnp.float32) + cold_got[1].astype(jnp.float32)).astype(jnp.bfloat16)
+    cold_far = swap(far, "blocks", 2)
+
+    total = summed.astype(jnp.float32) + arrived.astype(jnp.float32)
+    hidden = jnp.maximum(total, 0.0).astype(jnp.bfloat16)
+    partner = swap(hidden, "blocks", 1)
+    base = down(place, 0, hidden, hot_down)
+    base = down(place, 1, partner, hot_down, base, cold_kept, cold_got)
+    made = into_chunks(base, cold_far, parts)
+    out = made[0]
+    for m in others:
+        out = out + swap(made[m], "heads", m).astype(jnp.float32)
+    ffn_out = out.astype(jnp.bfloat16).reshape(steps, here, width)
+
+    stacked = jnp.stack(states).reshape(parts, steps, 1, here, width)
+    ordered = [
+        lax.dynamic_index_in_dim(stacked, c ^ h, axis=0, keepdims=False) for c in range(parts)
+    ]
+    attn_state = jnp.concatenate(ordered, axis=1).reshape(steps, all_rows, width)
+    return (attn_state, ffn_out)
+
+
 def solution(mesh):
     placed = (
         P(None, ("groups", "blocks"), "heads"),
@@ -130,8 +560,9 @@
         P("groups", "heads", None, None),
         P("groups", "heads", None),
     )
+    sizes = tuple(mesh.shape[a] for a in ("blocks", "heads"))
     return jax.shard_map(
-        local,
+        local_fast if sizes == (4, 4) else local,
         mesh=mesh,
         in_specs=placed,
         out_specs=(P(None, "groups", "blocks"), P(None, ("groups", "heads"), "blocks")),

time: 211 us -> 128 us (0.61)
  Pallas kernels: 0 us -> 54.9 us
  waiting for transfers between devices: 79.7 us -> 27.8 us
  local copies, waits for them, and re-layouts: 50.6 us -> 7.05 us
  matrix products: 23.9 us -> 0 us
  between operations: 13.9 us -> 0.93 us
  starting transfers between devices: 8.68 us -> 21.4 us
  blocking collectives: 21.5 us -> 10.6 us
  other arithmetic: 11.6 us -> 3.92 us
    pallas_call x0 -> x13, Pallas kernels: none -> 54.9 us  [the longest x2 9.91 us: down(): pl.pallas_call(down_kernel, grid_spec=pltpu.PrefetchScalarGridSpec(num_sc...]
    psum x2 -> x0, waiting for transfers between devices: 41.4 us -> none  [the longest x1 38 us: local(): lax.psum(partial_out.astype(jnp.bfloat16), 'heads').astype(jnp.float32)]
    ppermute x0 -> x26, waiting for transfers between devices: none -> 27.8 us  [swap(): return lax.ppermute(x, axis, [(i, i ^ m) for i in range(size)])]
    dot_general x8 -> x0, matrix products: 23.9 us -> none  [the longest x1 4.58 us: local(): jnp.einsum('trc,kch->trkh', normed, hot_up, preferred_element_type=jnp.fl...]
    ppermute x0 -> x26, starting transfers between devices: none -> 21.4 us  [swap(): return lax.ppermute(x, axis, [(i, i ^ m) for i in range(size)])]
    unnamed x4 -> x0, waiting for transfers between devices: 20.8 us -> none
    unnamed x30 -> x61, local copies, waits for them, and re-layouts: 22.5 us -> 3.76 us
    all_to_all x2 -> x0, waiting for transfers between devices: 17.5 us -> none  [the longest x1 10.7 us: local(): lax.all_to_all(outgoing, 'blocks', split_axis=0, concat_axis=3, tiled=True)]
  transfers between devices with their start and end apart: 5 -> 26, of which waited for: 5 -> 10; matrix products, arithmetic and copies ran while one was open for 14% -> 3% of each run, Pallas kernels for 0% -> 20%
where the time goes in v2:
time: 128 us; the launch traced here: 127 us
  Pallas kernels  54.9 us (43%)
  waiting for transfers between devices  27.8 us (22%)
  starting transfers between devices  21.4 us (17%)
  blocking collectives  10.6 us (8%)
  local copies, waits for them, and re-layouts  7.05 us (6%)
  other arithmetic  3.92 us (3%)
    ppermute x26, waiting for transfers between devices, swap(): return lax.ppermute(x, axis, [(i, i ^ m) for i in range(size)])  27.8 us
    ppermute x26, starting transfers between devices, swap(): return lax.ppermute(x, axis, [(i, i ^ m) for i in range(size)])  21.4 us
    all_gather x1, blocking collectives, local_fast(): gathered = lax.all_gather(attended, 'blocks', axis=0)  10.6 us
    pallas_call x2, Pallas kernels, down(): pl.pallas_call(down_kernel, grid_spec=pltpu.PrefetchScalarGridSpec(num_sc...  9.91 us
    pallas_call x2, Pallas kernels, up(): pl.pallas_call(up_kernel, grid_spec=pltpu.PrefetchScalarGridSpec(num_scal...  9.84 us
    pallas_call x1, Pallas kernels, attention(): pl.pallas_call(functools.partial(attention_kernel, here=here, steps=steps...  8.34 us
    pallas_call x2, Pallas kernels, cold_pieces(): pl.pallas_call(piece_kernel, grid_spec=pltpu.PrefetchScalarGridSpec(num_s...  6.29 us
    pallas_call x1, Pallas kernels, project(): pl.pallas_call(project_kernel, grid_spec=pltpu.PrefetchScalarGridSpec(num...  5.16 us
  transfers between devices with their start and end apart: 26, of which 10 were waited for; matrix products, arithmetic and copies ran while one was open for 3% of the time, Pallas kernels for 20%

profile of v2, /device:TPU:0, one launch (start us, length us, event | category | flops | bytes accessed | tf_op | source)
XLA Modules:
  0.0 126.6 jit_solution(1988410223737533464)
XLA Ops:
  0.7 1.3 %broadcast_in_dim.3.gain_ref = bf16[1,1536]{1,0:T(2,128)(2,1)} reshape(bf16[1536]{0:T(1024)(128)(2,1)} %param.23) | data formatting | bytes 6144 | tf_op jit(solution)/shard_map/broadcast_in_dim | solution.py:498
  2.0 8.3 %attention.1 = bf16[48,1536]{1,0:T(8,128)(2,1)} custom-call(s32[8]{0:T(128)} %lengths.1, bf16[32,1536]{1,0:T(8,128)(2,1)} %bitcast.40, bf16[1024,1536]{1,0:T(8,128)(2,1)} %bitcast.34, bf16[1024,1536]{1,0:T(8,128)(2,1)} %bitcast.35, bf16[32,1536]{1,0:T(8,128)(2,1)} %bitcast.41, bf16[32,1536]{1,0:T(8,128)(2,1)} %bitcast.42, ...), custom_call_target="tpu_custom_call" | custom-call | tf_op jit(solution)/shard_map/attention/pallas_call | solution.py:186
  10.3 10.6 %all-gather = bf16[192,1536]{1,0:T(8,128)(2,1)} all-gather(bf16[48,1536]{1,0:T(8,128)(2,1)} %attention.1), channel_id=2, replica_groups=mesh['groups'=2,'blocks'=4,'heads'=4] {'blocks'}, dimensions={0}, use_global_device_ids=true | all-gather | bytes 737280 | tf_op jit(solution)/shard_map/all_gather | solution.py:500
  20.9 0.6 stack.35.place
  21.5 5.2 %project.1 = (f32[32,1536]{1,0:T(8,128)}, bf16[32,1536]{1,0:T(8,128)(2,1)}, bf16[32,1536]{1,0:T(8,128)(2,1)}, bf16[32,1536]{1,0:T(8,128)(2,1)}) custom-call(s32[5]{0:T(128)} %stack.35.place, bf16[4,48,1536]{2,1,0:T(8,128)(2,1)} %bitcast.32, bf16[1536,1536]{1,0:T(8,128)(2,1)} %weight_ref.1), custom_call_target="tpu_custom_call" | custom-call | tf_op jit(solution)/shard_map/project/pallas_call | solution.py:223
  26.7 1.6 %collective-permute-start = (bf16[32,1536]{1,0:T(8,128)(2,1)}, bf16[32,1536]{1,0:T(8,128)(2,1)S(1)}, u32[]{:S(2)}, u32[]{:S(2)}) collective-permute-start(bf16[32,1536]{1,0:T(8,128)(2,1)} %get-tuple-element.11), channel_id=1, source_target_pairs={{0,1},{1,0},{2,3},{3,2},{4,5},{5,4},{6,7},{7,6},{8,9},{9,8},{10,11... | collective-permute-start | bytes 294920 | tf_op jit(solution)/shard_map/ppermute | solution.py:468
  28.3 2.6 %collective-permute-start.1 = (bf16[32,1536]{1,0:T(8,128)(2,1)}, bf16[32,1536]{1,0:T(8,128)(2,1)S(1)}, u32[]{:S(2)}, u32[]{:S(2)}) collective-permute-start(bf16[32,1536]{1,0:T(8,128)(2,1)} %get-tuple-element.12), channel_id=1, source_target_pairs={{0,2},{1,3},{2,0},{3,1},{4,6},{5,7},{6,4},{7,5},{8,10},{9,11},{10,... | collective-permute-start | bytes 294920 | tf_op jit(solution)/shard_map/ppermute | solution.py:468
  30.9 0.2 collective-permute-start.2
  31.1 0.6 dynamic-slice_bitcast_fusion.4.refs_0_
  31.7 0.2 collective-permute-done.refs_2_
  32.0 7.2 %collective-permute-done.1.refs_3_ = bf16[32,1536]{1,0:T(8,128)(2,1)S(1)} collective-permute-done((bf16[32,1536]{1,0:T(8,128)(2,1)}, bf16[32,1536]{1,0:T(8,128)(2,1)S(1)}, u32[]{:S(2)}, u32[]{:S(2)}) %collective-permute-start.1) | collective-permute-done | bytes 98336 | tf_op jit(solution)/shard_map/ppermute | solution.py:468
  39.2 0.6 copy-done.15
  39.8 0.0 copy-done.16
  39.8 1.8 %join.1.refs_0_ = bf16[32,1536]{1,0:T(8,128)(2,1)} custom-call(bf16[32,1536]{1,0:T(8,128)(2,1)} %dynamic-slice_bitcast_fusion.4.refs_0_, f32[32,1536]{1,0:T(8,128)} %get-tuple-element.10.refs_1_, bf16[32,1536]{1,0:T(8,128)(2,1)} %copy-done.14, bf16[32,1536]{1,0:T(8,128)(2,1)} %copy-done.15, bf16[32,1536]{1,0:T(8,128)(2,1)} %copy-done.16), custom_call_target="tpu_custom_call" | custom-call | tf_op jit(solution)/shard_map/join/pallas_call | solution.py:251
  41.7 0.5 collective-permute-start.10
  42.2 2.6 %collective-permute-start.5 = (bf16[32,1536]{1,0:T(8,128)(2,1)}, bf16[32,1536]{1,0:T(8,128)(2,1)S(1)}, u32[]{:S(2)}, u32[]{:S(2)}) collective-permute-start(bf16[32,1536]{1,0:T(8,128)(2,1)} %join.1.refs_0_), channel_id=1, source_target_pairs={{0,3},{1,2},{2,1},{3,0},{4,7},{5,6},{6,5},{7,4},{8,11},{9,10},{10,... | collective-permute-start | bytes 294920 | tf_op jit(solution)/shard_map/ppermute | solution.py:468
  44.8 0.7 collective-permute-start.4
  45.5 1.1 collective-permute-start.3
  46.6 2.4 %collective-permute-done.5.refs_3_ = bf16[32,1536]{1,0:T(8,128)(2,1)S(1)} collective-permute-done((bf16[32,1536]{1,0:T(8,128)(2,1)}, bf16[32,1536]{1,0:T(8,128)(2,1)S(1)}, u32[]{:S(2)}, u32[]{:S(2)}) %collective-permute-start.5) | collective-permute-done | bytes 98336 | tf_op jit(solution)/shard_map/ppermute | solution.py:468
  48.9 1.5 %collective-permute-start.13 = (bf16[32,1536]{1,0:T(8,128)(2,1)S(1)}, bf16[32,1536]{1,0:T(8,128)(2,1)S(1)}, u32[]{:S(2)}, u32[]{:S(2)}) collective-permute-start(bf16[32,1536]{1,0:T(8,128)(2,1)S(1)} %collective-permute-done.5.refs_3_), channel_id=1, source_target_pairs={{0,8},{4,12},{8,0},{12,4},{1,9},{5,13},{9,1},{13,5},{2,10},{6,14},... | collective-permute-start | bytes 294920 | tf_op jit(solution)/shard_map/ppermute | solution.py:468
  50.5 3.1 %collective-permute-done.4.refs_2_ = bf16[32,1536]{1,0:T(8,128)(2,1)S(1)} collective-permute-done((bf16[32,1536]{1,0:T(8,128)(2,1)}, bf16[32,1536]{1,0:T(8,128)(2,1)S(1)}, u32[]{:S(2)}, u32[]{:S(2)}) %collective-permute-start.4) | collective-permute-done | bytes 98336 | tf_op jit(solution)/shard_map/ppermute | solution.py:468
  53.5 1.5 %collective-permute-start.12 = (bf16[32,1536]{1,0:T(8,128)(2,1)S(1)}, bf16[32,1536]{1,0:T(8,128)(2,1)S(1)}, u32[]{:S(2)}, u32[]{:S(2)}) collective-permute-start(bf16[32,1536]{1,0:T(8,128)(2,1)S(1)} %collective-permute-done.4.refs_2_), channel_id=1, source_target_pairs={{0,8},{4,12},{8,0},{12,4},{1,9},{5,13},{9,1},{13,5},{2,10},{6,14},... | collective-permute-start | bytes 294920 | tf_op jit(solution)/shard_map/ppermute | solution.py:468
  55.1 0.5 collective-permute-start.11
  55.6 0.5 collective-permute-start.7
  56.1 0.1 collective-permute-start.17
  56.2 2.9 %collective-permute-done.12.refs_10_ = bf16[32,1536]{1,0:T(8,128)(2,1)S(1)} collective-permute-done((bf16[32,1536]{1,0:T(8,128)(2,1)S(1)}, bf16[32,1536]{1,0:T(8,128)(2,1)S(1)}, u32[]{:S(2)}, u32[]{:S(2)}) %collective-permute-start.12) | collective-permute-done | bytes 98336 | tf_op jit(solution)/shard_map/ppermute | solution.py:468
  59.1 1.2 collective-permute-done.11.refs_9_
  60.3 0.1 copy.18
  60.4 0.7 reshape.51.counts
  61.1 0.5 collective-permute-done.15.refs_13_
  61.6 0.0 copy-done.24
  61.7 0.0 copy-done.25
  61.7 0.0 copy-done.26
  61.7 0.0 copy-done.27
  61.8 0.6 copy-done.28
  62.4 4.7 %norm.1.rows_ref = bf16[128,6144]{1,0:T(8,128)(2,1)} custom-call(s32[5]{0:T(128)} %stack.35.place, bf16[4,48,1536]{2,1,0:T(8,128)(2,1)} %bitcast.33, bf16[32,1536]{1,0:T(8,128)(2,1)} %join.1.refs_0_, bf16[32,1536]{1,0:T(8,128)(2,1)} %copy-done.10, bf16[32,1536]{1,0:T(8,128)(2,1)} %copy-done.8, bf16[32,1536]{1,0:T(8,128)(2,1)} %copy-done.6, ...), custom_call_target="tpu_custom_call" | custom-call | tf_op jit(solution)/shard_map/norm/pallas_call | solution.py:282
  67.1 5.0 %cold_hidden.1.hidden_ref = bf16[128,256]{1,0:T(8,128)(2,1)} custom-call(s32[5]{0:T(128)} %stack.35.place, s32[8]{0:T(128)} %reshape.51.counts, bf16[128,6144]{1,0:T(8,128)(2,1)} %norm.1.rows_ref, s32[4,1,2,32]{3,2,1,0:T(2,128)} %lists_ref.1, bf16[2,6144,128]{2,1,0:T(8,128)(2,1)} %up_ref.1), custom_call_target="tpu_custom_call" | custom-call | tf_op jit(solution)/shard_map/cold_hidden/pallas_call | solution.py:358
  72.1 3.1 %cold_send.1 = bf16[2,128,1536]{2,1,0:T(8,128)(2,1)} custom-call(s32[5]{0:T(128)} %stack.35.place, bf16[128,256]{1,0:T(8,128)(2,1)} %cold_hidden.1.hidden_ref, bf16[2,128,6144]{2,1,0:T(8,128)(2,1)} %down_ref.3), custom_call_target="tpu_custom_call" | custom-call | tf_op jit(solution)/shard_map/cold_send/pallas_call | solution.py:389
  75.2 0.5 collective-permute-start.21
  75.7 4.9 %up_send.1 = bf16[128,1024]{1,0:T(8,128)(2,1)} custom-call(s32[5]{0:T(128)} %stack.35.place, bf16[128,6144]{1,0:T(8,128)(2,1)} %norm.1.rows_ref, bf16[16,1536,128]{2,1,0:T(8,128)(2,1)} %hot_ref.5), custom_call_target="tpu_custom_call" | custom-call | tf_op jit(solution)/shard_map/up_send/pallas_call | solution.py:308
  80.6 0.0 collective-permute-start.18
  80.7 4.9 %up_keep.1.refs_0_ = bf16[128,1024]{1,0:T(8,128)(2,1)} custom-call(s32[5]{0:T(128)} %stack.35.place, bf16[128,6144]{1,0:T(8,128)(2,1)} %norm.1.rows_ref, bf16[16,1536,128]{2,1,0:T(8,128)(2,1)} %hot_ref.5), custom_call_target="tpu_custom_call" | custom-call | tf_op jit(solution)/shard_map/up_keep/pallas_call | solution.py:308
  85.6 0.7 copy-done.13
  86.3 1.8 %join_hot.1 = bf16[128,1024]{1,0:T(8,128)(2,1)} custom-call(bf16[128,1024]{1,0:T(8,128)(2,1)} %up_keep.1.refs_0_, bf16[128,1024]{1,0:T(8,128)(2,1)} %copy-done.13), custom_call_target="tpu_custom_call" | custom-call | tf_op jit(solution)/shard_map/join_hot/pallas_call | solution.py:251
  88.1 1.5 %collective-permute-start.19 = (bf16[128,1024]{1,0:T(8,128)(2,1)}, bf16[128,1024]{1,0:T(8,128)(2,1)S(1)}, u32[]{:S(2)}, u32[]{:S(2)}) collective-permute-start(bf16[128,1024]{1,0:T(8,128)(2,1)} %join_hot.1), channel_id=1, source_target_pairs={{0,8},{4,12},{8,0},{12,4},{1,9},{5,13},{9,1},{13,5},{2,10},{6,14},... | collective-permute-start | bytes 786440 | tf_op jit(solution)/shard_map/ppermute | solution.py:468
  89.6 3.2 %cold_keep.1.refs_1_ = bf16[2,128,1536]{2,1,0:T(8,128)(2,1)} custom-call(s32[5]{0:T(128)} %stack.35.place, bf16[128,256]{1,0:T(8,128)(2,1)} %cold_hidden.1.hidden_ref, bf16[2,128,6144]{2,1,0:T(8,128)(2,1)} %down_ref.3), custom_call_target="tpu_custom_call" | custom-call | tf_op jit(solution)/shard_map/cold_keep/pallas_call | solution.py:389
  92.8 4.3 %collective-permute-done.19 = bf16[128,1024]{1,0:T(8,128)(2,1)S(1)} collective-permute-done((bf16[128,1024]{1,0:T(8,128)(2,1)}, bf16[128,1024]{1,0:T(8,128)(2,1)S(1)}, u32[]{:S(2)}, u32[]{:S(2)}) %collective-permute-start.19) | collective-permute-done | bytes 262176 | tf_op jit(solution)/shard_map/ppermute | solution.py:468
  97.1 0.1 maximum_convert_fusion.hidden_ref
  97.2 0.1 collective-permute-start.20
  97.3 1.4 %fusion = bf16[128,1536]{1,0:T(8,128)(2,1)S(1)} fusion(bf16[2,128,1536]{2,1,0:T(8,128)(2,1)S(1)} %collective-permute-done.21.refs_2_, bf16[2,128,1536]{2,1,0:T(8,128)(2,1)} %cold_keep.1.refs_1_), kind=kLoop, calls=%fused_computation.2 | loop fusion | flops 786432 | bytes 1179648 | tf_op jit(solution)/shard_map/convert_element_type | solution.py:523
  98.7 1.5 %collective-permute-start.22 = (bf16[128,1536]{1,0:T(8,128)(2,1)S(1)}, bf16[128,1536]{1,0:T(8,128)(2,1)S(1)}, u32[]{:S(2)}, u32[]{:S(2)}) collective-permute-start(bf16[128,1536]{1,0:T(8,128)(2,1)S(1)} %fusion), channel_id=1, source_target_pairs={{0,8},{4,12},{8,0},{12,4},{1,9},{5,13},{9,1},{13,5},{2,10},{6,14},... | collective-permute-start | bytes 1179656 | tf_op jit(solution)/shard_map/ppermute | solution.py:468
  100.2 0.1 pad_maximum_fusion
  100.3 4.8 %down_keep.1.refs_0_ = f32[128,1536]{1,0:T(8,128)} custom-call(s32[5]{0:T(128)} %stack.35.place, bf16[128,1024]{1,0:T(8,128)(2,1)} %copy-done.3, bf16[16,128,1536]{2,1,0:T(8,128)(2,1)} %hot_ref.7), custom_call_target="tpu_custom_call" | custom-call | tf_op jit(solution)/shard_map/down_keep/pallas_call | solution.py:424
  105.1 0.7 copy-done.12
  105.8 5.1 %down_got.1.base_ref = f32[128,1536]{1,0:T(8,128)} custom-call(s32[5]{0:T(128)} %stack.35.place, bf16[128,1024]{1,0:T(8,128)(2,1)} %copy-done.12, bf16[16,128,1536]{2,1,0:T(8,128)(2,1)} %hot_ref.7, f32[128,1536]{1,0:T(8,128)} %down_keep.1.refs_0_, bf16[2,128,1536]{2,1,0:T(8,128)(2,1)} %cold_keep.1.refs_1_, bf16[2,128,1536]{2,1,0:T(8,128)(2,1)} %copy-done.1), custom_call_target="tpu_custom_call" | custom-call | tf_op jit(solution)/shard_map/down_got/pallas_call | solution.py:424
  111.0 0.7 copy-done.5
  111.7 2.0 %into_chunks.1 = (f32[32,1536]{1,0:T(8,128)}, bf16[32,1536]{1,0:T(8,128)(2,1)}, bf16[32,1536]{1,0:T(8,128)(2,1)}, bf16[32,1536]{1,0:T(8,128)(2,1)}) custom-call(f32[128,1536]{1,0:T(8,128)} %down_got.1.base_ref, bf16[128,1536]{1,0:T(8,128)(2,1)} %copy-done.5), custom_call_target="tpu_custom_call" | custom-call | tf_op jit(solution)/shard_map/into_chunks/pallas_call | solution.py:456
  113.7 0.8 collective-permute-start.23
  114.5 1.9 %collective-permute-start.24 = (bf16[32,1536]{1,0:T(8,128)(2,1)}, bf16[32,1536]{1,0:T(8,128)(2,1)S(1)}, u32[]{:S(2)}, u32[]{:S(2)}) collective-permute-start(bf16[32,1536]{1,0:T(8,128)(2,1)} %get-tuple-element.16), channel_id=1, source_target_pairs={{0,2},{1,3},{2,0},{3,1},{4,6},{5,7},{6,4},{7,5},{8,10},{9,11},{10,... | collective-permute-start | bytes 294920 | tf_op jit(solution)/shard_map/ppermute | solution.py:468
  116.4 1.7 %collective-permute-start.25 = (bf16[32,1536]{1,0:T(8,128)(2,1)}, bf16[32,1536]{1,0:T(8,128)(2,1)S(1)}, u32[]{:S(2)}, u32[]{:S(2)}) collective-permute-start(bf16[32,1536]{1,0:T(8,128)(2,1)} %get-tuple-element.17), channel_id=1, source_target_pairs={{0,3},{1,2},{2,1},{3,0},{4,7},{5,6},{6,5},{7,4},{8,11},{9,10},{10,... | collective-permute-start | bytes 294920 | tf_op jit(solution)/shard_map/ppermute | solution.py:468
  118.1 0.8 maximum_bitcast_fusion
  118.9 1.8 %collective-permute-done.23 = bf16[32,1536]{1,0:T(8,128)(2,1)S(1)} collective-permute-done((bf16[32,1536]{1,0:T(8,128)(2,1)}, bf16[32,1536]{1,0:T(8,128)(2,1)S(1)}, u32[]{:S(2)}, u32[]{:S(2)}) %collective-permute-start.23) | collective-permute-done | bytes 98336 | tf_op jit(solution)/shard_map/ppermute | solution.py:468
  120.7 4.3 %collective-permute-done.24 = bf16[32,1536]{1,0:T(8,128)(2,1)S(1)} collective-permute-done((bf16[32,1536]{1,0:T(8,128)(2,1)}, bf16[32,1536]{1,0:T(8,128)(2,1)S(1)}, u32[]{:S(2)}, u32[]{:S(2)}) %collective-permute-start.24) | collective-permute-done | bytes 98336 | tf_op jit(solution)/shard_map/ppermute | solution.py:468
  125.0 1.6 %fusion.1 = bf16[4,8,1536]{2,1,0:T(8,128)(2,1)} fusion(bf16[32,1536]{1,0:T(8,128)(2,1)S(1)} %collective-permute-done.25, bf16[32,1536]{1,0:T(8,128)(2,1)S(1)} %collective-permute-done.24, f32[32,1536]{1,0:T(8,128)} %get-tuple-element.14, bf16[32,1536]{1,0:T(8,128)(2,1)S(1)} %collective-permute-done.23), kind=kLoop, calls=%fused_computation.6 | loop fusion | flops 344064 | bytes 589824 | tf_op jit(solution)/shard_map/reshape | solution.py:535
  (73 shorter events, 0.2 us)
Async XLA Ops:
  0.6 30.5 %copy-start = (bf16[4,32,1536]{2,1,0:T(8,128)(2,1)S(1)}, bf16[4,32,1536]{2,1,0:T(8,128)(2,1)}, u32[]{:S(2)}) copy-start(bf16[4,32,1536]{2,1,0:T(8,128)(2,1)} %param.22) | copy-start | bytes 1179652
  20.9 39.4 %copy-start.29 = (s32[4,1,2]{0,2,1:T(2,128)S(1)}, s32[4,1,2]{0,2,1:T(2,128)}, u32[]{:S(2)}) copy-start(s32[4,1,2]{0,2,1:T(2,128)} %param.29) | copy-start | bytes 100
  26.7 5.3 %collective-permute-start = (bf16[32,1536]{1,0:T(8,128)(2,1)}, bf16[32,1536]{1,0:T(8,128)(2,1)S(1)}, u32[]{:S(2)}, u32[]{:S(2)}) collective-permute-start(bf16[32,1536]{1,0:T(8,128)(2,1)} %get-tuple-element.11), channel_id=1, source_target_pairs={{0,1},{1,0},{2,3},{3,2},{4,5},{5,4},{6,7},{7,6},{8,9},{9,8},{10,11... | collective-permute-start | bytes 294920 | tf_op jit(solution)/shard_map/ppermute | solution.py:468
  28.3 10.9 %collective-permute-start.1 = (bf16[32,1536]{1,0:T(8,128)(2,1)}, bf16[32,1536]{1,0:T(8,128)(2,1)S(1)}, u32[]{:S(2)}, u32[]{:S(2)}) collective-permute-start(bf16[32,1536]{1,0:T(8,128)(2,1)} %get-tuple-element.12), channel_id=1, source_target_pairs={{0,2},{1,3},{2,0},{3,1},{4,6},{5,7},{6,4},{7,5},{8,10},{9,11},{10,... | collective-permute-start | bytes 294920 | tf_op jit(solution)/shard_map/ppermute | solution.py:468
  30.9 8.3 %collective-permute-start.2 = (bf16[32,1536]{1,0:T(8,128)(2,1)}, bf16[32,1536]{1,0:T(8,128)(2,1)S(1)}, u32[]{:S(2)}, u32[]{:S(2)}) collective-permute-start(bf16[32,1536]{1,0:T(8,128)(2,1)} %get-tuple-element.13), channel_id=1, source_target_pairs={{0,3},{1,2},{2,1},{3,0},{4,7},{5,6},{6,5},{7,4},{8,11},{9,10},{10,... | collective-permute-start | bytes 294920 | tf_op jit(solution)/shard_map/ppermute | solution.py:468
  32.0 7.2 %copy-start.14 = (bf16[32,1536]{1,0:T(8,128)(2,1)}, bf16[32,1536]{1,0:T(8,128)(2,1)S(1)}, u32[]{:S(2)}) copy-start(bf16[32,1536]{1,0:T(8,128)(2,1)S(1)} %collective-permute-done.refs_2_) | copy-start | bytes 294916
  39.2 0.6 copy-start.15
  39.2 0.7 copy-start.16
  41.7 4.9 %collective-permute-start.10 = (bf16[32,1536]{1,0:T(8,128)(2,1)}, bf16[32,1536]{1,0:T(8,128)(2,1)S(1)}, u32[]{:S(2)}, u32[]{:S(2)}) collective-permute-start(bf16[32,1536]{1,0:T(8,128)(2,1)} %join.1.refs_0_), channel_id=1, source_target_pairs={{0,8},{4,12},{8,0},{12,4},{1,9},{5,13},{9,1},{13,5},{2,10},{6,14},... | collective-permute-start | bytes 294920 | tf_op jit(solution)/shard_map/ppermute | solution.py:468
  42.2 6.8 %collective-permute-start.5 = (bf16[32,1536]{1,0:T(8,128)(2,1)}, bf16[32,1536]{1,0:T(8,128)(2,1)S(1)}, u32[]{:S(2)}, u32[]{:S(2)}) collective-permute-start(bf16[32,1536]{1,0:T(8,128)(2,1)} %join.1.refs_0_), channel_id=1, source_target_pairs={{0,3},{1,2},{2,1},{3,0},{4,7},{5,6},{6,5},{7,4},{8,11},{9,10},{10,... | collective-permute-start | bytes 294920 | tf_op jit(solution)/shard_map/ppermute | solution.py:468
  44.8 5.7 %collective-permute-start.6 = (bf16[32,1536]{1,0:T(8,128)(2,1)}, bf16[32,1536]{1,0:T(8,128)(2,1)S(1)}, u32[]{:S(2)}, u32[]{:S(2)}) collective-permute-start(bf16[32,1536]{1,0:T(8,128)(2,1)} %join.1.refs_0_), channel_id=1, source_target_pairs={{0,4},{4,0},{8,12},{12,8},{1,5},{5,1},{9,13},{13,9},{2,6},{6,2},{1... | collective-permute-start | bytes 294920 | tf_op jit(solution)/shard_map/ppermute | solution.py:468
  44.8 8.7 %collective-permute-start.4 = (bf16[32,1536]{1,0:T(8,128)(2,1)}, bf16[32,1536]{1,0:T(8,128)(2,1)S(1)}, u32[]{:S(2)}, u32[]{:S(2)}) collective-permute-start(bf16[32,1536]{1,0:T(8,128)(2,1)} %join.1.refs_0_), channel_id=1, source_target_pairs={{0,2},{1,3},{2,0},{3,1},{4,6},{5,7},{6,4},{7,5},{8,10},{9,11},{10,... | collective-permute-start | bytes 294920 | tf_op jit(solution)/shard_map/ppermute | solution.py:468
  45.5 9.6 %collective-permute-start.3 = (bf16[32,1536]{1,0:T(8,128)(2,1)}, bf16[32,1536]{1,0:T(8,128)(2,1)S(1)}, u32[]{:S(2)}, u32[]{:S(2)}) collective-permute-start(bf16[32,1536]{1,0:T(8,128)(2,1)} %join.1.refs_0_), channel_id=1, source_target_pairs={{0,1},{1,0},{2,3},{3,2},{4,5},{5,4},{6,7},{7,6},{8,9},{9,8},{10,11... | collective-permute-start | bytes 294920 | tf_op jit(solution)/shard_map/ppermute | solution.py:468
  46.6 15.0 %copy-start.17 = (bf16[32,1536]{1,0:T(8,128)(2,1)}, bf16[32,1536]{1,0:T(8,128)(2,1)S(1)}, u32[]{:S(2)}) copy-start(bf16[32,1536]{1,0:T(8,128)(2,1)S(1)} %collective-permute-done.10.refs_8_) | copy-start | bytes 294916
  46.6 9.0 %collective-permute-start.14 = (bf16[32,1536]{1,0:T(8,128)(2,1)S(1)}, bf16[32,1536]{1,0:T(8,128)(2,1)S(1)}, u32[]{:S(2)}, u32[]{:S(2)}) collective-permute-start(bf16[32,1536]{1,0:T(8,128)(2,1)S(1)} %collective-permute-done.10.refs_8_), channel_id=1, source_target_pairs={{0,4},{4,0},{8,12},{12,8},{1,5},{5,1},{9,13},{13,9},{2,6},{6,2},{1... | collective-permute-start | bytes 294920 | tf_op jit(solution)/shard_map/ppermute | solution.py:468
  48.9 12.6 %copy-start.6 = (bf16[32,1536]{1,0:T(8,128)(2,1)}, bf16[32,1536]{1,0:T(8,128)(2,1)S(1)}, u32[]{:S(2)}) copy-start(bf16[32,1536]{1,0:T(8,128)(2,1)S(1)} %collective-permute-done.5.refs_3_) | copy-start | bytes 294916
  48.9 6.6 %collective-permute-start.13 = (bf16[32,1536]{1,0:T(8,128)(2,1)S(1)}, bf16[32,1536]{1,0:T(8,128)(2,1)S(1)}, u32[]{:S(2)}, u32[]{:S(2)}) collective-permute-start(bf16[32,1536]{1,0:T(8,128)(2,1)S(1)} %collective-permute-done.5.refs_3_), channel_id=1, source_target_pairs={{0,8},{4,12},{8,0},{12,4},{1,9},{5,13},{9,1},{13,5},{2,10},{6,14},... | collective-permute-start | bytes 294920 | tf_op jit(solution)/shard_map/ppermute | solution.py:468
  50.5 11.1 %copy-start.18 = (bf16[32,1536]{1,0:T(8,128)(2,1)}, bf16[32,1536]{1,0:T(8,128)(2,1)S(1)}, u32[]{:S(2)}) copy-start(bf16[32,1536]{1,0:T(8,128)(2,1)S(1)} %collective-permute-done.6.refs_4_) | copy-start | bytes 294916
  50.5 5.6 %collective-permute-start.9 = (bf16[32,1536]{1,0:T(8,128)(2,1)S(1)}, bf16[32,1536]{1,0:T(8,128)(2,1)S(1)}, u32[]{:S(2)}, u32[]{:S(2)}) collective-permute-start(bf16[32,1536]{1,0:T(8,128)(2,1)S(1)} %collective-permute-done.5.refs_3_), channel_id=1, source_target_pairs={{0,4},{4,0},{8,12},{12,8},{1,5},{5,1},{9,13},{13,9},{2,6},{6,2},{1... | collective-permute-start | bytes 294920 | tf_op jit(solution)/shard_map/ppermute | solution.py:468
  53.5 8.0 %copy-start.8 = (bf16[32,1536]{1,0:T(8,128)(2,1)}, bf16[32,1536]{1,0:T(8,128)(2,1)S(1)}, u32[]{:S(2)}) copy-start(bf16[32,1536]{1,0:T(8,128)(2,1)S(1)} %collective-permute-done.4.refs_2_) | copy-start | bytes 294916
  53.5 5.5 %collective-permute-start.12 = (bf16[32,1536]{1,0:T(8,128)(2,1)S(1)}, bf16[32,1536]{1,0:T(8,128)(2,1)S(1)}, u32[]{:S(2)}, u32[]{:S(2)}) collective-permute-start(bf16[32,1536]{1,0:T(8,128)(2,1)S(1)} %collective-permute-done.4.refs_2_), channel_id=1, source_target_pairs={{0,8},{4,12},{8,0},{12,4},{1,9},{5,13},{9,1},{13,5},{2,10},{6,14},... | collective-permute-start | bytes 294920 | tf_op jit(solution)/shard_map/ppermute | solution.py:468
  55.1 6.5 %copy-start.10 = (bf16[32,1536]{1,0:T(8,128)(2,1)}, bf16[32,1536]{1,0:T(8,128)(2,1)S(1)}, u32[]{:S(2)}) copy-start(bf16[32,1536]{1,0:T(8,128)(2,1)S(1)} %collective-permute-done.3.refs_1_) | copy-start | bytes 294916
  55.1 5.2 %collective-permute-start.11 = (bf16[32,1536]{1,0:T(8,128)(2,1)S(1)}, bf16[32,1536]{1,0:T(8,128)(2,1)S(1)}, u32[]{:S(2)}, u32[]{:S(2)}) collective-permute-start(bf16[32,1536]{1,0:T(8,128)(2,1)S(1)} %collective-permute-done.3.refs_1_), channel_id=1, source_target_pairs={{0,8},{4,12},{8,0},{12,4},{1,9},{5,13},{9,1},{13,5},{2,10},{6,14},... | collective-permute-start | bytes 294920 | tf_op jit(solution)/shard_map/ppermute | solution.py:468
  55.6 6.0 %copy-start.19 = (bf16[32,1536]{1,0:T(8,128)(2,1)}, bf16[32,1536]{1,0:T(8,128)(2,1)S(1)}, u32[]{:S(2)}) copy-start(bf16[32,1536]{1,0:T(8,128)(2,1)S(1)} %collective-permute-done.14.refs_12_) | copy-start | bytes 294916
  55.6 5.4 %collective-permute-start.8 = (bf16[32,1536]{1,0:T(8,128)(2,1)S(1)}, bf16[32,1536]{1,0:T(8,128)(2,1)S(1)}, u32[]{:S(2)}, u32[]{:S(2)}) collective-permute-start(bf16[32,1536]{1,0:T(8,128)(2,1)S(1)} %collective-permute-done.4.refs_2_), channel_id=1, source_target_pairs={{0,4},{4,0},{8,12},{12,8},{1,5},{5,1},{9,13},{13,9},{2,6},{6,2},{1... | collective-permute-start | bytes 294920 | tf_op jit(solution)/shard_map/ppermute | solution.py:468
  55.6 6.0 %copy-start.20 = (bf16[32,1536]{1,0:T(8,128)(2,1)}, bf16[32,1536]{1,0:T(8,128)(2,1)S(1)}, u32[]{:S(2)}) copy-start(bf16[32,1536]{1,0:T(8,128)(2,1)S(1)} %collective-permute-done.13.refs_11_) | copy-start | bytes 294916
  55.6 5.4 %collective-permute-start.7 = (bf16[32,1536]{1,0:T(8,128)(2,1)S(1)}, bf16[32,1536]{1,0:T(8,128)(2,1)S(1)}, u32[]{:S(2)}, u32[]{:S(2)}) collective-permute-start(bf16[32,1536]{1,0:T(8,128)(2,1)S(1)} %collective-permute-done.3.refs_1_), channel_id=1, source_target_pairs={{0,4},{4,0},{8,12},{12,8},{1,5},{5,1},{9,13},{13,9},{2,6},{6,2},{1... | collective-permute-start | bytes 294920 | tf_op jit(solution)/shard_map/ppermute | solution.py:468
  56.1 5.5 %copy-start.21 = (bf16[32,1536]{1,0:T(8,128)(2,1)}, bf16[32,1536]{1,0:T(8,128)(2,1)S(1)}, u32[]{:S(2)}) copy-start(bf16[32,1536]{1,0:T(8,128)(2,1)S(1)} %collective-permute-done.9.refs_7_) | copy-start | bytes 294916
  56.1 4.9 %collective-permute-start.17 = (bf16[32,1536]{1,0:T(8,128)(2,1)S(1)}, bf16[32,1536]{1,0:T(8,128)(2,1)S(1)}, u32[]{:S(2)}, u32[]{:S(2)}) collective-permute-start(bf16[32,1536]{1,0:T(8,128)(2,1)S(1)} %collective-permute-done.13.refs_11_), channel_id=1, source_target_pairs={{0,4},{4,0},{8,12},{12,8},{1,5},{5,1},{9,13},{13,9},{2,6},{6,2},{1... | collective-permute-start | bytes 294920 | tf_op jit(solution)/shard_map/ppermute | solution.py:468
  59.1 2.5 %copy-start.22 = (bf16[32,1536]{1,0:T(8,128)(2,1)}, bf16[32,1536]{1,0:T(8,128)(2,1)S(1)}, u32[]{:S(2)}) copy-start(bf16[32,1536]{1,0:T(8,128)(2,1)S(1)} %collective-permute-done.12.refs_10_) | copy-start | bytes 294916
  59.1 2.0 %collective-permute-start.16 = (bf16[32,1536]{1,0:T(8,128)(2,1)S(1)}, bf16[32,1536]{1,0:T(8,128)(2,1)S(1)}, u32[]{:S(2)}, u32[]{:S(2)}) collective-permute-start(bf16[32,1536]{1,0:T(8,128)(2,1)S(1)} %collective-permute-done.12.refs_10_), channel_id=1, source_target_pairs={{0,4},{4,0},{8,12},{12,8},{1,5},{5,1},{9,13},{13,9},{2,6},{6,2},{1... | collective-permute-start | bytes 294920 | tf_op jit(solution)/shard_map/ppermute | solution.py:468
  60.3 1.4 %copy-start.23 = (bf16[32,1536]{1,0:T(8,128)(2,1)}, bf16[32,1536]{1,0:T(8,128)(2,1)S(1)}, u32[]{:S(2)}) copy-start(bf16[32,1536]{1,0:T(8,128)(2,1)S(1)} %collective-permute-done.11.refs_9_) | copy-start | bytes 294916
  60.3 1.3 %collective-permute-start.15 = (bf16[32,1536]{1,0:T(8,128)(2,1)S(1)}, bf16[32,1536]{1,0:T(8,128)(2,1)S(1)}, u32[]{:S(2)}, u32[]{:S(2)}) collective-permute-start(bf16[32,1536]{1,0:T(8,128)(2,1)S(1)} %collective-permute-done.11.refs_9_), channel_id=1, source_target_pairs={{0,4},{4,0},{8,12},{12,8},{1,5},{5,1},{9,13},{13,9},{2,6},{6,2},{1... | collective-permute-start | bytes 294920 | tf_op jit(solution)/shard_map/ppermute | solution.py:468
  61.0 0.6 copy-start.24
  61.0 0.7 copy-start.25
  61.0 0.7 copy-start.26
  61.1 0.7 copy-start.27
  61.8 0.6 copy-start.28
  75.2 22.1 %collective-permute-start.21 = (bf16[2,128,1536]{2,1,0:T(8,128)(2,1)}, bf16[2,128,1536]{2,1,0:T(8,128)(2,1)S(1)}, u32[]{:S(2)}, u32[]{:S(2)}) collective-permute-start(bf16[2,128,1536]{2,1,0:T(8,128)(2,1)} %cold_send.1), channel_id=1, source_target_pairs={{0,4},{4,0},{8,12},{12,8},{1,5},{5,1},{9,13},{13,9},{2,6},{6,2},{1... | collective-permute-start | bytes 2359304 | tf_op jit(solution)/shard_map/ppermute | solution.py:468
  80.6 4.9 %collective-permute-start.18 = (bf16[128,1024]{1,0:T(8,128)(2,1)}, bf16[128,1024]{1,0:T(8,128)(2,1)S(1)}, u32[]{:S(2)}, u32[]{:S(2)}) collective-permute-start(bf16[128,1024]{1,0:T(8,128)(2,1)} %up_send.1), channel_id=1, source_target_pairs={{0,4},{4,0},{8,12},{12,8},{1,5},{5,1},{9,13},{13,9},{2,6},{6,2},{1... | collective-permute-start | bytes 786440 | tf_op jit(solution)/shard_map/ppermute | solution.py:468
  85.6 0.7 copy-start.13
  88.1 9.0 %copy-start.2 = (bf16[128,1024]{1,0:T(8,128)(2,1)S(1)}, bf16[128,1024]{1,0:T(8,128)(2,1)}, u32[]{:S(2)}) copy-start(bf16[128,1024]{1,0:T(8,128)(2,1)} %join_hot.1) | copy-start | bytes 786436
  88.1 12.1 %copy-start.4 = (bf16[32,1536]{1,0:T(8,128)(2,1)S(1)}, bf16[32,1536]{1,0:T(8,128)(2,1)}, u32[]{:S(2)}) copy-start(bf16[32,1536]{1,0:T(8,128)(2,1)} %join.1.refs_0_) | copy-start | bytes 294916
  88.1 12.1 %copy-start.7 = (bf16[32,1536]{1,0:T(8,128)(2,1)S(1)}, bf16[32,1536]{1,0:T(8,128)(2,1)}, u32[]{:S(2)}) copy-start(bf16[32,1536]{1,0:T(8,128)(2,1)} %copy-done.6) | copy-start | bytes 294916
  88.1 12.1 %copy-start.9 = (bf16[32,1536]{1,0:T(8,128)(2,1)S(1)}, bf16[32,1536]{1,0:T(8,128)(2,1)}, u32[]{:S(2)}) copy-start(bf16[32,1536]{1,0:T(8,128)(2,1)} %copy-done.8) | copy-start | bytes 294916
  88.1 12.1 %copy-start.11 = (bf16[32,1536]{1,0:T(8,128)(2,1)S(1)}, bf16[32,1536]{1,0:T(8,128)(2,1)}, u32[]{:S(2)}) copy-start(bf16[32,1536]{1,0:T(8,128)(2,1)} %copy-done.10) | copy-start | bytes 294916
  88.1 9.0 %collective-permute-start.19 = (bf16[128,1024]{1,0:T(8,128)(2,1)}, bf16[128,1024]{1,0:T(8,128)(2,1)S(1)}, u32[]{:S(2)}, u32[]{:S(2)}) collective-permute-start(bf16[128,1024]{1,0:T(8,128)(2,1)} %join_hot.1), channel_id=1, source_target_pairs={{0,8},{4,12},{8,0},{12,4},{1,9},{5,13},{9,1},{13,5},{2,10},{6,14},... | collective-permute-start | bytes 786440 | tf_op jit(solution)/shard_map/ppermute | solution.py:468
  97.2 3.1 %copy-start.3 = (bf16[128,1024]{1,0:T(8,128)(2,1)}, bf16[128,1024]{1,0:T(8,128)(2,1)S(1)}, u32[]{:S(2)}) copy-start(bf16[128,1024]{1,0:T(8,128)(2,1)S(1)} %maximum_convert_fusion.hidden_ref) | copy-start | bytes 786436
  97.2 7.9 %collective-permute-start.20 = (bf16[128,1024]{1,0:T(8,128)(2,1)S(1)}, bf16[128,1024]{1,0:T(8,128)(2,1)S(1)}, u32[]{:S(2)}, u32[]{:S(2)}) collective-permute-start(bf16[128,1024]{1,0:T(8,128)(2,1)S(1)} %maximum_convert_fusion.hidden_ref), channel_id=1, source_target_pairs={{0,4},{4,0},{8,12},{12,8},{1,5},{5,1},{9,13},{13,9},{2,6},{6,2},{1... | collective-permute-start | bytes 786440 | tf_op jit(solution)/shard_map/ppermute | solution.py:468
  97.3 7.8 %copy-start.1 = (bf16[2,128,1536]{2,1,0:T(8,128)(2,1)}, bf16[2,128,1536]{2,1,0:T(8,128)(2,1)S(1)}, u32[]{:S(2)}) copy-start(bf16[2,128,1536]{2,1,0:T(8,128)(2,1)S(1)} %collective-permute-done.21.refs_2_) | copy-start | bytes 2359300
  98.7 12.3 %collective-permute-start.22 = (bf16[128,1536]{1,0:T(8,128)(2,1)S(1)}, bf16[128,1536]{1,0:T(8,128)(2,1)S(1)}, u32[]{:S(2)}, u32[]{:S(2)}) collective-permute-start(bf16[128,1536]{1,0:T(8,128)(2,1)S(1)} %fusion), channel_id=1, source_target_pairs={{0,8},{4,12},{8,0},{12,4},{1,9},{5,13},{9,1},{13,5},{2,10},{6,14},... | collective-permute-start | bytes 1179656 | tf_op jit(solution)/shard_map/ppermute | solution.py:468
  105.1 0.7 copy-start.12
  111.0 0.7 copy-start.5
  113.7 7.0 %collective-permute-start.23 = (bf16[32,1536]{1,0:T(8,128)(2,1)}, bf16[32,1536]{1,0:T(8,128)(2,1)S(1)}, u32[]{:S(2)}, u32[]{:S(2)}) collective-permute-start(bf16[32,1536]{1,0:T(8,128)(2,1)} %get-tuple-element.15), channel_id=1, source_target_pairs={{0,1},{1,0},{2,3},{3,2},{4,5},{5,4},{6,7},{7,6},{8,9},{9,8},{10,11... | collective-permute-start | bytes 294920 | tf_op jit(solution)/shard_map/ppermute | solution.py:468
  114.5 10.4 %collective-permute-start.24 = (bf16[32,1536]{1,0:T(8,128)(2,1)}, bf16[32,1536]{1,0:T(8,128)(2,1)S(1)}, u32[]{:S(2)}, u32[]{:S(2)}) collective-permute-start(bf16[32,1536]{1,0:T(8,128)(2,1)} %get-tuple-element.16), channel_id=1, source_target_pairs={{0,2},{1,3},{2,0},{3,1},{4,6},{5,7},{6,4},{7,5},{8,10},{9,11},{10,... | collective-permute-start | bytes 294920 | tf_op jit(solution)/shard_map/ppermute | solution.py:468
  116.4 8.5 %collective-permute-start.25 = (bf16[32,1536]{1,0:T(8,128)(2,1)}, bf16[32,1536]{1,0:T(8,128)(2,1)S(1)}, u32[]{:S(2)}, u32[]{:S(2)}) collective-permute-start(bf16[32,1536]{1,0:T(8,128)(2,1)} %get-tuple-element.17), channel_id=1, source_target_pairs={{0,3},{1,2},{2,1},{3,0},{4,7},{5,6},{6,5},{7,4},{8,11},{9,10},{10,... | collective-permute-start | bytes 294920 | tf_op jit(solution)/shard_map/ppermute | solution.py:468

commit v3 on v0

--- a/solution.py
+++ b/solution.py
@@ -1,8 +1,11 @@
+import functools
 import math
 
 import jax
 import jax.numpy as jnp
 from jax import lax
+from jax.experimental import pallas as pl
+from jax.experimental.pallas import tpu as pltpu
 from jax.sharding import PartitionSpec as P
 
 HD = 128
@@ -112,6 +115,546 @@
     return (state, ffn_out)
 
 
+VMEM = pl.BlockSpec(memory_space=pltpu.VMEM)
+SMEM = pl.BlockSpec(memory_space=pltpu.SMEM)
+AWAY = pl.BlockSpec(memory_space=pl.ANY)
+DMA = pltpu.SemaphoreType.DMA
+
+
+COSTS = {"cold_send": 60, "cold_keep": 10, "down_keep": 10, "down_got": 10}
+LIMITS = {
+    "attention": 123,
+    "project": 120,
+    "norm_up_send": 116,
+    "up_keep": 116,
+    "cold_send": 121,
+    "cold_keep": 121,
+    "down_keep": 116,
+    "down_got": 116,
+}
+
+
+def call(kernel, name, out_shape, specs, operands, scratch=()):
+    return pl.pallas_call(
+        kernel,
+        in_specs=specs,
+        out_specs=jax.tree.map(lambda _: VMEM, out_shape),
+        out_shape=out_shape,
+        scratch_shapes=list(scratch),
+        compiler_params=pltpu.CompilerParams(vmem_limit_bytes=LIMITS.get(name, 32) * 2**19),
+        cost_estimate=pl.CostEstimate(
+            flops=0, bytes_accessed=COSTS.get(name, 6) * 10**6, transcendentals=0
+        ),
+        name=name,
+    )(*operands)
+
+
+def begin(copies):
+    for copy in copies:
+        copy.start()
+
+
+def finish(copies):
+    for copy in copies:
+        copy.wait()
+
+
+def like(rows, width, dtype=jnp.bfloat16):
+    return jax.ShapeDtypeStruct((rows, width), dtype)
+
+
+def attention_kernel(
+    lengths, q, kn, vn, keys, values, out_ref, small, key_buf, value_buf, small_sems, sems, *, here, steps
+):
+    rows, width = q.shape
+    context = keys.shape[0] // here
+    wide = 2 * HD
+    parts = wide // HD
+    count = width // wide
+
+    def copies(i):
+        column = pl.ds(i * wide, wide)
+        return (
+            pltpu.make_async_copy(keys.at[:, column], key_buf.at[i], sems.at[0, i]),
+            pltpu.make_async_copy(values.at[:, column], value_buf.at[i], sems.at[1, i]),
+        )
+
+    heads = [
+        pltpu.make_async_copy(ref, small.at[i], small_sems.at[i]) for i, ref in enumerate((q, kn, vn))
+    ]
+    begin(heads)
+    for i in range(count):
+        begin(copies(i))
+    q_ref, kn_ref, vn_ref = small.at[0], small.at[1], small.at[2]
+
+    nt = (((1,), (1,)), ((), ()))
+    factor = 1.0 / math.sqrt(HD)
+    lane_head = lax.broadcasted_iota(jnp.int32, (rows, wide), 1) // HD
+    row = lax.broadcasted_iota(jnp.int32, (parts * rows, context), 0) % here
+    slot = lax.broadcasted_iota(jnp.int32, (parts * rows, context), 1)
+    limit = jnp.zeros_like(slot)
+    for r in range(here):
+        limit = jnp.where(row == r, lengths[r], limit)
+    open_slot = slot < limit
+    at = lax.broadcasted_iota(jnp.int32, (parts * rows, rows), 0) % rows
+    to = lax.broadcasted_iota(jnp.int32, (parts * rows, rows), 1)
+    seen = (at % here == to % here) & (to // here <= at // here)
+    finish(heads)
+    for i in range(count):
+        column = slice(i * wide, (i + 1) * wide)
+        q = q_ref[:, column]
+        split = jnp.concatenate(
+            [jnp.where(lane_head == j, q, jnp.zeros_like(q)) for j in range(parts)], axis=0
+        )
+        fresh = lax.dot_general(split, kn_ref[:, column], nt, preferred_element_type=jnp.float32)
+        fresh = jnp.where(seen, fresh * factor, -jnp.inf)
+        key_copy, value_copy = copies(i)
+        key_copy.wait()
+        scores = lax.dot_general(split, key_buf[i], nt, preferred_element_type=jnp.float32)
+        own = scores[:, :context]
+        for r in range(1, here):
+            own = jnp.where(row == r, scores[:, r * context : (r + 1) * context], own)
+        own = jnp.where(open_slot, own * factor, -jnp.inf)
+        top = jnp.maximum(
+            jnp.max(own, axis=-1, keepdims=True), jnp.max(fresh, axis=-1, keepdims=True)
+        )
+        own = jnp.exp(own - top)
+        fresh = jnp.exp(fresh - top)
+        scale = 1.0 / (
+            jnp.sum(own, axis=-1, keepdims=True) + jnp.sum(fresh, axis=-1, keepdims=True)
+        )
+        own = own * scale
+        spread = jnp.concatenate(
+            [jnp.where(row == r, own, 0.0).astype(jnp.bfloat16) for r in range(here)], axis=1
+        )
+        value_copy.wait()
+        got = jnp.dot(spread, value_buf[i], preferred_element_type=jnp.float32)
+        got = got + jnp.dot(
+            (fresh * scale).astype(jnp.bfloat16),
+            vn_ref[:, column],
+            preferred_element_type=jnp.float32,
+        )
+        answer = got[:rows]
+        for j in range(1, parts):
+            answer = jnp.where(lane_head == j, got[j * rows : (j + 1) * rows], answer)
+        out_ref[:, column] = answer.astype(jnp.bfloat16)
+
+
+def attention(queries, key_cache, value_cache, key_new, value_new, lengths):
+    steps, here, width = queries.shape
+    slots = here * key_cache.shape[1]
+    count = width // (2 * HD)
+    flat = lambda a: a.reshape(-1, width)
+    return call(
+        functools.partial(attention_kernel, here=here, steps=steps),
+        "attention",
+        like(steps * here, width),
+        [SMEM] + [AWAY] * 5,
+        (
+            lengths,
+            flat(queries),
+            flat(key_new),
+            flat(value_new),
+            flat(key_cache),
+            flat(value_cache),
+        ),
+        [
+            pltpu.VMEM((3, steps * here, width), jnp.bfloat16),
+            pltpu.VMEM((count, slots, 2 * HD), jnp.bfloat16),
+            pltpu.VMEM((count, slots, 2 * HD), jnp.bfloat16),
+            DMA((3,)),
+            DMA((2, count)),
+        ],
+    )
+
+
+def project_kernel(place, *refs, parts):
+    rows_refs, weight, outs = refs[:parts], refs[parts], refs[parts + 1 : -4]
+    held, weight_buf, total, sems = refs[-4:]
+    chunk = outs[0].shape[0]
+    depth = weight.shape[0]
+    count = 6
+    deep = depth // count
+    copies = [
+        pltpu.make_async_copy(
+            weight.at[pl.ds(i * deep, deep)], weight_buf.at[pl.ds(i * deep, deep)], sems.at[i]
+        )
+        for i in range(count)
+    ]
+    begin(copies)
+    for k, ref in enumerate(rows_refs):
+        held[k] = ref[...]
+    rows = jnp.concatenate([held[place[0] ^ place[1] ^ m] for m in range(parts)], axis=0)
+    for i in range(0, count, 2):
+        finish(copies[i : i + 2])
+        span = slice(i * deep, (i + 2) * deep)
+        made = jnp.dot(rows[:, span], weight_buf[span], preferred_element_type=jnp.float32)
+        if i:
+            made = made + total[...]
+        if i + 2 < count:
+            total[...] = made
+    for m, out in enumerate(outs):
+        out[...] = made[m * chunk : (m + 1) * chunk].astype(out.dtype)
+
+
+def project(place, gathered, weight):
+    parts = len(gathered)
+    chunk, depth = gathered[0].shape
+    width = weight.shape[1]
+    return call(
+        functools.partial(project_kernel, parts=parts),
+        "project",
+        [like(chunk, width, jnp.bfloat16 if m else jnp.float32) for m in range(parts)],
+        [SMEM] + [VMEM] * parts + [AWAY],
+        (place, *gathered, weight),
+        [
+            pltpu.VMEM((parts, chunk, depth), jnp.bfloat16),
+            pltpu.VMEM(weight.shape, jnp.bfloat16),
+            pltpu.VMEM((parts * chunk, width), jnp.float32),
+            DMA((6,)),
+        ],
+    )
+
+
+def join_kernel(*refs, terms):
+    total = refs[0][...].astype(jnp.float32)
+    for ref in refs[1:terms]:
+        total = total + ref[...].astype(jnp.float32)
+    refs[-1][...] = total.astype(refs[-1].dtype)
+
+
+def join(name, terms, after=()):
+    return call(
+        functools.partial(join_kernel, terms=len(terms)),
+        name,
+        like(*terms[0].shape),
+        [VMEM] * (len(terms) + len(after)),
+        (*terms, *after),
+    )
+
+
+def norm_kernel(place, gain_ref, hot, *refs, parts, blocks):
+    states, (sent_ref, own_ref, stat_ref, buf, sems) = refs[:-5], refs[-5:]
+    copies = half_copies(hot, place[2] ^ 1, buf, sems)
+    begin(copies)
+    chunk, width = states[0].shape
+    gain = gain_ref[...].astype(jnp.float32)
+    for m in range(parts):
+        place_rows = slice(m * chunk, (m + 1) * chunk)
+        rows = [states[k * parts + m][...].astype(jnp.float32) for k in range(blocks)]
+        total = rows[0]
+        for r in rows[1:]:
+            total = total + r
+        mean = jnp.sum(total, axis=-1, keepdims=True) / D
+        rows = [r - mean for r in rows]
+        total = rows[0] * rows[0]
+        for r in rows[1:]:
+            total = total + r * r
+        variance = jnp.sum(total, axis=-1, keepdims=True) / D
+        scale = lax.rsqrt(variance + 1e-05)
+        own_ref[place_rows, :] = (rows[0] * scale * gain).astype(jnp.bfloat16)
+        stat_ref[0, place_rows, :] = jnp.broadcast_to(mean, (chunk, HD))
+        stat_ref[1, place_rows, :] = jnp.broadcast_to(scale, (chunk, HD))
+    up_half(own_ref, copies, buf, sent_ref)
+
+
+def half_copies(hot, half, buf, sems):
+    count = buf.shape[0]
+    return [
+        pltpu.make_async_copy(
+            hot.at[pl.ds(half * count + i, 2)], buf.at[pl.ds(i, 2)], sems.at[i // 2]
+        )
+        for i in range(0, count, 2)
+    ]
+
+
+def half_scratch(hot):
+    count = hot.shape[0] // 2
+    return [pltpu.VMEM((count,) + hot.shape[1:], jnp.bfloat16), DMA((count // 2,))]
+
+
+def up_half(rows_ref, copies, buf, out_ref):
+    rows = rows_ref[...]
+    for i, copy in enumerate(copies):
+        copy.wait()
+        weight = jnp.concatenate([buf[2 * i], buf[2 * i + 1]], axis=1)
+        out_ref[:, 2 * i * HD : 2 * (i + 1) * HD] = jnp.dot(
+            rows, weight, preferred_element_type=jnp.float32
+        ).astype(out_ref.dtype)
+
+
+def norm(place, gain, hot, columns):
+    blocks, parts = len(columns), len(columns[0])
+    chunk, width = columns[0][0].shape
+    rows = parts * chunk
+    return call(
+        functools.partial(norm_kernel, parts=parts, blocks=blocks),
+        "norm_up_send",
+        [
+            like(rows, hot.shape[0] // 2 * HD),
+            like(rows, width),
+            jax.ShapeDtypeStruct((2, rows, HD), jnp.float32),
+        ],
+        [SMEM, VMEM, AWAY] + [VMEM] * (blocks * parts),
+        (place, gain, hot, *[a for column in columns for a in column]),
+        half_scratch(hot),
+    )
+
+
+def up_kernel(place, rows_ref, hot, out_ref, buf, sems):
+    copies = half_copies(hot, place[2], buf, sems)
+    begin(copies)
+    up_half(rows_ref, copies, buf, out_ref)
+
+
+def up_keep(place, rows, hot):
+    return call(
+        up_kernel,
+        "up_keep",
+        like(rows.shape[0], hot.shape[0] // 2 * HD),
+        [SMEM, VMEM, AWAY],
+        (place, rows, hot),
+        half_scratch(hot),
+    )
+
+
+def piece_copies(cold_down, block, width, buf, i, sems):
+    at = pl.ds(pl.multiple_of(block * width, width), width)
+    return [
+        pltpu.make_async_copy(cold_down.at[c, :, at], buf.at[i, c], sems.at[i, c]) for c in range(2)
+    ]
+
+
+def piece_scratch(cold_down, width):
+    return [pltpu.VMEM((2, 2, cold_down.shape[1], width), jnp.bfloat16), DMA((2, 2))]
+
+
+def piece(hidden, copies, buf, i):
+    finish(copies)
+    depth, width = buf.shape[2:]
+    return jnp.dot(
+        hidden, buf[i].reshape(2 * depth, width), preferred_element_type=jnp.float32
+    ).astype(jnp.bfloat16)
+
+
+def cold_kernel(place, counts, lists_ref, stat_ref, after, up, down, *refs, parts, steps):
+    blocks = lists_ref.shape[0]
+    gains, states = refs[:blocks], refs[blocks:-6]
+    hidden_ref, out_ref, up_buf, up_sems, down_buf, down_sems = refs[-6:]
+    chunk, width = states[0].shape
+    total = parts * chunk
+    here = chunk // steps
+    b = place[1]
+    up_copies = [
+        [
+            pltpu.make_async_copy(
+                up.at[c, pl.ds(pl.multiple_of((b ^ k) * width, width), width)],
+                up_buf.at[k, c],
+                up_sems.at[k, c],
+            )
+            for c in range(2)
+        ]
+        for k in range(blocks)
+    ]
+    down_copies = [
+        piece_copies(down, b ^ (2 * i + 1), width, down_buf, i, down_sems) for i in range(2)
+    ]
+    for copies in up_copies + down_copies:
+        begin(copies)
+    mean, scale = stat_ref[0][:, :1], stat_ref[1][:, :1]
+    sums = jnp.zeros((total, 2 * HD), jnp.float32)
+    for k in range(blocks):
+        rows = jnp.concatenate(
+            [states[k * parts + m][...] for m in range(parts)], axis=0
+        ).astype(jnp.float32)
+        gain = gains[k][...].astype(jnp.float32)
+        normed = ((rows - mean) * scale * gain).astype(jnp.bfloat16)
+        finish(up_copies[k])
+        weight = jnp.concatenate([up_buf[k, 0], up_buf[k, 1]], axis=1)
+        sums = sums + jnp.dot(normed, weight, preferred_element_type=jnp.float32)
+    slots = lists_ref.shape[3]
+    index = lax.broadcasted_iota(jnp.int32, (total, slots), 0)
+    slot = lax.broadcasted_iota(jnp.int32, (total, slots), 1)
+    owner = (index // chunk) ^ place[0]
+    row = (index // here % steps) * (parts * here) + owner * here + index % here
+    halves = []
+    for c in range(2):
+        hit = (row == lists_ref[b, 0, c : c + 1, :]) & (slot < counts[2 * b + c])
+        used = jnp.max(jnp.where(hit, 1.0, 0.0), axis=-1, keepdims=True)
+        halves.append((jnp.maximum(sums[:, c * HD : (c + 1) * HD], 0.0) * used))
+    hidden = jnp.concatenate(halves, axis=1).astype(jnp.bfloat16)
+    hidden_ref[...] = hidden
+    for i in range(2):
+        out_ref[i] = piece(hidden, down_copies[i], down_buf, i)
+
+
+def cold_send(place, counts, lists, stat, after, cold_up, cold_down, gains, columns, steps):
+    blocks, parts = len(columns), len(columns[0])
+    chunk, width = columns[0][0].shape
+    rows = parts * chunk
+    flat = [a for column in columns for a in column]
+    return call(
+        functools.partial(cold_kernel, parts=parts, steps=steps),
+        "cold_send",
+        [like(rows, 2 * HD), jax.ShapeDtypeStruct((blocks // 2, rows, width), jnp.bfloat16)],
+        [SMEM, SMEM, VMEM, VMEM, AWAY, AWAY, AWAY] + [VMEM] * (blocks + len(flat)),
+        (place, counts, lists, stat, after, cold_up, cold_down, *gains, *flat),
+        [pltpu.VMEM((blocks, 2, width, HD), jnp.bfloat16), DMA((blocks, 2))]
+        + piece_scratch(cold_down, width),
+    )
+
+
+def keep_kernel(place, hidden_ref, down, after, near_ref, far_ref, buf, sems):
+    width = near_ref.shape[1]
+    copies = [piece_copies(down, place[1] ^ (2 * i), width, buf, i, sems) for i in range(2)]
+    begin(copies[1] + copies[0])
+    hidden = hidden_ref[...]
+    far_ref[...] = piece(hidden, copies[1], buf, 1)
+    near_ref[...] = piece(hidden, copies[0], buf, 0)
+
+
+def cold_keep(place, hidden, cold_down, after, width):
+    rows = hidden.shape[0]
+    return call(
+        keep_kernel,
+        "cold_keep",
+        [like(rows, width), like(rows, width)],
+        [SMEM, VMEM, AWAY, AWAY],
+        (place, hidden, cold_down, after),
+        piece_scratch(cold_down, width),
+    )
+
+
+def down_kernel(place, hidden_ref, hot, *refs, half):
+    before, (out_ref, buf, sems) = refs[:-3], refs[-3:]
+    copies = half_copies(hot, place[2] ^ half, buf, sems)
+    begin(copies)
+    depth, width = buf.shape[1:]
+    for i in range(0, len(copies), 2):
+        finish(copies[i : i + 2])
+        made = jnp.dot(
+            hidden_ref[:, 2 * i * depth : 2 * (i + 2) * depth],
+            buf[2 * i : 2 * (i + 2)].reshape(4 * depth, width),
+            preferred_element_type=jnp.float32,
+        )
+        if i:
+            made = made + out_ref[...]
+        else:
+            for ref in before:
+                made = made + ref[...].astype(jnp.float32)
+        out_ref[...] = made
+
+
+def down(place, half, hidden, hot, *before):
+    return call(
+        functools.partial(down_kernel, half=half),
+        "down_got" if half else "down_keep",
+        like(hidden.shape[0], hot.shape[2], jnp.float32),
+        [SMEM, VMEM, AWAY] + [VMEM] * len(before),
+        (place, hidden, hot, *before),
+        half_scratch(hot),
+    )
+
+
+def chunks_kernel(base_ref, more_ref, *outs):
+    chunk = outs[0].shape[0]
+    for m, out in enumerate(outs):
+        rows = slice(m * chunk, (m + 1) * chunk)
+        out[...] = (base_ref[rows, :] + more_ref[rows, :].astype(jnp.float32)).astype(out.dtype)
+
+
+def into_chunks(base, more, parts):
+    rows, width = base.shape
+    return call(
+        chunks_kernel,
+        "into_chunks",
+        [like(rows // parts, width, jnp.bfloat16 if m else jnp.float32) for m in range(parts)],
+        [VMEM, VMEM],
+        (base, more),
+    )
+
+
+def swap(x, axis, m, size=4):
+    return lax.ppermute(x, axis, [(i, i ^ m) for i in range(size)])
+
+
+def local_fast(
+    queries,
+    key_cache,
+    value_cache,
+    key_new,
+    value_new,
+    lengths,
+    out_proj,
+    residual,
+    norm_gain,
+    hot_up,
+    hot_down,
+    cold_up,
+    cold_down,
+    block_rows,
+    block_counts,
+):
+    steps, here, _ = queries.shape
+    all_rows, width = residual.shape[1:]
+    parts = all_rows // here
+    blocks = block_rows.shape[0]
+    others = range(1, parts)
+    b = lax.axis_index("blocks")
+    h = lax.axis_index("heads")
+    place = jnp.stack([h, b, b % 2]).astype(jnp.int32)
+    counts = block_counts.reshape(-1)
+
+    attended = attention(queries, key_cache, value_cache, key_new, value_new, lengths)
+    across = swap(attended, "blocks", 2)
+    gathered = [attended, swap(attended, "blocks", 1), across, swap(across, "blocks", 1)]
+    pieces = project(place, gathered, out_proj)
+    got = [swap(pieces[m], "heads", m) for m in others]
+    gain = norm_gain[None]
+    gains = [gain] + [swap(gain, "blocks", k) for k in range(1, blocks)]
+    mine = lax.dynamic_slice(residual, (0, h * here, 0), (steps, here, width))
+    state = join("join", [mine.reshape(steps * here, width), pieces[0], *got], gains[1:])
+    states = [state] + [swap(state, "heads", m) for m in others]
+    across = [swap(s, "blocks", 2) for s in states]
+    columns = [
+        states,
+        [swap(s, "blocks", 1) for s in states],
+        across,
+        [swap(s, "blocks", 1) for s in across],
+    ]
+    sent, own, stat = norm(place, gain, hot_up, columns)
+    sent = swap(sent, "blocks", 1)
+    kept = up_keep(place, own, hot_up)
+    summed = join("join_hot", [kept, sent])
+    arrived = swap(summed, "blocks", 2)
+
+    cold, cold_sent = cold_send(
+        place, counts, block_rows, stat, summed, cold_up, cold_down, gains, columns, steps
+    )
+    cold_sent, arrived = lax.optimization_barrier((cold_sent, arrived))
+    cold_got = swap(cold_sent, "blocks", 1)
+    total = summed.astype(jnp.float32) + arrived.astype(jnp.float32)
+    hidden = jnp.maximum(total, 0.0).astype(jnp.bfloat16)
+    near, far = cold_keep(place, cold, cold_down, hidden, width)
+    far = (far.astype(jnp.float32) + cold_got[1].astype(jnp.float32)).astype(jnp.bfloat16)
+    cold_far = swap(far, "blocks", 2)
+    partner = swap(hidden, "blocks", 1)
+    base = down(place, 0, hidden, hot_down)
+    base = down(place, 1, partner, hot_down, base, near, cold_got[0])
+    made = into_chunks(base, cold_far, parts)
+    out = made[0]
+    for m in others:
+        out = out + swap(made[m], "heads", m).astype(jnp.float32)
+    ffn_out = out.astype(jnp.bfloat16).reshape(steps, here, width)
+
+    stacked = jnp.stack(states).reshape(parts, steps, 1, here, width)
+    ordered = [
+        lax.dynamic_index_in_dim(stacked, c ^ h, axis=0, keepdims=False) for c in range(parts)
+    ]
+    attn_state = jnp.concatenate(ordered, axis=1).reshape(steps, all_rows, width)
+    return (attn_state, ffn_out)
+
+
 def solution(mesh):
     placed = (
         P(None, ("groups", "blocks"), "heads"),
@@ -130,8 +673,9 @@
         P("groups", "heads", None, None),
         P("groups", "heads", None),
     )
+    sizes = tuple(mesh.shape[a] for a in ("blocks", "heads"))
     return jax.shard_map(
-        local,
+        local_fast if sizes == (4, 4) else local,
         mesh=mesh,
         in_specs=placed,
         out_specs=(P(None, "groups", "blocks"), P(None, ("groups", "heads"), "blocks")),

time: 211 us -> 111 us (0.53)
  waiting for transfers between devices: 79.7 us -> 30.4 us
  local copies, waits for them, and re-layouts: 50.6 us -> 6.94 us
  Pallas kernels: 0 us -> 41.1 us
  matrix products: 23.9 us -> 0 us
  blocking collectives: 21.5 us -> 0 us
  starting transfers between devices: 8.68 us -> 27.1 us
  between operations: 13.9 us -> 1.12 us
  other arithmetic: 11.6 us -> 3.34 us
    psum x2 -> x0, waiting for transfers between devices: 41.4 us -> none  [the longest x1 38 us: local(): lax.psum(partial_out.astype(jnp.bfloat16), 'heads').astype(jnp.float32)]
    pallas_call x0 -> x11, Pallas kernels: none -> 41.1 us  [call(): pl.pallas_call(kernel, in_specs=specs, out_specs=jax.tree.map(lambda _: V...]
    ppermute x0 -> x32, waiting for transfers between devices: none -> 30.4 us  [swap(): return lax.ppermute(x, axis, [(i, i ^ m) for i in range(size)])]
    ppermute x0 -> x32, starting transfers between devices: none -> 27.1 us  [swap(): return lax.ppermute(x, axis, [(i, i ^ m) for i in range(size)])]
    dot_general x8 -> x0, matrix products: 23.9 us -> none  [the longest x1 4.58 us: local(): jnp.einsum('trc,kch->trkh', normed, hot_up, preferred_element_type=jnp.fl...]
    unnamed x4 -> x0, waiting for transfers between devices: 20.8 us -> none
    all_to_all x2 -> x0, waiting for transfers between devices: 17.5 us -> none  [the longest x1 10.7 us: local(): lax.all_to_all(outgoing, 'blocks', split_axis=0, concat_axis=3, tiled=True)]
    unnamed x30 -> x75, local copies, waits for them, and re-layouts: 22.5 us -> 5.49 us
  transfers between devices with their start and end apart: 5 -> 32, of which waited for: 5 -> 14; matrix products, arithmetic and copies ran while one was open for 14% -> 4% of each run, Pallas kernels for 0% -> 24%
where the time goes in v3:
time: 111 us; the launch traced here: 110 us
  Pallas kernels  41.1 us (37%)
  waiting for transfers between devices  30.4 us (27%)
  starting transfers between devices  27.1 us (24%)
  local copies, waits for them, and re-layouts  6.94 us (6%)
  other arithmetic  3.34 us (3%)
  between operations  1.12 us (1%)
    pallas_call x11, Pallas kernels, call(): pl.pallas_call(kernel, in_specs=specs, out_specs=jax.tree.map(lambda _: V...  41.1 us
    ppermute x32, waiting for transfers between devices, swap(): return lax.ppermute(x, axis, [(i, i ^ m) for i in range(size)])  30.4 us
    ppermute x32, starting transfers between devices, swap(): return lax.ppermute(x, axis, [(i, i ^ m) for i in range(size)])  27.1 us
    unnamed x75, local copies, waits for them, and re-layouts  5.49 us
  transfers between devices with their start and end apart: 32, of which 14 were waited for; matrix products, arithmetic and copies ran while one was open for 4% of the time, Pallas kernels for 24%

profile of v3, /device:TPU:0, one launch (start us, length us, event | category | flops | bytes accessed | tf_op | source)
XLA Modules:
  0.0 110.1 jit_solution(15060341764784176622)
XLA Ops:
  0.7 9.3 %attention.1.refs_0_ = bf16[32,1536]{1,0:T(8,128)(2,1)} custom-call(s32[8]{0:T(128)} %lengths.1, bf16[32,1536]{1,0:T(8,128)(2,1)} %bitcast.41, bf16[32,1536]{1,0:T(8,128)(2,1)} %bitcast.42, bf16[32,1536]{1,0:T(8,128)(2,1)} %bitcast.43, bf16[1024,1536]{1,0:T(8,128)(2,1)} %bitcast.36, bf16[1024,1536]{1,0:T(8,128)(2,1)} %bitcast.37), custom_call_target="tpu_custom_call" | custom-call | bytes 6000000 | tf_op jit(solution)/shard_map/attention/pallas_call | solution.py:138
  9.9 3.0 %collective-permute-start.1 = (bf16[32,1536]{1,0:T(8,128)(2,1)}, bf16[32,1536]{1,0:T(8,128)(2,1)S(1)}, u32[]{:S(2)}, u32[]{:S(2)}) collective-permute-start(bf16[32,1536]{1,0:T(8,128)(2,1)} %attention.1.refs_0_), channel_id=1, source_target_pairs={{0,8},{4,12},{8,0},{12,4},{1,9},{5,13},{9,1},{13,5},{2,10},{6,14},... | collective-permute-start | bytes 294920 | tf_op jit(solution)/shard_map/ppermute | solution.py:578
  13.0 0.6 collective-permute-start.6
  13.6 0.1 collective-permute-start.7
  13.6 1.4 %collective-permute-start.8 = (bf16[1,1536]{1,0:T(2,128)(2,1)S(1)}, bf16[1,1536]{1,0:T(2,128)(2,1)S(1)}, u32[]{:S(2)}, u32[]{:S(2)}) collective-permute-start(bf16[1,1536]{1,0:T(2,128)(2,1)S(1)} %broadcast_in_dim.3.gain_ref.refs_0_), channel_id=1, source_target_pairs={{0,12},{4,8},{8,4},{12,0},{1,13},{5,9},{9,5},{13,1},{2,14},{6,10},... | collective-permute-start | bytes 9224 | tf_op jit(solution)/shard_map/ppermute | solution.py:578
  15.0 1.0 collective-permute-done.1.refs_2_
  16.0 0.7 pad_add_fusion.place
  16.7 0.6 collective-permute-done.2.refs_3_
  17.3 0.6 copy-done.33
  17.9 4.5 %project.1 = (f32[32,1536]{1,0:T(8,128)}, bf16[32,1536]{1,0:T(8,128)(2,1)}, bf16[32,1536]{1,0:T(8,128)(2,1)}, bf16[32,1536]{1,0:T(8,128)(2,1)}) custom-call(s32[3]{0:T(128)} %pad_add_fusion.place, bf16[32,1536]{1,0:T(8,128)(2,1)} %attention.1.refs_0_, bf16[32,1536]{1,0:T(8,128)(2,1)} %copy-done.32, bf16[32,1536]{1,0:T(8,128)(2,1)} %copy-done.31, ...), custom_call_target="tpu_custom_call" | custom-call | bytes 6000000 | tf_op jit(solution)/shard_map/project/pallas_call | solution.py:138
  22.5 2.0 %collective-permute-start.3 = (bf16[32,1536]{1,0:T(8,128)(2,1)}, bf16[32,1536]{1,0:T(8,128)(2,1)S(1)}, u32[]{:S(2)}, u32[]{:S(2)}) collective-permute-start(bf16[32,1536]{1,0:T(8,128)(2,1)} %get-tuple-element.20), channel_id=1, source_target_pairs={{0,1},{1,0},{2,3},{3,2},{4,5},{5,4},{6,7},{7,6},{8,9},{9,8},{10,11... | collective-permute-start | bytes 294920 | tf_op jit(solution)/shard_map/ppermute | solution.py:578
  24.5 2.6 %collective-permute-start.4 = (bf16[32,1536]{1,0:T(8,128)(2,1)}, bf16[32,1536]{1,0:T(8,128)(2,1)S(1)}, u32[]{:S(2)}, u32[]{:S(2)}) collective-permute-start(bf16[32,1536]{1,0:T(8,128)(2,1)} %get-tuple-element.21), channel_id=1, source_target_pairs={{0,2},{1,3},{2,0},{3,1},{4,6},{5,7},{6,4},{7,5},{8,10},{9,11},{10,... | collective-permute-start | bytes 294920 | tf_op jit(solution)/shard_map/ppermute | solution.py:578
  27.1 1.0 collective-permute-done.3.refs_2_
  28.1 7.3 %collective-permute-done.4.refs_3_ = bf16[32,1536]{1,0:T(8,128)(2,1)S(1)} collective-permute-done((bf16[32,1536]{1,0:T(8,128)(2,1)}, bf16[32,1536]{1,0:T(8,128)(2,1)S(1)}, u32[]{:S(2)}, u32[]{:S(2)}) %collective-permute-start.4) | collective-permute-done | bytes 98336 | tf_op jit(solution)/shard_map/ppermute | solution.py:578
  35.4 0.9 copy-done.6
  36.4 2.0 %collective-permute-start.9 = (bf16[32,1536]{1,0:T(8,128)(2,1)S(1)}, bf16[32,1536]{1,0:T(8,128)(2,1)S(1)}, u32[]{:S(2)}, u32[]{:S(2)}) collective-permute-start(bf16[32,1536]{1,0:T(8,128)(2,1)S(1)} %join.1.refs_0_.refs_4_), channel_id=1, source_target_pairs={{0,1},{1,0},{2,3},{3,2},{4,5},{5,4},{6,7},{7,6},{8,9},{9,8},{10,11... | collective-permute-start | bytes 294920 | tf_op jit(solution)/shard_map/ppermute | solution.py:578
  38.4 1.1 %collective-permute-start.10 = (bf16[32,1536]{1,0:T(8,128)(2,1)S(1)}, bf16[32,1536]{1,0:T(8,128)(2,1)S(1)}, u32[]{:S(2)}, u32[]{:S(2)}) collective-permute-start(bf16[32,1536]{1,0:T(8,128)(2,1)S(1)} %join.1.refs_0_.refs_4_), channel_id=1, source_target_pairs={{0,2},{1,3},{2,0},{3,1},{4,6},{5,7},{6,4},{7,5},{8,10},{9,11},{10,... | collective-permute-start | bytes 294920 | tf_op jit(solution)/shard_map/ppermute | solution.py:578
  39.6 1.4 %collective-permute-start.11 = (bf16[32,1536]{1,0:T(8,128)(2,1)S(1)}, bf16[32,1536]{1,0:T(8,128)(2,1)S(1)}, u32[]{:S(2)}, u32[]{:S(2)}) collective-permute-start(bf16[32,1536]{1,0:T(8,128)(2,1)S(1)} %join.1.refs_0_.refs_4_), channel_id=1, source_target_pairs={{0,3},{1,2},{2,1},{3,0},{4,7},{5,6},{6,5},{7,4},{8,11},{9,10},{10,... | collective-permute-start | bytes 294920 | tf_op jit(solution)/shard_map/ppermute | solution.py:578
  41.0 1.6 %collective-permute-start.16 = (bf16[32,1536]{1,0:T(8,128)(2,1)S(1)}, bf16[32,1536]{1,0:T(8,128)(2,1)S(1)}, u32[]{:S(2)}, u32[]{:S(2)}) collective-permute-start(bf16[32,1536]{1,0:T(8,128)(2,1)S(1)} %join.1.refs_0_.refs_4_), channel_id=1, source_target_pairs={{0,8},{4,12},{8,0},{12,4},{1,9},{5,13},{9,1},{13,5},{2,10},{6,14},... | collective-permute-start | bytes 294920 | tf_op jit(solution)/shard_map/ppermute | solution.py:578
  42.5 0.6 collective-permute-start.17
  43.1 5.3 %collective-permute-done.10.refs_2_.refs_6_ = bf16[32,1536]{1,0:T(8,128)(2,1)S(1)} collective-permute-done((bf16[32,1536]{1,0:T(8,128)(2,1)S(1)}, bf16[32,1536]{1,0:T(8,128)(2,1)S(1)}, u32[]{:S(2)}, u32[]{:S(2)}) %collective-permute-start.10) | collective-permute-done | bytes 98336 | tf_op jit(solution)/shard_map/ppermute | solution.py:578
  48.4 1.6 %collective-permute-start.18 = (bf16[32,1536]{1,0:T(8,128)(2,1)S(1)}, bf16[32,1536]{1,0:T(8,128)(2,1)S(1)}, u32[]{:S(2)}, u32[]{:S(2)}) collective-permute-start(bf16[32,1536]{1,0:T(8,128)(2,1)S(1)} %collective-permute-done.10.refs_2_.refs_6_), channel_id=1, source_target_pairs={{0,8},{4,12},{8,0},{12,4},{1,9},{5,13},{9,1},{13,5},{2,10},{6,14},... | collective-permute-start | bytes 294920 | tf_op jit(solution)/shard_map/ppermute | solution.py:578
  50.0 0.5 collective-permute-start.19
  50.5 0.5 collective-permute-start.14
  51.0 0.1 collective-permute-start.15
  51.1 2.0 %collective-permute-done.18.refs_10_.refs_14_ = bf16[32,1536]{1,0:T(8,128)(2,1)S(1)} collective-permute-done((bf16[32,1536]{1,0:T(8,128)(2,1)S(1)}, bf16[32,1536]{1,0:T(8,128)(2,1)S(1)}, u32[]{:S(2)}, u32[]{:S(2)}) %collective-permute-start.18) | collective-permute-done | bytes 98336 | tf_op jit(solution)/shard_map/ppermute | solution.py:578
  53.1 1.6 %collective-permute-done.19.refs_11_.refs_15_ = bf16[32,1536]{1,0:T(8,128)(2,1)S(1)} collective-permute-done((bf16[32,1536]{1,0:T(8,128)(2,1)S(1)}, bf16[32,1536]{1,0:T(8,128)(2,1)S(1)}, u32[]{:S(2)}, u32[]{:S(2)}) %collective-permute-start.19) | collective-permute-done | bytes 98336 | tf_op jit(solution)/shard_map/ppermute | solution.py:578
  54.6 0.5 collective-permute-start.22
  55.1 0.1 collective-permute-start.23
  55.3 0.7 collective-permute-done.21.refs_13_.refs_17_
  55.9 0.2 collective-permute-done.22.refs_14_.refs_18_
  56.1 0.4 collective-permute-done.23.refs_15_.refs_19_
  56.6 0.2 copy-done.27
  56.7 0.6 copy-done.28
  57.4 4.8 %norm_up_send.1 = (bf16[128,1024]{1,0:T(8,128)(2,1)}, bf16[128,1536]{1,0:T(8,128)(2,1)}, f32[2,128,128]{2,1,0:T(8,128)}) custom-call(s32[3]{0:T(128)} %pad_add_fusion.place, bf16[1,1536]{1,0:T(2,128)(2,1)} %copy-done.34, bf16[16,1536,128]{2,1,0:T(8,128)(2,1)} %hot.5, bf16[32,1536]{1,0:T(8,128)(2,1)} %copy-done.3, bf16[32,1536]{1,0:T(8,128)(2,1)} %copy-done.11, ...), custom_call_target="tpu_custom_call" | custom-call | bytes 6000000 | tf_op jit(solution)/shard_map/norm_up_send/pallas_call | solution.py:138
  62.2 0.4 collective-permute-start.24
  62.6 4.3 %up_keep.1.refs_0_ = bf16[128,1024]{1,0:T(8,128)(2,1)} custom-call(s32[3]{0:T(128)} %pad_add_fusion.place, bf16[128,1536]{1,0:T(8,128)(2,1)} %get-tuple-element.23.rows_ref, bf16[16,1536,128]{2,1,0:T(8,128)(2,1)} %hot.5), custom_call_target="tpu_custom_call" | custom-call | bytes 6000000 | tf_op jit(solution)/shard_map/up_keep/pallas_call | solution.py:138
  66.9 0.9 copy-done.5
  67.9 0.1 join_hot.1.after
  68.0 1.1 %collective-permute-start.25 = (bf16[128,1024]{1,0:T(8,128)(2,1)S(1)}, bf16[128,1024]{1,0:T(8,128)(2,1)S(1)}, u32[]{:S(2)}, u32[]{:S(2)}) collective-permute-start(bf16[128,1024]{1,0:T(8,128)(2,1)S(1)} %join_hot.1.after), channel_id=1, source_target_pairs={{0,8},{4,12},{8,0},{12,4},{1,9},{5,13},{9,1},{13,5},{2,10},{6,14},... | collective-permute-start | bytes 786440 | tf_op jit(solution)/shard_map/ppermute | solution.py:578
  69.1 0.1 copy.18
  69.2 0.6 reshape.49.counts
  69.8 6.0 %cold_send.1 = (bf16[128,256]{1,0:T(8,128)(2,1)}, bf16[2,128,1536]{2,1,0:T(8,128)(2,1)}) custom-call(s32[3]{0:T(128)} %pad_add_fusion.place, s32[8]{0:T(128)} %reshape.49.counts, s32[4,1,2,32]{3,2,1,0:T(2,128)} %lists_ref.1, f32[2,128,128]{2,1,0:T(8,128)} %get-tuple-element.25.stat_ref, bf16[128,1024]{1,0:T(8,128)(2,1)} %copy-done.2, ...), custom_call_target="tpu_custom_call" | custom-call | bytes 60000000 | tf_op jit(solution)/shard_map/cold_send/pallas_call | solution.py:138
  75.8 0.6 collective-permute-done.25
  76.5 1.0 maximum_convert_fusion.hidden_ref.after
  77.6 0.6 collective-permute-start.26
  78.1 0.1 copy-done.10
  78.3 3.3 %cold_keep.1 = (bf16[128,1536]{1,0:T(8,128)(2,1)}, bf16[128,1536]{1,0:T(8,128)(2,1)}) custom-call(s32[3]{0:T(128)} %pad_add_fusion.place, bf16[128,256]{1,0:T(8,128)(2,1)} %get-tuple-element.28.hidden_ref, bf16[2,128,6144]{2,1,0:T(8,128)(2,1)} %down.3, bf16[128,1024]{1,0:T(8,128)(2,1)} %copy-done.10), custom_call_target="tpu_custom_call" | custom-call | bytes 10000000 | tf_op jit(solution)/shard_map/cold_keep/pallas_call | solution.py:138
  81.6 4.1 %down_keep.1.refs_0_ = f32[128,1536]{1,0:T(8,128)} custom-call(s32[3]{0:T(128)} %pad_add_fusion.place, bf16[128,1024]{1,0:T(8,128)(2,1)} %copy-done.10, bf16[16,128,1536]{2,1,0:T(8,128)(2,1)} %hot.7), custom_call_target="tpu_custom_call" | custom-call | bytes 10000000 | tf_op jit(solution)/shard_map/down_keep/pallas_call | solution.py:138
  85.8 0.1 fusion
  85.9 1.1 %collective-permute-start.28 = (bf16[128,1536]{1,0:T(8,128)(2,1)S(1)}, bf16[128,1536]{1,0:T(8,128)(2,1)S(1)}, u32[]{:S(2)}, u32[]{:S(2)}) collective-permute-start(bf16[128,1536]{1,0:T(8,128)(2,1)S(1)} %fusion), channel_id=1, source_target_pairs={{0,8},{4,12},{8,0},{12,4},{1,9},{5,13},{9,1},{13,5},{2,10},{6,14},... | collective-permute-start | bytes 1179656 | tf_op jit(solution)/shard_map/ppermute | solution.py:578
  87.0 0.8 slice_bitcast_fusion.1.refs_2_
  87.8 0.7 copy-done.30
  88.5 4.7 %down_got.1.base_ref = f32[128,1536]{1,0:T(8,128)} custom-call(s32[3]{0:T(128)} %pad_add_fusion.place, bf16[128,1024]{1,0:T(8,128)(2,1)} %copy-done.30, bf16[16,128,1536]{2,1,0:T(8,128)(2,1)} %hot.7, f32[128,1536]{1,0:T(8,128)} %down_keep.1.refs_0_, bf16[128,1536]{1,0:T(8,128)(2,1)} %get-tuple-element.29.refs_1_, bf16[128,1536]{1,0:T(8,128)(2,1)} %slice_bitcast_fusion.1.refs_2_), custom_call_target="tpu_custom_call" | custom-call | bytes 10000000 | tf_op jit(solution)/shard_map/down_got/pallas_call | solution.py:138
  93.1 4.3 %collective-permute-done.28.more_ref = bf16[128,1536]{1,0:T(8,128)(2,1)S(1)} collective-permute-done((bf16[128,1536]{1,0:T(8,128)(2,1)S(1)}, bf16[128,1536]{1,0:T(8,128)(2,1)S(1)}, u32[]{:S(2)}, u32[]{:S(2)}) %collective-permute-start.28) | collective-permute-done | bytes 393248 | tf_op jit(solution)/shard_map/ppermute | solution.py:578
  97.4 1.1 %copy-done.1 = f32[128,1536]{1,0:T(8,128)S(1)} copy-done((f32[128,1536]{1,0:T(8,128)S(1)}, f32[128,1536]{1,0:T(8,128)}, u32[]{:S(2)}) %copy-start.1) | copy-done | bytes 786456
  98.6 0.1 into_chunks.1
  98.6 0.1 collective-permute-start.29
  98.8 2.7 %collective-permute-start.30 = (bf16[32,1536]{1,0:T(8,128)(2,1)S(1)}, bf16[32,1536]{1,0:T(8,128)(2,1)S(1)}, u32[]{:S(2)}, u32[]{:S(2)}) collective-permute-start(bf16[32,1536]{1,0:T(8,128)(2,1)S(1)} %get-tuple-element.34), channel_id=1, source_target_pairs={{0,2},{1,3},{2,0},{3,1},{4,6},{5,7},{6,4},{7,5},{8,10},{9,11},{10,... | collective-permute-start | bytes 294920 | tf_op jit(solution)/shard_map/ppermute | solution.py:578
  101.4 1.6 %collective-permute-start.31 = (bf16[32,1536]{1,0:T(8,128)(2,1)S(1)}, bf16[32,1536]{1,0:T(8,128)(2,1)S(1)}, u32[]{:S(2)}, u32[]{:S(2)}) collective-permute-start(bf16[32,1536]{1,0:T(8,128)(2,1)S(1)} %get-tuple-element.35), channel_id=1, source_target_pairs={{0,3},{1,2},{2,1},{3,0},{4,7},{5,6},{6,5},{7,4},{8,11},{9,10},{10,... | collective-permute-start | bytes 294920 | tf_op jit(solution)/shard_map/ppermute | solution.py:578
  103.1 0.8 maximum_bitcast_fusion
  103.9 0.5 collective-permute-done.29
  104.4 5.0 %collective-permute-done.30 = bf16[32,1536]{1,0:T(8,128)(2,1)S(1)} collective-permute-done((bf16[32,1536]{1,0:T(8,128)(2,1)S(1)}, bf16[32,1536]{1,0:T(8,128)(2,1)S(1)}, u32[]{:S(2)}, u32[]{:S(2)}) %collective-permute-start.30) | collective-permute-done | bytes 98336 | tf_op jit(solution)/shard_map/ppermute | solution.py:578
  109.4 0.7 fusion.1
  (97 shorter events, 0.4 us)
Async XLA Ops:
  0.6 26.4 %copy-start = (bf16[4,32,1536]{2,1,0:T(8,128)(2,1)S(1)}, bf16[4,32,1536]{2,1,0:T(8,128)(2,1)}, u32[]{:S(2)}) copy-start(bf16[4,32,1536]{2,1,0:T(8,128)(2,1)} %param.22) | copy-start | bytes 1179652
  0.6 12.3 %copy-start.35 = (bf16[1536]{0:T(1024)(128)(2,1)S(1)}, bf16[1536]{0:T(1024)(128)(2,1)}, u32[]{:S(2)}) copy-start(bf16[1536]{0:T(1024)(128)(2,1)} %param.23) | copy-start | bytes 9220
  9.9 6.0 %collective-permute-start.1 = (bf16[32,1536]{1,0:T(8,128)(2,1)}, bf16[32,1536]{1,0:T(8,128)(2,1)S(1)}, u32[]{:S(2)}, u32[]{:S(2)}) collective-permute-start(bf16[32,1536]{1,0:T(8,128)(2,1)} %attention.1.refs_0_), channel_id=1, source_target_pairs={{0,8},{4,12},{8,0},{12,4},{1,9},{5,13},{9,1},{13,5},{2,10},{6,14},... | collective-permute-start | bytes 294920 | tf_op jit(solution)/shard_map/ppermute | solution.py:578
  13.0 3.7 %collective-permute-start = (bf16[32,1536]{1,0:T(8,128)(2,1)}, bf16[32,1536]{1,0:T(8,128)(2,1)S(1)}, u32[]{:S(2)}, u32[]{:S(2)}) collective-permute-start(bf16[32,1536]{1,0:T(8,128)(2,1)} %attention.1.refs_0_), channel_id=1, source_target_pairs={{0,4},{4,0},{8,12},{12,8},{1,5},{5,1},{9,13},{13,9},{2,6},{6,2},{1... | collective-permute-start | bytes 294920 | tf_op jit(solution)/shard_map/ppermute | solution.py:578
  13.0 43.5 %copy-start.34 = (bf16[1,1536]{1,0:T(2,128)(2,1)}, bf16[1,1536]{1,0:T(2,128)(2,1)S(1)}, u32[]{:S(2)}) copy-start(bf16[1,1536]{1,0:T(2,128)(2,1)S(1)} %broadcast_in_dim.3.gain_ref.refs_0_) | copy-start | bytes 9220
  13.0 14.1 %collective-permute-start.6 = (bf16[1,1536]{1,0:T(2,128)(2,1)S(1)}, bf16[1,1536]{1,0:T(2,128)(2,1)S(1)}, u32[]{:S(2)}, u32[]{:S(2)}) collective-permute-start(bf16[1,1536]{1,0:T(2,128)(2,1)S(1)} %broadcast_in_dim.3.gain_ref.refs_0_), channel_id=1, source_target_pairs={{0,4},{4,0},{8,12},{12,8},{1,5},{5,1},{9,13},{13,9},{2,6},{6,2},{1... | collective-permute-start | bytes 9224 | tf_op jit(solution)/shard_map/ppermute | solution.py:578
  13.6 13.5 %collective-permute-start.7 = (bf16[1,1536]{1,0:T(2,128)(2,1)S(1)}, bf16[1,1536]{1,0:T(2,128)(2,1)S(1)}, u32[]{:S(2)}, u32[]{:S(2)}) collective-permute-start(bf16[1,1536]{1,0:T(2,128)(2,1)S(1)} %broadcast_in_dim.3.gain_ref.refs_0_), channel_id=1, source_target_pairs={{0,8},{4,12},{8,0},{12,4},{1,9},{5,13},{9,1},{13,5},{2,10},{6,14},... | collective-permute-start | bytes 9224 | tf_op jit(solution)/shard_map/ppermute | solution.py:578
  13.6 13.5 %collective-permute-start.8 = (bf16[1,1536]{1,0:T(2,128)(2,1)S(1)}, bf16[1,1536]{1,0:T(2,128)(2,1)S(1)}, u32[]{:S(2)}, u32[]{:S(2)}) collective-permute-start(bf16[1,1536]{1,0:T(2,128)(2,1)S(1)} %broadcast_in_dim.3.gain_ref.refs_0_), channel_id=1, source_target_pairs={{0,12},{4,8},{8,4},{12,0},{1,13},{5,9},{9,5},{13,1},{2,14},{6,10},... | collective-permute-start | bytes 9224 | tf_op jit(solution)/shard_map/ppermute | solution.py:578
  16.0 1.3 %copy-start.31 = (bf16[32,1536]{1,0:T(8,128)(2,1)}, bf16[32,1536]{1,0:T(8,128)(2,1)S(1)}, u32[]{:S(2)}) copy-start(bf16[32,1536]{1,0:T(8,128)(2,1)S(1)} %collective-permute-done.1.refs_2_) | copy-start | bytes 294916
  16.0 1.3 %collective-permute-start.2 = (bf16[32,1536]{1,0:T(8,128)(2,1)S(1)}, bf16[32,1536]{1,0:T(8,128)(2,1)S(1)}, u32[]{:S(2)}, u32[]{:S(2)}) collective-permute-start(bf16[32,1536]{1,0:T(8,128)(2,1)S(1)} %collective-permute-done.1.refs_2_), channel_id=1, source_target_pairs={{0,4},{4,0},{8,12},{12,8},{1,5},{5,1},{9,13},{13,9},{2,6},{6,2},{1... | collective-permute-start | bytes 294920 | tf_op jit(solution)/shard_map/ppermute | solution.py:578
  22.5 5.7 %collective-permute-start.3 = (bf16[32,1536]{1,0:T(8,128)(2,1)}, bf16[32,1536]{1,0:T(8,128)(2,1)S(1)}, u32[]{:S(2)}, u32[]{:S(2)}) collective-permute-start(bf16[32,1536]{1,0:T(8,128)(2,1)} %get-tuple-element.20), channel_id=1, source_target_pairs={{0,1},{1,0},{2,3},{3,2},{4,5},{5,4},{6,7},{7,6},{8,9},{9,8},{10,11... | collective-permute-start | bytes 294920 | tf_op jit(solution)/shard_map/ppermute | solution.py:578
  24.5 10.9 %collective-permute-start.4 = (bf16[32,1536]{1,0:T(8,128)(2,1)}, bf16[32,1536]{1,0:T(8,128)(2,1)S(1)}, u32[]{:S(2)}, u32[]{:S(2)}) collective-permute-start(bf16[32,1536]{1,0:T(8,128)(2,1)} %get-tuple-element.21), channel_id=1, source_target_pairs={{0,2},{1,3},{2,0},{3,1},{4,6},{5,7},{6,4},{7,5},{8,10},{9,11},{10,... | collective-permute-start | bytes 294920 | tf_op jit(solution)/shard_map/ppermute | solution.py:578
  27.1 35.1 %copy-start.7 = (bf16[1,1536]{1,0:T(2,128)(2,1)}, bf16[1,1536]{1,0:T(2,128)(2,1)S(1)}, u32[]{:S(2)}) copy-start(bf16[1,1536]{1,0:T(2,128)(2,1)S(1)} %collective-permute-done.6.refs_5_.refs_1_) | copy-start | bytes 9220
  27.1 8.4 %collective-permute-start.5 = (bf16[32,1536]{1,0:T(8,128)(2,1)}, bf16[32,1536]{1,0:T(8,128)(2,1)S(1)}, u32[]{:S(2)}, u32[]{:S(2)}) collective-permute-start(bf16[32,1536]{1,0:T(8,128)(2,1)} %get-tuple-element.22), channel_id=1, source_target_pairs={{0,3},{1,2},{2,1},{3,0},{4,7},{5,6},{6,5},{7,4},{8,11},{9,10},{10,... | collective-permute-start | bytes 294920 | tf_op jit(solution)/shard_map/ppermute | solution.py:578
  27.1 35.0 %copy-start.8 = (bf16[1,1536]{1,0:T(2,128)(2,1)}, bf16[1,1536]{1,0:T(2,128)(2,1)S(1)}, u32[]{:S(2)}) copy-start(bf16[1,1536]{1,0:T(2,128)(2,1)S(1)} %collective-permute-done.7.refs_6_.refs_2_) | copy-start | bytes 9220
  27.1 35.0 %copy-start.9 = (bf16[1,1536]{1,0:T(2,128)(2,1)}, bf16[1,1536]{1,0:T(2,128)(2,1)S(1)}, u32[]{:S(2)}) copy-start(bf16[1,1536]{1,0:T(2,128)(2,1)S(1)} %collective-permute-done.8.refs_7_.refs_3_) | copy-start | bytes 9220
  35.4 0.9 copy-start.6
  36.4 20.1 %copy-start.3 = (bf16[32,1536]{1,0:T(8,128)(2,1)}, bf16[32,1536]{1,0:T(8,128)(2,1)S(1)}, u32[]{:S(2)}) copy-start(bf16[32,1536]{1,0:T(8,128)(2,1)S(1)} %join.1.refs_0_.refs_4_) | copy-start | bytes 294916
  36.4 6.1 %collective-permute-start.9 = (bf16[32,1536]{1,0:T(8,128)(2,1)S(1)}, bf16[32,1536]{1,0:T(8,128)(2,1)S(1)}, u32[]{:S(2)}, u32[]{:S(2)}) collective-permute-start(bf16[32,1536]{1,0:T(8,128)(2,1)S(1)} %join.1.refs_0_.refs_4_), channel_id=1, source_target_pairs={{0,1},{1,0},{2,3},{3,2},{4,5},{5,4},{6,7},{7,6},{8,9},{9,8},{10,11... | collective-permute-start | bytes 294920 | tf_op jit(solution)/shard_map/ppermute | solution.py:578
  38.4 10.0 %collective-permute-start.10 = (bf16[32,1536]{1,0:T(8,128)(2,1)S(1)}, bf16[32,1536]{1,0:T(8,128)(2,1)S(1)}, u32[]{:S(2)}, u32[]{:S(2)}) collective-permute-start(bf16[32,1536]{1,0:T(8,128)(2,1)S(1)} %join.1.refs_0_.refs_4_), channel_id=1, source_target_pairs={{0,2},{1,3},{2,0},{3,1},{4,6},{5,7},{6,4},{7,5},{8,10},{9,11},{10,... | collective-permute-start | bytes 294920 | tf_op jit(solution)/shard_map/ppermute | solution.py:578
  39.6 10.4 %collective-permute-start.11 = (bf16[32,1536]{1,0:T(8,128)(2,1)S(1)}, bf16[32,1536]{1,0:T(8,128)(2,1)S(1)}, u32[]{:S(2)}, u32[]{:S(2)}) collective-permute-start(bf16[32,1536]{1,0:T(8,128)(2,1)S(1)} %join.1.refs_0_.refs_4_), channel_id=1, source_target_pairs={{0,3},{1,2},{2,1},{3,0},{4,7},{5,6},{6,5},{7,4},{8,11},{9,10},{10,... | collective-permute-start | bytes 294920 | tf_op jit(solution)/shard_map/ppermute | solution.py:578
  41.0 9.5 %collective-permute-start.16 = (bf16[32,1536]{1,0:T(8,128)(2,1)S(1)}, bf16[32,1536]{1,0:T(8,128)(2,1)S(1)}, u32[]{:S(2)}, u32[]{:S(2)}) collective-permute-start(bf16[32,1536]{1,0:T(8,128)(2,1)S(1)} %join.1.refs_0_.refs_4_), channel_id=1, source_target_pairs={{0,8},{4,12},{8,0},{12,4},{1,9},{5,13},{9,1},{13,5},{2,10},{6,14},... | collective-permute-start | bytes 294920 | tf_op jit(solution)/shard_map/ppermute | solution.py:578
  42.5 8.0 %collective-permute-start.12 = (bf16[32,1536]{1,0:T(8,128)(2,1)S(1)}, bf16[32,1536]{1,0:T(8,128)(2,1)S(1)}, u32[]{:S(2)}, u32[]{:S(2)}) collective-permute-start(bf16[32,1536]{1,0:T(8,128)(2,1)S(1)} %join.1.refs_0_.refs_4_), channel_id=1, source_target_pairs={{0,4},{4,0},{8,12},{12,8},{1,5},{5,1},{9,13},{13,9},{2,6},{6,2},{1... | collective-permute-start | bytes 294920 | tf_op jit(solution)/shard_map/ppermute | solution.py:578
  42.5 13.9 %copy-start.11 = (bf16[32,1536]{1,0:T(8,128)(2,1)}, bf16[32,1536]{1,0:T(8,128)(2,1)S(1)}, u32[]{:S(2)}) copy-start(bf16[32,1536]{1,0:T(8,128)(2,1)S(1)} %collective-permute-done.9.refs_1_.refs_5_) | copy-start | bytes 294916
  42.5 8.5 %collective-permute-start.17 = (bf16[32,1536]{1,0:T(8,128)(2,1)S(1)}, bf16[32,1536]{1,0:T(8,128)(2,1)S(1)}, u32[]{:S(2)}, u32[]{:S(2)}) collective-permute-start(bf16[32,1536]{1,0:T(8,128)(2,1)S(1)} %collective-permute-done.9.refs_1_.refs_5_), channel_id=1, source_target_pairs={{0,8},{4,12},{8,0},{12,4},{1,9},{5,13},{9,1},{13,5},{2,10},{6,14},... | collective-permute-start | bytes 294920 | tf_op jit(solution)/shard_map/ppermute | solution.py:578
  48.4 8.0 %copy-start.13 = (bf16[32,1536]{1,0:T(8,128)(2,1)}, bf16[32,1536]{1,0:T(8,128)(2,1)S(1)}, u32[]{:S(2)}) copy-start(bf16[32,1536]{1,0:T(8,128)(2,1)S(1)} %collective-permute-done.10.refs_2_.refs_6_) | copy-start | bytes 294916
  48.4 4.6 %collective-permute-start.18 = (bf16[32,1536]{1,0:T(8,128)(2,1)S(1)}, bf16[32,1536]{1,0:T(8,128)(2,1)S(1)}, u32[]{:S(2)}, u32[]{:S(2)}) collective-permute-start(bf16[32,1536]{1,0:T(8,128)(2,1)S(1)} %collective-permute-done.10.refs_2_.refs_6_), channel_id=1, source_target_pairs={{0,8},{4,12},{8,0},{12,4},{1,9},{5,13},{9,1},{13,5},{2,10},{6,14},... | collective-permute-start | bytes 294920 | tf_op jit(solution)/shard_map/ppermute | solution.py:578
  50.0 6.5 %copy-start.15 = (bf16[32,1536]{1,0:T(8,128)(2,1)}, bf16[32,1536]{1,0:T(8,128)(2,1)S(1)}, u32[]{:S(2)}) copy-start(bf16[32,1536]{1,0:T(8,128)(2,1)S(1)} %collective-permute-done.11.refs_3_.refs_7_) | copy-start | bytes 294916
  50.0 4.6 %collective-permute-start.19 = (bf16[32,1536]{1,0:T(8,128)(2,1)S(1)}, bf16[32,1536]{1,0:T(8,128)(2,1)S(1)}, u32[]{:S(2)}, u32[]{:S(2)}) collective-permute-start(bf16[32,1536]{1,0:T(8,128)(2,1)S(1)} %collective-permute-done.11.refs_3_.refs_7_), channel_id=1, source_target_pairs={{0,8},{4,12},{8,0},{12,4},{1,9},{5,13},{9,1},{13,5},{2,10},{6,14},... | collective-permute-start | bytes 294920 | tf_op jit(solution)/shard_map/ppermute | solution.py:578
  50.5 6.0 %copy-start.17 = (bf16[32,1536]{1,0:T(8,128)(2,1)}, bf16[32,1536]{1,0:T(8,128)(2,1)S(1)}, u32[]{:S(2)}) copy-start(bf16[32,1536]{1,0:T(8,128)(2,1)S(1)} %collective-permute-done.16.refs_8_.refs_12_) | copy-start | bytes 294916
  50.5 4.2 %collective-permute-start.13 = (bf16[32,1536]{1,0:T(8,128)(2,1)S(1)}, bf16[32,1536]{1,0:T(8,128)(2,1)S(1)}, u32[]{:S(2)}, u32[]{:S(2)}) collective-permute-start(bf16[32,1536]{1,0:T(8,128)(2,1)S(1)} %collective-permute-done.9.refs_1_.refs_5_), channel_id=1, source_target_pairs={{0,4},{4,0},{8,12},{12,8},{1,5},{5,1},{9,13},{13,9},{2,6},{6,2},{1... | collective-permute-start | bytes 294920 | tf_op jit(solution)/shard_map/ppermute | solution.py:578
  50.5 6.0 %copy-start.18 = (bf16[32,1536]{1,0:T(8,128)(2,1)}, bf16[32,1536]{1,0:T(8,128)(2,1)S(1)}, u32[]{:S(2)}) copy-start(bf16[32,1536]{1,0:T(8,128)(2,1)S(1)} %collective-permute-done.12.refs_4_.refs_8_) | copy-start | bytes 294916
  50.5 4.6 %collective-permute-start.14 = (bf16[32,1536]{1,0:T(8,128)(2,1)S(1)}, bf16[32,1536]{1,0:T(8,128)(2,1)S(1)}, u32[]{:S(2)}, u32[]{:S(2)}) collective-permute-start(bf16[32,1536]{1,0:T(8,128)(2,1)S(1)} %collective-permute-done.10.refs_2_.refs_6_), channel_id=1, source_target_pairs={{0,4},{4,0},{8,12},{12,8},{1,5},{5,1},{9,13},{13,9},{2,6},{6,2},{1... | collective-permute-start | bytes 294920 | tf_op jit(solution)/shard_map/ppermute | solution.py:578
  51.0 5.5 %copy-start.19 = (bf16[32,1536]{1,0:T(8,128)(2,1)}, bf16[32,1536]{1,0:T(8,128)(2,1)S(1)}, u32[]{:S(2)}) copy-start(bf16[32,1536]{1,0:T(8,128)(2,1)S(1)} %collective-permute-done.17.refs_9_.refs_13_) | copy-start | bytes 294916
  51.0 4.2 %collective-permute-start.15 = (bf16[32,1536]{1,0:T(8,128)(2,1)S(1)}, bf16[32,1536]{1,0:T(8,128)(2,1)S(1)}, u32[]{:S(2)}, u32[]{:S(2)}) collective-permute-start(bf16[32,1536]{1,0:T(8,128)(2,1)S(1)} %collective-permute-done.11.refs_3_.refs_7_), channel_id=1, source_target_pairs={{0,4},{4,0},{8,12},{12,8},{1,5},{5,1},{9,13},{13,9},{2,6},{6,2},{1... | collective-permute-start | bytes 294920 | tf_op jit(solution)/shard_map/ppermute | solution.py:578
  53.1 3.5 %copy-start.20 = (bf16[32,1536]{1,0:T(8,128)(2,1)}, bf16[32,1536]{1,0:T(8,128)(2,1)S(1)}, u32[]{:S(2)}) copy-start(bf16[32,1536]{1,0:T(8,128)(2,1)S(1)} %collective-permute-done.18.refs_10_.refs_14_) | copy-start | bytes 294916
  53.1 2.2 %collective-permute-start.20 = (bf16[32,1536]{1,0:T(8,128)(2,1)S(1)}, bf16[32,1536]{1,0:T(8,128)(2,1)S(1)}, u32[]{:S(2)}, u32[]{:S(2)}) collective-permute-start(bf16[32,1536]{1,0:T(8,128)(2,1)S(1)} %collective-permute-done.16.refs_8_.refs_12_), channel_id=1, source_target_pairs={{0,4},{4,0},{8,12},{12,8},{1,5},{5,1},{9,13},{13,9},{2,6},{6,2},{1... | collective-permute-start | bytes 294920 | tf_op jit(solution)/shard_map/ppermute | solution.py:578
  54.6 1.9 %copy-start.21 = (bf16[32,1536]{1,0:T(8,128)(2,1)}, bf16[32,1536]{1,0:T(8,128)(2,1)S(1)}, u32[]{:S(2)}) copy-start(bf16[32,1536]{1,0:T(8,128)(2,1)S(1)} %collective-permute-done.19.refs_11_.refs_15_) | copy-start | bytes 294916
  54.6 1.3 %collective-permute-start.21 = (bf16[32,1536]{1,0:T(8,128)(2,1)S(1)}, bf16[32,1536]{1,0:T(8,128)(2,1)S(1)}, u32[]{:S(2)}, u32[]{:S(2)}) collective-permute-start(bf16[32,1536]{1,0:T(8,128)(2,1)S(1)} %collective-permute-done.17.refs_9_.refs_13_), channel_id=1, source_target_pairs={{0,4},{4,0},{8,12},{12,8},{1,5},{5,1},{9,13},{13,9},{2,6},{6,2},{1... | collective-permute-start | bytes 294920 | tf_op jit(solution)/shard_map/ppermute | solution.py:578
  54.6 1.9 %copy-start.22 = (bf16[32,1536]{1,0:T(8,128)(2,1)}, bf16[32,1536]{1,0:T(8,128)(2,1)S(1)}, u32[]{:S(2)}) copy-start(bf16[32,1536]{1,0:T(8,128)(2,1)S(1)} %collective-permute-done.13.refs_5_.refs_9_) | copy-start | bytes 294916
  54.6 1.4 %collective-permute-start.22 = (bf16[32,1536]{1,0:T(8,128)(2,1)S(1)}, bf16[32,1536]{1,0:T(8,128)(2,1)S(1)}, u32[]{:S(2)}, u32[]{:S(2)}) collective-permute-start(bf16[32,1536]{1,0:T(8,128)(2,1)S(1)} %collective-permute-done.18.refs_10_.refs_14_), channel_id=1, source_target_pairs={{0,4},{4,0},{8,12},{12,8},{1,5},{5,1},{9,13},{13,9},{2,6},{6,2},{1... | collective-permute-start | bytes 294920 | tf_op jit(solution)/shard_map/ppermute | solution.py:578
  55.1 1.4 %copy-start.23 = (bf16[32,1536]{1,0:T(8,128)(2,1)}, bf16[32,1536]{1,0:T(8,128)(2,1)S(1)}, u32[]{:S(2)}) copy-start(bf16[32,1536]{1,0:T(8,128)(2,1)S(1)} %collective-permute-done.14.refs_6_.refs_10_) | copy-start | bytes 294916
  55.1 1.3 %collective-permute-start.23 = (bf16[32,1536]{1,0:T(8,128)(2,1)S(1)}, bf16[32,1536]{1,0:T(8,128)(2,1)S(1)}, u32[]{:S(2)}, u32[]{:S(2)}) collective-permute-start(bf16[32,1536]{1,0:T(8,128)(2,1)S(1)} %collective-permute-done.19.refs_11_.refs_15_), channel_id=1, source_target_pairs={{0,4},{4,0},{8,12},{12,8},{1,5},{5,1},{9,13},{13,9},{2,6},{6,2},{1... | collective-permute-start | bytes 294920 | tf_op jit(solution)/shard_map/ppermute | solution.py:578
  55.2 1.3 %copy-start.24 = (bf16[32,1536]{1,0:T(8,128)(2,1)}, bf16[32,1536]{1,0:T(8,128)(2,1)S(1)}, u32[]{:S(2)}) copy-start(bf16[32,1536]{1,0:T(8,128)(2,1)S(1)} %collective-permute-done.15.refs_7_.refs_11_) | copy-start | bytes 294916
  55.2 1.3 %copy-start.25 = (bf16[32,1536]{1,0:T(8,128)(2,1)}, bf16[32,1536]{1,0:T(8,128)(2,1)S(1)}, u32[]{:S(2)}) copy-start(bf16[32,1536]{1,0:T(8,128)(2,1)S(1)} %collective-permute-done.20.refs_12_.refs_16_) | copy-start | bytes 294916
  62.2 4.7 %collective-permute-start.24 = (bf16[128,1024]{1,0:T(8,128)(2,1)}, bf16[128,1024]{1,0:T(8,128)(2,1)S(1)}, u32[]{:S(2)}, u32[]{:S(2)}) collective-permute-start(bf16[128,1024]{1,0:T(8,128)(2,1)} %get-tuple-element.24), channel_id=1, source_target_pairs={{0,4},{4,0},{8,12},{12,8},{1,5},{5,1},{9,13},{13,9},{2,6},{6,2},{1... | collective-permute-start | bytes 786440 | tf_op jit(solution)/shard_map/ppermute | solution.py:578
  62.6 6.5 %copy-start.36 = (s32[4,1,2]{0,2,1:T(2,128)S(1)}, s32[4,1,2]{0,2,1:T(2,128)}, u32[]{:S(2)}) copy-start(s32[4,1,2]{0,2,1:T(2,128)} %param.29) | copy-start | bytes 100
  66.9 1.0 copy-start.5
  67.9 1.8 %copy-start.2 = (bf16[128,1024]{1,0:T(8,128)(2,1)}, bf16[128,1024]{1,0:T(8,128)(2,1)S(1)}, u32[]{:S(2)}) copy-start(bf16[128,1024]{1,0:T(8,128)(2,1)S(1)} %join_hot.1.after) | copy-start | bytes 786436
  68.0 8.4 %collective-permute-start.25 = (bf16[128,1024]{1,0:T(8,128)(2,1)S(1)}, bf16[128,1024]{1,0:T(8,128)(2,1)S(1)}, u32[]{:S(2)}, u32[]{:S(2)}) collective-permute-start(bf16[128,1024]{1,0:T(8,128)(2,1)S(1)} %join_hot.1.after), channel_id=1, source_target_pairs={{0,8},{4,12},{8,0},{12,4},{1,9},{5,13},{9,1},{13,5},{2,10},{6,14},... | collective-permute-start | bytes 786440 | tf_op jit(solution)/shard_map/ppermute | solution.py:578
  69.8 6.6 %copy-start.4 = (bf16[32,1536]{1,0:T(8,128)(2,1)S(1)}, bf16[32,1536]{1,0:T(8,128)(2,1)}, u32[]{:S(2)}) copy-start(bf16[32,1536]{1,0:T(8,128)(2,1)} %copy-done.3) | copy-start | bytes 294916
  69.8 6.6 %copy-start.12 = (bf16[32,1536]{1,0:T(8,128)(2,1)S(1)}, bf16[32,1536]{1,0:T(8,128)(2,1)}, u32[]{:S(2)}) copy-start(bf16[32,1536]{1,0:T(8,128)(2,1)} %copy-done.11) | copy-start | bytes 294916
  69.8 6.6 %copy-start.14 = (bf16[32,1536]{1,0:T(8,128)(2,1)S(1)}, bf16[32,1536]{1,0:T(8,128)(2,1)}, u32[]{:S(2)}) copy-start(bf16[32,1536]{1,0:T(8,128)(2,1)} %copy-done.13) | copy-start | bytes 294916
  69.8 6.6 %copy-start.16 = (bf16[32,1536]{1,0:T(8,128)(2,1)S(1)}, bf16[32,1536]{1,0:T(8,128)(2,1)}, u32[]{:S(2)}) copy-start(bf16[32,1536]{1,0:T(8,128)(2,1)} %copy-done.15) | copy-start | bytes 294916
  76.4 9.4 %collective-permute-start.27 = (bf16[2,128,1536]{2,1,0:T(8,128)(2,1)}, bf16[2,128,1536]{2,1,0:T(8,128)(2,1)S(1)}, u32[]{:S(2)}, u32[]{:S(2)}) collective-permute-start(bf16[2,128,1536]{2,1,0:T(8,128)(2,1)} %get-tuple-element.30), channel_id=1, source_target_pairs={{0,4},{4,0},{8,12},{12,8},{1,5},{5,1},{9,13},{13,9},{2,6},{6,2},{1... | collective-permute-start | bytes 2359304 | tf_op jit(solution)/shard_map/ppermute | solution.py:578
  77.6 0.7 copy-start.10
  77.6 10.2 %collective-permute-start.26 = (bf16[128,1024]{1,0:T(8,128)(2,1)S(1)}, bf16[128,1024]{1,0:T(8,128)(2,1)S(1)}, u32[]{:S(2)}, u32[]{:S(2)}) collective-permute-start(bf16[128,1024]{1,0:T(8,128)(2,1)S(1)} %maximum_convert_fusion.hidden_ref.after), channel_id=1, source_target_pairs={{0,4},{4,0},{8,12},{12,8},{1,5},{5,1},{9,13},{13,9},{2,6},{6,2},{1... | collective-permute-start | bytes 786440 | tf_op jit(solution)/shard_map/ppermute | solution.py:578
  81.6 4.2 %copy-start.29 = (bf16[128,1536]{1,0:T(8,128)(2,1)S(1)}, bf16[128,1536]{1,0:T(8,128)(2,1)}, u32[]{:S(2)}) copy-start(bf16[128,1536]{1,0:T(8,128)(2,1)} %get-tuple-element.31) | copy-start | bytes 1179652
  85.9 11.6 %collective-permute-start.28 = (bf16[128,1536]{1,0:T(8,128)(2,1)S(1)}, bf16[128,1536]{1,0:T(8,128)(2,1)S(1)}, u32[]{:S(2)}, u32[]{:S(2)}) collective-permute-start(bf16[128,1536]{1,0:T(8,128)(2,1)S(1)} %fusion), channel_id=1, source_target_pairs={{0,8},{4,12},{8,0},{12,4},{1,9},{5,13},{9,1},{13,5},{2,10},{6,14},... | collective-permute-start | bytes 1179656 | tf_op jit(solution)/shard_map/ppermute | solution.py:578
  87.8 0.7 copy-start.30
  97.4 1.1 %copy-start.1 = (f32[128,1536]{1,0:T(8,128)S(1)}, f32[128,1536]{1,0:T(8,128)}, u32[]{:S(2)}) copy-start(f32[128,1536]{1,0:T(8,128)} %down_got.1.base_ref) | copy-start | bytes 2359300
  98.6 5.7 %collective-permute-start.29 = (bf16[32,1536]{1,0:T(8,128)(2,1)S(1)}, bf16[32,1536]{1,0:T(8,128)(2,1)S(1)}, u32[]{:S(2)}, u32[]{:S(2)}) collective-permute-start(bf16[32,1536]{1,0:T(8,128)(2,1)S(1)} %get-tuple-element.33), channel_id=1, source_target_pairs={{0,1},{1,0},{2,3},{3,2},{4,5},{5,4},{6,7},{7,6},{8,9},{9,8},{10,11... | collective-permute-start | bytes 294920 | tf_op jit(solution)/shard_map/ppermute | solution.py:578
  98.8 10.6 %collective-permute-start.30 = (bf16[32,1536]{1,0:T(8,128)(2,1)S(1)}, bf16[32,1536]{1,0:T(8,128)(2,1)S(1)}, u32[]{:S(2)}, u32[]{:S(2)}) collective-permute-start(bf16[32,1536]{1,0:T(8,128)(2,1)S(1)} %get-tuple-element.34), channel_id=1, source_target_pairs={{0,2},{1,3},{2,0},{3,1},{4,6},{5,7},{6,4},{7,5},{8,10},{9,11},{10,... | collective-permute-start | bytes 294920 | tf_op jit(solution)/shard_map/ppermute | solution.py:578
  101.4 7.9 %collective-permute-start.31 = (bf16[32,1536]{1,0:T(8,128)(2,1)S(1)}, bf16[32,1536]{1,0:T(8,128)(2,1)S(1)}, u32[]{:S(2)}, u32[]{:S(2)}) collective-permute-start(bf16[32,1536]{1,0:T(8,128)(2,1)S(1)} %get-tuple-element.35), channel_id=1, source_target_pairs={{0,3},{1,2},{2,1},{3,0},{4,7},{5,6},{6,5},{7,4},{8,11},{9,10},{10,... | collective-permute-start | bytes 294920 | tf_op jit(solution)/shard_map/ppermute | solution.py:578
  (5 other events, 3.2 us)

commit v4 on v3

--- a/solution.py
+++ b/solution.py
@@ -119,19 +119,8 @@
 SMEM = pl.BlockSpec(memory_space=pltpu.SMEM)
 AWAY = pl.BlockSpec(memory_space=pl.ANY)
 DMA = pltpu.SemaphoreType.DMA
-
-
-COSTS = {"cold_send": 60, "cold_keep": 10, "down_keep": 10, "down_got": 10}
-LIMITS = {
-    "attention": 123,
-    "project": 120,
-    "norm_up_send": 116,
-    "up_keep": 116,
-    "cold_send": 121,
-    "cold_keep": 121,
-    "down_keep": 116,
-    "down_got": 116,
-}
+COSTS = {"join": 60, "attention": 20, "norm_up_send": 20, "up_keep": 20, "cold_send": 30, "cold_keep": 10, "down_keep": 0, "down_got": 0}
+LIMITS = {"attention": 123, "load_project": 100, "load_up": 88, "load_cold": 72, "load_down": 84}
 
 
 def call(kernel, name, out_shape, specs, operands, scratch=()):
@@ -141,9 +130,9 @@
         out_specs=jax.tree.map(lambda _: VMEM, out_shape),
         out_shape=out_shape,
         scratch_shapes=list(scratch),
-        compiler_params=pltpu.CompilerParams(vmem_limit_bytes=LIMITS.get(name, 32) * 2**19),
+        compiler_params=pltpu.CompilerParams(vmem_limit_bytes=LIMITS.get(name, 24) * 2**19),
         cost_estimate=pl.CostEstimate(
-            flops=0, bytes_accessed=COSTS.get(name, 6) * 10**6, transcendentals=0
+            flops=0, bytes_accessed=COSTS.get(name, 10) * 10**6, transcendentals=0
         ),
         name=name,
     )(*operands)
@@ -163,29 +152,52 @@
     return jax.ShapeDtypeStruct((rows, width), dtype)
 
 
+def load_kernel(after, *refs):
+    count = (len(refs) - 1) // 2
+    copies = [
+        pltpu.make_async_copy(source, target, refs[-1].at[i])
+        for i, (source, target) in enumerate(zip(refs[:count], refs[count:-1]))
+    ]
+    begin(copies)
+    finish(copies)
+
+
+def load(name, after, *arrays):
+    return call(
+        load_kernel,
+        name,
+        [jax.ShapeDtypeStruct(a.shape, a.dtype) for a in arrays],
+        [AWAY] * (1 + len(arrays)),
+        (after, *arrays),
+        [DMA((len(arrays),))],
+    )
+
+
 def attention_kernel(
-    lengths, q, kn, vn, keys, values, out_ref, small, key_buf, value_buf, small_sems, sems, *, here, steps
+    lengths, q, kn, vn, keys, values, out_ref, small, key_buf, value_buf, own_buf, prob_buf, sum_buf,
+    small_sems, sems, *, here, steps,
 ):
     rows, width = q.shape
     context = keys.shape[0] // here
     wide = 2 * HD
     parts = wide // HD
     count = width // wide
-
-    def copies(i):
-        column = pl.ds(i * wide, wide)
-        return (
-            pltpu.make_async_copy(keys.at[:, column], key_buf.at[i], sems.at[0, i]),
-            pltpu.make_async_copy(values.at[:, column], value_buf.at[i], sems.at[1, i]),
-        )
-
+    step_rows = 2
+    deep = step_rows * context
+    turns = here // step_rows
     heads = [
         pltpu.make_async_copy(ref, small.at[i], small_sems.at[i]) for i, ref in enumerate((q, kn, vn))
     ]
-    begin(heads)
-    for i in range(count):
-        begin(copies(i))
-    q_ref, kn_ref, vn_ref = small.at[0], small.at[1], small.at[2]
+    key_copies, value_copies = (
+        [
+            pltpu.make_async_copy(
+                ref.at[pl.ds(j * deep, deep)], buf.at[pl.ds(j * deep, deep)], sems.at[which, j]
+            )
+            for j in range(turns)
+        ]
+        for which, (ref, buf) in enumerate(((keys, key_buf), (values, value_buf)))
+    )
+    begin(heads + key_copies + value_copies)
 
     nt = (((1,), (1,)), ((), ()))
     factor = 1.0 / math.sqrt(HD)
@@ -199,22 +211,37 @@
     at = lax.broadcasted_iota(jnp.int32, (parts * rows, rows), 0) % rows
     to = lax.broadcasted_iota(jnp.int32, (parts * rows, rows), 1)
     seen = (at % here == to % here) & (to // here <= at // here)
+    columns = [slice(i * wide, (i + 1) * wide) for i in range(count)]
     finish(heads)
-    for i in range(count):
-        column = slice(i * wide, (i + 1) * wide)
-        q = q_ref[:, column]
-        split = jnp.concatenate(
-            [jnp.where(lane_head == j, q, jnp.zeros_like(q)) for j in range(parts)], axis=0
+    splits = []
+    for column in columns:
+        mine = small[0, :, column]
+        splits.append(
+            jnp.concatenate(
+                [jnp.where(lane_head == j, mine, jnp.zeros_like(mine)) for j in range(parts)], axis=0
+            )
         )
-        fresh = lax.dot_general(split, kn_ref[:, column], nt, preferred_element_type=jnp.float32)
+    for j in range(turns):
+        key_copies[j].wait()
+        for i, column in enumerate(columns):
+            scores = lax.dot_general(
+                splits[i],
+                key_buf[j * deep : (j + 1) * deep, column],
+                nt,
+                preferred_element_type=jnp.float32,
+            )
+            own = own_buf[i] if j else scores[:, :context]
+            for r in range(step_rows):
+                own = jnp.where(
+                    row == j * step_rows + r, scores[:, r * context : (r + 1) * context], own
+                )
+            own_buf[i] = own
+    for i, column in enumerate(columns):
+        fresh = lax.dot_general(
+            splits[i], small[1, :, column], nt, preferred_element_type=jnp.float32
+        )
         fresh = jnp.where(seen, fresh * factor, -jnp.inf)
-        key_copy, value_copy = copies(i)
-        key_copy.wait()
-        scores = lax.dot_general(split, key_buf[i], nt, preferred_element_type=jnp.float32)
-        own = scores[:, :context]
-        for r in range(1, here):
-            own = jnp.where(row == r, scores[:, r * context : (r + 1) * context], own)
-        own = jnp.where(open_slot, own * factor, -jnp.inf)
+        own = jnp.where(open_slot, own_buf[i] * factor, -jnp.inf)
         top = jnp.maximum(
             jnp.max(own, axis=-1, keepdims=True), jnp.max(fresh, axis=-1, keepdims=True)
         )
@@ -223,32 +250,47 @@
         scale = 1.0 / (
             jnp.sum(own, axis=-1, keepdims=True) + jnp.sum(fresh, axis=-1, keepdims=True)
         )
-        own = own * scale
-        spread = jnp.concatenate(
-            [jnp.where(row == r, own, 0.0).astype(jnp.bfloat16) for r in range(here)], axis=1
-        )
-        value_copy.wait()
-        got = jnp.dot(spread, value_buf[i], preferred_element_type=jnp.float32)
-        got = got + jnp.dot(
+        prob_buf[i] = own * scale
+        sum_buf[i] = jnp.dot(
             (fresh * scale).astype(jnp.bfloat16),
-            vn_ref[:, column],
+            small[2, :, column],
             preferred_element_type=jnp.float32,
         )
-        answer = got[:rows]
-        for j in range(1, parts):
-            answer = jnp.where(lane_head == j, got[j * rows : (j + 1) * rows], answer)
-        out_ref[:, column] = answer.astype(jnp.bfloat16)
+    for j in range(turns):
+        value_copies[j].wait()
+        for i, column in enumerate(columns):
+            probs = prob_buf[i]
+            spread = jnp.concatenate(
+                [
+                    jnp.where(row == j * step_rows + r, probs, 0.0).astype(jnp.bfloat16)
+                    for r in range(step_rows)
+                ],
+                axis=1,
+            )
+            got = sum_buf[i] + jnp.dot(
+                spread,
+                value_buf[j * deep : (j + 1) * deep, column],
+                preferred_element_type=jnp.float32,
+            )
+            if j + 1 < turns:
+                sum_buf[i] = got
+            else:
+                answer = got[:rows]
+                for p in range(1, parts):
+                    answer = jnp.where(lane_head == p, got[p * rows : (p + 1) * rows], answer)
+                out_ref[:, column] = answer.astype(jnp.bfloat16)
 
 
 def attention(queries, key_cache, value_cache, key_new, value_new, lengths):
     steps, here, width = queries.shape
-    slots = here * key_cache.shape[1]
+    context = key_cache.shape[1]
+    rows = steps * here
     count = width // (2 * HD)
     flat = lambda a: a.reshape(-1, width)
     return call(
         functools.partial(attention_kernel, here=here, steps=steps),
         "attention",
-        like(steps * here, width),
+        like(rows, width),
         [SMEM] + [AWAY] * 5,
         (
             lengths,
@@ -259,42 +301,31 @@
             flat(value_cache),
         ),
         [
-            pltpu.VMEM((3, steps * here, width), jnp.bfloat16),
-            pltpu.VMEM((count, slots, 2 * HD), jnp.bfloat16),
-            pltpu.VMEM((count, slots, 2 * HD), jnp.bfloat16),
+            pltpu.VMEM((3, rows, width), jnp.bfloat16),
+            pltpu.VMEM((here * context, width), jnp.bfloat16),
+            pltpu.VMEM((here * context, width), jnp.bfloat16),
+            pltpu.VMEM((count, 2 * rows, context), jnp.float32),
+            pltpu.VMEM((count, 2 * rows, context), jnp.float32),
+            pltpu.VMEM((count, 2 * rows, 2 * HD), jnp.float32),
             DMA((3,)),
-            DMA((2, count)),
+            DMA((2, here // 2)),
         ],
     )
 
 
 def project_kernel(place, *refs, parts):
-    rows_refs, weight, outs = refs[:parts], refs[parts], refs[parts + 1 : -4]
-    held, weight_buf, total, sems = refs[-4:]
+    rows_refs, weight_ref, outs, held = refs[:parts], refs[parts], refs[parts + 1 : -1], refs[-1]
     chunk = outs[0].shape[0]
-    depth = weight.shape[0]
-    count = 6
-    deep = depth // count
-    copies = [
-        pltpu.make_async_copy(
-            weight.at[pl.ds(i * deep, deep)], weight_buf.at[pl.ds(i * deep, deep)], sems.at[i]
-        )
-        for i in range(count)
-    ]
-    begin(copies)
     for k, ref in enumerate(rows_refs):
         held[k] = ref[...]
     rows = jnp.concatenate([held[place[0] ^ place[1] ^ m] for m in range(parts)], axis=0)
-    for i in range(0, count, 2):
-        finish(copies[i : i + 2])
-        span = slice(i * deep, (i + 2) * deep)
-        made = jnp.dot(rows[:, span], weight_buf[span], preferred_element_type=jnp.float32)
-        if i:
-            made = made + total[...]
-        if i + 2 < count:
-            total[...] = made
-    for m, out in enumerate(outs):
-        out[...] = made[m * chunk : (m + 1) * chunk].astype(out.dtype)
+    width = weight_ref.shape[1]
+    wide = width // 3
+    for i in range(3):
+        column = slice(i * wide, (i + 1) * wide)
+        made = jnp.dot(rows, weight_ref[:, column], preferred_element_type=jnp.float32)
+        for m, out in enumerate(outs):
+            out[:, column] = made[m * chunk : (m + 1) * chunk].astype(out.dtype)
 
 
 def project(place, gathered, weight):
@@ -305,14 +336,9 @@
         functools.partial(project_kernel, parts=parts),
         "project",
         [like(chunk, width, jnp.bfloat16 if m else jnp.float32) for m in range(parts)],
-        [SMEM] + [VMEM] * parts + [AWAY],
+        [SMEM] + [VMEM] * (parts + 1),
         (place, *gathered, weight),
-        [
-            pltpu.VMEM((parts, chunk, depth), jnp.bfloat16),
-            pltpu.VMEM(weight.shape, jnp.bfloat16),
-            pltpu.VMEM((parts * chunk, width), jnp.float32),
-            DMA((6,)),
-        ],
+        [pltpu.VMEM((parts, chunk, depth), jnp.bfloat16)],
     )
 
 
@@ -333,10 +359,8 @@
     )
 
 
-def norm_kernel(place, gain_ref, hot, *refs, parts, blocks):
-    states, (sent_ref, own_ref, stat_ref, buf, sems) = refs[:-5], refs[-5:]
-    copies = half_copies(hot, place[2] ^ 1, buf, sems)
-    begin(copies)
+def norm_kernel(place, gain_ref, hot_ref, *refs, parts, blocks):
+    states, (sent_ref, own_ref, stat_ref) = refs[:-3], refs[-3:]
     chunk, width = states[0].shape
     gain = gain_ref[...].astype(jnp.float32)
     for m in range(parts):
@@ -355,30 +379,16 @@
         own_ref[place_rows, :] = (rows[0] * scale * gain).astype(jnp.bfloat16)
         stat_ref[0, place_rows, :] = jnp.broadcast_to(mean, (chunk, HD))
         stat_ref[1, place_rows, :] = jnp.broadcast_to(scale, (chunk, HD))
-    up_half(own_ref, copies, buf, sent_ref)
-
-
-def half_copies(hot, half, buf, sems):
-    count = buf.shape[0]
-    return [
-        pltpu.make_async_copy(
-            hot.at[pl.ds(half * count + i, 2)], buf.at[pl.ds(i, 2)], sems.at[i // 2]
-        )
-        for i in range(0, count, 2)
-    ]
-
-
-def half_scratch(hot):
-    count = hot.shape[0] // 2
-    return [pltpu.VMEM((count,) + hot.shape[1:], jnp.bfloat16), DMA((count // 2,))]
-
-
-def up_half(rows_ref, copies, buf, out_ref):
+    up_half(own_ref, hot_ref, place[2] ^ 1, sent_ref)
+
+
+def up_half(rows_ref, hot_ref, half, out_ref):
+    count = hot_ref.shape[0] // 2
     rows = rows_ref[...]
-    for i, copy in enumerate(copies):
-        copy.wait()
-        weight = jnp.concatenate([buf[2 * i], buf[2 * i + 1]], axis=1)
-        out_ref[:, 2 * i * HD : 2 * (i + 1) * HD] = jnp.dot(
+    for i in range(0, count, 2):
+        at = half * count + i
+        weight = jnp.concatenate([hot_ref[at], hot_ref[at + 1]], axis=1)
+        out_ref[:, i * HD : (i + 2) * HD] = jnp.dot(
             rows, weight, preferred_element_type=jnp.float32
         ).astype(out_ref.dtype)
 
@@ -395,16 +405,13 @@
             like(rows, width),
             jax.ShapeDtypeStruct((2, rows, HD), jnp.float32),
         ],
-        [SMEM, VMEM, AWAY] + [VMEM] * (blocks * parts),
+        [SMEM] + [VMEM] * (2 + blocks * parts),
         (place, gain, hot, *[a for column in columns for a in column]),
-        half_scratch(hot),
-    )
-
-
-def up_kernel(place, rows_ref, hot, out_ref, buf, sems):
-    copies = half_copies(hot, place[2], buf, sems)
-    begin(copies)
-    up_half(rows_ref, copies, buf, out_ref)
+    )
+
+
+def up_kernel(place, rows_ref, hot_ref, out_ref):
+    up_half(rows_ref, hot_ref, place[2], out_ref)
 
 
 def up_keep(place, rows, hot):
@@ -412,55 +419,26 @@
         up_kernel,
         "up_keep",
         like(rows.shape[0], hot.shape[0] // 2 * HD),
-        [SMEM, VMEM, AWAY],
+        [SMEM, VMEM, VMEM],
         (place, rows, hot),
-        half_scratch(hot),
-    )
-
-
-def piece_copies(cold_down, block, width, buf, i, sems):
+    )
+
+
+def pieces_of(hidden, down_ref, block, width):
+    depth = down_ref.shape[1]
     at = pl.ds(pl.multiple_of(block * width, width), width)
-    return [
-        pltpu.make_async_copy(cold_down.at[c, :, at], buf.at[i, c], sems.at[i, c]) for c in range(2)
-    ]
-
-
-def piece_scratch(cold_down, width):
-    return [pltpu.VMEM((2, 2, cold_down.shape[1], width), jnp.bfloat16), DMA((2, 2))]
-
-
-def piece(hidden, copies, buf, i):
-    finish(copies)
-    depth, width = buf.shape[2:]
-    return jnp.dot(
-        hidden, buf[i].reshape(2 * depth, width), preferred_element_type=jnp.float32
-    ).astype(jnp.bfloat16)
-
-
-def cold_kernel(place, counts, lists_ref, stat_ref, after, up, down, *refs, parts, steps):
+    weight = jnp.concatenate([down_ref[0, :, at], down_ref[1, :, at]], axis=0)
+    return jnp.dot(hidden, weight, preferred_element_type=jnp.float32).astype(jnp.bfloat16)
+
+
+def cold_kernel(place, counts, lists_ref, stat_ref, after, up_ref, down_ref, *refs, parts, steps):
     blocks = lists_ref.shape[0]
-    gains, states = refs[:blocks], refs[blocks:-6]
-    hidden_ref, out_ref, up_buf, up_sems, down_buf, down_sems = refs[-6:]
+    gains, states = refs[:blocks], refs[blocks:-2]
+    hidden_ref, out_ref = refs[-2:]
     chunk, width = states[0].shape
     total = parts * chunk
     here = chunk // steps
     b = place[1]
-    up_copies = [
-        [
-            pltpu.make_async_copy(
-                up.at[c, pl.ds(pl.multiple_of((b ^ k) * width, width), width)],
-                up_buf.at[k, c],
-                up_sems.at[k, c],
-            )
-            for c in range(2)
-        ]
-        for k in range(blocks)
-    ]
-    down_copies = [
-        piece_copies(down, b ^ (2 * i + 1), width, down_buf, i, down_sems) for i in range(2)
-    ]
-    for copies in up_copies + down_copies:
-        begin(copies)
     mean, scale = stat_ref[0][:, :1], stat_ref[1][:, :1]
     sums = jnp.zeros((total, 2 * HD), jnp.float32)
     for k in range(blocks):
@@ -469,8 +447,8 @@
         ).astype(jnp.float32)
         gain = gains[k][...].astype(jnp.float32)
         normed = ((rows - mean) * scale * gain).astype(jnp.bfloat16)
-        finish(up_copies[k])
-        weight = jnp.concatenate([up_buf[k, 0], up_buf[k, 1]], axis=1)
+        at = pl.ds(pl.multiple_of((b ^ k) * width, width), width)
+        weight = jnp.concatenate([up_ref[0, at, :], up_ref[1, at, :]], axis=1)
         sums = sums + jnp.dot(normed, weight, preferred_element_type=jnp.float32)
     slots = lists_ref.shape[3]
     index = lax.broadcasted_iota(jnp.int32, (total, slots), 0)
@@ -484,8 +462,8 @@
         halves.append((jnp.maximum(sums[:, c * HD : (c + 1) * HD], 0.0) * used))
     hidden = jnp.concatenate(halves, axis=1).astype(jnp.bfloat16)
     hidden_ref[...] = hidden
-    for i in range(2):
-        out_ref[i] = piece(hidden, down_copies[i], down_buf, i)
+    for i in range(blocks // 2):
+        out_ref[i] = pieces_of(hidden, down_ref, b ^ (2 * i + 1), width)
 
 
 def cold_send(place, counts, lists, stat, after, cold_up, cold_down, gains, columns, steps):
@@ -497,20 +475,16 @@
         functools.partial(cold_kernel, parts=parts, steps=steps),
         "cold_send",
         [like(rows, 2 * HD), jax.ShapeDtypeStruct((blocks // 2, rows, width), jnp.bfloat16)],
-        [SMEM, SMEM, VMEM, VMEM, AWAY, AWAY, AWAY] + [VMEM] * (blocks + len(flat)),
+        [SMEM, SMEM, VMEM, VMEM, AWAY, VMEM, VMEM] + [VMEM] * (blocks + len(flat)),
         (place, counts, lists, stat, after, cold_up, cold_down, *gains, *flat),
-        [pltpu.VMEM((blocks, 2, width, HD), jnp.bfloat16), DMA((blocks, 2))]
-        + piece_scratch(cold_down, width),
-    )
-
-
-def keep_kernel(place, hidden_ref, down, after, near_ref, far_ref, buf, sems):
+    )
+
+
+def keep_kernel(place, hidden_ref, down_ref, after, near_ref, far_ref):
     width = near_ref.shape[1]
-    copies = [piece_copies(down, place[1] ^ (2 * i), width, buf, i, sems) for i in range(2)]
-    begin(copies[1] + copies[0])
     hidden = hidden_ref[...]
-    far_ref[...] = piece(hidden, copies[1], buf, 1)
-    near_ref[...] = piece(hidden, copies[0], buf, 0)
+    far_ref[...] = pieces_of(hidden, down_ref, place[1] ^ 2, width)
+    near_ref[...] = pieces_of(hidden, down_ref, place[1], width)
 
 
 def cold_keep(place, hidden, cold_down, after, width):
@@ -519,30 +493,24 @@
         keep_kernel,
         "cold_keep",
         [like(rows, width), like(rows, width)],
-        [SMEM, VMEM, AWAY, AWAY],
+        [SMEM, VMEM, VMEM, AWAY],
         (place, hidden, cold_down, after),
-        piece_scratch(cold_down, width),
-    )
-
-
-def down_kernel(place, hidden_ref, hot, *refs, half):
-    before, (out_ref, buf, sems) = refs[:-3], refs[-3:]
-    copies = half_copies(hot, place[2] ^ half, buf, sems)
-    begin(copies)
-    depth, width = buf.shape[1:]
-    for i in range(0, len(copies), 2):
-        finish(copies[i : i + 2])
-        made = jnp.dot(
-            hidden_ref[:, 2 * i * depth : 2 * (i + 2) * depth],
-            buf[2 * i : 2 * (i + 2)].reshape(4 * depth, width),
-            preferred_element_type=jnp.float32,
-        )
-        if i:
-            made = made + out_ref[...]
-        else:
-            for ref in before:
-                made = made + ref[...].astype(jnp.float32)
-        out_ref[...] = made
+    )
+
+
+def down_kernel(place, hidden_ref, hot_ref, *refs, half):
+    count, depth = hot_ref.shape[0] // 2, hot_ref.shape[1]
+    width = hot_ref.shape[2]
+    wide = width // 3
+    hidden = hidden_ref[...]
+    first = (place[2] ^ half) * count
+    for i in range(3):
+        column = slice(i * wide, (i + 1) * wide)
+        weight = hot_ref[pl.ds(first, count), :, column].reshape(count * depth, wide)
+        made = jnp.dot(hidden, weight, preferred_element_type=jnp.float32)
+        for ref in refs[:-1]:
+            made = made + ref[:, column].astype(jnp.float32)
+        refs[-1][:, column] = made
 
 
 def down(place, half, hidden, hot, *before):
@@ -550,9 +518,8 @@
         functools.partial(down_kernel, half=half),
         "down_got" if half else "down_keep",
         like(hidden.shape[0], hot.shape[2], jnp.float32),
-        [SMEM, VMEM, AWAY] + [VMEM] * len(before),
+        [SMEM, VMEM, VMEM] + [VMEM] * len(before),
         (place, hidden, hot, *before),
-        half_scratch(hot),
     )
 
 
@@ -610,6 +577,8 @@
     gathered = [attended, swap(attended, "blocks", 1), across, swap(across, "blocks", 1)]
     pieces = project(place, gathered, out_proj)
     got = [swap(pieces[m], "heads", m) for m in others]
+    (hot_up,) = load("load_up", pieces[1], hot_up)
+    got, hot_up = lax.optimization_barrier((got, hot_up))
     gain = norm_gain[None]
     gains = [gain] + [swap(gain, "blocks", k) for k in range(1, blocks)]
     mine = lax.dynamic_slice(residual, (0, h * here, 0), (steps, here, width))
@@ -637,8 +606,9 @@
     hidden = jnp.maximum(total, 0.0).astype(jnp.bfloat16)
     near, far = cold_keep(place, cold, cold_down, hidden, width)
     far = (far.astype(jnp.float32) + cold_got[1].astype(jnp.float32)).astype(jnp.bfloat16)
+    partner = swap(hidden, "blocks", 1)
+    hidden, far = lax.optimization_barrier((hidden, far))
     cold_far = swap(far, "blocks", 2)
-    partner = swap(hidden, "blocks", 1)
     base = down(place, 0, hidden, hot_down)
     base = down(place, 1, partner, hot_down, base, near, cold_got[0])
     made = into_chunks(base, cold_far, parts)

time: 111 us -> 93.1 us (0.84)
  Pallas kernels: 41.1 us -> 19.7 us
  local copies, waits for them, and re-layouts: 6.94 us -> 14.7 us
  waiting for transfers between devices: 30.4 us -> 25.7 us
  starting transfers between devices: 27.1 us -> 29.9 us
  other arithmetic: 3.34 us -> 1.79 us
    pallas_call x11 -> x12, Pallas kernels: 41.1 us -> 19.7 us  [call(): pl.pallas_call(kernel, in_specs=specs, out_specs=jax.tree.map(lambda _: V...]
    unnamed x75 -> x23, local copies, waits for them, and re-layouts: 5.49 us -> 14.6 us
    ppermute x32, waiting for transfers between devices: 30.4 us -> 25.7 us  [swap(): return lax.ppermute(x, axis, [(i, i ^ m) for i in range(size)])]
    ppermute x32, starting transfers between devices: 27.1 us -> 29.9 us  [swap(): return lax.ppermute(x, axis, [(i, i ^ m) for i in range(size)])]
  transfers between devices with their start and end apart: 32 -> 32, of which waited for: 14 -> 13; matrix products, arithmetic and copies ran while one was open for 4% -> 1% of each run, Pallas kernels for 24% -> 10%
where the time goes in v4:
time: 93.1 us; the launch traced here: 92.7 us
  starting transfers between devices  29.9 us (32%)
  waiting for transfers between devices  25.7 us (28%)
  Pallas kernels  19.7 us (21%)
  local copies, waits for them, and re-layouts  14.7 us (16%)
  other arithmetic  1.79 us (2%)
    ppermute x32, starting transfers between devices, swap(): return lax.ppermute(x, axis, [(i, i ^ m) for i in range(size)])  29.9 us
    ppermute x32, waiting for transfers between devices, swap(): return lax.ppermute(x, axis, [(i, i ^ m) for i in range(size)])  25.7 us
    pallas_call x12, Pallas kernels, call(): pl.pallas_call(kernel, in_specs=specs, out_specs=jax.tree.map(lambda _: V...  19.7 us
    unnamed x23, local copies, waits for them, and re-layouts  14.6 us
  transfers between devices with their start and end apart: 32, of which 13 were waited for; matrix products, arithmetic and copies ran while one was open for 1% of the time, Pallas kernels for 10%

profile of v4, /device:TPU:0, one launch (start us, length us, event | category | flops | bytes accessed | tf_op | source)
XLA Modules:
  0.0 92.7 jit_solution(13066245831193918083)
XLA Ops:
  0.7 7.3 %attention.1.refs_0_ = bf16[32,1536]{1,0:T(8,128)(2,1)} custom-call(s32[8]{0:T(128)} %lengths.1, bf16[32,1536]{1,0:T(8,128)(2,1)} %bitcast.41, bf16[32,1536]{1,0:T(8,128)(2,1)} %bitcast.42, bf16[32,1536]{1,0:T(8,128)(2,1)} %bitcast.43, bf16[1024,1536]{1,0:T(8,128)(2,1)} %bitcast.39, bf16[1024,1536]{1,0:T(8,128)(2,1)} %bitcast.40), custom_call_target="tpu_custom_call" | custom-call | bytes 20000000 | tf_op jit(solution)/shard_map/attention/pallas_call | solution.py:127
  8.0 3.0 %collective-permute-start.1 = (bf16[32,1536]{1,0:T(8,128)(2,1)}, bf16[32,1536]{1,0:T(8,128)(2,1)S(1)}, u32[]{:S(2)}, u32[]{:S(2)}) collective-permute-start(bf16[32,1536]{1,0:T(8,128)(2,1)} %attention.1.refs_0_), channel_id=1, source_target_pairs={{0,8},{4,12},{8,0},{12,4},{1,9},{5,13},{9,1},{13,5},{2,10},{6,14},... | collective-permute-start | bytes 294920 | tf_op jit(solution)/shard_map/ppermute | solution.py:545
  11.0 3.0 %collective-permute-done.1.refs_2_ = bf16[32,1536]{1,0:T(8,128)(2,1)S(1)} collective-permute-done((bf16[32,1536]{1,0:T(8,128)(2,1)}, bf16[32,1536]{1,0:T(8,128)(2,1)S(1)}, u32[]{:S(2)}, u32[]{:S(2)}) %collective-permute-start.1) | collective-permute-done | bytes 98336 | tf_op jit(solution)/shard_map/ppermute | solution.py:545
  14.0 0.1 pad_add_fusion.place
  14.1 1.2 %collective-permute-done.2.refs_3_ = bf16[32,1536]{1,0:T(8,128)(2,1)S(1)} collective-permute-done((bf16[32,1536]{1,0:T(8,128)(2,1)S(1)}, bf16[32,1536]{1,0:T(8,128)(2,1)S(1)}, u32[]{:S(2)}, u32[]{:S(2)}) %collective-permute-start.2) | collective-permute-done | bytes 98336 | tf_op jit(solution)/shard_map/ppermute | solution.py:545
  15.3 2.3 %copy-done.5 = bf16[1536,1536]{1,0:T(8,128)(2,1)S(1)} copy-done((bf16[1536,1536]{1,0:T(8,128)(2,1)S(1)}, bf16[1536,1536]{1,0:T(8,128)(2,1)}, u32[]{:S(2)}) %copy-start.5) | copy-done | bytes 4718616
  17.7 0.9 copy-done.7
  18.5 1.3 %project.1 = (f32[32,1536]{1,0:T(8,128)S(1)}, bf16[32,1536]{1,0:T(8,128)(2,1)S(1)}, bf16[32,1536]{1,0:T(8,128)(2,1)S(1)}, bf16[32,1536]{1,0:T(8,128)(2,1)S(1)}) custom-call(s32[3]{0:T(128)S(1)} %pad_add_fusion.place, bf16[32,1536]{1,0:T(8,128)(2,1)S(1)} %copy-done.7, bf16[32,1536]{1,0:T(8,128)(2,1)S(1)} %collective-permute-done.refs_1_, ...), custom_call_target="tpu_custom_call" | custom-call | bytes 10000000 | tf_op jit(solution)/shard_map/project/pallas_call | solution.py:127
  19.9 1.9 %collective-permute-start.3 = (bf16[32,1536]{1,0:T(8,128)(2,1)S(1)}, bf16[32,1536]{1,0:T(8,128)(2,1)S(1)}, u32[]{:S(2)}, u32[]{:S(2)}) collective-permute-start(bf16[32,1536]{1,0:T(8,128)(2,1)S(1)} %get-tuple-element.26.after), channel_id=1, source_target_pairs={{0,1},{1,0},{2,3},{3,2},{4,5},{5,4},{6,7},{7,6},{8,9},{9,8},{10,11... | collective-permute-start | bytes 294920 | tf_op jit(solution)/shard_map/ppermute | solution.py:545
  21.8 0.1 collective-permute-start.6
  21.9 1.6 %collective-permute-start.7 = (bf16[1,1536]{1,0:T(2,128)(2,1)S(1)}, bf16[1,1536]{1,0:T(2,128)(2,1)S(1)}, u32[]{:S(2)}, u32[]{:S(2)}) collective-permute-start(bf16[1,1536]{1,0:T(2,128)(2,1)S(1)} %broadcast_in_dim.3.gain_ref.refs_0_), channel_id=1, source_target_pairs={{0,8},{4,12},{8,0},{12,4},{1,9},{5,13},{9,1},{13,5},{2,10},{6,14},... | collective-permute-start | bytes 9224 | tf_op jit(solution)/shard_map/ppermute | solution.py:545
  23.5 0.3 collective-permute-start.8
  23.8 2.6 %collective-permute-start.4 = (bf16[32,1536]{1,0:T(8,128)(2,1)S(1)}, bf16[32,1536]{1,0:T(8,128)(2,1)S(1)}, u32[]{:S(2)}, u32[]{:S(2)}) collective-permute-start(bf16[32,1536]{1,0:T(8,128)(2,1)S(1)} %get-tuple-element.27), channel_id=1, source_target_pairs={{0,2},{1,3},{2,0},{3,1},{4,6},{5,7},{6,4},{7,5},{8,10},{9,11},{10,... | collective-permute-start | bytes 294920 | tf_op jit(solution)/shard_map/ppermute | solution.py:545
  26.4 2.3 %collective-permute-start.5 = (bf16[32,1536]{1,0:T(8,128)(2,1)S(1)}, bf16[32,1536]{1,0:T(8,128)(2,1)S(1)}, u32[]{:S(2)}, u32[]{:S(2)}) collective-permute-start(bf16[32,1536]{1,0:T(8,128)(2,1)S(1)} %get-tuple-element.28), channel_id=1, source_target_pairs={{0,3},{1,2},{2,1},{3,0},{4,7},{5,6},{6,5},{7,4},{8,11},{9,10},{10,... | collective-permute-start | bytes 294920 | tf_op jit(solution)/shard_map/ppermute | solution.py:545
  28.7 2.8 %load_up.1.hot_ref = bf16[16,1536,128]{2,1,0:T(8,128)(2,1)S(1)} custom-call(bf16[32,1536]{1,0:T(8,128)(2,1)S(1)} %get-tuple-element.26.after, bf16[16,1536,128]{2,1,0:T(8,128)(2,1)} %refs_0_.1), custom_call_target="tpu_custom_call" | custom-call | bytes 10000000 | tf_op jit(solution)/shard_map/load_up/pallas_call | solution.py:127
  31.5 2.3 %collective-permute-done.4.refs_3_ = bf16[32,1536]{1,0:T(8,128)(2,1)S(1)} collective-permute-done((bf16[32,1536]{1,0:T(8,128)(2,1)S(1)}, bf16[32,1536]{1,0:T(8,128)(2,1)S(1)}, u32[]{:S(2)}, u32[]{:S(2)}) %collective-permute-start.4) | collective-permute-done | bytes 98336 | tf_op jit(solution)/shard_map/ppermute | solution.py:545
  33.8 0.1 join.1.refs_0_.refs_4_
  33.9 2.7 %collective-permute-start.9 = (bf16[32,1536]{1,0:T(8,128)(2,1)S(1)}, bf16[32,1536]{1,0:T(8,128)(2,1)S(1)}, u32[]{:S(2)}, u32[]{:S(2)}) collective-permute-start(bf16[32,1536]{1,0:T(8,128)(2,1)S(1)} %join.1.refs_0_.refs_4_), channel_id=1, source_target_pairs={{0,1},{1,0},{2,3},{3,2},{4,5},{5,4},{6,7},{7,6},{8,9},{9,8},{10,11... | collective-permute-start | bytes 294920 | tf_op jit(solution)/shard_map/ppermute | solution.py:545
  36.6 1.3 %collective-permute-start.10 = (bf16[32,1536]{1,0:T(8,128)(2,1)S(1)}, bf16[32,1536]{1,0:T(8,128)(2,1)S(1)}, u32[]{:S(2)}, u32[]{:S(2)}) collective-permute-start(bf16[32,1536]{1,0:T(8,128)(2,1)S(1)} %join.1.refs_0_.refs_4_), channel_id=1, source_target_pairs={{0,2},{1,3},{2,0},{3,1},{4,6},{5,7},{6,4},{7,5},{8,10},{9,11},{10,... | collective-permute-start | bytes 294920 | tf_op jit(solution)/shard_map/ppermute | solution.py:545
  37.8 1.4 %collective-permute-start.11 = (bf16[32,1536]{1,0:T(8,128)(2,1)S(1)}, bf16[32,1536]{1,0:T(8,128)(2,1)S(1)}, u32[]{:S(2)}, u32[]{:S(2)}) collective-permute-start(bf16[32,1536]{1,0:T(8,128)(2,1)S(1)} %join.1.refs_0_.refs_4_), channel_id=1, source_target_pairs={{0,3},{1,2},{2,1},{3,0},{4,7},{5,6},{6,5},{7,4},{8,11},{9,10},{10,... | collective-permute-start | bytes 294920 | tf_op jit(solution)/shard_map/ppermute | solution.py:545
  39.2 1.5 %collective-permute-start.16 = (bf16[32,1536]{1,0:T(8,128)(2,1)S(1)}, bf16[32,1536]{1,0:T(8,128)(2,1)S(1)}, u32[]{:S(2)}, u32[]{:S(2)}) collective-permute-start(bf16[32,1536]{1,0:T(8,128)(2,1)S(1)} %join.1.refs_0_.refs_4_), channel_id=1, source_target_pairs={{0,8},{4,12},{8,0},{12,4},{1,9},{5,13},{9,1},{13,5},{2,10},{6,14},... | collective-permute-start | bytes 294920 | tf_op jit(solution)/shard_map/ppermute | solution.py:545
  40.8 0.6 collective-permute-start.17
  41.3 5.5 %collective-permute-done.10.refs_2_.refs_6_ = bf16[32,1536]{1,0:T(8,128)(2,1)S(1)} collective-permute-done((bf16[32,1536]{1,0:T(8,128)(2,1)S(1)}, bf16[32,1536]{1,0:T(8,128)(2,1)S(1)}, u32[]{:S(2)}, u32[]{:S(2)}) %collective-permute-start.10) | collective-permute-done | bytes 98336 | tf_op jit(solution)/shard_map/ppermute | solution.py:545
  46.8 1.5 %collective-permute-start.18 = (bf16[32,1536]{1,0:T(8,128)(2,1)S(1)}, bf16[32,1536]{1,0:T(8,128)(2,1)S(1)}, u32[]{:S(2)}, u32[]{:S(2)}) collective-permute-start(bf16[32,1536]{1,0:T(8,128)(2,1)S(1)} %collective-permute-done.10.refs_2_.refs_6_), channel_id=1, source_target_pairs={{0,8},{4,12},{8,0},{12,4},{1,9},{5,13},{9,1},{13,5},{2,10},{6,14},... | collective-permute-start | bytes 294920 | tf_op jit(solution)/shard_map/ppermute | solution.py:545
  48.4 0.5 collective-permute-start.19
  48.9 0.5 collective-permute-start.14
  49.4 0.1 collective-permute-start.15
  49.5 2.0 %collective-permute-done.18.refs_10_.refs_14_ = bf16[32,1536]{1,0:T(8,128)(2,1)S(1)} collective-permute-done((bf16[32,1536]{1,0:T(8,128)(2,1)S(1)}, bf16[32,1536]{1,0:T(8,128)(2,1)S(1)}, u32[]{:S(2)}, u32[]{:S(2)}) %collective-permute-start.18) | collective-permute-done | bytes 98336 | tf_op jit(solution)/shard_map/ppermute | solution.py:545
  51.5 1.5 %collective-permute-done.19.refs_11_.refs_15_ = bf16[32,1536]{1,0:T(8,128)(2,1)S(1)} collective-permute-done((bf16[32,1536]{1,0:T(8,128)(2,1)S(1)}, bf16[32,1536]{1,0:T(8,128)(2,1)S(1)}, u32[]{:S(2)}, u32[]{:S(2)}) %collective-permute-start.19) | collective-permute-done | bytes 98336 | tf_op jit(solution)/shard_map/ppermute | solution.py:545
  53.0 0.5 collective-permute-start.22
  53.5 0.1 collective-permute-start.23
  53.6 0.7 collective-permute-done.21.refs_13_.refs_17_
  54.3 0.2 collective-permute-done.22.refs_14_.refs_18_
  54.5 0.4 collective-permute-done.23.refs_15_.refs_19_
  54.8 1.9 %norm_up_send.1 = (bf16[128,1024]{1,0:T(8,128)(2,1)S(1)}, bf16[128,1536]{1,0:T(8,128)(2,1)S(1)}, f32[2,128,128]{2,1,0:T(8,128)S(1)}) custom-call(s32[3]{0:T(128)S(1)} %pad_add_fusion.place, bf16[1,1536]{1,0:T(2,128)(2,1)S(1)} %broadcast_in_dim.3.gain_ref.refs_0_, bf16[16,1536,128]{2,1,0:T(8,128)(2,1)S(1)} %load_up.1.hot_ref, ...), custom_call_target="tpu_custom_call" | custom-call | bytes 20000000 | tf_op jit(solution)/shard_map/norm_up_send/pallas_call | solution.py:127
  56.7 0.2 collective-permute-start.24
  56.9 1.1 %up_keep.1.refs_0_ = bf16[128,1024]{1,0:T(8,128)(2,1)S(1)} custom-call(s32[3]{0:T(128)S(1)} %pad_add_fusion.place, bf16[128,1536]{1,0:T(8,128)(2,1)S(1)} %get-tuple-element.33.rows_ref, bf16[16,1536,128]{2,1,0:T(8,128)(2,1)S(1)} %load_up.1.hot_ref), custom_call_target="tpu_custom_call" | custom-call | bytes 20000000 | tf_op jit(solution)/shard_map/up_keep/pallas_call | solution.py:127
  58.1 0.3 collective-permute-done.24.refs_1_
  58.3 0.1 join_hot.1.after
  58.4 1.1 %collective-permute-start.25 = (bf16[128,1024]{1,0:T(8,128)(2,1)S(1)}, bf16[128,1024]{1,0:T(8,128)(2,1)S(1)}, u32[]{:S(2)}, u32[]{:S(2)}) collective-permute-start(bf16[128,1024]{1,0:T(8,128)(2,1)S(1)} %join_hot.1.after), channel_id=1, source_target_pairs={{0,8},{4,12},{8,0},{12,4},{1,9},{5,13},{9,1},{13,5},{2,10},{6,14},... | collective-permute-start | bytes 786440 | tf_op jit(solution)/shard_map/ppermute | solution.py:545
  59.5 0.1 copy.18
  59.6 0.1 reshape.49.counts
  59.7 1.9 %copy-done.3 = bf16[2,128,6144]{2,1,0:T(8,128)(2,1)S(1)} copy-done((bf16[2,128,6144]{2,1,0:T(8,128)(2,1)S(1)}, bf16[2,128,6144]{2,1,0:T(8,128)(2,1)}, u32[]{:S(2)}) %copy-start.3) | copy-done | bytes 3145752
  61.6 1.9 %copy-done.6 = bf16[2,6144,128]{2,1,0:T(8,128)(2,1)S(1)} copy-done((bf16[2,6144,128]{2,1,0:T(8,128)(2,1)S(1)}, bf16[2,6144,128]{2,1,0:T(8,128)(2,1)}, u32[]{:S(2)}) %copy-start.6) | copy-done | bytes 3145752
  63.5 1.9 %cold_send.1 = (bf16[128,256]{1,0:T(8,128)(2,1)S(1)}, bf16[2,128,1536]{2,1,0:T(8,128)(2,1)S(1)}) custom-call(s32[3]{0:T(128)S(1)} %pad_add_fusion.place, s32[8]{0:T(128)S(1)} %reshape.49.counts, s32[4,1,2,32]{3,2,1,0:T(2,128)S(1)} %copy-done.8, f32[2,128,128]{2,1,0:T(8,128)S(1)} %get-tuple-element.35.stat_ref, bf16[128,1024]{1,0:T(8,128)(2,1)S(1)} %join_hot.1.after, ...), custom_call_target="tpu_custom_call" | custom-call | bytes 30000000 | tf_op jit(solution)/shard_map/cold_send/pallas_call | solution.py:127
  65.4 1.4 %collective-permute-done.25 = bf16[128,1024]{1,0:T(8,128)(2,1)S(1)} collective-permute-done((bf16[128,1024]{1,0:T(8,128)(2,1)S(1)}, bf16[128,1024]{1,0:T(8,128)(2,1)S(1)}, u32[]{:S(2)}, u32[]{:S(2)}) %collective-permute-start.25) | collective-permute-done | bytes 262176 | tf_op jit(solution)/shard_map/ppermute | solution.py:545
  66.9 0.1 maximum_convert_fusion.after.hidden_ref
  67.0 0.6 collective-permute-start.26
  67.6 1.9 %copy-done.4 = bf16[2,128,6144]{2,1,0:T(8,128)(2,1)S(1)} copy-done((bf16[2,128,6144]{2,1,0:T(8,128)(2,1)S(1)}, bf16[2,128,6144]{2,1,0:T(8,128)(2,1)}, u32[]{:S(2)}) %copy-start.4) | copy-done | bytes 3145752
  69.5 0.9 %cold_keep.1 = (bf16[128,1536]{1,0:T(8,128)(2,1)S(1)}, bf16[128,1536]{1,0:T(8,128)(2,1)S(1)}) custom-call(s32[3]{0:T(128)S(1)} %pad_add_fusion.place, bf16[128,256]{1,0:T(8,128)(2,1)S(1)} %get-tuple-element.38.hidden_ref, bf16[2,128,6144]{2,1,0:T(8,128)(2,1)S(1)} %copy-done.4, bf16[128,1024]{1,0:T(8,128)(2,1)S(1)} %maximum_convert_fusion.after.hidden_ref), custom_call_target="tpu_custom_call" | custom-call | bytes 10000000 | tf_op jit(solution)/shard_map/cold_keep/pallas_call | solution.py:127
  70.4 0.1 fusion
  70.5 1.1 %collective-permute-start.28 = (bf16[128,1536]{1,0:T(8,128)(2,1)S(1)}, bf16[128,1536]{1,0:T(8,128)(2,1)S(1)}, u32[]{:S(2)}, u32[]{:S(2)}) collective-permute-start(bf16[128,1536]{1,0:T(8,128)(2,1)S(1)} %fusion), channel_id=1, source_target_pairs={{0,8},{4,12},{8,0},{12,4},{1,9},{5,13},{9,1},{13,5},{2,10},{6,14},... | collective-permute-start | bytes 1179656 | tf_op jit(solution)/shard_map/ppermute | solution.py:545
  71.6 2.8 %copy-done.1 = bf16[16,128,1536]{2,1,0:T(8,128)(2,1)S(1)} copy-done((bf16[16,128,1536]{2,1,0:T(8,128)(2,1)S(1)}, bf16[16,128,1536]{2,1,0:T(8,128)(2,1)}, u32[]{:S(2)}) %copy-start.1) | copy-done | bytes 6291480
  74.4 1.1 %down_keep.1.refs_0_ = f32[128,1536]{1,0:T(8,128)S(1)} custom-call(s32[3]{0:T(128)S(1)} %pad_add_fusion.place, bf16[128,1024]{1,0:T(8,128)(2,1)S(1)} %maximum_convert_fusion.after.hidden_ref, bf16[16,128,1536]{2,1,0:T(8,128)(2,1)S(1)} %copy-done.1), custom_call_target="tpu_custom_call" | custom-call | tf_op jit(solution)/shard_map/down_keep/pallas_call | solution.py:127
  75.6 2.8 %copy-done.2 = bf16[16,128,1536]{2,1,0:T(8,128)(2,1)S(1)} copy-done((bf16[16,128,1536]{2,1,0:T(8,128)(2,1)S(1)}, bf16[16,128,1536]{2,1,0:T(8,128)(2,1)}, u32[]{:S(2)}) %copy-start.2) | copy-done | bytes 6291480
  78.4 1.2 %down_got.1.base_ref = f32[128,1536]{1,0:T(8,128)S(1)} custom-call(s32[3]{0:T(128)S(1)} %pad_add_fusion.place, bf16[128,1024]{1,0:T(8,128)(2,1)S(1)} %collective-permute-done.26.hidden_ref, bf16[16,128,1536]{2,1,0:T(8,128)(2,1)S(1)} %copy-done.2, f32[128,1536]{1,0:T(8,128)S(1)} %down_keep.1.refs_0_, bf16[128,1536]{1,0:T(8,128)(2,1)S(1)} %get-tuple-element.42.refs_1_, ...), custom_call_target="tpu_custom_call" | custom-call | tf_op jit(solution)/shard_map/down_got/pallas_call | solution.py:127
  79.6 2.1 %collective-permute-done.28.more_ref = bf16[128,1536]{1,0:T(8,128)(2,1)S(1)} collective-permute-done((bf16[128,1536]{1,0:T(8,128)(2,1)S(1)}, bf16[128,1536]{1,0:T(8,128)(2,1)S(1)}, u32[]{:S(2)}, u32[]{:S(2)}) %collective-permute-start.28) | collective-permute-done | bytes 393248 | tf_op jit(solution)/shard_map/ppermute | solution.py:545
  81.6 0.1 into_chunks.1
  81.7 0.5 collective-permute-start.29
  82.2 2.6 %collective-permute-start.30 = (bf16[32,1536]{1,0:T(8,128)(2,1)S(1)}, bf16[32,1536]{1,0:T(8,128)(2,1)S(1)}, u32[]{:S(2)}, u32[]{:S(2)}) collective-permute-start(bf16[32,1536]{1,0:T(8,128)(2,1)S(1)} %get-tuple-element.46), channel_id=1, source_target_pairs={{0,2},{1,3},{2,0},{3,1},{4,6},{5,7},{6,4},{7,5},{8,10},{9,11},{10,... | collective-permute-start | bytes 294920 | tf_op jit(solution)/shard_map/ppermute | solution.py:545
  84.8 1.3 %collective-permute-start.31 = (bf16[32,1536]{1,0:T(8,128)(2,1)S(1)}, bf16[32,1536]{1,0:T(8,128)(2,1)S(1)}, u32[]{:S(2)}, u32[]{:S(2)}) collective-permute-start(bf16[32,1536]{1,0:T(8,128)(2,1)S(1)} %get-tuple-element.47), channel_id=1, source_target_pairs={{0,3},{1,2},{2,1},{3,0},{4,7},{5,6},{6,5},{7,4},{8,11},{9,10},{10,... | collective-permute-start | bytes 294920 | tf_op jit(solution)/shard_map/ppermute | solution.py:545
  86.1 0.8 maximum_bitcast_fusion
  86.9 5.0 %collective-permute-done.30 = bf16[32,1536]{1,0:T(8,128)(2,1)S(1)} collective-permute-done((bf16[32,1536]{1,0:T(8,128)(2,1)S(1)}, bf16[32,1536]{1,0:T(8,128)(2,1)S(1)}, u32[]{:S(2)}, u32[]{:S(2)}) %collective-permute-start.30) | collective-permute-done | bytes 98336 | tf_op jit(solution)/shard_map/ppermute | solution.py:545
  92.0 0.7 fusion.1
  (46 shorter events, 0.2 us)
Async XLA Ops:
  0.6 28.1 %copy-start = (bf16[4,32,1536]{2,1,0:T(8,128)(2,1)S(1)}, bf16[4,32,1536]{2,1,0:T(8,128)(2,1)}, u32[]{:S(2)}) copy-start(bf16[4,32,1536]{2,1,0:T(8,128)(2,1)} %param.22) | copy-start | bytes 1179652
  0.6 21.2 %copy-start.9 = (bf16[1536]{0:T(1024)(128)(2,1)S(1)}, bf16[1536]{0:T(1024)(128)(2,1)}, u32[]{:S(2)}) copy-start(bf16[1536]{0:T(1024)(128)(2,1)} %param.23) | copy-start | bytes 9220
  8.0 6.0 %collective-permute-start.1 = (bf16[32,1536]{1,0:T(8,128)(2,1)}, bf16[32,1536]{1,0:T(8,128)(2,1)S(1)}, u32[]{:S(2)}, u32[]{:S(2)}) collective-permute-start(bf16[32,1536]{1,0:T(8,128)(2,1)} %attention.1.refs_0_), channel_id=1, source_target_pairs={{0,8},{4,12},{8,0},{12,4},{1,9},{5,13},{9,1},{13,5},{2,10},{6,14},... | collective-permute-start | bytes 294920 | tf_op jit(solution)/shard_map/ppermute | solution.py:545
  11.0 3.1 %collective-permute-start = (bf16[32,1536]{1,0:T(8,128)(2,1)}, bf16[32,1536]{1,0:T(8,128)(2,1)S(1)}, u32[]{:S(2)}, u32[]{:S(2)}) collective-permute-start(bf16[32,1536]{1,0:T(8,128)(2,1)} %attention.1.refs_0_), channel_id=1, source_target_pairs={{0,4},{4,0},{8,12},{12,8},{1,5},{5,1},{9,13},{13,9},{2,6},{6,2},{1... | collective-permute-start | bytes 294920 | tf_op jit(solution)/shard_map/ppermute | solution.py:545
  14.0 1.3 %collective-permute-start.2 = (bf16[32,1536]{1,0:T(8,128)(2,1)S(1)}, bf16[32,1536]{1,0:T(8,128)(2,1)S(1)}, u32[]{:S(2)}, u32[]{:S(2)}) collective-permute-start(bf16[32,1536]{1,0:T(8,128)(2,1)S(1)} %collective-permute-done.1.refs_2_), channel_id=1, source_target_pairs={{0,4},{4,0},{8,12},{12,8},{1,5},{5,1},{9,13},{13,9},{2,6},{6,2},{1... | collective-permute-start | bytes 294920 | tf_op jit(solution)/shard_map/ppermute | solution.py:545
  15.3 2.3 %copy-start.5 = (bf16[1536,1536]{1,0:T(8,128)(2,1)S(1)}, bf16[1536,1536]{1,0:T(8,128)(2,1)}, u32[]{:S(2)}) copy-start(bf16[1536,1536]{1,0:T(8,128)(2,1)} %refs_4_.1) | copy-start | bytes 14155780
  17.6 0.9 copy-start.7
  19.9 6.5 %collective-permute-start.3 = (bf16[32,1536]{1,0:T(8,128)(2,1)S(1)}, bf16[32,1536]{1,0:T(8,128)(2,1)S(1)}, u32[]{:S(2)}, u32[]{:S(2)}) collective-permute-start(bf16[32,1536]{1,0:T(8,128)(2,1)S(1)} %get-tuple-element.26.after), channel_id=1, source_target_pairs={{0,1},{1,0},{2,3},{3,2},{4,5},{5,4},{6,7},{7,6},{8,9},{9,8},{10,11... | collective-permute-start | bytes 294920 | tf_op jit(solution)/shard_map/ppermute | solution.py:545
  21.8 12.0 %collective-permute-start.6 = (bf16[1,1536]{1,0:T(2,128)(2,1)S(1)}, bf16[1,1536]{1,0:T(2,128)(2,1)S(1)}, u32[]{:S(2)}, u32[]{:S(2)}) collective-permute-start(bf16[1,1536]{1,0:T(2,128)(2,1)S(1)} %broadcast_in_dim.3.gain_ref.refs_0_), channel_id=1, source_target_pairs={{0,4},{4,0},{8,12},{12,8},{1,5},{5,1},{9,13},{13,9},{2,6},{6,2},{1... | collective-permute-start | bytes 9224 | tf_op jit(solution)/shard_map/ppermute | solution.py:545
  21.9 11.9 %collective-permute-start.7 = (bf16[1,1536]{1,0:T(2,128)(2,1)S(1)}, bf16[1,1536]{1,0:T(2,128)(2,1)S(1)}, u32[]{:S(2)}, u32[]{:S(2)}) collective-permute-start(bf16[1,1536]{1,0:T(2,128)(2,1)S(1)} %broadcast_in_dim.3.gain_ref.refs_0_), channel_id=1, source_target_pairs={{0,8},{4,12},{8,0},{12,4},{1,9},{5,13},{9,1},{13,5},{2,10},{6,14},... | collective-permute-start | bytes 9224 | tf_op jit(solution)/shard_map/ppermute | solution.py:545
  23.5 10.3 %collective-permute-start.8 = (bf16[1,1536]{1,0:T(2,128)(2,1)S(1)}, bf16[1,1536]{1,0:T(2,128)(2,1)S(1)}, u32[]{:S(2)}, u32[]{:S(2)}) collective-permute-start(bf16[1,1536]{1,0:T(2,128)(2,1)S(1)} %broadcast_in_dim.3.gain_ref.refs_0_), channel_id=1, source_target_pairs={{0,12},{4,8},{8,4},{12,0},{1,13},{5,9},{9,5},{13,1},{2,14},{6,10},... | collective-permute-start | bytes 9224 | tf_op jit(solution)/shard_map/ppermute | solution.py:545
  23.8 10.0 %collective-permute-start.4 = (bf16[32,1536]{1,0:T(8,128)(2,1)S(1)}, bf16[32,1536]{1,0:T(8,128)(2,1)S(1)}, u32[]{:S(2)}, u32[]{:S(2)}) collective-permute-start(bf16[32,1536]{1,0:T(8,128)(2,1)S(1)} %get-tuple-element.27), channel_id=1, source_target_pairs={{0,2},{1,3},{2,0},{3,1},{4,6},{5,7},{6,4},{7,5},{8,10},{9,11},{10,... | collective-permute-start | bytes 294920 | tf_op jit(solution)/shard_map/ppermute | solution.py:545
  26.4 7.5 %collective-permute-start.5 = (bf16[32,1536]{1,0:T(8,128)(2,1)S(1)}, bf16[32,1536]{1,0:T(8,128)(2,1)S(1)}, u32[]{:S(2)}, u32[]{:S(2)}) collective-permute-start(bf16[32,1536]{1,0:T(8,128)(2,1)S(1)} %get-tuple-element.28), channel_id=1, source_target_pairs={{0,3},{1,2},{2,1},{3,0},{4,7},{5,6},{6,5},{7,4},{8,11},{9,10},{10,... | collective-permute-start | bytes 294920 | tf_op jit(solution)/shard_map/ppermute | solution.py:545
  33.9 6.8 %collective-permute-start.9 = (bf16[32,1536]{1,0:T(8,128)(2,1)S(1)}, bf16[32,1536]{1,0:T(8,128)(2,1)S(1)}, u32[]{:S(2)}, u32[]{:S(2)}) collective-permute-start(bf16[32,1536]{1,0:T(8,128)(2,1)S(1)} %join.1.refs_0_.refs_4_), channel_id=1, source_target_pairs={{0,1},{1,0},{2,3},{3,2},{4,5},{5,4},{6,7},{7,6},{8,9},{9,8},{10,11... | collective-permute-start | bytes 294920 | tf_op jit(solution)/shard_map/ppermute | solution.py:545
  36.6 10.3 %collective-permute-start.10 = (bf16[32,1536]{1,0:T(8,128)(2,1)S(1)}, bf16[32,1536]{1,0:T(8,128)(2,1)S(1)}, u32[]{:S(2)}, u32[]{:S(2)}) collective-permute-start(bf16[32,1536]{1,0:T(8,128)(2,1)S(1)} %join.1.refs_0_.refs_4_), channel_id=1, source_target_pairs={{0,2},{1,3},{2,0},{3,1},{4,6},{5,7},{6,4},{7,5},{8,10},{9,11},{10,... | collective-permute-start | bytes 294920 | tf_op jit(solution)/shard_map/ppermute | solution.py:545
  37.8 10.6 %collective-permute-start.11 = (bf16[32,1536]{1,0:T(8,128)(2,1)S(1)}, bf16[32,1536]{1,0:T(8,128)(2,1)S(1)}, u32[]{:S(2)}, u32[]{:S(2)}) collective-permute-start(bf16[32,1536]{1,0:T(8,128)(2,1)S(1)} %join.1.refs_0_.refs_4_), channel_id=1, source_target_pairs={{0,3},{1,2},{2,1},{3,0},{4,7},{5,6},{6,5},{7,4},{8,11},{9,10},{10,... | collective-permute-start | bytes 294920 | tf_op jit(solution)/shard_map/ppermute | solution.py:545
  39.2 9.7 %collective-permute-start.16 = (bf16[32,1536]{1,0:T(8,128)(2,1)S(1)}, bf16[32,1536]{1,0:T(8,128)(2,1)S(1)}, u32[]{:S(2)}, u32[]{:S(2)}) collective-permute-start(bf16[32,1536]{1,0:T(8,128)(2,1)S(1)} %join.1.refs_0_.refs_4_), channel_id=1, source_target_pairs={{0,8},{4,12},{8,0},{12,4},{1,9},{5,13},{9,1},{13,5},{2,10},{6,14},... | collective-permute-start | bytes 294920 | tf_op jit(solution)/shard_map/ppermute | solution.py:545
  40.7 8.1 %collective-permute-start.12 = (bf16[32,1536]{1,0:T(8,128)(2,1)S(1)}, bf16[32,1536]{1,0:T(8,128)(2,1)S(1)}, u32[]{:S(2)}, u32[]{:S(2)}) collective-permute-start(bf16[32,1536]{1,0:T(8,128)(2,1)S(1)} %join.1.refs_0_.refs_4_), channel_id=1, source_target_pairs={{0,4},{4,0},{8,12},{12,8},{1,5},{5,1},{9,13},{13,9},{2,6},{6,2},{1... | collective-permute-start | bytes 294920 | tf_op jit(solution)/shard_map/ppermute | solution.py:545
  40.8 8.6 %collective-permute-start.17 = (bf16[32,1536]{1,0:T(8,128)(2,1)S(1)}, bf16[32,1536]{1,0:T(8,128)(2,1)S(1)}, u32[]{:S(2)}, u32[]{:S(2)}) collective-permute-start(bf16[32,1536]{1,0:T(8,128)(2,1)S(1)} %collective-permute-done.9.refs_1_.refs_5_), channel_id=1, source_target_pairs={{0,8},{4,12},{8,0},{12,4},{1,9},{5,13},{9,1},{13,5},{2,10},{6,14},... | collective-permute-start | bytes 294920 | tf_op jit(solution)/shard_map/ppermute | solution.py:545
  46.8 4.6 %collective-permute-start.18 = (bf16[32,1536]{1,0:T(8,128)(2,1)S(1)}, bf16[32,1536]{1,0:T(8,128)(2,1)S(1)}, u32[]{:S(2)}, u32[]{:S(2)}) collective-permute-start(bf16[32,1536]{1,0:T(8,128)(2,1)S(1)} %collective-permute-done.10.refs_2_.refs_6_), channel_id=1, source_target_pairs={{0,8},{4,12},{8,0},{12,4},{1,9},{5,13},{9,1},{13,5},{2,10},{6,14},... | collective-permute-start | bytes 294920 | tf_op jit(solution)/shard_map/ppermute | solution.py:545
  48.4 4.6 %collective-permute-start.19 = (bf16[32,1536]{1,0:T(8,128)(2,1)S(1)}, bf16[32,1536]{1,0:T(8,128)(2,1)S(1)}, u32[]{:S(2)}, u32[]{:S(2)}) collective-permute-start(bf16[32,1536]{1,0:T(8,128)(2,1)S(1)} %collective-permute-done.11.refs_3_.refs_7_), channel_id=1, source_target_pairs={{0,8},{4,12},{8,0},{12,4},{1,9},{5,13},{9,1},{13,5},{2,10},{6,14},... | collective-permute-start | bytes 294920 | tf_op jit(solution)/shard_map/ppermute | solution.py:545
  48.9 4.1 %collective-permute-start.13 = (bf16[32,1536]{1,0:T(8,128)(2,1)S(1)}, bf16[32,1536]{1,0:T(8,128)(2,1)S(1)}, u32[]{:S(2)}, u32[]{:S(2)}) collective-permute-start(bf16[32,1536]{1,0:T(8,128)(2,1)S(1)} %collective-permute-done.9.refs_1_.refs_5_), channel_id=1, source_target_pairs={{0,4},{4,0},{8,12},{12,8},{1,5},{5,1},{9,13},{13,9},{2,6},{6,2},{1... | collective-permute-start | bytes 294920 | tf_op jit(solution)/shard_map/ppermute | solution.py:545
  48.9 4.6 %collective-permute-start.14 = (bf16[32,1536]{1,0:T(8,128)(2,1)S(1)}, bf16[32,1536]{1,0:T(8,128)(2,1)S(1)}, u32[]{:S(2)}, u32[]{:S(2)}) collective-permute-start(bf16[32,1536]{1,0:T(8,128)(2,1)S(1)} %collective-permute-done.10.refs_2_.refs_6_), channel_id=1, source_target_pairs={{0,4},{4,0},{8,12},{12,8},{1,5},{5,1},{9,13},{13,9},{2,6},{6,2},{1... | collective-permute-start | bytes 294920 | tf_op jit(solution)/shard_map/ppermute | solution.py:545
  49.4 4.2 %collective-permute-start.15 = (bf16[32,1536]{1,0:T(8,128)(2,1)S(1)}, bf16[32,1536]{1,0:T(8,128)(2,1)S(1)}, u32[]{:S(2)}, u32[]{:S(2)}) collective-permute-start(bf16[32,1536]{1,0:T(8,128)(2,1)S(1)} %collective-permute-done.11.refs_3_.refs_7_), channel_id=1, source_target_pairs={{0,4},{4,0},{8,12},{12,8},{1,5},{5,1},{9,13},{13,9},{2,6},{6,2},{1... | collective-permute-start | bytes 294920 | tf_op jit(solution)/shard_map/ppermute | solution.py:545
  51.5 2.1 %collective-permute-start.20 = (bf16[32,1536]{1,0:T(8,128)(2,1)S(1)}, bf16[32,1536]{1,0:T(8,128)(2,1)S(1)}, u32[]{:S(2)}, u32[]{:S(2)}) collective-permute-start(bf16[32,1536]{1,0:T(8,128)(2,1)S(1)} %collective-permute-done.16.refs_8_.refs_12_), channel_id=1, source_target_pairs={{0,4},{4,0},{8,12},{12,8},{1,5},{5,1},{9,13},{13,9},{2,6},{6,2},{1... | collective-permute-start | bytes 294920 | tf_op jit(solution)/shard_map/ppermute | solution.py:545
  53.0 1.3 %collective-permute-start.21 = (bf16[32,1536]{1,0:T(8,128)(2,1)S(1)}, bf16[32,1536]{1,0:T(8,128)(2,1)S(1)}, u32[]{:S(2)}, u32[]{:S(2)}) collective-permute-start(bf16[32,1536]{1,0:T(8,128)(2,1)S(1)} %collective-permute-done.17.refs_9_.refs_13_), channel_id=1, source_target_pairs={{0,4},{4,0},{8,12},{12,8},{1,5},{5,1},{9,13},{13,9},{2,6},{6,2},{1... | collective-permute-start | bytes 294920 | tf_op jit(solution)/shard_map/ppermute | solution.py:545
  53.0 1.5 %collective-permute-start.22 = (bf16[32,1536]{1,0:T(8,128)(2,1)S(1)}, bf16[32,1536]{1,0:T(8,128)(2,1)S(1)}, u32[]{:S(2)}, u32[]{:S(2)}) collective-permute-start(bf16[32,1536]{1,0:T(8,128)(2,1)S(1)} %collective-permute-done.18.refs_10_.refs_14_), channel_id=1, source_target_pairs={{0,4},{4,0},{8,12},{12,8},{1,5},{5,1},{9,13},{13,9},{2,6},{6,2},{1... | collective-permute-start | bytes 294920 | tf_op jit(solution)/shard_map/ppermute | solution.py:545
  53.5 1.3 %collective-permute-start.23 = (bf16[32,1536]{1,0:T(8,128)(2,1)S(1)}, bf16[32,1536]{1,0:T(8,128)(2,1)S(1)}, u32[]{:S(2)}, u32[]{:S(2)}) collective-permute-start(bf16[32,1536]{1,0:T(8,128)(2,1)S(1)} %collective-permute-done.19.refs_11_.refs_15_), channel_id=1, source_target_pairs={{0,4},{4,0},{8,12},{12,8},{1,5},{5,1},{9,13},{13,9},{2,6},{6,2},{1... | collective-permute-start | bytes 294920 | tf_op jit(solution)/shard_map/ppermute | solution.py:545
  56.7 2.8 %copy-start.10 = (s32[4,1,2]{0,2,1:T(2,128)S(1)}, s32[4,1,2]{0,2,1:T(2,128)}, u32[]{:S(2)}) copy-start(s32[4,1,2]{0,2,1:T(2,128)} %param.29) | copy-start | bytes 100
  56.7 3.0 %copy-start.8 = (s32[4,1,2,32]{3,2,1,0:T(2,128)S(1)}, s32[4,1,2,32]{3,2,1,0:T(2,128)}, u32[]{:S(2)}) copy-start(s32[4,1,2,32]{3,2,1,0:T(2,128)} %lists_ref.1) | copy-start | bytes 3076
  56.7 1.6 %collective-permute-start.24 = (bf16[128,1024]{1,0:T(8,128)(2,1)S(1)}, bf16[128,1024]{1,0:T(8,128)(2,1)S(1)}, u32[]{:S(2)}, u32[]{:S(2)}) collective-permute-start(bf16[128,1024]{1,0:T(8,128)(2,1)S(1)} %get-tuple-element.34), channel_id=1, source_target_pairs={{0,4},{4,0},{8,12},{12,8},{1,5},{5,1},{9,13},{13,9},{2,6},{6,2},{1... | collective-permute-start | bytes 786440 | tf_op jit(solution)/shard_map/ppermute | solution.py:545
  58.4 8.4 %collective-permute-start.25 = (bf16[128,1024]{1,0:T(8,128)(2,1)S(1)}, bf16[128,1024]{1,0:T(8,128)(2,1)S(1)}, u32[]{:S(2)}, u32[]{:S(2)}) collective-permute-start(bf16[128,1024]{1,0:T(8,128)(2,1)S(1)} %join_hot.1.after), channel_id=1, source_target_pairs={{0,8},{4,12},{8,0},{12,4},{1,9},{5,13},{9,1},{13,5},{2,10},{6,14},... | collective-permute-start | bytes 786440 | tf_op jit(solution)/shard_map/ppermute | solution.py:545
  59.7 1.9 %copy-start.3 = (bf16[2,128,6144]{2,1,0:T(8,128)(2,1)S(1)}, bf16[2,128,6144]{2,1,0:T(8,128)(2,1)}, u32[]{:S(2)}) copy-start(bf16[2,128,6144]{2,1,0:T(8,128)(2,1)} %down_ref.3) | copy-start | bytes 9437188
  61.6 1.9 %copy-start.6 = (bf16[2,6144,128]{2,1,0:T(8,128)(2,1)S(1)}, bf16[2,6144,128]{2,1,0:T(8,128)(2,1)}, u32[]{:S(2)}) copy-start(bf16[2,6144,128]{2,1,0:T(8,128)(2,1)} %up_ref.1) | copy-start | bytes 9437188
  66.8 3.6 %collective-permute-start.27 = (bf16[2,128,1536]{2,1,0:T(8,128)(2,1)S(1)}, bf16[2,128,1536]{2,1,0:T(8,128)(2,1)S(1)}, u32[]{:S(2)}, u32[]{:S(2)}) collective-permute-start(bf16[2,128,1536]{2,1,0:T(8,128)(2,1)S(1)} %get-tuple-element.40), channel_id=1, source_target_pairs={{0,4},{4,0},{8,12},{12,8},{1,5},{5,1},{9,13},{13,9},{2,6},{6,2},{1... | collective-permute-start | bytes 2359304 | tf_op jit(solution)/shard_map/ppermute | solution.py:545
  67.0 8.6 %collective-permute-start.26 = (bf16[128,1024]{1,0:T(8,128)(2,1)S(1)}, bf16[128,1024]{1,0:T(8,128)(2,1)S(1)}, u32[]{:S(2)}, u32[]{:S(2)}) collective-permute-start(bf16[128,1024]{1,0:T(8,128)(2,1)S(1)} %maximum_convert_fusion.after.hidden_ref), channel_id=1, source_target_pairs={{0,4},{4,0},{8,12},{12,8},{1,5},{5,1},{9,13},{13,9},{2,6},{6,2},{1... | collective-permute-start | bytes 786440 | tf_op jit(solution)/shard_map/ppermute | solution.py:545
  67.6 1.9 %copy-start.4 = (bf16[2,128,6144]{2,1,0:T(8,128)(2,1)S(1)}, bf16[2,128,6144]{2,1,0:T(8,128)(2,1)}, u32[]{:S(2)}) copy-start(bf16[2,128,6144]{2,1,0:T(8,128)(2,1)} %down_ref.3) | copy-start | bytes 9437188
  70.5 11.1 %collective-permute-start.28 = (bf16[128,1536]{1,0:T(8,128)(2,1)S(1)}, bf16[128,1536]{1,0:T(8,128)(2,1)S(1)}, u32[]{:S(2)}, u32[]{:S(2)}) collective-permute-start(bf16[128,1536]{1,0:T(8,128)(2,1)S(1)} %fusion), channel_id=1, source_target_pairs={{0,8},{4,12},{8,0},{12,4},{1,9},{5,13},{9,1},{13,5},{2,10},{6,14},... | collective-permute-start | bytes 1179656 | tf_op jit(solution)/shard_map/ppermute | solution.py:545
  71.6 2.8 %copy-start.1 = (bf16[16,128,1536]{2,1,0:T(8,128)(2,1)S(1)}, bf16[16,128,1536]{2,1,0:T(8,128)(2,1)}, u32[]{:S(2)}) copy-start(bf16[16,128,1536]{2,1,0:T(8,128)(2,1)} %hot_ref.3) | copy-start | bytes 18874372
  75.6 2.8 %copy-start.2 = (bf16[16,128,1536]{2,1,0:T(8,128)(2,1)S(1)}, bf16[16,128,1536]{2,1,0:T(8,128)(2,1)}, u32[]{:S(2)}) copy-start(bf16[16,128,1536]{2,1,0:T(8,128)(2,1)} %hot_ref.3) | copy-start | bytes 18874372
  81.7 5.3 %collective-permute-start.29 = (bf16[32,1536]{1,0:T(8,128)(2,1)S(1)}, bf16[32,1536]{1,0:T(8,128)(2,1)S(1)}, u32[]{:S(2)}, u32[]{:S(2)}) collective-permute-start(bf16[32,1536]{1,0:T(8,128)(2,1)S(1)} %get-tuple-element.45), channel_id=1, source_target_pairs={{0,1},{1,0},{2,3},{3,2},{4,5},{5,4},{6,7},{7,6},{8,9},{9,8},{10,11... | collective-permute-start | bytes 294920 | tf_op jit(solution)/shard_map/ppermute | solution.py:545
  82.2 9.8 %collective-permute-start.30 = (bf16[32,1536]{1,0:T(8,128)(2,1)S(1)}, bf16[32,1536]{1,0:T(8,128)(2,1)S(1)}, u32[]{:S(2)}, u32[]{:S(2)}) collective-permute-start(bf16[32,1536]{1,0:T(8,128)(2,1)S(1)} %get-tuple-element.46), channel_id=1, source_target_pairs={{0,2},{1,3},{2,0},{3,1},{4,6},{5,7},{6,4},{7,5},{8,10},{9,11},{10,... | collective-permute-start | bytes 294920 | tf_op jit(solution)/shard_map/ppermute | solution.py:545
  84.8 7.2 %collective-permute-start.31 = (bf16[32,1536]{1,0:T(8,128)(2,1)S(1)}, bf16[32,1536]{1,0:T(8,128)(2,1)S(1)}, u32[]{:S(2)}, u32[]{:S(2)}) collective-permute-start(bf16[32,1536]{1,0:T(8,128)(2,1)S(1)} %get-tuple-element.47), channel_id=1, source_target_pairs={{0,3},{1,2},{2,1},{3,0},{4,7},{5,6},{6,5},{7,4},{8,11},{9,10},{10,... | collective-permute-start | bytes 294920 | tf_op jit(solution)/shard_map/ppermute | solution.py:545

commit v5 on v4

--- a/solution.py
+++ b/solution.py
@@ -119,7 +119,7 @@
 SMEM = pl.BlockSpec(memory_space=pltpu.SMEM)
 AWAY = pl.BlockSpec(memory_space=pl.ANY)
 DMA = pltpu.SemaphoreType.DMA
-COSTS = {"join": 60, "attention": 20, "norm_up_send": 20, "up_keep": 20, "cold_send": 30, "cold_keep": 10, "down_keep": 0, "down_got": 0}
+COSTS = {"join": 60, "attention": 20, "norm_up_send": 20, "up_keep": 20, "cold_send": 30, "cold_keep": 0, "down": 0}
 LIMITS = {"attention": 123, "load_project": 100, "load_up": 88, "load_cold": 72, "load_down": 84}
 
 
@@ -182,7 +182,7 @@
     wide = 2 * HD
     parts = wide // HD
     count = width // wide
-    step_rows = 2
+    step_rows = 8
     deep = step_rows * context
     turns = here // step_rows
     heads = [
@@ -308,7 +308,7 @@
             pltpu.VMEM((count, 2 * rows, context), jnp.float32),
             pltpu.VMEM((count, 2 * rows, 2 * HD), jnp.float32),
             DMA((3,)),
-            DMA((2, here // 2)),
+            DMA((2, here // 8)),
         ],
     )
 
@@ -433,8 +433,8 @@
 
 def cold_kernel(place, counts, lists_ref, stat_ref, after, up_ref, down_ref, *refs, parts, steps):
     blocks = lists_ref.shape[0]
-    gains, states = refs[:blocks], refs[blocks:-2]
-    hidden_ref, out_ref = refs[-2:]
+    gains, states = refs[:blocks], refs[blocks:-3]
+    near_ref, out_ref, far_ref = refs[-3:]
     chunk, width = states[0].shape
     total = parts * chunk
     here = chunk // steps
@@ -461,9 +461,10 @@
         used = jnp.max(jnp.where(hit, 1.0, 0.0), axis=-1, keepdims=True)
         halves.append((jnp.maximum(sums[:, c * HD : (c + 1) * HD], 0.0) * used))
     hidden = jnp.concatenate(halves, axis=1).astype(jnp.bfloat16)
-    hidden_ref[...] = hidden
     for i in range(blocks // 2):
         out_ref[i] = pieces_of(hidden, down_ref, b ^ (2 * i + 1), width)
+    far_ref[...] = pieces_of(hidden, down_ref, b ^ 2, width)
+    near_ref[...] = pieces_of(hidden, down_ref, b, width)
 
 
 def cold_send(place, counts, lists, stat, after, cold_up, cold_down, gains, columns, steps):
@@ -474,68 +475,58 @@
     return call(
         functools.partial(cold_kernel, parts=parts, steps=steps),
         "cold_send",
-        [like(rows, 2 * HD), jax.ShapeDtypeStruct((blocks // 2, rows, width), jnp.bfloat16)],
+        [
+            like(rows, width),
+            jax.ShapeDtypeStruct((blocks // 2, rows, width), jnp.bfloat16),
+            like(rows, width),
+        ],
         [SMEM, SMEM, VMEM, VMEM, AWAY, VMEM, VMEM] + [VMEM] * (blocks + len(flat)),
         (place, counts, lists, stat, after, cold_up, cold_down, *gains, *flat),
     )
 
 
-def keep_kernel(place, hidden_ref, down_ref, after, near_ref, far_ref):
-    width = near_ref.shape[1]
-    hidden = hidden_ref[...]
-    far_ref[...] = pieces_of(hidden, down_ref, place[1] ^ 2, width)
-    near_ref[...] = pieces_of(hidden, down_ref, place[1], width)
-
-
-def cold_keep(place, hidden, cold_down, after, width):
-    rows = hidden.shape[0]
-    return call(
-        keep_kernel,
-        "cold_keep",
-        [like(rows, width), like(rows, width)],
-        [SMEM, VMEM, VMEM, AWAY],
-        (place, hidden, cold_down, after),
-    )
-
-
-def down_kernel(place, hidden_ref, hot_ref, *refs, half):
+def down_kernel(place, hidden_ref, partner_ref, hot_ref, *refs):
     count, depth = hot_ref.shape[0] // 2, hot_ref.shape[1]
     width = hot_ref.shape[2]
     wide = width // 3
-    hidden = hidden_ref[...]
-    first = (place[2] ^ half) * count
     for i in range(3):
         column = slice(i * wide, (i + 1) * wide)
-        weight = hot_ref[pl.ds(first, count), :, column].reshape(count * depth, wide)
-        made = jnp.dot(hidden, weight, preferred_element_type=jnp.float32)
-        for ref in refs[:-1]:
+        made = refs[0][:, column].astype(jnp.float32)
+        for ref in refs[1:-1]:
             made = made + ref[:, column].astype(jnp.float32)
+        for half, rows_ref in enumerate((hidden_ref, partner_ref)):
+            first = (place[2] ^ half) * count
+            weight = hot_ref[pl.ds(first, count), :, column].reshape(count * depth, wide)
+            made = made + jnp.dot(rows_ref[...], weight, preferred_element_type=jnp.float32)
         refs[-1][:, column] = made
 
 
-def down(place, half, hidden, hot, *before):
-    return call(
-        functools.partial(down_kernel, half=half),
-        "down_got" if half else "down_keep",
+def down(place, hidden, partner, hot, *before):
+    return call(
+        down_kernel,
+        "down",
         like(hidden.shape[0], hot.shape[2], jnp.float32),
-        [SMEM, VMEM, VMEM] + [VMEM] * len(before),
-        (place, hidden, hot, *before),
-    )
-
-
-def chunks_kernel(base_ref, more_ref, *outs):
+        [SMEM] + [VMEM] * (3 + len(before)),
+        (place, hidden, partner, hot, *before),
+    )
+
+
+def chunks_kernel(base_ref, more_ref, *outs, first):
     chunk = outs[0].shape[0]
-    for m, out in enumerate(outs):
-        rows = slice(m * chunk, (m + 1) * chunk)
-        out[...] = (base_ref[rows, :] + more_ref[rows, :].astype(jnp.float32)).astype(out.dtype)
-
-
-def into_chunks(base, more, parts):
-    rows, width = base.shape
-    return call(
-        chunks_kernel,
-        "into_chunks",
-        [like(rows // parts, width, jnp.bfloat16 if m else jnp.float32) for m in range(parts)],
+    for i, out in enumerate(outs):
+        rows = slice(i * chunk, (i + 1) * chunk)
+        from_base = slice((first + i) * chunk, (first + i + 1) * chunk)
+        out[...] = (base_ref[from_base, :] + more_ref[rows, :].astype(jnp.float32)).astype(out.dtype)
+
+
+def into_chunks(base, more, first, parts):
+    width = base.shape[1]
+    count = parts // 2
+    chunk = more.shape[0] // count
+    return call(
+        functools.partial(chunks_kernel, first=first),
+        "chunks_early" if first else "chunks_late",
+        [like(chunk, width, jnp.bfloat16 if first + i else jnp.float32) for i in range(count)],
         [VMEM, VMEM],
         (base, more),
     )
@@ -566,7 +557,7 @@
     all_rows, width = residual.shape[1:]
     parts = all_rows // here
     blocks = block_rows.shape[0]
-    others = range(1, parts)
+    others = range(parts - 1, 0, -1)
     b = lax.axis_index("blocks")
     h = lax.axis_index("heads")
     place = jnp.stack([h, b, b % 2]).astype(jnp.int32)
@@ -575,15 +566,17 @@
     attended = attention(queries, key_cache, value_cache, key_new, value_new, lengths)
     across = swap(attended, "blocks", 2)
     gathered = [attended, swap(attended, "blocks", 1), across, swap(across, "blocks", 1)]
+    gain = norm_gain[None]
+    gains = [gain] + [swap(gain, "blocks", k) for k in range(1, blocks)]
+    gathered, gains = lax.optimization_barrier((gathered, gains))
     pieces = project(place, gathered, out_proj)
     got = [swap(pieces[m], "heads", m) for m in others]
     (hot_up,) = load("load_up", pieces[1], hot_up)
     got, hot_up = lax.optimization_barrier((got, hot_up))
-    gain = norm_gain[None]
-    gains = [gain] + [swap(gain, "blocks", k) for k in range(1, blocks)]
     mine = lax.dynamic_slice(residual, (0, h * here, 0), (steps, here, width))
-    state = join("join", [mine.reshape(steps * here, width), pieces[0], *got], gains[1:])
-    states = [state] + [swap(state, "heads", m) for m in others]
+    state = join("join", [mine.reshape(steps * here, width), pieces[0], *got])
+    moved = {m: swap(state, "heads", m) for m in others}
+    states = [state] + [moved[m] for m in range(1, parts)]
     across = [swap(s, "blocks", 2) for s in states]
     columns = [
         states,
@@ -597,24 +590,31 @@
     summed = join("join_hot", [kept, sent])
     arrived = swap(summed, "blocks", 2)
 
-    cold, cold_sent = cold_send(
+    near, cold_sent, far = cold_send(
         place, counts, block_rows, stat, summed, cold_up, cold_down, gains, columns, steps
     )
     cold_sent, arrived = lax.optimization_barrier((cold_sent, arrived))
     cold_got = swap(cold_sent, "blocks", 1)
     total = summed.astype(jnp.float32) + arrived.astype(jnp.float32)
     hidden = jnp.maximum(total, 0.0).astype(jnp.bfloat16)
-    near, far = cold_keep(place, cold, cold_down, hidden, width)
-    far = (far.astype(jnp.float32) + cold_got[1].astype(jnp.float32)).astype(jnp.bfloat16)
+    far = far.astype(jnp.float32) + cold_got[1].astype(jnp.float32)
+    half = far.shape[0] // 2
+    late, early = far[:half].astype(jnp.bfloat16), far[half:].astype(jnp.bfloat16)
     partner = swap(hidden, "blocks", 1)
-    hidden, far = lax.optimization_barrier((hidden, far))
-    cold_far = swap(far, "blocks", 2)
-    base = down(place, 0, hidden, hot_down)
-    base = down(place, 1, partner, hot_down, base, near, cold_got[0])
-    made = into_chunks(base, cold_far, parts)
+    hidden, late, early = lax.optimization_barrier((hidden, late, early))
+    early = swap(early, "blocks", 2)
+    late = swap(late, "blocks", 2)
+    base = down(place, hidden, partner, hot_down, near, cold_got[0])
+    made = into_chunks(base, early, parts // 2, parts)
+    arrived = [
+        swap(made[i], "heads", parts // 2 + i) for i in reversed(range(parts // 2))
+    ]
+    made, late = lax.optimization_barrier((made, late))
+    made = into_chunks(base, late, 0, parts)
+    arrived += [swap(made[i], "heads", i) for i in range(1, parts // 2)]
     out = made[0]
-    for m in others:
-        out = out + swap(made[m], "heads", m).astype(jnp.float32)
+    for piece in arrived:
+        out = out + piece.astype(jnp.float32)
     ffn_out = out.astype(jnp.bfloat16).reshape(steps, here, width)
 
     stacked = jnp.stack(states).reshape(parts, steps, 1, here, width)

time: 93.1 us -> 83.9 us (0.901)
  local copies, waits for them, and re-layouts: 14.7 us -> 10.1 us
  starting transfers between devices: 29.9 us -> 27.4 us
  Pallas kernels: 19.7 us -> 18.3 us
    unnamed x23 -> x19, local copies, waits for them, and re-layouts: 14.6 us -> 9.91 us
    ppermute x32 -> x33, starting transfers between devices: 29.9 us -> 27.4 us  [swap(): return lax.ppermute(x, axis, [(i, i ^ m) for i in range(size)])]
    pallas_call x12 -> x11, Pallas kernels: 19.7 us -> 18.3 us  [call(): pl.pallas_call(kernel, in_specs=specs, out_specs=jax.tree.map(lambda _: V...]
    ppermute x32 -> x33, waiting for transfers between devices: 25.7 us -> 25.1 us  [swap(): return lax.ppermute(x, axis, [(i, i ^ m) for i in range(size)])]
  transfers between devices with their start and end apart: 32 -> 33, of which waited for: 13 -> 17; matrix products, arithmetic and copies ran while one was open for 1% -> 2% of each run, Pallas kernels for 10% -> 11%
where the time goes in v5:
time: 83.9 us; the launch traced here: 83.6 us
  starting transfers between devices  27.4 us (33%)
  waiting for transfers between devices  25.1 us (30%)
  Pallas kernels  18.3 us (22%)
  local copies, waits for them, and re-layouts  10.1 us (12%)
  other arithmetic  1.79 us (2%)
  between operations  0.84 us (1%)
    ppermute x33, starting transfers between devices, swap(): return lax.ppermute(x, axis, [(i, i ^ m) for i in range(size)])  27.4 us
    ppermute x33, waiting for transfers between devices, swap(): return lax.ppermute(x, axis, [(i, i ^ m) for i in range(size)])  25.1 us
    pallas_call x11, Pallas kernels, call(): pl.pallas_call(kernel, in_specs=specs, out_specs=jax.tree.map(lambda _: V...  18.3 us
    unnamed x19, local copies, waits for them, and re-layouts  9.91 us
  transfers between devices with their start and end apart: 33, of which 17 were waited for; matrix products, arithmetic and copies ran while one was open for 2% of the time, Pallas kernels for 11%

profile of v5, /device:TPU:0, one launch (start us, length us, event | category | flops | bytes accessed | tf_op | source)
XLA Modules:
  0.0 83.6 jit_solution(3098927110543800754)
XLA Ops:
  0.7 6.2 %attention.1.refs_0_ = bf16[32,1536]{1,0:T(8,128)(2,1)} custom-call(s32[8]{0:T(128)} %lengths.1, bf16[32,1536]{1,0:T(8,128)(2,1)} %bitcast.41, bf16[32,1536]{1,0:T(8,128)(2,1)} %bitcast.42, bf16[32,1536]{1,0:T(8,128)(2,1)} %bitcast.43, bf16[1024,1536]{1,0:T(8,128)(2,1)} %bitcast.39, bf16[1024,1536]{1,0:T(8,128)(2,1)} %bitcast.40), custom_call_target="tpu_custom_call" | custom-call | bytes 20000000 | tf_op jit(solution)/shard_map/attention/pallas_call | solution.py:127
  6.9 3.0 %collective-permute-start.1 = (bf16[32,1536]{1,0:T(8,128)(2,1)}, bf16[32,1536]{1,0:T(8,128)(2,1)S(1)}, u32[]{:S(2)}, u32[]{:S(2)}) collective-permute-start(bf16[32,1536]{1,0:T(8,128)(2,1)} %attention.1.refs_0_), channel_id=1, source_target_pairs={{0,8},{4,12},{8,0},{12,4},{1,9},{5,13},{9,1},{13,5},{2,10},{6,14},... | collective-permute-start | bytes 294920 | tf_op jit(solution)/shard_map/ppermute | solution.py:536
  9.9 0.1 collective-permute-start.3
  10.0 0.1 collective-permute-start.4
  10.1 1.8 %collective-permute-start.5 = (bf16[1,1536]{1,0:T(2,128)(2,1)S(1)}, bf16[1,1536]{1,0:T(2,128)(2,1)S(1)}, u32[]{:S(2)}, u32[]{:S(2)}) collective-permute-start(bf16[1,1536]{1,0:T(2,128)(2,1)S(1)} %broadcast_in_dim.3.gain_ref.refs_0_), channel_id=1, source_target_pairs={{0,12},{4,8},{8,4},{12,0},{1,13},{5,9},{9,5},{13,1},{2,14},{6,10},... | collective-permute-start | bytes 9224 | tf_op jit(solution)/shard_map/ppermute | solution.py:536
  11.9 0.3 collective-permute-start
  12.2 0.7 collective-permute-done.1.refs_2_
  12.9 0.1 pad_add_fusion.place
  13.0 0.7 collective-permute-done.4.refs_2_
  13.7 0.5 collective-permute-done.2.refs_3_
  14.2 2.3 %copy-done.2 = bf16[1536,1536]{1,0:T(8,128)(2,1)S(1)} copy-done((bf16[1536,1536]{1,0:T(8,128)(2,1)S(1)}, bf16[1536,1536]{1,0:T(8,128)(2,1)}, u32[]{:S(2)}) %copy-start.2) | copy-done | bytes 4718616
  16.6 0.9 %copy-done.5 = bf16[32,1536]{1,0:T(8,128)(2,1)S(1)} copy-done((bf16[32,1536]{1,0:T(8,128)(2,1)S(1)}, bf16[32,1536]{1,0:T(8,128)(2,1)}, u32[]{:S(2)}) %copy-start.5) | copy-done | bytes 98328
  17.5 1.3 %project.1 = (f32[32,1536]{1,0:T(8,128)S(1)}, bf16[32,1536]{1,0:T(8,128)(2,1)S(1)}, bf16[32,1536]{1,0:T(8,128)(2,1)S(1)}, bf16[32,1536]{1,0:T(8,128)(2,1)S(1)}) custom-call(s32[3]{0:T(128)S(1)} %pad_add_fusion.place, bf16[32,1536]{1,0:T(8,128)(2,1)S(1)} %copy-done.5, bf16[32,1536]{1,0:T(8,128)(2,1)S(1)} %collective-permute-done.refs_1_, ...), custom_call_target="tpu_custom_call" | custom-call | bytes 10000000 | tf_op jit(solution)/shard_map/project/pallas_call | solution.py:127
  18.8 4.0 %collective-permute-start.6 = (bf16[32,1536]{1,0:T(8,128)(2,1)S(1)}, bf16[32,1536]{1,0:T(8,128)(2,1)S(1)}, u32[]{:S(2)}, u32[]{:S(2)}) collective-permute-start(bf16[32,1536]{1,0:T(8,128)(2,1)S(1)} %get-tuple-element.39), channel_id=1, source_target_pairs={{0,3},{1,2},{2,1},{3,0},{4,7},{5,6},{6,5},{7,4},{8,11},{9,10},{10,... | collective-permute-start | bytes 294920 | tf_op jit(solution)/shard_map/ppermute | solution.py:536
  22.8 0.6 collective-permute-start.8
  23.5 2.8 %load_up.1.hot_ref = bf16[16,1536,128]{2,1,0:T(8,128)(2,1)S(1)} custom-call(bf16[32,1536]{1,0:T(8,128)(2,1)S(1)} %get-tuple-element.41.after, bf16[16,1536,128]{2,1,0:T(8,128)(2,1)} %refs_0_.1), custom_call_target="tpu_custom_call" | custom-call | bytes 10000000 | tf_op jit(solution)/shard_map/load_up/pallas_call | solution.py:127
  26.3 0.2 collective-permute-done.6.refs_2_
  26.5 4.9 %collective-permute-done.7.refs_3_ = bf16[32,1536]{1,0:T(8,128)(2,1)S(1)} collective-permute-done((bf16[32,1536]{1,0:T(8,128)(2,1)S(1)}, bf16[32,1536]{1,0:T(8,128)(2,1)S(1)}, u32[]{:S(2)}, u32[]{:S(2)}) %collective-permute-start.7) | collective-permute-done | bytes 98336 | tf_op jit(solution)/shard_map/ppermute | solution.py:536
  31.4 0.1 join.1.refs_0_.refs_4_
  31.5 0.6 collective-permute-start.9
  32.1 2.5 %collective-permute-start.10 = (bf16[32,1536]{1,0:T(8,128)(2,1)S(1)}, bf16[32,1536]{1,0:T(8,128)(2,1)S(1)}, u32[]{:S(2)}, u32[]{:S(2)}) collective-permute-start(bf16[32,1536]{1,0:T(8,128)(2,1)S(1)} %join.1.refs_0_.refs_4_), channel_id=1, source_target_pairs={{0,2},{1,3},{2,0},{3,1},{4,6},{5,7},{6,4},{7,5},{8,10},{9,11},{10,... | collective-permute-start | bytes 294920 | tf_op jit(solution)/shard_map/ppermute | solution.py:536
  34.6 1.3 %collective-permute-start.11 = (bf16[32,1536]{1,0:T(8,128)(2,1)S(1)}, bf16[32,1536]{1,0:T(8,128)(2,1)S(1)}, u32[]{:S(2)}, u32[]{:S(2)}) collective-permute-start(bf16[32,1536]{1,0:T(8,128)(2,1)S(1)} %join.1.refs_0_.refs_4_), channel_id=1, source_target_pairs={{0,3},{1,2},{2,1},{3,0},{4,7},{5,6},{6,5},{7,4},{8,11},{9,10},{10,... | collective-permute-start | bytes 294920 | tf_op jit(solution)/shard_map/ppermute | solution.py:536
  35.9 1.5 %collective-permute-start.16 = (bf16[32,1536]{1,0:T(8,128)(2,1)S(1)}, bf16[32,1536]{1,0:T(8,128)(2,1)S(1)}, u32[]{:S(2)}, u32[]{:S(2)}) collective-permute-start(bf16[32,1536]{1,0:T(8,128)(2,1)S(1)} %join.1.refs_0_.refs_4_), channel_id=1, source_target_pairs={{0,8},{4,12},{8,0},{12,4},{1,9},{5,13},{9,1},{13,5},{2,10},{6,14},... | collective-permute-start | bytes 294920 | tf_op jit(solution)/shard_map/ppermute | solution.py:536
  37.4 0.8 collective-permute-start.17
  38.2 3.8 %collective-permute-done.10.refs_2_.refs_6_ = bf16[32,1536]{1,0:T(8,128)(2,1)S(1)} collective-permute-done((bf16[32,1536]{1,0:T(8,128)(2,1)S(1)}, bf16[32,1536]{1,0:T(8,128)(2,1)S(1)}, u32[]{:S(2)}, u32[]{:S(2)}) %collective-permute-start.10) | collective-permute-done | bytes 98336 | tf_op jit(solution)/shard_map/ppermute | solution.py:536
  42.0 1.5 %collective-permute-start.18 = (bf16[32,1536]{1,0:T(8,128)(2,1)S(1)}, bf16[32,1536]{1,0:T(8,128)(2,1)S(1)}, u32[]{:S(2)}, u32[]{:S(2)}) collective-permute-start(bf16[32,1536]{1,0:T(8,128)(2,1)S(1)} %collective-permute-done.10.refs_2_.refs_6_), channel_id=1, source_target_pairs={{0,8},{4,12},{8,0},{12,4},{1,9},{5,13},{9,1},{13,5},{2,10},{6,14},... | collective-permute-start | bytes 294920 | tf_op jit(solution)/shard_map/ppermute | solution.py:536
  43.4 0.6 collective-permute-start.19
  44.0 0.5 collective-permute-start.14
  44.5 0.1 collective-permute-start.15
  44.6 2.0 %collective-permute-done.18.refs_10_.refs_14_ = bf16[32,1536]{1,0:T(8,128)(2,1)S(1)} collective-permute-done((bf16[32,1536]{1,0:T(8,128)(2,1)S(1)}, bf16[32,1536]{1,0:T(8,128)(2,1)S(1)}, u32[]{:S(2)}, u32[]{:S(2)}) %collective-permute-start.18) | collective-permute-done | bytes 98336 | tf_op jit(solution)/shard_map/ppermute | solution.py:536
  46.6 1.5 %collective-permute-done.19.refs_11_.refs_15_ = bf16[32,1536]{1,0:T(8,128)(2,1)S(1)} collective-permute-done((bf16[32,1536]{1,0:T(8,128)(2,1)S(1)}, bf16[32,1536]{1,0:T(8,128)(2,1)S(1)}, u32[]{:S(2)}, u32[]{:S(2)}) %collective-permute-start.19) | collective-permute-done | bytes 98336 | tf_op jit(solution)/shard_map/ppermute | solution.py:536
  48.1 0.5 collective-permute-start.22
  48.6 0.1 collective-permute-start.23
  48.6 0.7 collective-permute-done.21.refs_13_.refs_17_
  49.3 0.2 collective-permute-done.22.refs_14_.refs_18_
  49.5 0.4 collective-permute-done.23.refs_15_.refs_19_
  49.9 1.9 %norm_up_send.1 = (bf16[128,1024]{1,0:T(8,128)(2,1)S(1)}, bf16[128,1536]{1,0:T(8,128)(2,1)S(1)}, f32[2,128,128]{2,1,0:T(8,128)S(1)}) custom-call(s32[3]{0:T(128)S(1)} %pad_add_fusion.place, bf16[1,1536]{1,0:T(2,128)(2,1)S(1)} %broadcast_in_dim.3.gain_ref.refs_0_, bf16[16,1536,128]{2,1,0:T(8,128)(2,1)S(1)} %load_up.1.hot_ref, ...), custom_call_target="tpu_custom_call" | custom-call | bytes 20000000 | tf_op jit(solution)/shard_map/norm_up_send/pallas_call | solution.py:127
  51.8 0.2 collective-permute-start.24
  52.0 1.1 %up_keep.1.refs_0_ = bf16[128,1024]{1,0:T(8,128)(2,1)S(1)} custom-call(s32[3]{0:T(128)S(1)} %pad_add_fusion.place, bf16[128,1536]{1,0:T(8,128)(2,1)S(1)} %get-tuple-element.46.rows_ref, bf16[16,1536,128]{2,1,0:T(8,128)(2,1)S(1)} %load_up.1.hot_ref), custom_call_target="tpu_custom_call" | custom-call | bytes 20000000 | tf_op jit(solution)/shard_map/up_keep/pallas_call | solution.py:127
  53.1 0.3 collective-permute-done.24.refs_1_
  53.4 0.1 join_hot.1.after
  53.4 1.1 %collective-permute-start.25 = (bf16[128,1024]{1,0:T(8,128)(2,1)S(1)}, bf16[128,1024]{1,0:T(8,128)(2,1)S(1)}, u32[]{:S(2)}, u32[]{:S(2)}) collective-permute-start(bf16[128,1024]{1,0:T(8,128)(2,1)S(1)} %join_hot.1.after), channel_id=1, source_target_pairs={{0,8},{4,12},{8,0},{12,4},{1,9},{5,13},{9,1},{13,5},{2,10},{6,14},... | collective-permute-start | bytes 786440 | tf_op jit(solution)/shard_map/ppermute | solution.py:536
  54.6 0.1 copy.18
  54.6 0.1 reshape.49.counts
  54.7 1.9 %copy-done.3 = bf16[2,6144,128]{2,1,0:T(8,128)(2,1)S(1)} copy-done((bf16[2,6144,128]{2,1,0:T(8,128)(2,1)S(1)}, bf16[2,6144,128]{2,1,0:T(8,128)(2,1)}, u32[]{:S(2)}) %copy-start.3) | copy-done | bytes 3145752
  56.6 1.9 %copy-done.4 = bf16[2,128,6144]{2,1,0:T(8,128)(2,1)S(1)} copy-done((bf16[2,128,6144]{2,1,0:T(8,128)(2,1)S(1)}, bf16[2,128,6144]{2,1,0:T(8,128)(2,1)}, u32[]{:S(2)}) %copy-start.4) | copy-done | bytes 3145752
  58.5 3.2 %cold_send.1 = (bf16[128,1536]{1,0:T(8,128)(2,1)S(1)}, bf16[2,128,1536]{2,1,0:T(8,128)(2,1)}, bf16[128,1536]{1,0:T(8,128)(2,1)S(1)}) custom-call(s32[3]{0:T(128)S(1)} %pad_add_fusion.place, s32[8]{0:T(128)S(1)} %reshape.49.counts, s32[4,1,2,32]{3,2,1,0:T(2,128)S(1)} %copy-done.6, f32[2,128,128]{2,1,0:T(8,128)S(1)} %get-tuple-element.48.stat_ref, ...), custom_call_target="tpu_custom_call" | custom-call | bytes 30000000 | tf_op jit(solution)/shard_map/cold_send/pallas_call | solution.py:127
  61.7 0.2 collective-permute-done.25
  61.9 0.1 pad_maximum_fusion
  62.0 0.1 maximum_convert_fusion.hidden_ref
  62.1 0.6 collective-permute-start.27
  62.6 1.7 %collective-permute-done.26 = bf16[2,128,1536]{2,1,0:T(8,128)(2,1)S(1)} collective-permute-done((bf16[2,128,1536]{2,1,0:T(8,128)(2,1)}, bf16[2,128,1536]{2,1,0:T(8,128)(2,1)S(1)}, u32[]{:S(2)}, u32[]{:S(2)}) %collective-permute-start.26) | collective-permute-done | bytes 786464 | tf_op jit(solution)/shard_map/ppermute | solution.py:536
  64.4 0.1 fusion
  64.5 1.1 %collective-permute-start.28 = (bf16[64,1536]{1,0:T(8,128)(2,1)S(1)}, bf16[64,1536]{1,0:T(8,128)(2,1)S(1)}, u32[]{:S(2)}, u32[]{:S(2)}) collective-permute-start(bf16[64,1536]{1,0:T(8,128)(2,1)S(1)} %get-tuple-element.59), channel_id=1, source_target_pairs={{0,8},{4,12},{8,0},{12,4},{1,9},{5,13},{9,1},{13,5},{2,10},{6,14},... | collective-permute-start | bytes 589832 | tf_op jit(solution)/shard_map/ppermute | solution.py:536
  65.6 1.0 %collective-permute-start.29 = (bf16[64,1536]{1,0:T(8,128)(2,1)S(1)}, bf16[64,1536]{1,0:T(8,128)(2,1)S(1)}, u32[]{:S(2)}, u32[]{:S(2)}) collective-permute-start(bf16[64,1536]{1,0:T(8,128)(2,1)S(1)} %get-tuple-element.62), channel_id=1, source_target_pairs={{0,8},{4,12},{8,0},{12,4},{1,9},{5,13},{9,1},{13,5},{2,10},{6,14},... | collective-permute-start | bytes 589832 | tf_op jit(solution)/shard_map/ppermute | solution.py:536
  66.6 2.8 %copy-done.1 = bf16[16,128,1536]{2,1,0:T(8,128)(2,1)S(1)} copy-done((bf16[16,128,1536]{2,1,0:T(8,128)(2,1)S(1)}, bf16[16,128,1536]{2,1,0:T(8,128)(2,1)}, u32[]{:S(2)}) %copy-start.1) | copy-done | bytes 6291480
  69.4 1.6 %down.1.base_ref = f32[128,1536]{1,0:T(8,128)S(1)} custom-call(s32[3]{0:T(128)S(1)} %pad_add_fusion.place, bf16[128,1024]{1,0:T(8,128)(2,1)S(1)} %maximum_convert_fusion.hidden_ref, bf16[128,1024]{1,0:T(8,128)(2,1)S(1)} %collective-permute-done.27.partner_ref, bf16[16,128,1536]{2,1,0:T(8,128)(2,1)S(1)} %copy-done.1, ...), custom_call_target="tpu_custom_call" | custom-call | tf_op jit(solution)/shard_map/down/pallas_call | solution.py:127
  71.1 1.2 %collective-permute-done.28.more_ref = bf16[64,1536]{1,0:T(8,128)(2,1)S(1)} collective-permute-done((bf16[64,1536]{1,0:T(8,128)(2,1)S(1)}, bf16[64,1536]{1,0:T(8,128)(2,1)S(1)}, u32[]{:S(2)}, u32[]{:S(2)}) %collective-permute-start.28) | collective-permute-done | bytes 196640 | tf_op jit(solution)/shard_map/ppermute | solution.py:536
  72.3 2.4 %collective-permute-start.30 = (bf16[32,1536]{1,0:T(8,128)(2,1)S(1)}, bf16[32,1536]{1,0:T(8,128)(2,1)S(1)}, u32[]{:S(2)}, u32[]{:S(2)}) collective-permute-start(bf16[32,1536]{1,0:T(8,128)(2,1)S(1)} %get-tuple-element.61), channel_id=1, source_target_pairs={{0,3},{1,2},{2,1},{3,0},{4,7},{5,6},{6,5},{7,4},{8,11},{9,10},{10,... | collective-permute-start | bytes 294920 | tf_op jit(solution)/shard_map/ppermute | solution.py:536
  74.7 1.0 %collective-permute-done.29.more_ref = bf16[64,1536]{1,0:T(8,128)(2,1)S(1)} collective-permute-done((bf16[64,1536]{1,0:T(8,128)(2,1)S(1)}, bf16[64,1536]{1,0:T(8,128)(2,1)S(1)}, u32[]{:S(2)}, u32[]{:S(2)}) %collective-permute-start.29) | collective-permute-done | bytes 196640 | tf_op jit(solution)/shard_map/ppermute | solution.py:536
  75.8 1.1 %collective-permute-start.32 = (bf16[32,1536]{1,0:T(8,128)(2,1)S(1)}, bf16[32,1536]{1,0:T(8,128)(2,1)S(1)}, u32[]{:S(2)}, u32[]{:S(2)}) collective-permute-start(bf16[32,1536]{1,0:T(8,128)(2,1)S(1)} %get-tuple-element.65), channel_id=1, source_target_pairs={{0,1},{1,0},{2,3},{3,2},{4,5},{5,4},{6,7},{7,6},{8,9},{9,8},{10,11... | collective-permute-start | bytes 294920 | tf_op jit(solution)/shard_map/ppermute | solution.py:536
  76.9 0.8 maximum_bitcast_fusion
  77.7 5.2 %collective-permute-done.32 = bf16[32,1536]{1,0:T(8,128)(2,1)S(1)} collective-permute-done((bf16[32,1536]{1,0:T(8,128)(2,1)S(1)}, bf16[32,1536]{1,0:T(8,128)(2,1)S(1)}, u32[]{:S(2)}, u32[]{:S(2)}) %collective-permute-start.32) | collective-permute-done | bytes 98336 | tf_op jit(solution)/shard_map/ppermute | solution.py:536
  82.9 0.7 fusion.1
  (44 shorter events, 0.3 us)
Async XLA Ops:
  0.6 22.8 %copy-start = (bf16[4,32,1536]{2,1,0:T(8,128)(2,1)S(1)}, bf16[4,32,1536]{2,1,0:T(8,128)(2,1)}, u32[]{:S(2)}) copy-start(bf16[4,32,1536]{2,1,0:T(8,128)(2,1)} %param.22) | copy-start | bytes 1179652
  0.6 9.3 %copy-start.7 = (bf16[1536]{0:T(1024)(128)(2,1)S(1)}, bf16[1536]{0:T(1024)(128)(2,1)}, u32[]{:S(2)}) copy-start(bf16[1536]{0:T(1024)(128)(2,1)} %param.23) | copy-start | bytes 9220
  6.9 6.0 %collective-permute-start.1 = (bf16[32,1536]{1,0:T(8,128)(2,1)}, bf16[32,1536]{1,0:T(8,128)(2,1)S(1)}, u32[]{:S(2)}, u32[]{:S(2)}) collective-permute-start(bf16[32,1536]{1,0:T(8,128)(2,1)} %attention.1.refs_0_), channel_id=1, source_target_pairs={{0,8},{4,12},{8,0},{12,4},{1,9},{5,13},{9,1},{13,5},{2,10},{6,14},... | collective-permute-start | bytes 294920 | tf_op jit(solution)/shard_map/ppermute | solution.py:536
  9.9 3.1 %collective-permute-start.3 = (bf16[1,1536]{1,0:T(2,128)(2,1)S(1)}, bf16[1,1536]{1,0:T(2,128)(2,1)S(1)}, u32[]{:S(2)}, u32[]{:S(2)}) collective-permute-start(bf16[1,1536]{1,0:T(2,128)(2,1)S(1)} %broadcast_in_dim.3.gain_ref.refs_0_), channel_id=1, source_target_pairs={{0,4},{4,0},{8,12},{12,8},{1,5},{5,1},{9,13},{13,9},{2,6},{6,2},{1... | collective-permute-start | bytes 9224 | tf_op jit(solution)/shard_map/ppermute | solution.py:536
  10.0 3.7 %collective-permute-start.4 = (bf16[1,1536]{1,0:T(2,128)(2,1)S(1)}, bf16[1,1536]{1,0:T(2,128)(2,1)S(1)}, u32[]{:S(2)}, u32[]{:S(2)}) collective-permute-start(bf16[1,1536]{1,0:T(2,128)(2,1)S(1)} %broadcast_in_dim.3.gain_ref.refs_0_), channel_id=1, source_target_pairs={{0,8},{4,12},{8,0},{12,4},{1,9},{5,13},{9,1},{13,5},{2,10},{6,14},... | collective-permute-start | bytes 9224 | tf_op jit(solution)/shard_map/ppermute | solution.py:536
  10.1 3.6 %collective-permute-start.5 = (bf16[1,1536]{1,0:T(2,128)(2,1)S(1)}, bf16[1,1536]{1,0:T(2,128)(2,1)S(1)}, u32[]{:S(2)}, u32[]{:S(2)}) collective-permute-start(bf16[1,1536]{1,0:T(2,128)(2,1)S(1)} %broadcast_in_dim.3.gain_ref.refs_0_), channel_id=1, source_target_pairs={{0,12},{4,8},{8,4},{12,0},{1,13},{5,9},{9,5},{13,1},{2,14},{6,10},... | collective-permute-start | bytes 9224 | tf_op jit(solution)/shard_map/ppermute | solution.py:536
  11.9 1.8 %collective-permute-start = (bf16[32,1536]{1,0:T(8,128)(2,1)}, bf16[32,1536]{1,0:T(8,128)(2,1)S(1)}, u32[]{:S(2)}, u32[]{:S(2)}) collective-permute-start(bf16[32,1536]{1,0:T(8,128)(2,1)} %attention.1.refs_0_), channel_id=1, source_target_pairs={{0,4},{4,0},{8,12},{12,8},{1,5},{5,1},{9,13},{13,9},{2,6},{6,2},{1... | collective-permute-start | bytes 294920 | tf_op jit(solution)/shard_map/ppermute | solution.py:536
  12.9 1.3 %collective-permute-start.2 = (bf16[32,1536]{1,0:T(8,128)(2,1)S(1)}, bf16[32,1536]{1,0:T(8,128)(2,1)S(1)}, u32[]{:S(2)}, u32[]{:S(2)}) collective-permute-start(bf16[32,1536]{1,0:T(8,128)(2,1)S(1)} %collective-permute-done.1.refs_2_), channel_id=1, source_target_pairs={{0,4},{4,0},{8,12},{12,8},{1,5},{5,1},{9,13},{13,9},{2,6},{6,2},{1... | collective-permute-start | bytes 294920 | tf_op jit(solution)/shard_map/ppermute | solution.py:536
  14.2 2.3 %copy-start.2 = (bf16[1536,1536]{1,0:T(8,128)(2,1)S(1)}, bf16[1536,1536]{1,0:T(8,128)(2,1)}, u32[]{:S(2)}) copy-start(bf16[1536,1536]{1,0:T(8,128)(2,1)} %refs_4_.1) | copy-start | bytes 14155780
  16.6 0.9 %copy-start.5 = (bf16[32,1536]{1,0:T(8,128)(2,1)S(1)}, bf16[32,1536]{1,0:T(8,128)(2,1)}, u32[]{:S(2)}) copy-start(bf16[32,1536]{1,0:T(8,128)(2,1)} %attention.1.refs_0_) | copy-start | bytes 294916
  18.8 7.7 %collective-permute-start.6 = (bf16[32,1536]{1,0:T(8,128)(2,1)S(1)}, bf16[32,1536]{1,0:T(8,128)(2,1)S(1)}, u32[]{:S(2)}, u32[]{:S(2)}) collective-permute-start(bf16[32,1536]{1,0:T(8,128)(2,1)S(1)} %get-tuple-element.39), channel_id=1, source_target_pairs={{0,3},{1,2},{2,1},{3,0},{4,7},{5,6},{6,5},{7,4},{8,11},{9,10},{10,... | collective-permute-start | bytes 294920 | tf_op jit(solution)/shard_map/ppermute | solution.py:536
  22.8 8.6 %collective-permute-start.7 = (bf16[32,1536]{1,0:T(8,128)(2,1)S(1)}, bf16[32,1536]{1,0:T(8,128)(2,1)S(1)}, u32[]{:S(2)}, u32[]{:S(2)}) collective-permute-start(bf16[32,1536]{1,0:T(8,128)(2,1)S(1)} %get-tuple-element.40), channel_id=1, source_target_pairs={{0,2},{1,3},{2,0},{3,1},{4,6},{5,7},{6,4},{7,5},{8,10},{9,11},{10,... | collective-permute-start | bytes 294920 | tf_op jit(solution)/shard_map/ppermute | solution.py:536
  22.8 8.6 %collective-permute-start.8 = (bf16[32,1536]{1,0:T(8,128)(2,1)S(1)}, bf16[32,1536]{1,0:T(8,128)(2,1)S(1)}, u32[]{:S(2)}, u32[]{:S(2)}) collective-permute-start(bf16[32,1536]{1,0:T(8,128)(2,1)S(1)} %get-tuple-element.41.after), channel_id=1, source_target_pairs={{0,1},{1,0},{2,3},{3,2},{4,5},{5,4},{6,7},{7,6},{8,9},{9,8},{10,11... | collective-permute-start | bytes 294920 | tf_op jit(solution)/shard_map/ppermute | solution.py:536
  31.5 5.9 %collective-permute-start.9 = (bf16[32,1536]{1,0:T(8,128)(2,1)S(1)}, bf16[32,1536]{1,0:T(8,128)(2,1)S(1)}, u32[]{:S(2)}, u32[]{:S(2)}) collective-permute-start(bf16[32,1536]{1,0:T(8,128)(2,1)S(1)} %join.1.refs_0_.refs_4_), channel_id=1, source_target_pairs={{0,1},{1,0},{2,3},{3,2},{4,5},{5,4},{6,7},{7,6},{8,9},{9,8},{10,11... | collective-permute-start | bytes 294920 | tf_op jit(solution)/shard_map/ppermute | solution.py:536
  32.1 9.9 %collective-permute-start.10 = (bf16[32,1536]{1,0:T(8,128)(2,1)S(1)}, bf16[32,1536]{1,0:T(8,128)(2,1)S(1)}, u32[]{:S(2)}, u32[]{:S(2)}) collective-permute-start(bf16[32,1536]{1,0:T(8,128)(2,1)S(1)} %join.1.refs_0_.refs_4_), channel_id=1, source_target_pairs={{0,2},{1,3},{2,0},{3,1},{4,6},{5,7},{6,4},{7,5},{8,10},{9,11},{10,... | collective-permute-start | bytes 294920 | tf_op jit(solution)/shard_map/ppermute | solution.py:536
  34.6 8.9 %collective-permute-start.11 = (bf16[32,1536]{1,0:T(8,128)(2,1)S(1)}, bf16[32,1536]{1,0:T(8,128)(2,1)S(1)}, u32[]{:S(2)}, u32[]{:S(2)}) collective-permute-start(bf16[32,1536]{1,0:T(8,128)(2,1)S(1)} %join.1.refs_0_.refs_4_), channel_id=1, source_target_pairs={{0,3},{1,2},{2,1},{3,0},{4,7},{5,6},{6,5},{7,4},{8,11},{9,10},{10,... | collective-permute-start | bytes 294920 | tf_op jit(solution)/shard_map/ppermute | solution.py:536
  35.9 8.1 %collective-permute-start.16 = (bf16[32,1536]{1,0:T(8,128)(2,1)S(1)}, bf16[32,1536]{1,0:T(8,128)(2,1)S(1)}, u32[]{:S(2)}, u32[]{:S(2)}) collective-permute-start(bf16[32,1536]{1,0:T(8,128)(2,1)S(1)} %join.1.refs_0_.refs_4_), channel_id=1, source_target_pairs={{0,8},{4,12},{8,0},{12,4},{1,9},{5,13},{9,1},{13,5},{2,10},{6,14},... | collective-permute-start | bytes 294920 | tf_op jit(solution)/shard_map/ppermute | solution.py:536
  37.4 6.6 %collective-permute-start.12 = (bf16[32,1536]{1,0:T(8,128)(2,1)S(1)}, bf16[32,1536]{1,0:T(8,128)(2,1)S(1)}, u32[]{:S(2)}, u32[]{:S(2)}) collective-permute-start(bf16[32,1536]{1,0:T(8,128)(2,1)S(1)} %join.1.refs_0_.refs_4_), channel_id=1, source_target_pairs={{0,4},{4,0},{8,12},{12,8},{1,5},{5,1},{9,13},{13,9},{2,6},{6,2},{1... | collective-permute-start | bytes 294920 | tf_op jit(solution)/shard_map/ppermute | solution.py:536
  37.4 7.1 %collective-permute-start.17 = (bf16[32,1536]{1,0:T(8,128)(2,1)S(1)}, bf16[32,1536]{1,0:T(8,128)(2,1)S(1)}, u32[]{:S(2)}, u32[]{:S(2)}) collective-permute-start(bf16[32,1536]{1,0:T(8,128)(2,1)S(1)} %collective-permute-done.9.refs_1_.refs_5_), channel_id=1, source_target_pairs={{0,8},{4,12},{8,0},{12,4},{1,9},{5,13},{9,1},{13,5},{2,10},{6,14},... | collective-permute-start | bytes 294920 | tf_op jit(solution)/shard_map/ppermute | solution.py:536
  42.0 4.6 %collective-permute-start.18 = (bf16[32,1536]{1,0:T(8,128)(2,1)S(1)}, bf16[32,1536]{1,0:T(8,128)(2,1)S(1)}, u32[]{:S(2)}, u32[]{:S(2)}) collective-permute-start(bf16[32,1536]{1,0:T(8,128)(2,1)S(1)} %collective-permute-done.10.refs_2_.refs_6_), channel_id=1, source_target_pairs={{0,8},{4,12},{8,0},{12,4},{1,9},{5,13},{9,1},{13,5},{2,10},{6,14},... | collective-permute-start | bytes 294920 | tf_op jit(solution)/shard_map/ppermute | solution.py:536
  43.4 4.6 %collective-permute-start.19 = (bf16[32,1536]{1,0:T(8,128)(2,1)S(1)}, bf16[32,1536]{1,0:T(8,128)(2,1)S(1)}, u32[]{:S(2)}, u32[]{:S(2)}) collective-permute-start(bf16[32,1536]{1,0:T(8,128)(2,1)S(1)} %collective-permute-done.11.refs_3_.refs_7_), channel_id=1, source_target_pairs={{0,8},{4,12},{8,0},{12,4},{1,9},{5,13},{9,1},{13,5},{2,10},{6,14},... | collective-permute-start | bytes 294920 | tf_op jit(solution)/shard_map/ppermute | solution.py:536
  44.0 4.1 %collective-permute-start.13 = (bf16[32,1536]{1,0:T(8,128)(2,1)S(1)}, bf16[32,1536]{1,0:T(8,128)(2,1)S(1)}, u32[]{:S(2)}, u32[]{:S(2)}) collective-permute-start(bf16[32,1536]{1,0:T(8,128)(2,1)S(1)} %collective-permute-done.9.refs_1_.refs_5_), channel_id=1, source_target_pairs={{0,4},{4,0},{8,12},{12,8},{1,5},{5,1},{9,13},{13,9},{2,6},{6,2},{1... | collective-permute-start | bytes 294920 | tf_op jit(solution)/shard_map/ppermute | solution.py:536
  44.0 4.6 %collective-permute-start.14 = (bf16[32,1536]{1,0:T(8,128)(2,1)S(1)}, bf16[32,1536]{1,0:T(8,128)(2,1)S(1)}, u32[]{:S(2)}, u32[]{:S(2)}) collective-permute-start(bf16[32,1536]{1,0:T(8,128)(2,1)S(1)} %collective-permute-done.10.refs_2_.refs_6_), channel_id=1, source_target_pairs={{0,4},{4,0},{8,12},{12,8},{1,5},{5,1},{9,13},{13,9},{2,6},{6,2},{1... | collective-permute-start | bytes 294920 | tf_op jit(solution)/shard_map/ppermute | solution.py:536
  44.5 4.1 %collective-permute-start.15 = (bf16[32,1536]{1,0:T(8,128)(2,1)S(1)}, bf16[32,1536]{1,0:T(8,128)(2,1)S(1)}, u32[]{:S(2)}, u32[]{:S(2)}) collective-permute-start(bf16[32,1536]{1,0:T(8,128)(2,1)S(1)} %collective-permute-done.11.refs_3_.refs_7_), channel_id=1, source_target_pairs={{0,4},{4,0},{8,12},{12,8},{1,5},{5,1},{9,13},{13,9},{2,6},{6,2},{1... | collective-permute-start | bytes 294920 | tf_op jit(solution)/shard_map/ppermute | solution.py:536
  46.6 2.1 %collective-permute-start.20 = (bf16[32,1536]{1,0:T(8,128)(2,1)S(1)}, bf16[32,1536]{1,0:T(8,128)(2,1)S(1)}, u32[]{:S(2)}, u32[]{:S(2)}) collective-permute-start(bf16[32,1536]{1,0:T(8,128)(2,1)S(1)} %collective-permute-done.16.refs_8_.refs_12_), channel_id=1, source_target_pairs={{0,4},{4,0},{8,12},{12,8},{1,5},{5,1},{9,13},{13,9},{2,6},{6,2},{1... | collective-permute-start | bytes 294920 | tf_op jit(solution)/shard_map/ppermute | solution.py:536
  48.0 1.3 %collective-permute-start.21 = (bf16[32,1536]{1,0:T(8,128)(2,1)S(1)}, bf16[32,1536]{1,0:T(8,128)(2,1)S(1)}, u32[]{:S(2)}, u32[]{:S(2)}) collective-permute-start(bf16[32,1536]{1,0:T(8,128)(2,1)S(1)} %collective-permute-done.17.refs_9_.refs_13_), channel_id=1, source_target_pairs={{0,4},{4,0},{8,12},{12,8},{1,5},{5,1},{9,13},{13,9},{2,6},{6,2},{1... | collective-permute-start | bytes 294920 | tf_op jit(solution)/shard_map/ppermute | solution.py:536
  48.1 1.5 %collective-permute-start.22 = (bf16[32,1536]{1,0:T(8,128)(2,1)S(1)}, bf16[32,1536]{1,0:T(8,128)(2,1)S(1)}, u32[]{:S(2)}, u32[]{:S(2)}) collective-permute-start(bf16[32,1536]{1,0:T(8,128)(2,1)S(1)} %collective-permute-done.18.refs_10_.refs_14_), channel_id=1, source_target_pairs={{0,4},{4,0},{8,12},{12,8},{1,5},{5,1},{9,13},{13,9},{2,6},{6,2},{1... | collective-permute-start | bytes 294920 | tf_op jit(solution)/shard_map/ppermute | solution.py:536
  48.6 1.3 %collective-permute-start.23 = (bf16[32,1536]{1,0:T(8,128)(2,1)S(1)}, bf16[32,1536]{1,0:T(8,128)(2,1)S(1)}, u32[]{:S(2)}, u32[]{:S(2)}) collective-permute-start(bf16[32,1536]{1,0:T(8,128)(2,1)S(1)} %collective-permute-done.19.refs_11_.refs_15_), channel_id=1, source_target_pairs={{0,4},{4,0},{8,12},{12,8},{1,5},{5,1},{9,13},{13,9},{2,6},{6,2},{1... | collective-permute-start | bytes 294920 | tf_op jit(solution)/shard_map/ppermute | solution.py:536
  51.7 2.8 %copy-start.8 = (s32[4,1,2]{0,2,1:T(2,128)S(1)}, s32[4,1,2]{0,2,1:T(2,128)}, u32[]{:S(2)}) copy-start(s32[4,1,2]{0,2,1:T(2,128)} %param.29) | copy-start | bytes 100
  51.8 3.0 %copy-start.6 = (s32[4,1,2,32]{3,2,1,0:T(2,128)S(1)}, s32[4,1,2,32]{3,2,1,0:T(2,128)}, u32[]{:S(2)}) copy-start(s32[4,1,2,32]{3,2,1,0:T(2,128)} %lists_ref.1) | copy-start | bytes 3076
  51.8 1.6 %collective-permute-start.24 = (bf16[128,1024]{1,0:T(8,128)(2,1)S(1)}, bf16[128,1024]{1,0:T(8,128)(2,1)S(1)}, u32[]{:S(2)}, u32[]{:S(2)}) collective-permute-start(bf16[128,1024]{1,0:T(8,128)(2,1)S(1)} %get-tuple-element.47), channel_id=1, source_target_pairs={{0,4},{4,0},{8,12},{12,8},{1,5},{5,1},{9,13},{13,9},{2,6},{6,2},{1... | collective-permute-start | bytes 786440 | tf_op jit(solution)/shard_map/ppermute | solution.py:536
  53.4 8.4 %collective-permute-start.25 = (bf16[128,1024]{1,0:T(8,128)(2,1)S(1)}, bf16[128,1024]{1,0:T(8,128)(2,1)S(1)}, u32[]{:S(2)}, u32[]{:S(2)}) collective-permute-start(bf16[128,1024]{1,0:T(8,128)(2,1)S(1)} %join_hot.1.after), channel_id=1, source_target_pairs={{0,8},{4,12},{8,0},{12,4},{1,9},{5,13},{9,1},{13,5},{2,10},{6,14},... | collective-permute-start | bytes 786440 | tf_op jit(solution)/shard_map/ppermute | solution.py:536
  54.7 1.9 %copy-start.3 = (bf16[2,6144,128]{2,1,0:T(8,128)(2,1)S(1)}, bf16[2,6144,128]{2,1,0:T(8,128)(2,1)}, u32[]{:S(2)}) copy-start(bf16[2,6144,128]{2,1,0:T(8,128)(2,1)} %up_ref.1) | copy-start | bytes 9437188
  56.6 1.9 %copy-start.4 = (bf16[2,128,6144]{2,1,0:T(8,128)(2,1)S(1)}, bf16[2,128,6144]{2,1,0:T(8,128)(2,1)}, u32[]{:S(2)}) copy-start(bf16[2,128,6144]{2,1,0:T(8,128)(2,1)} %down_ref.1) | copy-start | bytes 9437188
  61.9 2.5 %collective-permute-start.26 = (bf16[2,128,1536]{2,1,0:T(8,128)(2,1)}, bf16[2,128,1536]{2,1,0:T(8,128)(2,1)S(1)}, u32[]{:S(2)}, u32[]{:S(2)}) collective-permute-start(bf16[2,128,1536]{2,1,0:T(8,128)(2,1)} %get-tuple-element.56), channel_id=1, source_target_pairs={{0,4},{4,0},{8,12},{12,8},{1,5},{5,1},{9,13},{13,9},{2,6},{6,2},{1... | collective-permute-start | bytes 2359304 | tf_op jit(solution)/shard_map/ppermute | solution.py:536
  62.1 4.6 %collective-permute-start.27 = (bf16[128,1024]{1,0:T(8,128)(2,1)S(1)}, bf16[128,1024]{1,0:T(8,128)(2,1)S(1)}, u32[]{:S(2)}, u32[]{:S(2)}) collective-permute-start(bf16[128,1024]{1,0:T(8,128)(2,1)S(1)} %maximum_convert_fusion.hidden_ref), channel_id=1, source_target_pairs={{0,4},{4,0},{8,12},{12,8},{1,5},{5,1},{9,13},{13,9},{2,6},{6,2},{1... | collective-permute-start | bytes 786440 | tf_op jit(solution)/shard_map/ppermute | solution.py:536
  64.5 7.8 %collective-permute-start.28 = (bf16[64,1536]{1,0:T(8,128)(2,1)S(1)}, bf16[64,1536]{1,0:T(8,128)(2,1)S(1)}, u32[]{:S(2)}, u32[]{:S(2)}) collective-permute-start(bf16[64,1536]{1,0:T(8,128)(2,1)S(1)} %get-tuple-element.59), channel_id=1, source_target_pairs={{0,8},{4,12},{8,0},{12,4},{1,9},{5,13},{9,1},{13,5},{2,10},{6,14},... | collective-permute-start | bytes 589832 | tf_op jit(solution)/shard_map/ppermute | solution.py:536
  65.6 10.1 %collective-permute-start.29 = (bf16[64,1536]{1,0:T(8,128)(2,1)S(1)}, bf16[64,1536]{1,0:T(8,128)(2,1)S(1)}, u32[]{:S(2)}, u32[]{:S(2)}) collective-permute-start(bf16[64,1536]{1,0:T(8,128)(2,1)S(1)} %get-tuple-element.62), channel_id=1, source_target_pairs={{0,8},{4,12},{8,0},{12,4},{1,9},{5,13},{9,1},{13,5},{2,10},{6,14},... | collective-permute-start | bytes 589832 | tf_op jit(solution)/shard_map/ppermute | solution.py:536
  66.6 2.8 %copy-start.1 = (bf16[16,128,1536]{2,1,0:T(8,128)(2,1)S(1)}, bf16[16,128,1536]{2,1,0:T(8,128)(2,1)}, u32[]{:S(2)}) copy-start(bf16[16,128,1536]{2,1,0:T(8,128)(2,1)} %hot_ref.1) | copy-start | bytes 18874372
  72.3 10.5 %collective-permute-start.30 = (bf16[32,1536]{1,0:T(8,128)(2,1)S(1)}, bf16[32,1536]{1,0:T(8,128)(2,1)S(1)}, u32[]{:S(2)}, u32[]{:S(2)}) collective-permute-start(bf16[32,1536]{1,0:T(8,128)(2,1)S(1)} %get-tuple-element.61), channel_id=1, source_target_pairs={{0,3},{1,2},{2,1},{3,0},{4,7},{5,6},{6,5},{7,4},{8,11},{9,10},{10,... | collective-permute-start | bytes 294920 | tf_op jit(solution)/shard_map/ppermute | solution.py:536
  74.7 8.1 %collective-permute-start.31 = (bf16[32,1536]{1,0:T(8,128)(2,1)S(1)}, bf16[32,1536]{1,0:T(8,128)(2,1)S(1)}, u32[]{:S(2)}, u32[]{:S(2)}) collective-permute-start(bf16[32,1536]{1,0:T(8,128)(2,1)S(1)} %get-tuple-element.60), channel_id=1, source_target_pairs={{0,2},{1,3},{2,0},{3,1},{4,6},{5,7},{6,4},{7,5},{8,10},{9,11},{10,... | collective-permute-start | bytes 294920 | tf_op jit(solution)/shard_map/ppermute | solution.py:536
  75.8 7.1 %collective-permute-start.32 = (bf16[32,1536]{1,0:T(8,128)(2,1)S(1)}, bf16[32,1536]{1,0:T(8,128)(2,1)S(1)}, u32[]{:S(2)}, u32[]{:S(2)}) collective-permute-start(bf16[32,1536]{1,0:T(8,128)(2,1)S(1)} %get-tuple-element.65), channel_id=1, source_target_pairs={{0,1},{1,0},{2,3},{3,2},{4,5},{5,4},{6,7},{7,6},{8,9},{9,8},{10,11... | collective-permute-start | bytes 294920 | tf_op jit(solution)/shard_map/ppermute | solution.py:536

commit v6 on v5

--- a/solution.py
+++ b/solution.py
@@ -119,7 +119,7 @@
 SMEM = pl.BlockSpec(memory_space=pltpu.SMEM)
 AWAY = pl.BlockSpec(memory_space=pl.ANY)
 DMA = pltpu.SemaphoreType.DMA
-COSTS = {"join": 60, "attention": 20, "norm_up_send": 20, "up_keep": 20, "cold_send": 30, "cold_keep": 0, "down": 0}
+COSTS = {"hold": 60, "join": 60, "attention": 20, "norm_up_send": 20, "up_keep": 20, "cold_send": 30, "cold_keep": 0, "down": 0}
 LIMITS = {"attention": 123, "load_project": 100, "load_up": 88, "load_cold": 72, "load_down": 84}
 
 
@@ -565,7 +565,7 @@
 
     attended = attention(queries, key_cache, value_cache, key_new, value_new, lengths)
     across = swap(attended, "blocks", 2)
-    gathered = [attended, swap(attended, "blocks", 1), across, swap(across, "blocks", 1)]
+    gathered = [join("hold", [attended]), swap(attended, "blocks", 1), across, swap(across, "blocks", 1)]
     gain = norm_gain[None]
     gains = [gain] + [swap(gain, "blocks", k) for k in range(1, blocks)]
     gathered, gains = lax.optimization_barrier((gathered, gains))

time: 83.9 us -> 83.2 us (level)
  waiting for transfers between devices: 25.1 us -> 24.2 us
    ppermute x33, waiting for transfers between devices: 25.1 us -> 24.2 us  [swap(): return lax.ppermute(x, axis, [(i, i ^ m) for i in range(size)])]
    pallas_call x11 -> x12, Pallas kernels: 18.3 us -> 18.3 us  [call(): pl.pallas_call(kernel, in_specs=specs, out_specs=jax.tree.map(lambda _: V...]
  transfers between devices with their start and end apart: 33 -> 33, of which waited for: 17 -> 16; matrix products, arithmetic and copies ran while one was open for 2% -> 2% of each run, Pallas kernels for 11% -> 11%
where the time goes in v6:
time: 83.2 us; the launch traced here: 82.9 us
  starting transfers between devices  27.5 us (33%)
  waiting for transfers between devices  24.2 us (29%)
  Pallas kernels  18.3 us (22%)
  local copies, waits for them, and re-layouts  10.1 us (12%)
  other arithmetic  1.79 us (2%)
  between operations  0.86 us (1%)
    ppermute x33, starting transfers between devices, swap(): return lax.ppermute(x, axis, [(i, i ^ m) for i in range(size)])  27.5 us
    ppermute x33, waiting for transfers between devices, swap(): return lax.ppermute(x, axis, [(i, i ^ m) for i in range(size)])  24.2 us
    pallas_call x12, Pallas kernels, call(): pl.pallas_call(kernel, in_specs=specs, out_specs=jax.tree.map(lambda _: V...  18.3 us
    unnamed x19, local copies, waits for them, and re-layouts  9.91 us
  transfers between devices with their start and end apart: 33, of which 16 were waited for; matrix products, arithmetic and copies ran while one was open for 2% of the time, Pallas kernels for 11%

profile of v6, /device:TPU:0, one launch (start us, length us, event | category | flops | bytes accessed | tf_op | source)
XLA Modules:
  0.0 82.9 jit_solution(9387958359707407809)
XLA Ops:
  0.6 0.0 copy-start
  0.7 6.2 %attention.1.refs_0_ = bf16[32,1536]{1,0:T(8,128)(2,1)} custom-call(s32[8]{0:T(128)} %lengths.1, bf16[32,1536]{1,0:T(8,128)(2,1)} %bitcast.41, bf16[32,1536]{1,0:T(8,128)(2,1)} %bitcast.42, bf16[32,1536]{1,0:T(8,128)(2,1)} %bitcast.43, bf16[1024,1536]{1,0:T(8,128)(2,1)} %bitcast.39, bf16[1024,1536]{1,0:T(8,128)(2,1)} %bitcast.40), custom_call_target="tpu_custom_call" | custom-call | bytes 20000000 | tf_op jit(solution)/shard_map/attention/pallas_call | solution.py:127
  6.9 3.0 %collective-permute-start.1 = (bf16[32,1536]{1,0:T(8,128)(2,1)}, bf16[32,1536]{1,0:T(8,128)(2,1)S(1)}, u32[]{:S(2)}, u32[]{:S(2)}) collective-permute-start(bf16[32,1536]{1,0:T(8,128)(2,1)} %attention.1.refs_0_), channel_id=1, source_target_pairs={{0,8},{4,12},{8,0},{12,4},{1,9},{5,13},{9,1},{13,5},{2,10},{6,14},... | collective-permute-start | bytes 294920 | tf_op jit(solution)/shard_map/ppermute | solution.py:536
  9.9 0.1 collective-permute-start.3
  10.0 0.1 collective-permute-start.4
  10.1 1.8 %collective-permute-start.5 = (bf16[1,1536]{1,0:T(2,128)(2,1)S(1)}, bf16[1,1536]{1,0:T(2,128)(2,1)S(1)}, u32[]{:S(2)}, u32[]{:S(2)}) collective-permute-start(bf16[1,1536]{1,0:T(2,128)(2,1)S(1)} %broadcast_in_dim.3.gain_ref.refs_0_), channel_id=1, source_target_pairs={{0,12},{4,8},{8,4},{12,0},{1,13},{5,9},{9,5},{13,1},{2,14},{6,10},... | collective-permute-start | bytes 9224 | tf_op jit(solution)/shard_map/ppermute | solution.py:536
  11.9 0.3 collective-permute-start
  12.2 0.7 collective-permute-done.1.refs_2_
  12.9 0.1 pad_add_fusion.place
  13.0 0.9 %copy-done.5 = bf16[32,1536]{1,0:T(8,128)(2,1)S(1)} copy-done((bf16[32,1536]{1,0:T(8,128)(2,1)S(1)}, bf16[32,1536]{1,0:T(8,128)(2,1)}, u32[]{:S(2)}) %copy-start.5) | copy-done | bytes 98328
  13.9 0.3 collective-permute-done.2.refs_3_
  14.2 2.3 %copy-done.2 = bf16[1536,1536]{1,0:T(8,128)(2,1)S(1)} copy-done((bf16[1536,1536]{1,0:T(8,128)(2,1)S(1)}, bf16[1536,1536]{1,0:T(8,128)(2,1)}, u32[]{:S(2)}) %copy-start.2) | copy-done | bytes 4718616
  16.6 1.3 %project.1 = (f32[32,1536]{1,0:T(8,128)S(1)}, bf16[32,1536]{1,0:T(8,128)(2,1)S(1)}, bf16[32,1536]{1,0:T(8,128)(2,1)S(1)}, bf16[32,1536]{1,0:T(8,128)(2,1)S(1)}) custom-call(s32[3]{0:T(128)S(1)} %pad_add_fusion.place, bf16[32,1536]{1,0:T(8,128)(2,1)S(1)} %hold.1.refs_0_, bf16[32,1536]{1,0:T(8,128)(2,1)S(1)} %collective-permute-done.refs_1_, ...), custom_call_target="tpu_custom_call" | custom-call | bytes 10000000 | tf_op jit(solution)/shard_map/project/pallas_call | solution.py:127
  17.9 4.0 %collective-permute-start.6 = (bf16[32,1536]{1,0:T(8,128)(2,1)S(1)}, bf16[32,1536]{1,0:T(8,128)(2,1)S(1)}, u32[]{:S(2)}, u32[]{:S(2)}) collective-permute-start(bf16[32,1536]{1,0:T(8,128)(2,1)S(1)} %get-tuple-element.39), channel_id=1, source_target_pairs={{0,3},{1,2},{2,1},{3,0},{4,7},{5,6},{6,5},{7,4},{8,11},{9,10},{10,... | collective-permute-start | bytes 294920 | tf_op jit(solution)/shard_map/ppermute | solution.py:536
  21.9 0.6 collective-permute-start.8
  22.6 2.8 %load_up.1.hot_ref = bf16[16,1536,128]{2,1,0:T(8,128)(2,1)S(1)} custom-call(bf16[32,1536]{1,0:T(8,128)(2,1)S(1)} %get-tuple-element.41.after, bf16[16,1536,128]{2,1,0:T(8,128)(2,1)} %refs_0_.1), custom_call_target="tpu_custom_call" | custom-call | bytes 10000000 | tf_op jit(solution)/shard_map/load_up/pallas_call | solution.py:127
  25.4 0.2 collective-permute-done.6.refs_2_
  25.6 5.0 %collective-permute-done.7.refs_3_ = bf16[32,1536]{1,0:T(8,128)(2,1)S(1)} collective-permute-done((bf16[32,1536]{1,0:T(8,128)(2,1)S(1)}, bf16[32,1536]{1,0:T(8,128)(2,1)S(1)}, u32[]{:S(2)}, u32[]{:S(2)}) %collective-permute-start.7) | collective-permute-done | bytes 98336 | tf_op jit(solution)/shard_map/ppermute | solution.py:536
  30.6 0.1 join.1.refs_0_.refs_4_
  30.7 0.6 collective-permute-start.9
  31.2 2.5 %collective-permute-start.10 = (bf16[32,1536]{1,0:T(8,128)(2,1)S(1)}, bf16[32,1536]{1,0:T(8,128)(2,1)S(1)}, u32[]{:S(2)}, u32[]{:S(2)}) collective-permute-start(bf16[32,1536]{1,0:T(8,128)(2,1)S(1)} %join.1.refs_0_.refs_4_), channel_id=1, source_target_pairs={{0,2},{1,3},{2,0},{3,1},{4,6},{5,7},{6,4},{7,5},{8,10},{9,11},{10,... | collective-permute-start | bytes 294920 | tf_op jit(solution)/shard_map/ppermute | solution.py:536
  33.8 1.3 %collective-permute-start.11 = (bf16[32,1536]{1,0:T(8,128)(2,1)S(1)}, bf16[32,1536]{1,0:T(8,128)(2,1)S(1)}, u32[]{:S(2)}, u32[]{:S(2)}) collective-permute-start(bf16[32,1536]{1,0:T(8,128)(2,1)S(1)} %join.1.refs_0_.refs_4_), channel_id=1, source_target_pairs={{0,3},{1,2},{2,1},{3,0},{4,7},{5,6},{6,5},{7,4},{8,11},{9,10},{10,... | collective-permute-start | bytes 294920 | tf_op jit(solution)/shard_map/ppermute | solution.py:536
  35.1 1.5 %collective-permute-start.16 = (bf16[32,1536]{1,0:T(8,128)(2,1)S(1)}, bf16[32,1536]{1,0:T(8,128)(2,1)S(1)}, u32[]{:S(2)}, u32[]{:S(2)}) collective-permute-start(bf16[32,1536]{1,0:T(8,128)(2,1)S(1)} %join.1.refs_0_.refs_4_), channel_id=1, source_target_pairs={{0,8},{4,12},{8,0},{12,4},{1,9},{5,13},{9,1},{13,5},{2,10},{6,14},... | collective-permute-start | bytes 294920 | tf_op jit(solution)/shard_map/ppermute | solution.py:536
  36.6 0.9 %collective-permute-start.17 = (bf16[32,1536]{1,0:T(8,128)(2,1)S(1)}, bf16[32,1536]{1,0:T(8,128)(2,1)S(1)}, u32[]{:S(2)}, u32[]{:S(2)}) collective-permute-start(bf16[32,1536]{1,0:T(8,128)(2,1)S(1)} %collective-permute-done.9.refs_1_.refs_5_), channel_id=1, source_target_pairs={{0,8},{4,12},{8,0},{12,4},{1,9},{5,13},{9,1},{13,5},{2,10},{6,14},... | collective-permute-start | bytes 294920 | tf_op jit(solution)/shard_map/ppermute | solution.py:536
  37.5 3.8 %collective-permute-done.10.refs_2_.refs_6_ = bf16[32,1536]{1,0:T(8,128)(2,1)S(1)} collective-permute-done((bf16[32,1536]{1,0:T(8,128)(2,1)S(1)}, bf16[32,1536]{1,0:T(8,128)(2,1)S(1)}, u32[]{:S(2)}, u32[]{:S(2)}) %collective-permute-start.10) | collective-permute-done | bytes 98336 | tf_op jit(solution)/shard_map/ppermute | solution.py:536
  41.3 1.5 %collective-permute-start.18 = (bf16[32,1536]{1,0:T(8,128)(2,1)S(1)}, bf16[32,1536]{1,0:T(8,128)(2,1)S(1)}, u32[]{:S(2)}, u32[]{:S(2)}) collective-permute-start(bf16[32,1536]{1,0:T(8,128)(2,1)S(1)} %collective-permute-done.10.refs_2_.refs_6_), channel_id=1, source_target_pairs={{0,8},{4,12},{8,0},{12,4},{1,9},{5,13},{9,1},{13,5},{2,10},{6,14},... | collective-permute-start | bytes 294920 | tf_op jit(solution)/shard_map/ppermute | solution.py:536
  42.7 0.6 collective-permute-start.19
  43.3 0.5 collective-permute-start.14
  43.8 0.1 collective-permute-start.15
  43.9 2.0 %collective-permute-done.18.refs_10_.refs_14_ = bf16[32,1536]{1,0:T(8,128)(2,1)S(1)} collective-permute-done((bf16[32,1536]{1,0:T(8,128)(2,1)S(1)}, bf16[32,1536]{1,0:T(8,128)(2,1)S(1)}, u32[]{:S(2)}, u32[]{:S(2)}) %collective-permute-start.18) | collective-permute-done | bytes 98336 | tf_op jit(solution)/shard_map/ppermute | solution.py:536
  45.9 1.5 %collective-permute-done.19.refs_11_.refs_15_ = bf16[32,1536]{1,0:T(8,128)(2,1)S(1)} collective-permute-done((bf16[32,1536]{1,0:T(8,128)(2,1)S(1)}, bf16[32,1536]{1,0:T(8,128)(2,1)S(1)}, u32[]{:S(2)}, u32[]{:S(2)}) %collective-permute-start.19) | collective-permute-done | bytes 98336 | tf_op jit(solution)/shard_map/ppermute | solution.py:536
  47.3 0.5 collective-permute-start.22
  47.9 0.1 collective-permute-start.23
  47.9 0.7 collective-permute-done.21.refs_13_.refs_17_
  48.6 0.2 collective-permute-done.22.refs_14_.refs_18_
  48.8 0.4 collective-permute-done.23.refs_15_.refs_19_
  49.2 1.9 %norm_up_send.1 = (bf16[128,1024]{1,0:T(8,128)(2,1)S(1)}, bf16[128,1536]{1,0:T(8,128)(2,1)S(1)}, f32[2,128,128]{2,1,0:T(8,128)S(1)}) custom-call(s32[3]{0:T(128)S(1)} %pad_add_fusion.place, bf16[1,1536]{1,0:T(2,128)(2,1)S(1)} %broadcast_in_dim.3.gain_ref.refs_0_, bf16[16,1536,128]{2,1,0:T(8,128)(2,1)S(1)} %load_up.1.hot_ref, ...), custom_call_target="tpu_custom_call" | custom-call | bytes 20000000 | tf_op jit(solution)/shard_map/norm_up_send/pallas_call | solution.py:127
  51.1 0.2 collective-permute-start.24
  51.3 1.1 %up_keep.1.refs_0_ = bf16[128,1024]{1,0:T(8,128)(2,1)S(1)} custom-call(s32[3]{0:T(128)S(1)} %pad_add_fusion.place, bf16[128,1536]{1,0:T(8,128)(2,1)S(1)} %get-tuple-element.46.rows_ref, bf16[16,1536,128]{2,1,0:T(8,128)(2,1)S(1)} %load_up.1.hot_ref), custom_call_target="tpu_custom_call" | custom-call | bytes 20000000 | tf_op jit(solution)/shard_map/up_keep/pallas_call | solution.py:127
  52.4 0.3 collective-permute-done.24.refs_1_
  52.7 0.1 join_hot.1.after
  52.7 1.1 %collective-permute-start.25 = (bf16[128,1024]{1,0:T(8,128)(2,1)S(1)}, bf16[128,1024]{1,0:T(8,128)(2,1)S(1)}, u32[]{:S(2)}, u32[]{:S(2)}) collective-permute-start(bf16[128,1024]{1,0:T(8,128)(2,1)S(1)} %join_hot.1.after), channel_id=1, source_target_pairs={{0,8},{4,12},{8,0},{12,4},{1,9},{5,13},{9,1},{13,5},{2,10},{6,14},... | collective-permute-start | bytes 786440 | tf_op jit(solution)/shard_map/ppermute | solution.py:536
  53.8 0.1 copy.18
  53.9 0.1 reshape.49.counts
  54.0 1.9 %copy-done.3 = bf16[2,6144,128]{2,1,0:T(8,128)(2,1)S(1)} copy-done((bf16[2,6144,128]{2,1,0:T(8,128)(2,1)S(1)}, bf16[2,6144,128]{2,1,0:T(8,128)(2,1)}, u32[]{:S(2)}) %copy-start.3) | copy-done | bytes 3145752
  55.9 1.9 %copy-done.4 = bf16[2,128,6144]{2,1,0:T(8,128)(2,1)S(1)} copy-done((bf16[2,128,6144]{2,1,0:T(8,128)(2,1)S(1)}, bf16[2,128,6144]{2,1,0:T(8,128)(2,1)}, u32[]{:S(2)}) %copy-start.4) | copy-done | bytes 3145752
  57.8 3.2 %cold_send.1 = (bf16[128,1536]{1,0:T(8,128)(2,1)S(1)}, bf16[2,128,1536]{2,1,0:T(8,128)(2,1)}, bf16[128,1536]{1,0:T(8,128)(2,1)S(1)}) custom-call(s32[3]{0:T(128)S(1)} %pad_add_fusion.place, s32[8]{0:T(128)S(1)} %reshape.49.counts, s32[4,1,2,32]{3,2,1,0:T(2,128)S(1)} %copy-done.6, f32[2,128,128]{2,1,0:T(8,128)S(1)} %get-tuple-element.48.stat_ref, ...), custom_call_target="tpu_custom_call" | custom-call | bytes 30000000 | tf_op jit(solution)/shard_map/cold_send/pallas_call | solution.py:127
  61.0 0.2 collective-permute-done.25
  61.2 0.1 pad_maximum_fusion
  61.3 0.1 maximum_convert_fusion.hidden_ref
  61.4 0.6 collective-permute-start.27
  61.9 1.7 %collective-permute-done.26 = bf16[2,128,1536]{2,1,0:T(8,128)(2,1)S(1)} collective-permute-done((bf16[2,128,1536]{2,1,0:T(8,128)(2,1)}, bf16[2,128,1536]{2,1,0:T(8,128)(2,1)S(1)}, u32[]{:S(2)}, u32[]{:S(2)}) %collective-permute-start.26) | collective-permute-done | bytes 786464 | tf_op jit(solution)/shard_map/ppermute | solution.py:536
  63.7 0.1 fusion
  63.8 1.1 %collective-permute-start.28 = (bf16[64,1536]{1,0:T(8,128)(2,1)S(1)}, bf16[64,1536]{1,0:T(8,128)(2,1)S(1)}, u32[]{:S(2)}, u32[]{:S(2)}) collective-permute-start(bf16[64,1536]{1,0:T(8,128)(2,1)S(1)} %get-tuple-element.59), channel_id=1, source_target_pairs={{0,8},{4,12},{8,0},{12,4},{1,9},{5,13},{9,1},{13,5},{2,10},{6,14},... | collective-permute-start | bytes 589832 | tf_op jit(solution)/shard_map/ppermute | solution.py:536
  64.9 1.0 %collective-permute-start.29 = (bf16[64,1536]{1,0:T(8,128)(2,1)S(1)}, bf16[64,1536]{1,0:T(8,128)(2,1)S(1)}, u32[]{:S(2)}, u32[]{:S(2)}) collective-permute-start(bf16[64,1536]{1,0:T(8,128)(2,1)S(1)} %get-tuple-element.62), channel_id=1, source_target_pairs={{0,8},{4,12},{8,0},{12,4},{1,9},{5,13},{9,1},{13,5},{2,10},{6,14},... | collective-permute-start | bytes 589832 | tf_op jit(solution)/shard_map/ppermute | solution.py:536
  65.9 2.8 %copy-done.1 = bf16[16,128,1536]{2,1,0:T(8,128)(2,1)S(1)} copy-done((bf16[16,128,1536]{2,1,0:T(8,128)(2,1)S(1)}, bf16[16,128,1536]{2,1,0:T(8,128)(2,1)}, u32[]{:S(2)}) %copy-start.1) | copy-done | bytes 6291480
  68.7 1.6 %down.1.base_ref = f32[128,1536]{1,0:T(8,128)S(1)} custom-call(s32[3]{0:T(128)S(1)} %pad_add_fusion.place, bf16[128,1024]{1,0:T(8,128)(2,1)S(1)} %maximum_convert_fusion.hidden_ref, bf16[128,1024]{1,0:T(8,128)(2,1)S(1)} %collective-permute-done.27.partner_ref, bf16[16,128,1536]{2,1,0:T(8,128)(2,1)S(1)} %copy-done.1, ...), custom_call_target="tpu_custom_call" | custom-call | tf_op jit(solution)/shard_map/down/pallas_call | solution.py:127
  70.4 1.2 %collective-permute-done.28.more_ref = bf16[64,1536]{1,0:T(8,128)(2,1)S(1)} collective-permute-done((bf16[64,1536]{1,0:T(8,128)(2,1)S(1)}, bf16[64,1536]{1,0:T(8,128)(2,1)S(1)}, u32[]{:S(2)}, u32[]{:S(2)}) %collective-permute-start.28) | collective-permute-done | bytes 196640 | tf_op jit(solution)/shard_map/ppermute | solution.py:536
  71.6 2.4 %collective-permute-start.30 = (bf16[32,1536]{1,0:T(8,128)(2,1)S(1)}, bf16[32,1536]{1,0:T(8,128)(2,1)S(1)}, u32[]{:S(2)}, u32[]{:S(2)}) collective-permute-start(bf16[32,1536]{1,0:T(8,128)(2,1)S(1)} %get-tuple-element.61), channel_id=1, source_target_pairs={{0,3},{1,2},{2,1},{3,0},{4,7},{5,6},{6,5},{7,4},{8,11},{9,10},{10,... | collective-permute-start | bytes 294920 | tf_op jit(solution)/shard_map/ppermute | solution.py:536
  74.0 1.0 %collective-permute-done.29.more_ref = bf16[64,1536]{1,0:T(8,128)(2,1)S(1)} collective-permute-done((bf16[64,1536]{1,0:T(8,128)(2,1)S(1)}, bf16[64,1536]{1,0:T(8,128)(2,1)S(1)}, u32[]{:S(2)}, u32[]{:S(2)}) %collective-permute-start.29) | collective-permute-done | bytes 196640 | tf_op jit(solution)/shard_map/ppermute | solution.py:536
  75.0 1.1 %collective-permute-start.32 = (bf16[32,1536]{1,0:T(8,128)(2,1)S(1)}, bf16[32,1536]{1,0:T(8,128)(2,1)S(1)}, u32[]{:S(2)}, u32[]{:S(2)}) collective-permute-start(bf16[32,1536]{1,0:T(8,128)(2,1)S(1)} %get-tuple-element.65), channel_id=1, source_target_pairs={{0,1},{1,0},{2,3},{3,2},{4,5},{5,4},{6,7},{7,6},{8,9},{9,8},{10,11... | collective-permute-start | bytes 294920 | tf_op jit(solution)/shard_map/ppermute | solution.py:536
  76.2 0.8 maximum_bitcast_fusion
  77.0 5.2 %collective-permute-done.32 = bf16[32,1536]{1,0:T(8,128)(2,1)S(1)} collective-permute-done((bf16[32,1536]{1,0:T(8,128)(2,1)S(1)}, bf16[32,1536]{1,0:T(8,128)(2,1)S(1)}, u32[]{:S(2)}, u32[]{:S(2)}) %collective-permute-start.32) | collective-permute-done | bytes 98336 | tf_op jit(solution)/shard_map/ppermute | solution.py:536
  82.2 0.7 fusion.1
  (45 shorter events, 0.3 us)
Async XLA Ops:
  0.6 21.9 %copy-start = (bf16[4,32,1536]{2,1,0:T(8,128)(2,1)S(1)}, bf16[4,32,1536]{2,1,0:T(8,128)(2,1)}, u32[]{:S(2)}) copy-start(bf16[4,32,1536]{2,1,0:T(8,128)(2,1)} %param.22) | copy-start | bytes 1179652
  0.6 9.3 %copy-start.7 = (bf16[1536]{0:T(1024)(128)(2,1)S(1)}, bf16[1536]{0:T(1024)(128)(2,1)}, u32[]{:S(2)}) copy-start(bf16[1536]{0:T(1024)(128)(2,1)} %param.23) | copy-start | bytes 9220
  6.9 6.0 %collective-permute-start.1 = (bf16[32,1536]{1,0:T(8,128)(2,1)}, bf16[32,1536]{1,0:T(8,128)(2,1)S(1)}, u32[]{:S(2)}, u32[]{:S(2)}) collective-permute-start(bf16[32,1536]{1,0:T(8,128)(2,1)} %attention.1.refs_0_), channel_id=1, source_target_pairs={{0,8},{4,12},{8,0},{12,4},{1,9},{5,13},{9,1},{13,5},{2,10},{6,14},... | collective-permute-start | bytes 294920 | tf_op jit(solution)/shard_map/ppermute | solution.py:536
  9.9 4.0 %collective-permute-start.3 = (bf16[1,1536]{1,0:T(2,128)(2,1)S(1)}, bf16[1,1536]{1,0:T(2,128)(2,1)S(1)}, u32[]{:S(2)}, u32[]{:S(2)}) collective-permute-start(bf16[1,1536]{1,0:T(2,128)(2,1)S(1)} %broadcast_in_dim.3.gain_ref.refs_0_), channel_id=1, source_target_pairs={{0,4},{4,0},{8,12},{12,8},{1,5},{5,1},{9,13},{13,9},{2,6},{6,2},{1... | collective-permute-start | bytes 9224 | tf_op jit(solution)/shard_map/ppermute | solution.py:536
  10.0 3.9 %collective-permute-start.4 = (bf16[1,1536]{1,0:T(2,128)(2,1)S(1)}, bf16[1,1536]{1,0:T(2,128)(2,1)S(1)}, u32[]{:S(2)}, u32[]{:S(2)}) collective-permute-start(bf16[1,1536]{1,0:T(2,128)(2,1)S(1)} %broadcast_in_dim.3.gain_ref.refs_0_), channel_id=1, source_target_pairs={{0,8},{4,12},{8,0},{12,4},{1,9},{5,13},{9,1},{13,5},{2,10},{6,14},... | collective-permute-start | bytes 9224 | tf_op jit(solution)/shard_map/ppermute | solution.py:536
  10.1 3.8 %collective-permute-start.5 = (bf16[1,1536]{1,0:T(2,128)(2,1)S(1)}, bf16[1,1536]{1,0:T(2,128)(2,1)S(1)}, u32[]{:S(2)}, u32[]{:S(2)}) collective-permute-start(bf16[1,1536]{1,0:T(2,128)(2,1)S(1)} %broadcast_in_dim.3.gain_ref.refs_0_), channel_id=1, source_target_pairs={{0,12},{4,8},{8,4},{12,0},{1,13},{5,9},{9,5},{13,1},{2,14},{6,10},... | collective-permute-start | bytes 9224 | tf_op jit(solution)/shard_map/ppermute | solution.py:536
  11.9 2.1 %collective-permute-start = (bf16[32,1536]{1,0:T(8,128)(2,1)}, bf16[32,1536]{1,0:T(8,128)(2,1)S(1)}, u32[]{:S(2)}, u32[]{:S(2)}) collective-permute-start(bf16[32,1536]{1,0:T(8,128)(2,1)} %attention.1.refs_0_), channel_id=1, source_target_pairs={{0,4},{4,0},{8,12},{12,8},{1,5},{5,1},{9,13},{13,9},{2,6},{6,2},{1... | collective-permute-start | bytes 294920 | tf_op jit(solution)/shard_map/ppermute | solution.py:536
  12.9 1.3 %collective-permute-start.2 = (bf16[32,1536]{1,0:T(8,128)(2,1)S(1)}, bf16[32,1536]{1,0:T(8,128)(2,1)S(1)}, u32[]{:S(2)}, u32[]{:S(2)}) collective-permute-start(bf16[32,1536]{1,0:T(8,128)(2,1)S(1)} %collective-permute-done.1.refs_2_), channel_id=1, source_target_pairs={{0,4},{4,0},{8,12},{12,8},{1,5},{5,1},{9,13},{13,9},{2,6},{6,2},{1... | collective-permute-start | bytes 294920 | tf_op jit(solution)/shard_map/ppermute | solution.py:536
  13.0 0.9 %copy-start.5 = (bf16[32,1536]{1,0:T(8,128)(2,1)S(1)}, bf16[32,1536]{1,0:T(8,128)(2,1)}, u32[]{:S(2)}) copy-start(bf16[32,1536]{1,0:T(8,128)(2,1)} %attention.1.refs_0_) | copy-start | bytes 294916
  14.2 2.3 %copy-start.2 = (bf16[1536,1536]{1,0:T(8,128)(2,1)S(1)}, bf16[1536,1536]{1,0:T(8,128)(2,1)}, u32[]{:S(2)}) copy-start(bf16[1536,1536]{1,0:T(8,128)(2,1)} %refs_4_.1) | copy-start | bytes 14155780
  17.9 7.7 %collective-permute-start.6 = (bf16[32,1536]{1,0:T(8,128)(2,1)S(1)}, bf16[32,1536]{1,0:T(8,128)(2,1)S(1)}, u32[]{:S(2)}, u32[]{:S(2)}) collective-permute-start(bf16[32,1536]{1,0:T(8,128)(2,1)S(1)} %get-tuple-element.39), channel_id=1, source_target_pairs={{0,3},{1,2},{2,1},{3,0},{4,7},{5,6},{6,5},{7,4},{8,11},{9,10},{10,... | collective-permute-start | bytes 294920 | tf_op jit(solution)/shard_map/ppermute | solution.py:536
  21.9 8.7 %collective-permute-start.7 = (bf16[32,1536]{1,0:T(8,128)(2,1)S(1)}, bf16[32,1536]{1,0:T(8,128)(2,1)S(1)}, u32[]{:S(2)}, u32[]{:S(2)}) collective-permute-start(bf16[32,1536]{1,0:T(8,128)(2,1)S(1)} %get-tuple-element.40), channel_id=1, source_target_pairs={{0,2},{1,3},{2,0},{3,1},{4,6},{5,7},{6,4},{7,5},{8,10},{9,11},{10,... | collective-permute-start | bytes 294920 | tf_op jit(solution)/shard_map/ppermute | solution.py:536
  21.9 8.7 %collective-permute-start.8 = (bf16[32,1536]{1,0:T(8,128)(2,1)S(1)}, bf16[32,1536]{1,0:T(8,128)(2,1)S(1)}, u32[]{:S(2)}, u32[]{:S(2)}) collective-permute-start(bf16[32,1536]{1,0:T(8,128)(2,1)S(1)} %get-tuple-element.41.after), channel_id=1, source_target_pairs={{0,1},{1,0},{2,3},{3,2},{4,5},{5,4},{6,7},{7,6},{8,9},{9,8},{10,11... | collective-permute-start | bytes 294920 | tf_op jit(solution)/shard_map/ppermute | solution.py:536
  30.7 5.9 %collective-permute-start.9 = (bf16[32,1536]{1,0:T(8,128)(2,1)S(1)}, bf16[32,1536]{1,0:T(8,128)(2,1)S(1)}, u32[]{:S(2)}, u32[]{:S(2)}) collective-permute-start(bf16[32,1536]{1,0:T(8,128)(2,1)S(1)} %join.1.refs_0_.refs_4_), channel_id=1, source_target_pairs={{0,1},{1,0},{2,3},{3,2},{4,5},{5,4},{6,7},{7,6},{8,9},{9,8},{10,11... | collective-permute-start | bytes 294920 | tf_op jit(solution)/shard_map/ppermute | solution.py:536
  31.2 10.0 %collective-permute-start.10 = (bf16[32,1536]{1,0:T(8,128)(2,1)S(1)}, bf16[32,1536]{1,0:T(8,128)(2,1)S(1)}, u32[]{:S(2)}, u32[]{:S(2)}) collective-permute-start(bf16[32,1536]{1,0:T(8,128)(2,1)S(1)} %join.1.refs_0_.refs_4_), channel_id=1, source_target_pairs={{0,2},{1,3},{2,0},{3,1},{4,6},{5,7},{6,4},{7,5},{8,10},{9,11},{10,... | collective-permute-start | bytes 294920 | tf_op jit(solution)/shard_map/ppermute | solution.py:536
  33.8 9.0 %collective-permute-start.11 = (bf16[32,1536]{1,0:T(8,128)(2,1)S(1)}, bf16[32,1536]{1,0:T(8,128)(2,1)S(1)}, u32[]{:S(2)}, u32[]{:S(2)}) collective-permute-start(bf16[32,1536]{1,0:T(8,128)(2,1)S(1)} %join.1.refs_0_.refs_4_), channel_id=1, source_target_pairs={{0,3},{1,2},{2,1},{3,0},{4,7},{5,6},{6,5},{7,4},{8,11},{9,10},{10,... | collective-permute-start | bytes 294920 | tf_op jit(solution)/shard_map/ppermute | solution.py:536
  35.1 8.2 %collective-permute-start.16 = (bf16[32,1536]{1,0:T(8,128)(2,1)S(1)}, bf16[32,1536]{1,0:T(8,128)(2,1)S(1)}, u32[]{:S(2)}, u32[]{:S(2)}) collective-permute-start(bf16[32,1536]{1,0:T(8,128)(2,1)S(1)} %join.1.refs_0_.refs_4_), channel_id=1, source_target_pairs={{0,8},{4,12},{8,0},{12,4},{1,9},{5,13},{9,1},{13,5},{2,10},{6,14},... | collective-permute-start | bytes 294920 | tf_op jit(solution)/shard_map/ppermute | solution.py:536
  36.6 6.7 %collective-permute-start.12 = (bf16[32,1536]{1,0:T(8,128)(2,1)S(1)}, bf16[32,1536]{1,0:T(8,128)(2,1)S(1)}, u32[]{:S(2)}, u32[]{:S(2)}) collective-permute-start(bf16[32,1536]{1,0:T(8,128)(2,1)S(1)} %join.1.refs_0_.refs_4_), channel_id=1, source_target_pairs={{0,4},{4,0},{8,12},{12,8},{1,5},{5,1},{9,13},{13,9},{2,6},{6,2},{1... | collective-permute-start | bytes 294920 | tf_op jit(solution)/shard_map/ppermute | solution.py:536
  36.6 7.2 %collective-permute-start.17 = (bf16[32,1536]{1,0:T(8,128)(2,1)S(1)}, bf16[32,1536]{1,0:T(8,128)(2,1)S(1)}, u32[]{:S(2)}, u32[]{:S(2)}) collective-permute-start(bf16[32,1536]{1,0:T(8,128)(2,1)S(1)} %collective-permute-done.9.refs_1_.refs_5_), channel_id=1, source_target_pairs={{0,8},{4,12},{8,0},{12,4},{1,9},{5,13},{9,1},{13,5},{2,10},{6,14},... | collective-permute-start | bytes 294920 | tf_op jit(solution)/shard_map/ppermute | solution.py:536
  41.3 4.6 %collective-permute-start.18 = (bf16[32,1536]{1,0:T(8,128)(2,1)S(1)}, bf16[32,1536]{1,0:T(8,128)(2,1)S(1)}, u32[]{:S(2)}, u32[]{:S(2)}) collective-permute-start(bf16[32,1536]{1,0:T(8,128)(2,1)S(1)} %collective-permute-done.10.refs_2_.refs_6_), channel_id=1, source_target_pairs={{0,8},{4,12},{8,0},{12,4},{1,9},{5,13},{9,1},{13,5},{2,10},{6,14},... | collective-permute-start | bytes 294920 | tf_op jit(solution)/shard_map/ppermute | solution.py:536
  42.7 4.6 %collective-permute-start.19 = (bf16[32,1536]{1,0:T(8,128)(2,1)S(1)}, bf16[32,1536]{1,0:T(8,128)(2,1)S(1)}, u32[]{:S(2)}, u32[]{:S(2)}) collective-permute-start(bf16[32,1536]{1,0:T(8,128)(2,1)S(1)} %collective-permute-done.11.refs_3_.refs_7_), channel_id=1, source_target_pairs={{0,8},{4,12},{8,0},{12,4},{1,9},{5,13},{9,1},{13,5},{2,10},{6,14},... | collective-permute-start | bytes 294920 | tf_op jit(solution)/shard_map/ppermute | solution.py:536
  43.3 4.1 %collective-permute-start.13 = (bf16[32,1536]{1,0:T(8,128)(2,1)S(1)}, bf16[32,1536]{1,0:T(8,128)(2,1)S(1)}, u32[]{:S(2)}, u32[]{:S(2)}) collective-permute-start(bf16[32,1536]{1,0:T(8,128)(2,1)S(1)} %collective-permute-done.9.refs_1_.refs_5_), channel_id=1, source_target_pairs={{0,4},{4,0},{8,12},{12,8},{1,5},{5,1},{9,13},{13,9},{2,6},{6,2},{1... | collective-permute-start | bytes 294920 | tf_op jit(solution)/shard_map/ppermute | solution.py:536
  43.3 4.6 %collective-permute-start.14 = (bf16[32,1536]{1,0:T(8,128)(2,1)S(1)}, bf16[32,1536]{1,0:T(8,128)(2,1)S(1)}, u32[]{:S(2)}, u32[]{:S(2)}) collective-permute-start(bf16[32,1536]{1,0:T(8,128)(2,1)S(1)} %collective-permute-done.10.refs_2_.refs_6_), channel_id=1, source_target_pairs={{0,4},{4,0},{8,12},{12,8},{1,5},{5,1},{9,13},{13,9},{2,6},{6,2},{1... | collective-permute-start | bytes 294920 | tf_op jit(solution)/shard_map/ppermute | solution.py:536
  43.8 4.1 %collective-permute-start.15 = (bf16[32,1536]{1,0:T(8,128)(2,1)S(1)}, bf16[32,1536]{1,0:T(8,128)(2,1)S(1)}, u32[]{:S(2)}, u32[]{:S(2)}) collective-permute-start(bf16[32,1536]{1,0:T(8,128)(2,1)S(1)} %collective-permute-done.11.refs_3_.refs_7_), channel_id=1, source_target_pairs={{0,4},{4,0},{8,12},{12,8},{1,5},{5,1},{9,13},{13,9},{2,6},{6,2},{1... | collective-permute-start | bytes 294920 | tf_op jit(solution)/shard_map/ppermute | solution.py:536
  45.9 2.1 %collective-permute-start.20 = (bf16[32,1536]{1,0:T(8,128)(2,1)S(1)}, bf16[32,1536]{1,0:T(8,128)(2,1)S(1)}, u32[]{:S(2)}, u32[]{:S(2)}) collective-permute-start(bf16[32,1536]{1,0:T(8,128)(2,1)S(1)} %collective-permute-done.16.refs_8_.refs_12_), channel_id=1, source_target_pairs={{0,4},{4,0},{8,12},{12,8},{1,5},{5,1},{9,13},{13,9},{2,6},{6,2},{1... | collective-permute-start | bytes 294920 | tf_op jit(solution)/shard_map/ppermute | solution.py:536
  47.3 1.3 %collective-permute-start.21 = (bf16[32,1536]{1,0:T(8,128)(2,1)S(1)}, bf16[32,1536]{1,0:T(8,128)(2,1)S(1)}, u32[]{:S(2)}, u32[]{:S(2)}) collective-permute-start(bf16[32,1536]{1,0:T(8,128)(2,1)S(1)} %collective-permute-done.17.refs_9_.refs_13_), channel_id=1, source_target_pairs={{0,4},{4,0},{8,12},{12,8},{1,5},{5,1},{9,13},{13,9},{2,6},{6,2},{1... | collective-permute-start | bytes 294920 | tf_op jit(solution)/shard_map/ppermute | solution.py:536
  47.3 1.5 %collective-permute-start.22 = (bf16[32,1536]{1,0:T(8,128)(2,1)S(1)}, bf16[32,1536]{1,0:T(8,128)(2,1)S(1)}, u32[]{:S(2)}, u32[]{:S(2)}) collective-permute-start(bf16[32,1536]{1,0:T(8,128)(2,1)S(1)} %collective-permute-done.18.refs_10_.refs_14_), channel_id=1, source_target_pairs={{0,4},{4,0},{8,12},{12,8},{1,5},{5,1},{9,13},{13,9},{2,6},{6,2},{1... | collective-permute-start | bytes 294920 | tf_op jit(solution)/shard_map/ppermute | solution.py:536
  47.9 1.3 %collective-permute-start.23 = (bf16[32,1536]{1,0:T(8,128)(2,1)S(1)}, bf16[32,1536]{1,0:T(8,128)(2,1)S(1)}, u32[]{:S(2)}, u32[]{:S(2)}) collective-permute-start(bf16[32,1536]{1,0:T(8,128)(2,1)S(1)} %collective-permute-done.19.refs_11_.refs_15_), channel_id=1, source_target_pairs={{0,4},{4,0},{8,12},{12,8},{1,5},{5,1},{9,13},{13,9},{2,6},{6,2},{1... | collective-permute-start | bytes 294920 | tf_op jit(solution)/shard_map/ppermute | solution.py:536
  51.0 2.8 %copy-start.8 = (s32[4,1,2]{0,2,1:T(2,128)S(1)}, s32[4,1,2]{0,2,1:T(2,128)}, u32[]{:S(2)}) copy-start(s32[4,1,2]{0,2,1:T(2,128)} %param.29) | copy-start | bytes 100
  51.1 3.0 %copy-start.6 = (s32[4,1,2,32]{3,2,1,0:T(2,128)S(1)}, s32[4,1,2,32]{3,2,1,0:T(2,128)}, u32[]{:S(2)}) copy-start(s32[4,1,2,32]{3,2,1,0:T(2,128)} %lists_ref.1) | copy-start | bytes 3076
  51.1 1.6 %collective-permute-start.24 = (bf16[128,1024]{1,0:T(8,128)(2,1)S(1)}, bf16[128,1024]{1,0:T(8,128)(2,1)S(1)}, u32[]{:S(2)}, u32[]{:S(2)}) collective-permute-start(bf16[128,1024]{1,0:T(8,128)(2,1)S(1)} %get-tuple-element.47), channel_id=1, source_target_pairs={{0,4},{4,0},{8,12},{12,8},{1,5},{5,1},{9,13},{13,9},{2,6},{6,2},{1... | collective-permute-start | bytes 786440 | tf_op jit(solution)/shard_map/ppermute | solution.py:536
  52.7 8.4 %collective-permute-start.25 = (bf16[128,1024]{1,0:T(8,128)(2,1)S(1)}, bf16[128,1024]{1,0:T(8,128)(2,1)S(1)}, u32[]{:S(2)}, u32[]{:S(2)}) collective-permute-start(bf16[128,1024]{1,0:T(8,128)(2,1)S(1)} %join_hot.1.after), channel_id=1, source_target_pairs={{0,8},{4,12},{8,0},{12,4},{1,9},{5,13},{9,1},{13,5},{2,10},{6,14},... | collective-permute-start | bytes 786440 | tf_op jit(solution)/shard_map/ppermute | solution.py:536
  54.0 1.9 %copy-start.3 = (bf16[2,6144,128]{2,1,0:T(8,128)(2,1)S(1)}, bf16[2,6144,128]{2,1,0:T(8,128)(2,1)}, u32[]{:S(2)}) copy-start(bf16[2,6144,128]{2,1,0:T(8,128)(2,1)} %up_ref.1) | copy-start | bytes 9437188
  55.9 1.9 %copy-start.4 = (bf16[2,128,6144]{2,1,0:T(8,128)(2,1)S(1)}, bf16[2,128,6144]{2,1,0:T(8,128)(2,1)}, u32[]{:S(2)}) copy-start(bf16[2,128,6144]{2,1,0:T(8,128)(2,1)} %down_ref.1) | copy-start | bytes 9437188
  61.2 2.5 %collective-permute-start.26 = (bf16[2,128,1536]{2,1,0:T(8,128)(2,1)}, bf16[2,128,1536]{2,1,0:T(8,128)(2,1)S(1)}, u32[]{:S(2)}, u32[]{:S(2)}) collective-permute-start(bf16[2,128,1536]{2,1,0:T(8,128)(2,1)} %get-tuple-element.56), channel_id=1, source_target_pairs={{0,4},{4,0},{8,12},{12,8},{1,5},{5,1},{9,13},{13,9},{2,6},{6,2},{1... | collective-permute-start | bytes 2359304 | tf_op jit(solution)/shard_map/ppermute | solution.py:536
  61.4 4.6 %collective-permute-start.27 = (bf16[128,1024]{1,0:T(8,128)(2,1)S(1)}, bf16[128,1024]{1,0:T(8,128)(2,1)S(1)}, u32[]{:S(2)}, u32[]{:S(2)}) collective-permute-start(bf16[128,1024]{1,0:T(8,128)(2,1)S(1)} %maximum_convert_fusion.hidden_ref), channel_id=1, source_target_pairs={{0,4},{4,0},{8,12},{12,8},{1,5},{5,1},{9,13},{13,9},{2,6},{6,2},{1... | collective-permute-start | bytes 786440 | tf_op jit(solution)/shard_map/ppermute | solution.py:536
  63.8 7.8 %collective-permute-start.28 = (bf16[64,1536]{1,0:T(8,128)(2,1)S(1)}, bf16[64,1536]{1,0:T(8,128)(2,1)S(1)}, u32[]{:S(2)}, u32[]{:S(2)}) collective-permute-start(bf16[64,1536]{1,0:T(8,128)(2,1)S(1)} %get-tuple-element.59), channel_id=1, source_target_pairs={{0,8},{4,12},{8,0},{12,4},{1,9},{5,13},{9,1},{13,5},{2,10},{6,14},... | collective-permute-start | bytes 589832 | tf_op jit(solution)/shard_map/ppermute | solution.py:536
  64.9 10.1 %collective-permute-start.29 = (bf16[64,1536]{1,0:T(8,128)(2,1)S(1)}, bf16[64,1536]{1,0:T(8,128)(2,1)S(1)}, u32[]{:S(2)}, u32[]{:S(2)}) collective-permute-start(bf16[64,1536]{1,0:T(8,128)(2,1)S(1)} %get-tuple-element.62), channel_id=1, source_target_pairs={{0,8},{4,12},{8,0},{12,4},{1,9},{5,13},{9,1},{13,5},{2,10},{6,14},... | collective-permute-start | bytes 589832 | tf_op jit(solution)/shard_map/ppermute | solution.py:536
  65.9 2.8 %copy-start.1 = (bf16[16,128,1536]{2,1,0:T(8,128)(2,1)S(1)}, bf16[16,128,1536]{2,1,0:T(8,128)(2,1)}, u32[]{:S(2)}) copy-start(bf16[16,128,1536]{2,1,0:T(8,128)(2,1)} %hot_ref.1) | copy-start | bytes 18874372
  71.6 10.5 %collective-permute-start.30 = (bf16[32,1536]{1,0:T(8,128)(2,1)S(1)}, bf16[32,1536]{1,0:T(8,128)(2,1)S(1)}, u32[]{:S(2)}, u32[]{:S(2)}) collective-permute-start(bf16[32,1536]{1,0:T(8,128)(2,1)S(1)} %get-tuple-element.61), channel_id=1, source_target_pairs={{0,3},{1,2},{2,1},{3,0},{4,7},{5,6},{6,5},{7,4},{8,11},{9,10},{10,... | collective-permute-start | bytes 294920 | tf_op jit(solution)/shard_map/ppermute | solution.py:536
  74.0 8.1 %collective-permute-start.31 = (bf16[32,1536]{1,0:T(8,128)(2,1)S(1)}, bf16[32,1536]{1,0:T(8,128)(2,1)S(1)}, u32[]{:S(2)}, u32[]{:S(2)}) collective-permute-start(bf16[32,1536]{1,0:T(8,128)(2,1)S(1)} %get-tuple-element.60), channel_id=1, source_target_pairs={{0,2},{1,3},{2,0},{3,1},{4,6},{5,7},{6,4},{7,5},{8,10},{9,11},{10,... | collective-permute-start | bytes 294920 | tf_op jit(solution)/shard_map/ppermute | solution.py:536
  75.0 7.1 %collective-permute-start.32 = (bf16[32,1536]{1,0:T(8,128)(2,1)S(1)}, bf16[32,1536]{1,0:T(8,128)(2,1)S(1)}, u32[]{:S(2)}, u32[]{:S(2)}) collective-permute-start(bf16[32,1536]{1,0:T(8,128)(2,1)S(1)} %get-tuple-element.65), channel_id=1, source_target_pairs={{0,1},{1,0},{2,3},{3,2},{4,5},{5,4},{6,7},{7,6},{8,9},{9,8},{10,11... | collective-permute-start | bytes 294920 | tf_op jit(solution)/shard_map/ppermute | solution.py:536
